TPU v7x, 32 devices: a whole 2x2x4 slice. The times are simulated.
32 devices in a mesh: dp: 16 (over z, y, core), tensor: 2 (over x).
Axes of the slice: x: 2, y: 2, z: 4, core: 2. Of those that a mesh axis runs over, the one named last changes fastest.
Arguments:
- inputs: bfloat16 [4096, 1536], P(('dp', 'tensor')), may hold values from -6 to 6
- clip_ids: int32 [4096], P('dp'), may hold values from 0 to 2, as said below
- positions: int32 [4096], P('dp'), may hold values from 0 to 4095
- text_tokens: bfloat16 [768, 4096], P('dp'), may hold values from -6 to 6
- conditioning: bfloat16 [3, 1024], replicated, may hold values from -6 to 6
- ada_weight: bfloat16 [1024, 9216], P('dp'), may hold values from -0.1875 to 0.1875
- ada_bias: bfloat16 [9216], replicated, may hold values from -4 to 4
- first_norm_gain: bfloat16 [1536], replicated, may hold values from 0.25 to 1.75
- query_gain: bfloat16 [64], replicated, may hold values from 0.25 to 1.75
- key_gain: bfloat16 [64], replicated, may hold values from 0.25 to 1.75
- text_key_gain: bfloat16 [64], replicated, may hold values from 0.25 to 1.75
- head_gate: bfloat16 [24], replicated, may hold values from 0.19921875 to 1.5
- qkv_weight: bfloat16 [3, 1536, 1536], P(None, 'dp', 'tensor'), may hold values from -0.15625 to 0.15625
- out_weight: bfloat16 [1536, 1536], P('tensor', 'dp'), may hold values from -2.5 to 2.5
- text_kv_weight: bfloat16 [2, 4096, 1536], P(None, 'dp', 'tensor'), may hold values from -0.09375 to 0.09375
- second_norm_gain: bfloat16 [1536], replicated, may hold values from 0.25 to 1.75
- gate_up_weight: bfloat16 [2, 1536, 4096], P(None, 'dp', 'tensor'), may hold values from -0.15625 to 0.15625
- down_weight: bfloat16 [4096, 1536], P('tensor', 'dp'), may hold values from -0.09375 to 0.09375
- grad_output: bfloat16 [4096, 1536], P(('dp', 'tensor')), may hold values from -6 to 6
Outputs:
- output: bfloat16 [4096, 1536], P(('dp', 'tensor'))
- grad_inputs: float32 [4096, 1536], P(('dp', 'tensor'))
- grad_text: float32 [768, 4096], P('dp', 'tensor')
- grad_conditioning: float32 [3, 1024], replicated
- grad_ada_weight: float32 [1024, 9216], P('dp')
- grad_ada_bias: float32 [9216], replicated
- grad_first_gain: float32 [1536], replicated
- grad_query_gain: float32 [64], replicated
- grad_key_gain: float32 [64], replicated
- grad_text_key_gain: float32 [64], replicated
- grad_head_gate: float32 [24], replicated
- grad_qkv_weight: float32 [3, 1536, 1536], P(None, 'dp', 'tensor')
- grad_out_weight: float32 [1536, 1536], P('tensor', 'dp')
- grad_text_kv_weight: float32 [2, 4096, 1536], P(None, 'dp', 'tensor')
- grad_second_gain: float32 [1536], replicated
- grad_gate_up_weight: float32 [2, 1536, 4096], P(None, 'dp', 'tensor')
- grad_down_weight: float32 [4096, 1536], P('tensor', 'dp')
Inputs may be any that keep to these rules, and one draw needn't show every extreme that they name: `clip_ids`: in block j of 256 rows (one index of dp), the rows of clip 0 come first, at least 128 and at most 224 of them, and all other rows belong to clip 1 + j // 8.
All inputs are finite; a program needn't handle non-finite values.
Results may differ from a plain program's by a relative error of at most 0.019.
Values may be sent and summed in bfloat16 or wider, within the bound.
No kernel may reach another device: no remote copies, remote signals or barrier semaphores. Data moves between devices by JAX's collectives and lax.ppermute only.
A program may use at most 384 MiB of HBM per device.

v0:
```python
import jax
import jax.numpy as jnp
from jax import lax
from jax.sharding import PartitionSpec as P

TXT = 256


eps_norm = 1e-06
neg_fill = -1e30
highest = lax.Precision.HIGHEST


def norm_rows(values, gains):
    return values * lax.rsqrt(jnp.mean(values * values, axis=-1, keepdims=True) + eps_norm) * gains


def rotate(values, cosine_table, sine_table):
    half_size = values.shape[-1] // 2
    former = values[..., :half_size]
    latter = values[..., half_size:]
    cosine = cosine_table[:, None, :]
    sine_part = sine_table[:, None, :]
    return jnp.concatenate(
        [former * cosine - latter * sine_part, latter * cosine + former * sine_part], axis=-1
    )


def rope_tables(positions, head_size):
    half_size = head_size // 2
    frequency = 10000.0 ** (-(jnp.arange(half_size, dtype=jnp.float32) * 2.0 / head_size))
    angles = positions.astype(jnp.float32)[:, None] * frequency[None, :]
    return (jnp.cos(angles), jnp.sin(angles))


def modulated(values, gains, shifts, scales):
    return norm_rows(values, gains) * (1.0 + scales) + shifts


def dot_float(left, right):
    return jnp.dot(left, right, preferred_element_type=jnp.float32)


def contract(formula, left, right):
    return jnp.einsum(formula, left, right, preferred_element_type=jnp.float32)


def gather_rows(values):
    return lax.all_gather(values, "tensor", axis=0, tiled=True)


def sum_rows(values):
    return lax.psum_scatter(
        values.astype(jnp.bfloat16), "tensor", scatter_dimension=0, tiled=True
    ).astype(jnp.float32)


def gather_grads(values):
    return lax.all_gather(values, "tensor", axis=0, tiled=True)


def sum_grads(values):
    return lax.psum_scatter(
        values.astype(jnp.bfloat16), "tensor", scatter_dimension=0, tiled=True
    ).astype(jnp.float32)


def block_size(total_rows):
    size_now = 1024
    while total_rows % size_now:
        size_now //= 2
    return size_now


def masked_scores(queries, key_block, query_ids, key_ids, score_scale):
    scores = contract("qhd,khd->hqk", queries, key_block) * score_scale
    keep_mask = (query_ids[:, None] == key_ids[None, :])[None]
    return (jnp.where(keep_mask, scores, neg_fill), keep_mask)


def shards(
    inputs,
    clip_ids,
    positions,
    text_tokens,
    conditioning,
    ada_weight,
    ada_bias,
    first_norm_gain,
    query_gain,
    key_gain,
    text_key_gain,
    head_gate,
    qkv_weight,
    out_weight,
    text_kv_weight,
    second_norm_gain,
    gate_up_weight,
    down_weight,
    grad_output,
):
    tensor_index = lax.axis_index("tensor")
    dp_index = lax.axis_index("dp")
    row_count = inputs.shape[0]
    token_count = clip_ids.shape[0]
    head_size = query_gain.shape[0]
    local_heads = qkv_weight.shape[2] // head_size
    local_width = local_heads * head_size
    clip_count = conditioning.shape[0]
    score_scale = head_size ** (-0.5)
    qkv_full, out_full, text_full, gate_up_full, down_full, ada_full = (
        lax.all_gather(qkv_weight, "dp", axis=1, tiled=True),
        lax.all_gather(out_weight, "dp", axis=1, tiled=True),
        lax.all_gather(text_kv_weight, "dp", axis=1, tiled=True),
        lax.all_gather(gate_up_weight, "dp", axis=1, tiled=True),
        lax.all_gather(down_weight, "dp", axis=1, tiled=True),
        lax.all_gather(ada_weight, "dp", axis=0, tiled=True),
    )
    cond_float = conditioning.astype(jnp.float32)
    silu_cond = jax.nn.silu(cond_float).astype(jnp.bfloat16)
    modulation = dot_float(silu_cond, ada_full) + ada_bias.astype(jnp.float32)
    row_ids = lax.dynamic_slice_in_dim(clip_ids, tensor_index * row_count, row_count)
    one_hot = (row_ids[:, None] == jnp.arange(clip_count, dtype=jnp.int32)[None, :]).astype(
        jnp.float32
    )
    token_mod = jnp.dot(one_hot, modulation, precision=highest, preferred_element_type=jnp.float32)
    shift_one, scale_one, gate_one, shift_two, scale_two, gate_two = jnp.split(token_mod, 6, axis=1)
    input_rows = inputs.astype(jnp.float32)
    first_gain = first_norm_gain.astype(jnp.float32)
    normed_one = modulated(input_rows, first_gain, shift_one, scale_one).astype(jnp.bfloat16)
    normed_all = gather_rows(normed_one)
    query_raw = dot_float(normed_all, qkv_full[0]).reshape(token_count, local_heads, head_size)
    key_raw = dot_float(normed_all, qkv_full[1]).reshape(token_count, local_heads, head_size)
    value_flat = dot_float(normed_all, qkv_full[2]).astype(jnp.bfloat16)
    cosine_table, sine_table = rope_tables(positions, head_size)
    q_gain = query_gain.astype(jnp.float32)
    k_gain = key_gain.astype(jnp.float32)
    ky_gain = text_key_gain.astype(jnp.float32)

    def rotate_heads(raw_heads, gains):
        return rotate(norm_rows(raw_heads, gains), cosine_table, sine_table)

    query_heads = rotate_heads(query_raw, q_gain).astype(jnp.bfloat16)
    key_heads = rotate_heads(key_raw, k_gain).astype(jnp.bfloat16)
    text_rows = text_tokens.shape[0]
    text_key_raw = dot_float(text_tokens, text_full[0]).reshape(text_rows, local_heads, head_size)
    text_key_flat = (
        norm_rows(text_key_raw, ky_gain).astype(jnp.bfloat16).reshape(text_rows, local_width)
    )
    text_value_flat = dot_float(text_tokens, text_full[1]).astype(jnp.bfloat16)
    text_key_all, text_value_all = (
        lax.all_gather(text_key_flat, "dp", axis=0, tiled=True),
        lax.all_gather(text_value_flat, "dp", axis=0, tiled=True),
    )
    text_total = text_key_all.shape[0]
    other_clip = jnp.max(clip_ids)

    def two_clips(table):
        joined = jnp.concatenate(
            [table[:TXT], lax.dynamic_slice_in_dim(table, other_clip * TXT, TXT)], axis=0
        )
        return joined.reshape(2 * TXT, local_heads, head_size)

    cross_keys = two_clips(text_key_all)
    cross_values = two_clips(text_value_all)
    cross_ids = jnp.concatenate(
        [jnp.zeros((TXT,), jnp.int32), jnp.full((TXT,), other_clip, jnp.int32)]
    )
    cross_scores, cross_mask = masked_scores(
        query_heads, cross_keys, clip_ids, cross_ids, score_scale
    )
    cross_max = jnp.max(cross_scores, axis=-1, keepdims=True)
    cross_exp = jnp.where(cross_mask, jnp.exp(cross_scores - cross_max), 0.0)
    cross_probs = cross_exp / jnp.sum(cross_exp, axis=-1, keepdims=True)
    cross_low = cross_probs.astype(jnp.bfloat16)
    cross_out = contract("hqk,khd->qhd", cross_low, cross_values)
    key_all, value_all, key_ids = (
        lax.all_gather(key_heads.reshape(token_count, local_width), "dp", axis=0, tiled=True),
        lax.all_gather(value_flat, "dp", axis=0, tiled=True),
        lax.all_gather(clip_ids, "dp", axis=0, tiled=True),
    )
    total_rows = key_all.shape[0]
    block_rows = block_size(total_rows)
    block_count = total_rows // block_rows
    key_blocks = key_all.reshape(block_count, block_rows, local_heads, head_size)
    value_blocks = value_all.reshape(block_count, block_rows, local_heads, head_size)
    id_blocks = key_ids.reshape(block_count, block_rows)

    def stats_step(state_pair, block_data):
        running_max, running_sum = state_pair
        key_block, id_block = block_data
        scores, keep_mask = masked_scores(query_heads, key_block, clip_ids, id_block, score_scale)
        new_max = jnp.maximum(running_max, jnp.max(scores, axis=-1))
        weights = jnp.where(keep_mask, jnp.exp(scores - new_max[..., None]), 0.0)
        new_sum = running_sum * jnp.exp(running_max - new_max) + jnp.sum(weights, axis=-1)
        return ((new_max, new_sum), None)

    start_state = (
        jnp.full((local_heads, token_count), neg_fill, jnp.float32),
        jnp.zeros((local_heads, token_count), jnp.float32),
    )
    (row_max, row_sum), _ = lax.scan(stats_step, start_state, (key_blocks, id_blocks))
    log_total = row_max + jnp.log(row_sum)

    def value_step(running_out, block_data):
        key_block, value_block, id_block = block_data
        scores, keep_mask = masked_scores(query_heads, key_block, clip_ids, id_block, score_scale)
        probs_low = jnp.where(keep_mask, jnp.exp(scores - log_total[..., None]), 0.0).astype(
            jnp.bfloat16
        )
        return (running_out + contract("hqk,khd->qhd", probs_low, value_block), None)

    self_out, _ = lax.scan(
        value_step,
        jnp.zeros((token_count, local_heads, head_size), jnp.float32),
        (key_blocks, value_blocks, id_blocks),
    )
    gate_heads = jnp.tanh(
        lax.dynamic_slice_in_dim(
            head_gate.astype(jnp.float32), tensor_index * local_heads, local_heads
        )
    )
    mixed_low = (
        (self_out + gate_heads[None, :, None] * cross_out)
        .astype(jnp.bfloat16)
        .reshape(token_count, local_width)
    )
    attn_rows = sum_rows(dot_float(mixed_low, out_full))
    after_attn = input_rows + gate_one * attn_rows
    second_gain = second_norm_gain.astype(jnp.float32)
    normed_two = modulated(after_attn, second_gain, shift_two, scale_two).astype(jnp.bfloat16)
    normed_two_all = gather_rows(normed_two)
    gate_values = dot_float(normed_two_all, gate_up_full[0])
    up_values = dot_float(normed_two_all, gate_up_full[1])
    hidden_low = (jax.nn.silu(gate_values) * up_values).astype(jnp.bfloat16)
    ffn_rows = sum_rows(dot_float(hidden_low, down_full))
    result_rows = after_attn + gate_two * ffn_rows
    output = result_rows.astype(jnp.bfloat16)
    grad_two = grad_output.astype(jnp.float32)
    grad_ffn = gather_grads((gate_two * grad_two).astype(jnp.bfloat16))
    grad_gate_two = grad_two * ffn_rows
    grad_hidden = contract("tc,fc->tf", grad_ffn, down_full)
    grad_down = contract("tf,tc->fc", hidden_low, grad_ffn)
    sigmoid_gate = jax.nn.sigmoid(gate_values)
    grad_gate_low = (
        grad_hidden * up_values * sigmoid_gate * (1.0 + gate_values * (1.0 - sigmoid_gate))
    ).astype(jnp.bfloat16)
    grad_up_low = (grad_hidden * gate_values * sigmoid_gate).astype(jnp.bfloat16)
    grad_gate_up = jnp.stack(
        [
            contract("td,tf->df", normed_two_all, grad_gate_low),
            contract("td,tf->df", normed_two_all, grad_up_low),
        ]
    )
    grad_normed_two = sum_grads(
        contract("tf,df->td", grad_gate_low, gate_up_full[0])
        + contract("tf,df->td", grad_up_low, gate_up_full[1])
    )
    _, pull_two = jax.vjp(modulated, after_attn, second_gain, shift_two, scale_two)
    back_two, grad_second_gain, grad_shift_two, grad_scale_two = pull_two(grad_normed_two)
    grad_after = grad_two + back_two
    grad_attn = gather_grads((gate_one * grad_after).astype(jnp.bfloat16))
    grad_gate_one = grad_after * attn_rows
    grad_out_full = contract("tc,td->cd", mixed_low, grad_attn)
    grad_mixed = (
        contract("td,cd->tc", grad_attn, out_full)
        .astype(jnp.bfloat16)
        .reshape(token_count, local_heads, head_size)
    )
    grad_cross = (gate_heads[None, :, None] * grad_mixed.astype(jnp.float32)).astype(jnp.bfloat16)
    grad_heads = (1.0 - gate_heads * gate_heads) * jnp.sum(
        grad_mixed.astype(jnp.float32) * cross_out, axis=(0, 2)
    )
    grad_cross_probs = contract("qhd,khd->hqk", grad_cross, cross_values)
    grad_cross_scores = (
        cross_probs
        * (grad_cross_probs - jnp.sum(cross_probs * grad_cross_probs, axis=-1, keepdims=True))
    ).astype(jnp.bfloat16)
    query_grad_cross = contract("hqk,khd->qhd", grad_cross_scores, cross_keys) * score_scale
    text_key_grad = contract("hqk,qhd->khd", grad_cross_scores, query_heads) * score_scale
    text_value_grad = contract("hqk,qhd->khd", cross_low, grad_cross)
    delta_rows = jnp.sum(grad_mixed.astype(jnp.float32) * self_out, axis=-1).T
    query_start = jnp.zeros((token_count, local_heads, head_size), jnp.float32)

    def grad_step(query_total, block_data):
        key_block, value_block, id_block = block_data
        scores, keep_mask = masked_scores(query_heads, key_block, clip_ids, id_block, score_scale)
        probs = jnp.where(keep_mask, jnp.exp(scores - log_total[..., None]), 0.0)
        value_grad = contract("hqk,qhd->khd", probs.astype(jnp.bfloat16), grad_mixed)
        prob_grad = contract("qhd,khd->hqk", grad_mixed, value_block)
        score_grad = (probs * (prob_grad - delta_rows[..., None])).astype(jnp.bfloat16)
        query_total = query_total + contract("hqk,khd->qhd", score_grad, key_block) * score_scale
        key_grad = contract("hqk,qhd->khd", score_grad, query_heads) * score_scale
        return (query_total, (key_grad, value_grad))

    query_grad_self, (key_grads, value_grads) = lax.scan(
        grad_step, query_start, (key_blocks, value_blocks, id_blocks)
    )
    key_grad_sum, value_grad_sum = (
        lax.psum_scatter(
            key_grads.reshape(total_rows, local_width), "dp", scatter_dimension=0, tiled=True
        ),
        lax.psum_scatter(
            value_grads.reshape(total_rows, local_width), "dp", scatter_dimension=0, tiled=True
        ),
    )
    query_grad_low = (query_grad_self + query_grad_cross).astype(jnp.bfloat16).astype(jnp.float32)
    _, pull_query = jax.vjp(rotate_heads, query_raw, q_gain)
    query_raw_grad, grad_q_gain = pull_query(query_grad_low)
    query_raw_low = query_raw_grad.astype(jnp.bfloat16).reshape(token_count, local_width)
    key_grad_low = (
        key_grad_sum.reshape(token_count, local_heads, head_size)
        .astype(jnp.bfloat16)
        .astype(jnp.float32)
    )
    _, pull_key = jax.vjp(rotate_heads, key_raw, k_gain)
    key_raw_grad, grad_k_gain = pull_key(key_grad_low)
    key_raw_low = key_raw_grad.astype(jnp.bfloat16).reshape(token_count, local_width)
    value_grad_low = value_grad_sum.astype(jnp.bfloat16)

    def place_rows(block_grad):
        flat_grad = block_grad.reshape(2 * TXT, local_width)
        buffer = jnp.zeros((text_total, local_width), jnp.float32)
        buffer = lax.dynamic_update_slice_in_dim(buffer, flat_grad[TXT:], other_clip * TXT, 0)
        return lax.dynamic_update_slice_in_dim(buffer, flat_grad[:TXT], 0, 0)

    text_key_sum, text_value_sum = (
        lax.psum_scatter(place_rows(text_key_grad), "dp", scatter_dimension=0, tiled=True),
        lax.psum_scatter(place_rows(text_value_grad), "dp", scatter_dimension=0, tiled=True),
    )
    text_key_low = (
        text_key_sum.reshape(text_rows, local_heads, head_size)
        .astype(jnp.bfloat16)
        .astype(jnp.float32)
    )
    _, pull_text = jax.vjp(norm_rows, text_key_raw, ky_gain)
    text_raw_grad, grad_ky_gain = pull_text(text_key_low)
    text_raw_low = text_raw_grad.astype(jnp.bfloat16).reshape(text_rows, local_width)
    text_value_low = text_value_sum.astype(jnp.bfloat16)
    grad_text_kv = jnp.stack(
        [
            contract("rc,rd->cd", text_tokens, text_raw_low),
            contract("rc,rd->cd", text_tokens, text_value_low),
        ]
    )
    grad_text_part = contract("rd,cd->rc", text_raw_low, text_full[0]) + contract(
        "rd,cd->rc", text_value_low, text_full[1]
    )
    grad_text = lax.psum_scatter(
        grad_text_part.astype(jnp.bfloat16), "tensor", scatter_dimension=1, tiled=True
    ).astype(jnp.float32)
    grad_qkv = jnp.stack(
        [
            contract("td,tc->dc", normed_all, query_raw_low),
            contract("td,tc->dc", normed_all, key_raw_low),
            contract("td,tc->dc", normed_all, value_grad_low),
        ]
    )
    grad_normed_one = sum_grads(
        contract("tc,dc->td", query_raw_low, qkv_full[0])
        + contract("tc,dc->td", key_raw_low, qkv_full[1])
        + contract("tc,dc->td", value_grad_low, qkv_full[2])
    )
    qkv_shard, out_shard, text_shard, gate_up_shard, down_shard = (
        lax.psum_scatter(grad_qkv, "dp", scatter_dimension=1, tiled=True),
        lax.psum_scatter(grad_out_full, "dp", scatter_dimension=1, tiled=True),
        lax.psum_scatter(grad_text_kv, "dp", scatter_dimension=1, tiled=True),
        lax.psum_scatter(grad_gate_up, "dp", scatter_dimension=1, tiled=True),
        lax.psum_scatter(grad_down, "dp", scatter_dimension=1, tiled=True),
    )
    _, pull_one = jax.vjp(modulated, input_rows, first_gain, shift_one, scale_one)
    back_one, grad_first_gain, grad_shift_one, grad_scale_one = pull_one(grad_normed_one)
    grad_inputs = grad_after + back_one
    grad_token_mod = jnp.concatenate(
        [
            grad_shift_one,
            grad_scale_one,
            grad_gate_one,
            grad_shift_two,
            grad_scale_two,
            grad_gate_two,
        ],
        axis=1,
    )
    grad_mod_part = jnp.dot(
        one_hot.T, grad_token_mod, precision=highest, preferred_element_type=jnp.float32
    )
    grad_gate_part = lax.dynamic_update_slice_in_dim(
        jnp.zeros((head_gate.shape[0],), jnp.float32), grad_heads, tensor_index * local_heads, 0
    )
    grad_mod, first_gain_sum, second_gain_sum, q_gain_sum, k_gain_sum, ky_gain_sum, gate_sum = (
        lax.psum(
            (
                grad_mod_part,
                grad_first_gain,
                grad_second_gain,
                grad_q_gain,
                grad_k_gain,
                grad_ky_gain,
                grad_gate_part,
            ),
            ("dp", "tensor"),
        )
    )
    grad_mod_low = grad_mod.astype(jnp.bfloat16)
    grad_ada_bias = jnp.sum(grad_mod_low.astype(jnp.float32), axis=0)
    cond_rows = ada_weight.shape[0]
    silu_slice = lax.dynamic_slice_in_dim(silu_cond, dp_index * cond_rows, cond_rows, axis=1)
    grad_ada = contract("cr,cm->rm", silu_slice, grad_mod_low)
    cond_sigmoid = jax.nn.sigmoid(cond_float)
    grad_conditioning = (
        contract("cm,rm->cr", grad_mod_low, ada_full)
        * cond_sigmoid
        * (1.0 + cond_float * (1.0 - cond_sigmoid))
    )
    return (
        output,
        grad_inputs,
        grad_text,
        grad_conditioning,
        grad_ada,
        grad_ada_bias,
        first_gain_sum,
        q_gain_sum,
        k_gain_sum,
        ky_gain_sum,
        gate_sum,
        qkv_shard,
        out_shard,
        text_shard,
        second_gain_sum,
        gate_up_shard,
        down_shard,
    )


def solution(mesh):
    placed = (
        P(("dp", "tensor"), None),
        P("dp"),
        P("dp"),
        P("dp", None),
        P(),
        P("dp", None),
        P(),
        P(),
        P(),
        P(),
        P(),
        P(),
        P(None, "dp", "tensor"),
        P("tensor", "dp"),
        P(None, "dp", "tensor"),
        P(),
        P(None, "dp", "tensor"),
        P("tensor", "dp"),
        P(("dp", "tensor"), None),
    )
    return jax.shard_map(
        shards,
        mesh=mesh,
        in_specs=placed,
        out_specs=(
            P(("dp", "tensor"), None),
            P(("dp", "tensor"), None),
            P("dp", "tensor"),
            P(),
            P("dp", None),
            P(),
            P(),
            P(),
            P(),
            P(),
            P(),
            P(None, "dp", "tensor"),
            P("tensor", "dp"),
            P(None, "dp", "tensor"),
            P(),
            P(None, "dp", "tensor"),
            P("tensor", "dp"),
        ),
        check_vma=False,
    )
```

profile of v0, /device:TPU:0, one launch (start us, length us, event | category | flops | bytes accessed | tf_op | source)
XLA Modules:
  0.0 2650.1 jit_solution(7936002723424203116)
XLA Ops:
  10.7 103.2 %all-gather.20.cloned.1.call-done = bf16[2,4096,768]{2,1,0:T(8,128)(2,1)} async-done(((bf16[2,256,768]{2,1,0:T(8,128)(2,1)}), bf16[2,4096,768]{2,1,0:T(8,128)(2,1)}) %all-gather.20.cloned.1.call-update) | async-done | bytes 12582928 | tf_op jit(solution)/shard_map/all_gather | solution.py:114
  118.7 6.5 slice_bitcast_fusion.9
  125.3 8.8 copy.88
  134.0 6.1 multiply_reduce_fusion.12
  141.9 70.7 %all-gather.12.cloned.1.call-done = bf16[1024,9216]{1,0:T(8,128)(2,1)} async-done(((bf16[64,9216]{1,0:T(8,128)(2,1)}), bf16[1024,9216]{1,0:T(8,128)(2,1)}) %all-gather.12.cloned.1.call-update) | async-done | bytes 18874384 | tf_op jit(solution)/shard_map/all_gather | solution.py:117
  212.6 8.9 convolution_add_fusion
  226.1 12.0 all_gather.46
  238.0 43.6 %all-gather.14.cloned.1.call-done = bf16[3,1536,768]{2,1,0:T(8,128)(2,1)} async-done(((bf16[3,96,768]{2,1,0:T(8,128)(2,1)}), bf16[3,1536,768]{2,1,0:T(8,128)(2,1)}) %all-gather.14.cloned.1.call-update) | async-done | bytes 7077904 | tf_op jit(solution)/shard_map/all_gather | solution.py:112
  309.4 18.9 all-gather
  328.6 32.6 %all-gather.24.cloned.1.call-done = bf16[768,768]{1,0:T(8,128)(2,1)} async-done(((bf16[48,768]{1,0:T(8,128)(2,1)}), bf16[768,768]{1,0:T(8,128)(2,1)}) %all-gather.24.cloned.1.call-update) | async-done | bytes 1179664 | tf_op jit(solution)/shard_map/all_gather | solution.py:152
  372.4 52.4 %all-gather.16.cloned.1.call-done = bf16[4096,768]{1,0:T(8,128)(2,1)} async-done(((bf16[256,768]{1,0:T(8,128)(2,1)}), bf16[4096,768]{1,0:T(8,128)(2,1)}) %all-gather.16.cloned.1.call-update) | async-done | bytes 6291472 | tf_op jit(solution)/shard_map/all_gather | solution.py:179
  424.8 8.9 copy.81
  433.7 11.2 reshape.368
  444.9 7.5 copy.85
  452.4 39.4 %all-gather.18.cloned.1.call-done = bf16[4096,768]{0,1:T(8,128)(2,1)} async-done(((bf16[256,768]{0,1:T(8,128)(2,1)}), bf16[4096,768]{0,1:T(8,128)(2,1)}) %all-gather.18.cloned.1.call-update) | async-done | bytes 6291472 | tf_op jit(solution)/shard_map/all_gather | solution.py:178
  491.8 11.2 reshape.370
  503.0 7.5 copy.86
  510.5 28.3 %while.39 = (s32[]{:T(128)}, f32[12,256]{1,0:T(8,128)S(1)}, f32[12,256]{1,0:T(8,128)S(1)}, s32[256]{0:T(256)S(1)}, s32[4,1024]{1,0:T(4,128)S(1)}, /*index=5*/bf1...) while((s32[]{:T(128)}, f32[12,256]{1,0:T(8,128)S(1)}, ...), condition=%wide.region_6.7_spmd.clone, body=%wide.region_3.6_spmd.clone.sunk | while | flops 428096512 | bytes 28091512 | solution.py:202
  538.8 30.4 %while.40 = (s32[]{:T(128)}, f32[256,12,64]{0,2,1:T(8,128)}, bf16[4,1024,12,64]{1,3,2,0:T(8,128)(2,1)}, s32[256]{0:T(256)S(1)}, s32[4,1024]{1,0:T(4,128)S(1)}, /...) while((s32[]{:T(128)}, f32[256,12,64]{0,2,1:T(8,128)}, ...), condition=%wide.region_8.9_spmd.clone, body=%wide.region_7.8_spmd.clone.sunk | while | flops 821690368 | bytes 5663354 | solution.py:213
  539.5 7.1 fusion.267
  546.8 7.3 fusion.267
  554.3 7.3 fusion.267
  561.9 7.3 fusion.267
  579.3 14.6 reduce-scatter.15.cloned.1.call-done
  597.7 11.5 all_gather.58
  609.2 10.9 all_gather.55
  620.1 77.0 %all-gather.28.cloned.1.call-done = bf16[2,1536,2048]{2,1,0:T(8,128)(2,1)} async-done(((bf16[2,96,2048]{2,1,0:T(8,128)(2,1)}), bf16[2,1536,2048]{2,1,0:T(8,128)(2,1)}) %all-gather.28.cloned.1.call-update) | async-done | bytes 12582928 | tf_op jit(solution)/shard_map/all_gather | solution.py:115
  697.1 5.9 fusion.82
  703.0 6.1 fusion.80
  709.1 50.6 %all-gather.30.cloned.1.call-done = bf16[2048,1536]{0,1:T(8,128)(2,1)} async-done(((bf16[2048,96]{0,1:T(8,128)(2,1)}), bf16[2048,1536]{0,1:T(8,128)(2,1)}) %all-gather.30.cloned.1.call-update) | async-done | bytes 6291472 | tf_op jit(solution)/shard_map/all_gather | solution.py:116
  759.7 7.6 multiply_convert_fusion.1
  775.9 5.8 convolution_convert_fusion.1
  781.8 10.2 reduce-scatter.19.cloned.1.call-done
  794.1 18.2 reduce-scatter.17.cloned.1.call-done
  815.8 11.7 all_gather.59
  853.6 594.3 %while.41 = (s32[]{:T(128)}, f32[256,12,64]{0,2,1:T(8,128)}, f32[4,1024,12,64]{1,0,3,2:T(4,128)}, f32[4,1024,12,64]{1,0,3,2:T(4,128)}, bf16[4,1024,12,64]{1,3,2,...) while((s32[]{:T(128)}, f32[256,12,64]{0,2,1:T(8,128)}, ...), condition=%wide.region_20.21_spmd.clone, body=%wide.region_19.20_spmd.clone.sunk | while | flops 2052653056 | bytes 96834760 | solution.py:296
  887.5 57.8 %dynamic_update_slice.36 = f32[4,1024,12,64]{1,0,3,2:T(4,128)} dynamic-update-slice(f32[4,1024,12,64]{1,0,3,2:T(4,128)} %get-tuple-element.752, f32[1,1024,12,64]{1,0,3,2:T(1,128)} %copy.143, s32[]{:T(128)S(6)} %copy.166, s32[]{:T(128)} %constant.62.clone.1..sunk.2, s32[]{:T(128)} %constant.62.clone.1..sunk.2, s32[]{:T(128)} %constant.62.clone.1..sunk.2) | dynamic-update-slice | bytes 6291460 | tf_op jit(solution)/shard_map/while/body/jit(dynamic_update_index_in_dim)/dynamic_update_slice | solution.py:296
  945.2 57.4 %dynamic_update_slice.37 = f32[4,1024,12,64]{1,0,3,2:T(4,128)} dynamic-update-slice(f32[4,1024,12,64]{1,0,3,2:T(4,128)} %get-tuple-element.753, f32[1,1024,12,64]{1,0,3,2:T(1,128)S(1)} %copy.144, s32[]{:T(128)S(6)} %copy.166, s32[]{:T(128)} %constant.62.clone.1..sunk.2, s32[]{:T(128)} %constant.62.clone.1..sunk.2, s32[]{:T(128)} %constant.62.clone.1..sunk.2) | dynamic-update-slice | bytes 6291460 | tf_op jit(solution)/shard_map/while/body/jit(dynamic_update_index_in_dim)/dynamic_update_slice | solution.py:296
  1013.2 5.8 fusion.279
  1036.0 57.6 %dynamic_update_slice.36 = f32[4,1024,12,64]{1,0,3,2:T(4,128)} dynamic-update-slice(f32[4,1024,12,64]{1,0,3,2:T(4,128)} %get-tuple-element.752, f32[1,1024,12,64]{1,0,3,2:T(1,128)} %copy.143, s32[]{:T(128)S(6)} %copy.166, s32[]{:T(128)} %constant.62.clone.1..sunk.2, s32[]{:T(128)} %constant.62.clone.1..sunk.2, s32[]{:T(128)} %constant.62.clone.1..sunk.2) | dynamic-update-slice | bytes 6291460 | tf_op jit(solution)/shard_map/while/body/jit(dynamic_update_index_in_dim)/dynamic_update_slice | solution.py:296
  1093.6 57.4 %dynamic_update_slice.37 = f32[4,1024,12,64]{1,0,3,2:T(4,128)} dynamic-update-slice(f32[4,1024,12,64]{1,0,3,2:T(4,128)} %get-tuple-element.753, f32[1,1024,12,64]{1,0,3,2:T(1,128)S(1)} %copy.144, s32[]{:T(128)S(6)} %copy.166, s32[]{:T(128)} %constant.62.clone.1..sunk.2, s32[]{:T(128)} %constant.62.clone.1..sunk.2, s32[]{:T(128)} %constant.62.clone.1..sunk.2) | dynamic-update-slice | bytes 6291460 | tf_op jit(solution)/shard_map/while/body/jit(dynamic_update_index_in_dim)/dynamic_update_slice | solution.py:296
  1161.6 5.8 fusion.279
  1184.3 57.6 %dynamic_update_slice.36 = f32[4,1024,12,64]{1,0,3,2:T(4,128)} dynamic-update-slice(f32[4,1024,12,64]{1,0,3,2:T(4,128)} %get-tuple-element.752, f32[1,1024,12,64]{1,0,3,2:T(1,128)} %copy.143, s32[]{:T(128)S(6)} %copy.166, s32[]{:T(128)} %constant.62.clone.1..sunk.2, s32[]{:T(128)} %constant.62.clone.1..sunk.2, s32[]{:T(128)} %constant.62.clone.1..sunk.2) | dynamic-update-slice | bytes 6291460 | tf_op jit(solution)/shard_map/while/body/jit(dynamic_update_index_in_dim)/dynamic_update_slice | solution.py:296
  1242.0 57.4 %dynamic_update_slice.37 = f32[4,1024,12,64]{1,0,3,2:T(4,128)} dynamic-update-slice(f32[4,1024,12,64]{1,0,3,2:T(4,128)} %get-tuple-element.753, f32[1,1024,12,64]{1,0,3,2:T(1,128)S(1)} %copy.144, s32[]{:T(128)S(6)} %copy.166, s32[]{:T(128)} %constant.62.clone.1..sunk.2, s32[]{:T(128)} %constant.62.clone.1..sunk.2, s32[]{:T(128)} %constant.62.clone.1..sunk.2) | dynamic-update-slice | bytes 6291460 | tf_op jit(solution)/shard_map/while/body/jit(dynamic_update_index_in_dim)/dynamic_update_slice | solution.py:296
  1309.9 5.8 fusion.279
  1332.7 57.6 %dynamic_update_slice.36 = f32[4,1024,12,64]{1,0,3,2:T(4,128)} dynamic-update-slice(f32[4,1024,12,64]{1,0,3,2:T(4,128)} %get-tuple-element.752, f32[1,1024,12,64]{1,0,3,2:T(1,128)} %copy.143, s32[]{:T(128)S(6)} %copy.166, s32[]{:T(128)} %constant.62.clone.1..sunk.2, s32[]{:T(128)} %constant.62.clone.1..sunk.2, s32[]{:T(128)} %constant.62.clone.1..sunk.2) | dynamic-update-slice | bytes 6291460 | tf_op jit(solution)/shard_map/while/body/jit(dynamic_update_index_in_dim)/dynamic_update_slice | solution.py:296
  1390.3 57.4 %dynamic_update_slice.37 = f32[4,1024,12,64]{1,0,3,2:T(4,128)} dynamic-update-slice(f32[4,1024,12,64]{1,0,3,2:T(4,128)} %get-tuple-element.753, f32[1,1024,12,64]{1,0,3,2:T(1,128)S(1)} %copy.144, s32[]{:T(128)S(6)} %copy.166, s32[]{:T(128)} %constant.62.clone.1..sunk.2, s32[]{:T(128)} %constant.62.clone.1..sunk.2, s32[]{:T(128)} %constant.62.clone.1..sunk.2) | dynamic-update-slice | bytes 6291460 | tf_op jit(solution)/shard_map/while/body/jit(dynamic_update_index_in_dim)/dynamic_update_slice | solution.py:296
  1447.9 21.9 copy.136
  1469.9 23.3 copy.137
  1503.0 6.7 fusion.75
  1509.7 5.8 fusion.86
  1515.7 89.1 %reduce-scatter.21.cloned.1.call-done = f32[256,768]{0,1:T(8,128)} async-done(((f32[4096,768]{0,1:T(8,128)}), f32[256,768]{0,1:T(8,128)}) %reduce-scatter.21.cloned.1.call-update) | async-done | bytes 786448 | tf_op jit(solution)/shard_map/reduce_scatter | solution.py:300
  1615.4 127.7 %reduce-scatter.23.cloned.1.call-done = f32[256,768]{0,1:T(8,128)} async-done(((f32[4096,768]{0,1:T(8,128)}), f32[256,768]{0,1:T(8,128)}) %reduce-scatter.23.cloned.1.call-update) | async-done | bytes 786448 | tf_op jit(solution)/shard_map/reduce_scatter | solution.py:303
  1750.9 8.6 pad_maximum_fusion
  1763.8 6.5 fusion.180
  1775.4 8.6 pad_maximum_fusion.1
  1794.8 18.1 pad_maximum_fusion.2
  1826.8 46.9 %all-reduce.7 = (bf16[3,9216]{1,0:T(4,128)(2,1)S(1)}, f32[1536]{0:T(1024)}, f32[64]{0:T(128)}, f32[64]{0:T(128)}, f32[64]{0:T(128)}, /*index=5*/f32[24]{0:T(128)}, f32[1536]{0:T(1024)}) all-reduce(f32[3,9216]{1,0:T(4,128)S(1)} %fusion.152, f32[1536]{0:T(1024)S(1)} %copy-done.71, ...), channel_id=1, replica_groups=mesh['dp'=16,'tensor'=2] {'dp','tensor'}, use_global_device_ids=true, to_apply=%region_32.33 | all-reduce | flops 30936 | bytes 192192 | tf_op jit(solution)/shard_map/psum | solution.py:392
  1877.2 12.6 fusion.115
  1889.8 137.8 %reduce-scatter.37.cloned.1.call-done = f32[2,256,768]{1,2,0:T(8,128)} async-done(((f32[2,4096,768]{1,2,0:T(8,128)}), f32[2,256,768]{1,2,0:T(8,128)}) %reduce-scatter.37.cloned.1.call-update) | async-done | bytes 1572880 | tf_op jit(solution)/shard_map/reduce_scatter | solution.py:367
  2030.6 76.6 %reduce-scatter.35.cloned.1.call-done = f32[768,96]{0,1:T(8,128)} async-done(((f32[768,1536]{0,1:T(8,128)}), f32[768,96]{0,1:T(8,128)}) %reduce-scatter.35.cloned.1.call-update) | async-done | bytes 294928 | tf_op jit(solution)/shard_map/reduce_scatter | solution.py:366
  2107.2 138.5 %reduce-scatter.41.cloned.1.call-done = f32[2048,96]{0,1:T(8,128)} async-done(((f32[2048,1536]{0,1:T(8,128)}), f32[2048,96]{0,1:T(8,128)}) %reduce-scatter.41.cloned.1.call-update) | async-done | bytes 786448 | tf_op jit(solution)/shard_map/reduce_scatter | solution.py:369
  2245.6 247.7 %reduce-scatter.39.cloned.1.call-done = f32[2,96,2048]{2,1,0:T(8,128)} async-done(((f32[2,1536,2048]{2,1,0:T(8,128)}), f32[2,96,2048]{2,1,0:T(8,128)}) %reduce-scatter.39.cloned.1.call-update) | async-done | bytes 1572880 | tf_op jit(solution)/shard_map/reduce_scatter | solution.py:368
  2493.4 149.3 %reduce-scatter.33.cloned.1.call-done = f32[3,96,768]{2,1,0:T(8,128)} async-done(((f32[3,1536,768]{2,1,0:T(8,128)}), f32[3,96,768]{2,1,0:T(8,128)}) %reduce-scatter.33.cloned.1.call-update) | async-done | bytes 884752 | tf_op jit(solution)/shard_map/reduce_scatter | solution.py:365
  (480 shorter events, 319.5 us)
Async XLA Ops:
  7.2 106.7 %copy-start = (bf16[48,4096]{1,0:T(8,128)(2,1)S(1)}, bf16[48,4096]{1,0:T(8,128)(2,1)}, u32[]{:S(2)}) copy-start(bf16[48,4096]{1,0:T(8,128)(2,1)} %param.28) | copy-start | bytes 1179652
  7.2 111.4 %copy-start.99 = (bf16[64]{0:T(256)(128)(2,1)S(1)}, bf16[64]{0:T(256)(128)(2,1)}, u32[]{:S(2)}) copy-start(bf16[64]{0:T(256)(128)(2,1)} %param.35) | copy-start | bytes 388
  7.2 111.4 %copy-start.86 = (bf16[1536]{0:T(1024)(128)(2,1)S(1)}, bf16[1536]{0:T(1024)(128)(2,1)}, u32[]{:S(2)}) copy-start(bf16[1536]{0:T(1024)(128)(2,1)} %param.32) | copy-start | bytes 9220
  7.2 111.4 %copy-start.72 = (bf16[9216]{0:T(1024)(128)(2,1)S(1)}, bf16[9216]{0:T(1024)(128)(2,1)}, u32[]{:S(2)}) copy-start(bf16[9216]{0:T(1024)(128)(2,1)} %param.31) | copy-start | bytes 55300
  7.2 111.4 %copy-start.45 = (s32[256]{0:T(256)S(1)}, s32[256]{0:T(256)}, u32[]{:S(2)}) copy-start(s32[256]{0:T(256)} %param.26) | copy-start | bytes 3076
  7.2 106.6 %all-gather.20.cloned.1.call-start = ((), (), s32[]{:S(2)}) async-start(), calls=%async_computation.18 | async-start | bytes 13369344 | tf_op jit(solution)/shard_map/all_gather | solution.py:114
  8.0 204.7 %all-gather.12.cloned.1.call-start = ((), (), s32[]{:S(2)}) async-start(), calls=%async_computation.14 | async-start | bytes 20054016 | tf_op jit(solution)/shard_map/all_gather | solution.py:117
  8.7 272.9 %all-gather.14.cloned.1.call-start = ((), (), s32[]{:S(2)}) async-start(), calls=%async_computation.15 | async-start | bytes 7520256 | tf_op jit(solution)/shard_map/all_gather | solution.py:112
  9.5 319.2 %all-gather.22.cloned.1.call-start = ((), (), s32[]{:S(2)}) async-start(), calls=%async_computation.19 | async-start | bytes 1253376 | tf_op jit(solution)/shard_map/all_gather | solution.py:153
  10.7 114.6 %copy-start.94 = (f32[128]{0:T(128)}, f32[128]{0:T(128)S(1)}, u32[]{:S(2)}) copy-start(f32[128]{0:T(128)S(1)} %fusion.135) | copy-start | bytes 1540
  118.5 242.8 %all-gather.24.cloned.1.call-start = ((), (), s32[]{:S(2)}) async-start(), calls=%async_computation.20 | async-start | bytes 1253376 | tf_op jit(solution)/shard_map/all_gather | solution.py:152
  118.5 105.1 %copy-start.85 = (f32[128]{0:T(128)}, f32[128]{0:T(128)S(1)}, u32[]{:S(2)}) copy-start(f32[128]{0:T(128)S(1)} %fusion.167) | copy-start | bytes 1540
  118.6 21.6 copy-start.84
  118.6 105.0 %copy-start.60 = (f32[1536]{0:T(1024)}, f32[1536]{0:T(1024)S(1)}, u32[]{:S(2)}) copy-start(f32[1536]{0:T(1024)S(1)} %convert_element_type.186) | copy-start | bytes 18436
  118.7 102.8 %copy-start.88 = (s32[128]{0:T(128)}, s32[128]{0:T(128)S(1)}, u32[]{:S(2)}) copy-start(s32[128]{0:T(128)S(1)} %dynamic_slice.47) | copy-start | bytes 1540
  134.0 78.6 %copy-start.62 = (bf16[3,1024]{1,0:T(4,128)(2,1)S(1)}, bf16[3,1024]{1,0:T(4,128)(2,1)}, u32[]{:S(2)}) copy-start(bf16[3,1024]{1,0:T(4,128)(2,1)} %param.29) | copy-start | bytes 18436
  140.2 81.4 %copy-start.64 = (f32[48,12]{0,1:T(8,128)}, f32[48,12]{0,1:T(8,128)S(1)}, u32[]{:S(2)}) copy-start(f32[48,12]{0,1:T(8,128)S(1)} %get-tuple-element.498) | copy-start | bytes 6916
  140.2 81.4 %copy-start.58 = (f32[48,12]{0,1:T(8,128)}, f32[48,12]{0,1:T(8,128)S(1)}, u32[]{:S(2)}) copy-start(f32[48,12]{0,1:T(8,128)S(1)} %fusion.165) | copy-start | bytes 6916
  141.9 83.9 %copy-start.8 = (bf16[128,1536]{1,0:T(8,128)(2,1)S(1)}, bf16[128,1536]{1,0:T(8,128)(2,1)}, u32[]{:S(2)}) copy-start(bf16[128,1536]{1,0:T(8,128)(2,1)} %param.25) | copy-start | bytes 1179652
  141.9 282.9 %all-gather.16.cloned.1.call-start = ((), (), s32[]{:S(2)}) async-start(), calls=%async_computation.16 | async-start | bytes 6684672 | tf_op jit(solution)/shard_map/all_gather | solution.py:179
  221.6 63.5 %copy-start.100 = (bf16[64]{0:T(256)(128)(2,1)S(1)}, bf16[64]{0:T(256)(128)(2,1)}, u32[]{:S(2)}) copy-start(bf16[64]{0:T(256)(128)(2,1)} %param.33) | copy-start | bytes 388
  221.6 63.5 %copy-start.101 = (bf16[64]{0:T(256)(128)(2,1)S(1)}, bf16[64]{0:T(256)(128)(2,1)}, u32[]{:S(2)}) copy-start(bf16[64]{0:T(256)(128)(2,1)} %param.34) | copy-start | bytes 388
  221.6 63.5 %copy-start.93 = (s32[256]{0:T(256)S(1)}, s32[256]{0:T(256)}, u32[]{:S(2)}) copy-start(s32[256]{0:T(256)} %param.27) | copy-start | bytes 3076
  238.0 63.5 %copy-start.2 = (bf16[256,1536]{1,0:T(8,128)(2,1)}, bf16[256,1536]{1,0:T(8,128)(2,1)S(1)}, u32[]{:S(2)}) copy-start(bf16[256,1536]{1,0:T(8,128)(2,1)S(1)} %all_gather.46) | copy-start | bytes 2359300
  284.8 207.0 %all-gather.18.cloned.1.call-start = ((), (), s32[]{:S(2)}) async-start(), calls=%async_computation.17 | async-start | bytes 6684672 | tf_op jit(solution)/shard_map/all_gather | solution.py:178
  285.4 20.1 copy-start.47
  306.6 267.7 %all-gather.26.cloned.1.call-start = ((), (), s32[]{:S(2)}) async-start(), calls=%async_computation.21 | async-start | bytes 2506752 | tf_op jit(solution)/shard_map/all_gather | solution.py:113
  307.3 286.5 %reduce-scatter.15.cloned.1.call-start = ((), (), s32[]{:S(2)}) async-start(), calls=%async_computation.22 | async-start | bytes 1179648 | tf_op jit(solution)/shard_map/reduce_scatter | solution.py:53
  308.7 58.3 %copy-start.97 = (f32[24]{0:T(128)}, f32[24]{0:T(128)S(1)}, u32[]{:S(2)}) copy-start(f32[24]{0:T(128)S(1)} %convert_element_type.193) | copy-start | bytes 292
  328.6 240.5 %copy-start.103 = (f32[12]{0:T(128)}, f32[12]{0:T(128)S(1)}, u32[]{:S(2)}) copy-start(f32[12]{0:T(128)S(1)} %dynamic-slice_tanh_fusion) | copy-start | bytes 148
  372.4 196.8 %copy-start.75 = (f32[12,256]{1,0:T(8,128)}, f32[12,256]{1,0:T(8,128)S(1)}, u32[]{:S(2)}) copy-start(f32[12,256]{1,0:T(8,128)S(1)} %get-tuple-element.500) | copy-start | bytes 36868
  538.8 30.4 %copy-start.44 = (bf16[512,768]{0,1:T(8,128)(2,1)S(1)}, bf16[512,768]{0,1:T(8,128)(2,1)}, u32[]{:S(2)}) copy-start(bf16[512,768]{0,1:T(8,128)(2,1)} %copy.87) | copy-start | bytes 2359300
  574.3 34.9 %copy-start.36 = (bf16[256,12,64]{0,2,1:T(8,128)(2,1)}, bf16[256,12,64]{0,2,1:T(8,128)(2,1)S(1)}, u32[]{:S(2)}) copy-start(bf16[256,12,64]{0,2,1:T(8,128)(2,1)S(1)} %get-tuple-element.502) | copy-start | bytes 1179652
  574.3 21.1 copy-start.20
  577.9 119.2 %all-gather.28.cloned.1.call-start = ((), (), s32[]{:S(2)}) async-start(), calls=%async_computation.23 | async-start | bytes 13369344 | tf_op jit(solution)/shard_map/all_gather | solution.py:115
  578.5 181.2 %all-gather.30.cloned.1.call-start = ((), (), s32[]{:S(2)}) async-start(), calls=%async_computation.24 | async-start | bytes 6684672 | tf_op jit(solution)/shard_map/all_gather | solution.py:116
  579.2 212.8 %reduce-scatter.19.cloned.1.call-start = ((), (), s32[]{:S(2)}) async-start(), calls=%async_computation.26 | async-start | bytes 1179648 | tf_op jit(solution)/shard_map/reduce_scatter | solution.py:63
  595.4 216.9 %copy-start.6 = (f32[128,1536]{1,0:T(8,128)}, f32[128,1536]{1,0:T(8,128)S(1)}, u32[]{:S(2)}) copy-start(f32[128,1536]{1,0:T(8,128)S(1)} %get-tuple-element.458) | copy-start | bytes 2359300
  609.2 150.5 %copy-start.24 = (bf16[256,1536]{1,0:T(8,128)(2,1)}, bf16[256,1536]{1,0:T(8,128)(2,1)S(1)}, u32[]{:S(2)}) copy-start(bf16[256,1536]{1,0:T(8,128)(2,1)S(1)} %all_gather.58) | copy-start | bytes 2359300
  620.1 88.9 %copy-start.12 = (bf16[256,1536]{1,0:T(8,128)(2,1)}, bf16[256,1536]{1,0:T(8,128)(2,1)S(1)}, u32[]{:S(2)}) copy-start(bf16[256,1536]{1,0:T(8,128)(2,1)S(1)} %all_gather.55) | copy-start | bytes 2359300
  775.8 36.5 %reduce-scatter.17.cloned.1.call-start = ((), (), s32[]{:S(2)}) async-start(), calls=%async_computation.25 | async-start | bytes 1179648 | tf_op jit(solution)/shard_map/reduce_scatter | solution.py:53
  781.7 717.0 %reduce-scatter.27.cloned.1.call-start = ((), (), s32[]{:S(2)}) async-start(), calls=%async_computation.30 | async-start | bytes 2506752 | tf_op jit(solution)/shard_map/reduce_scatter | solution.py:328
  794.1 37.0 %copy-start.76 = (f32[12,256]{1,0:T(8,128)S(1)}, f32[12,256]{1,0:T(8,128)}, u32[]{:S(2)}) copy-start(f32[12,256]{1,0:T(8,128)} %copy-done.75) | copy-start | bytes 36868
  794.1 37.0 %copy-start.104 = (f32[12]{0:T(128)S(1)}, f32[12]{0:T(128)}, u32[]{:S(2)}) copy-start(f32[12]{0:T(128)} %copy-done.103) | copy-start | bytes 148
  843.4 666.3 %reduce-scatter.29.cloned.1.call-start = ((), (), s32[]{:S(2)}) async-start(), calls=%async_computation.31 | async-start | bytes 2506752 | tf_op jit(solution)/shard_map/reduce_scatter | solution.py:329
  853.5 751.2 %reduce-scatter.21.cloned.1.call-start = ((), (), s32[]{:S(2)}) async-start(), calls=%async_computation.27 | async-start | bytes 13369344 | tf_op jit(solution)/shard_map/reduce_scatter | solution.py:300
  1469.8 273.2 %reduce-scatter.23.cloned.1.call-start = ((), (), s32[]{:S(2)}) async-start(), calls=%async_computation.28 | async-start | bytes 13369344 | tf_op jit(solution)/shard_map/reduce_scatter | solution.py:303
  1493.2 323.1 %reduce-scatter.31.cloned.1.call-start = ((), (), s32[]{:S(2)}) async-start(), calls=%async_computation.32 | async-start | bytes 589824 | tf_op jit(solution)/shard_map/reduce_scatter | solution.py:349
  1509.7 96.4 %copy-start.48 = (f32[256,32]{0,1:T(8,128)S(1)}, f32[256,32]{0,1:T(8,128)}, u32[]{:S(2)}) copy-start(f32[256,32]{0,1:T(8,128)} %copy-done.47) | copy-start | bytes 98308
  1509.7 96.4 %copy-start.50 = (f32[256,32]{0,1:T(8,128)S(1)}, f32[256,32]{0,1:T(8,128)}, u32[]{:S(2)}) copy-start(f32[256,32]{0,1:T(8,128)} %copy-done.49) | copy-start | bytes 98308
  1509.7 97.9 %copy-start.52 = (f32[256,12]{0,1:T(8,128)S(1)}, f32[256,12]{0,1:T(8,128)}, u32[]{:S(2)}) copy-start(f32[256,12]{0,1:T(8,128)} %copy-done.51) | copy-start | bytes 36868
  1509.7 97.9 %copy-start.81 = (f32[64]{0:T(128)S(1)}, f32[64]{0:T(128)}, u32[]{:S(2)}) copy-start(f32[64]{0:T(128)} %copy-done.80) | copy-start | bytes 772
  1509.7 100.1 %copy-start.69 = (f32[256,12]{0,1:T(8,128)S(1)}, f32[256,12]{0,1:T(8,128)}, u32[]{:S(2)}) copy-start(f32[256,12]{0,1:T(8,128)} %copy-done.68) | copy-start | bytes 36868
  1509.7 100.1 %copy-start.54 = (f32[256,12]{0,1:T(8,128)S(1)}, f32[256,12]{0,1:T(8,128)}, u32[]{:S(2)}) copy-start(f32[256,12]{0,1:T(8,128)} %copy-done.53) | copy-start | bytes 36868
  1509.7 100.1 %copy-start.83 = (f32[64]{0:T(128)S(1)}, f32[64]{0:T(128)}, u32[]{:S(2)}) copy-start(f32[64]{0:T(128)} %copy-done.82) | copy-start | bytes 772
  1509.7 101.8 %slice-start = ((s8[7077888]{0:T(1024)(128)(4,1)}), s8[2883584]{0:T(1024)(128)(4,1)S(1)}, s32[]{:S(2)}) async-start(s8[7077888]{0:T(1024)(128)(4,1)} %bitcast.333), calls=%async_computation.38 | async-start | bytes 5767168
  1515.6 94.9 %copy-start.67 = (f32[256,12]{0,1:T(8,128)S(1)}, f32[256,12]{0,1:T(8,128)}, u32[]{:S(2)}) copy-start(f32[256,12]{0,1:T(8,128)} %copy-done.66) | copy-start | bytes 36868
  1515.6 302.4 %reduce-scatter.25.cloned.1.call-start = ((), (), s32[]{:S(2)}) async-start(), calls=%async_computation.29 | async-start | bytes 1179648 | tf_op jit(solution)/shard_map/reduce_scatter | solution.py:63
  1747.2 280.4 %reduce-scatter.37.cloned.1.call-start = ((), (), s32[]{:S(2)}) async-start(), calls=%async_computation.35 | async-start | bytes 26738688 | tf_op jit(solution)/shard_map/reduce_scatter | solution.py:367
  1759.5 347.6 %reduce-scatter.35.cloned.1.call-start = ((), (), s32[]{:S(2)}) async-start(), calls=%async_computation.34 | async-start | bytes 5013504 | tf_op jit(solution)/shard_map/reduce_scatter | solution.py:366
  1763.7 482.0 %reduce-scatter.41.cloned.1.call-start = ((), (), s32[]{:S(2)}) async-start(), calls=%async_computation.37 | async-start | bytes 13369344 | tf_op jit(solution)/shard_map/reduce_scatter | solution.py:369
  1770.3 723.1 %reduce-scatter.39.cloned.1.call-start = ((), (), s32[]{:S(2)}) async-start(), calls=%async_computation.36 | async-start | bytes 26738688 | tf_op jit(solution)/shard_map/reduce_scatter | solution.py:368
  1784.0 858.7 %reduce-scatter.33.cloned.1.call-start = ((), (), s32[]{:S(2)}) async-start(), calls=%async_computation.33 | async-start | bytes 15040512 | tf_op jit(solution)/shard_map/reduce_scatter | solution.py:365
  1824.6 52.5 %copy-start.63 = (bf16[3,1024]{1,0:T(4,128)(2,1)S(1)}, bf16[3,1024]{1,0:T(4,128)(2,1)}, u32[]{:S(2)}) copy-start(bf16[3,1024]{1,0:T(4,128)(2,1)} %param.29) | copy-start | bytes 18436
  (75 other events, 466.2 us)
Sparse Core Ops, SparseCore 0:
  10.4 103.4 all-gather.19
  115.5 97.1 all-gather.11
  214.9 66.6 all-gather.13
  284.3 36.7 all-gather.21
  323.8 37.3 all-gather.23
  363.9 60.7 all-gather.15
  427.5 64.2 all-gather.17
  494.1 40.4 all-gather.25
  578.0 15.8 reduce-scatter.14
  596.3 100.7 all-gather.27
  699.7 60.0 all-gather.29
  775.9 16.0 reduce-scatter.18
  794.8 17.4 reduce-scatter.16
  843.5 62.9 reduce-scatter.26
  910.1 61.9 reduce-scatter.28
  1470.0 134.7 reduce-scatter.20
  1609.2 133.8 reduce-scatter.22
  1745.8 12.2 reduce-scatter.30
  1761.0 17.4 reduce-scatter.24
  1782.9 244.5 reduce-scatter.36
  2032.5 74.6 reduce-scatter.34
  2111.8 133.8 reduce-scatter.40
  2250.3 242.9 reduce-scatter.38
  2498.0 144.6 reduce-scatter.32
where the time goes:
time: 2670 us; the launch traced here: 2650 us
  waiting for transfers between devices  1480 us (55%)
  local copies, waits for them, and re-layouts  654 us (24%)
  matrix products  283 us (11%)
  blocking collectives  112 us (4%)
  other arithmetic  97.8 us (4%)
    dynamic_update_slice x16, local copies, waits for them, and re-layouts, shards(): lax.scan(grad_step, query_start, (key_blocks, value_blocks, id_blocks))  501 us
    reduce_scatter x1, waiting for transfers between devices, shards(): lax.psum_scatter(grad_gate_up, 'dp', scatter_dimension=1, tiled=True)  248 us
    dot_general x53, matrix products, contract(): return jnp.einsum(formula, left, right, preferred_element_type=jnp.float32)  224 us
    reduce_scatter x1, waiting for transfers between devices, shards(): lax.psum_scatter(grad_qkv, 'dp', scatter_dimension=1, tiled=True)  149 us
    reduce_scatter x1, waiting for transfers between devices, shards(): lax.psum_scatter(grad_down, 'dp', scatter_dimension=1, tiled=True)  138 us
    reduce_scatter x1, waiting for transfers between devices, shards(): lax.psum_scatter(grad_text_kv, 'dp', scatter_dimension=1, tiled=True)  138 us
    reduce_scatter x1, waiting for transfers between devices, shards(): lax.psum_scatter(value_grads.reshape(total_rows, local_width), 'dp', scat...  128 us
    all_gather x1, waiting for transfers between devices, shards(): lax.all_gather(text_kv_weight, 'dp', axis=1, tiled=True)  103 us
  transfers between devices with their start and end apart: 24, of which 18 were waited for; matrix products, arithmetic and copies ran while one was open for 37% of the time, Pallas kernels for 0%

commit v1 on v0

v1 whole, which is shorter than its diff:
```python
import functools

import jax
import jax.numpy as jnp
from jax import lax
from jax.experimental import pallas as pl
from jax.experimental.pallas import tpu as pltpu
from jax.sharding import PartitionSpec as P

TXT = 256
GROUP = 8
SPLIT = 4
EPS = 1e-06
MASK = -1e4
LOW = jnp.bfloat16
FLOAT = jnp.float32
MIB = 1024 * 1024


def pick_tile(total, most):
    size = most
    while total % size:
        size //= 2
    return size


def matmul(left, right, left_dim, right_dim):
    return lax.dot_general(
        left, right, (((left_dim,), (right_dim,)), ((), ())), preferred_element_type=jnp.float32
    )


def build_keys(kv_ref, kf_ref, keys_ref, values_ref):
    lanes = lax.broadcasted_iota(jnp.int32, kv_ref.shape, 1)
    kv = kv_ref[...]
    keys_ref[...] = jnp.where(lanes < 64, kv, kf_ref[...])
    values_ref[...] = jnp.where(
        lanes < 64, jnp.where(lanes < 3, 1.0, 0.0).astype(jnp.bfloat16), kv
    )


def forward_kernel(
    chunk, q_ref, sel_ref, qf_ref, kv_ref, kf_ref, tkv_ref, tf_ref, gate_ref,
    mixed_ref, outs_ref, stats_ref, keys, values, text_keys, text_values,
):
    @pl.when(pl.program_id(1) == 0)
    def _():
        build_keys(kv_ref, kf_ref, keys, values)
        build_keys(tkv_ref, tf_ref, text_keys, text_values)

    rows = q_ref.shape[0]
    query = (matmul(q_ref[...], sel_ref[0], 1, 0) + qf_ref[...].astype(jnp.float32)).astype(
        jnp.bfloat16
    )

    def attend(key_part, value_part):
        scores = matmul(query, key_part, 1, 1)
        return matmul(jnp.exp(scores).astype(jnp.bfloat16), value_part, 1, 0)

    def step(index, total):
        part = pl.ds(pl.multiple_of(index * chunk, chunk), chunk)
        return total + attend(keys[part, :], values[part, :])

    own = lax.fori_loop(
        0, keys.shape[0] // chunk, step, jnp.zeros((rows, 128), jnp.float32), unroll=2
    )
    text_chunk = pick_tile(text_keys.shape[0], 256)

    def text_step(index, total):
        part = pl.ds(pl.multiple_of(index * text_chunk, text_chunk), text_chunk)
        return total + attend(text_keys[part, :], text_values[part, :])

    cross = lax.fori_loop(
        0, text_keys.shape[0] // text_chunk, text_step, jnp.zeros((rows, 128), jnp.float32), unroll=True
    )
    own_inverse = 1.0 / own[:, 0:1]
    cross_inverse = 1.0 / cross[:, 0:1]
    own = own * own_inverse
    cross = cross * cross_inverse
    lanes = lax.broadcasted_iota(jnp.int32, own.shape, 1)
    gate = gate_ref[0, 0:1, :]
    mixed_ref[...] = (own + gate * cross).astype(jnp.bfloat16)
    outs_ref[...] = jnp.where(lanes < 64, pltpu.roll(cross, 64, 1), own)
    stats_ref[...] = jnp.where(lanes == 0, own_inverse, cross_inverse)


def attention_forward(q, sel, qf, kv, kf, tkv, tf, gates):
    rows, width = q.shape
    heads = sel.shape[0]
    total, text_total = kv.shape[0], tkv.shape[0]
    tile = pick_tile(rows, 256)
    chunk = pick_tile(total, 512)
    head_block = lambda h, i: (i, h)
    out = jax.ShapeDtypeStruct((rows, heads * 128), jnp.float32)
    pairs = rows * heads * (total + text_total)
    return pl.pallas_call(
        functools.partial(forward_kernel, chunk),
        grid=(heads, rows // tile),
        in_specs=[
            pl.BlockSpec((tile, width), lambda h, i: (i, 0)),
            pl.BlockSpec((1, width, 128), lambda h, i: (h, 0, 0)),
            pl.BlockSpec((tile, 128), lambda h, i: (i, 0)),
            pl.BlockSpec((total, 128), lambda h, i: (0, h)),
            pl.BlockSpec((total, 128), lambda h, i: (0, 0)),
            pl.BlockSpec((text_total, 128), lambda h, i: (0, h)),
            pl.BlockSpec((text_total, 128), lambda h, i: (0, 0)),
            pl.BlockSpec((1, 8, 128), lambda h, i: (h, 0, 0)),
        ],
        out_specs=[pl.BlockSpec((tile, 128), head_block)] * 3,
        out_shape=[jax.ShapeDtypeStruct((rows, heads * 128), jnp.bfloat16), out, out],
        scratch_shapes=[
            pltpu.VMEM((total, 128), jnp.bfloat16),
            pltpu.VMEM((total, 128), jnp.bfloat16),
            pltpu.VMEM((text_total, 128), jnp.bfloat16),
            pltpu.VMEM((text_total, 128), jnp.bfloat16),
        ],
        compiler_params=pltpu.CompilerParams(vmem_limit_bytes=48 * 1024 * 1024),
        cost_estimate=pl.CostEstimate(
            flops=pairs * 512, bytes_accessed=8 * total * heads * 128, transcendentals=pairs
        ),
    )(q, sel, qf, kv, kf, tkv, tf, gates)


def backward_kernel(
    chunk, q_ref, dm_ref, sel_ref, msel_ref, qf_ref, kv_ref, kf_ref, tkv_ref, tf_ref, gate_ref,
    outs_ref, stats_ref, dq_ref, dkv_ref, dt_ref, dg_ref,
    keys, values, text_keys, text_values, acc, text_acc,
):
    tile_index = pl.program_id(1)

    @pl.when(tile_index == 0)
    def _():
        build_keys(kv_ref, kf_ref, keys, values)
        build_keys(tkv_ref, tf_ref, text_keys, text_values)
        acc[...] = jnp.zeros_like(acc)
        text_acc[...] = jnp.zeros_like(text_acc)
        dg_ref[...] = jnp.zeros_like(dg_ref)

    rows = q_ref.shape[0]
    query_wide = matmul(q_ref[...], sel_ref[0], 1, 0)
    query = (query_wide + qf_ref[...].astype(jnp.float32)).astype(jnp.bfloat16)
    query_low = query_wide.astype(jnp.bfloat16)
    grads = matmul(dm_ref[...], msel_ref[0], 1, 0)
    outs = outs_ref[...]
    lanes = lax.broadcasted_iota(jnp.int32, outs.shape, 1)
    gate = gate_ref[0, 0:1, :]
    cross_out = jnp.where(lanes < 64, 0.0, pltpu.roll(outs, 64, 1))
    dg_ref[...] += jnp.sum((grads * cross_out).reshape(rows // 8, 8, 128), axis=0)
    cross_grads = (gate * grads).astype(jnp.bfloat16).astype(jnp.float32)

    def widen(grad, out, inverse):
        delta = -jnp.sum(grad * out, axis=1, keepdims=True) * inverse
        first = delta.astype(jnp.bfloat16).astype(jnp.float32)
        second = (delta - first).astype(jnp.bfloat16).astype(jnp.float32)
        third = delta - first - second
        features = jnp.where(lanes == 0, first, jnp.where(lanes == 1, second, third))
        scaled = grad * inverse
        whole = jnp.where(lanes < 3, features, scaled).astype(jnp.bfloat16)
        return whole, scaled.astype(jnp.bfloat16)

    stats = stats_ref[...]
    own_wide, own_low = widen(grads, outs, stats[:, 0:1])
    cross_wide, cross_low = widen(cross_grads, cross_out, stats[:, 1:2])

    def attend(key_part, value_part, wide, pair):
        weights = jnp.exp(matmul(key_part, query, 1, 1))
        grad_scores = (weights * matmul(value_part, wide, 1, 1)).astype(jnp.bfloat16)
        low = weights.astype(jnp.bfloat16)
        grad_pair = matmul(jnp.concatenate([grad_scores, low], axis=1), pair, 1, 0)
        return grad_pair, matmul(grad_scores, key_part, 0, 0)

    own_pair = jnp.concatenate([query_low, own_low], axis=0)
    cross_pair = jnp.concatenate([query_low, cross_low], axis=0)

    def step(index, total):
        part = pl.ds(pl.multiple_of(index * chunk, chunk), chunk)
        grad_pair, grad_query = attend(keys[part, :], values[part, :], own_wide, own_pair)
        acc[part, :] += grad_pair
        return total + grad_query

    query_grad = lax.fori_loop(
        0, keys.shape[0] // chunk, step, jnp.zeros((rows, 128), jnp.float32), unroll=2
    )
    text_chunk = pick_tile(text_keys.shape[0], 256)

    def text_step(index, total):
        part = pl.ds(pl.multiple_of(index * text_chunk, text_chunk), text_chunk)
        grad_pair, grad_query = attend(
            text_keys[part, :], text_values[part, :], cross_wide, cross_pair
        )
        text_acc[part, :] += grad_pair
        return total + grad_query

    query_grad = lax.fori_loop(
        0, text_keys.shape[0] // text_chunk, text_step, query_grad, unroll=True
    )
    dq_ref[...] = (query_grad * 0.125).astype(jnp.bfloat16)

    @pl.when(tile_index == pl.num_programs(1) - 1)
    def _():
        dkv_ref[...] = acc[...].astype(jnp.bfloat16)
        dt_ref[...] = text_acc[...].astype(jnp.bfloat16)


def attention_backward(q, dm, sel, msel, qf, kv, kf, tkv, tf, gates, outs, stats):
    rows, width = q.shape
    heads = sel.shape[0]
    total, text_total = kv.shape[0], tkv.shape[0]
    tile = pick_tile(rows, 256)
    chunk = pick_tile(total, 512)
    low = jnp.bfloat16
    pairs = rows * heads * (total + text_total)
    return pl.pallas_call(
        functools.partial(backward_kernel, chunk),
        grid=(heads, rows // tile),
        in_specs=[
            pl.BlockSpec((tile, width), lambda h, i: (i, 0)),
            pl.BlockSpec((tile, width), lambda h, i: (i, 0)),
            pl.BlockSpec((1, width, 128), lambda h, i: (h, 0, 0)),
            pl.BlockSpec((1, width, 128), lambda h, i: (h, 0, 0)),
            pl.BlockSpec((tile, 128), lambda h, i: (i, 0)),
            pl.BlockSpec((total, 128), lambda h, i: (0, h)),
            pl.BlockSpec((total, 128), lambda h, i: (0, 0)),
            pl.BlockSpec((text_total, 128), lambda h, i: (0, h)),
            pl.BlockSpec((text_total, 128), lambda h, i: (0, 0)),
            pl.BlockSpec((1, 8, 128), lambda h, i: (h, 0, 0)),
            pl.BlockSpec((tile, 128), lambda h, i: (i, h)),
            pl.BlockSpec((tile, 128), lambda h, i: (i, h)),
        ],
        out_specs=[
            pl.BlockSpec((tile, 128), lambda h, i: (i, h)),
            pl.BlockSpec((total, 128), lambda h, i: (0, h)),
            pl.BlockSpec((text_total, 128), lambda h, i: (0, h)),
            pl.BlockSpec((8, 128), lambda h, i: (0, h)),
        ],
        out_shape=[
            jax.ShapeDtypeStruct((rows, heads * 128), low),
            jax.ShapeDtypeStruct((total, heads * 128), low),
            jax.ShapeDtypeStruct((text_total, heads * 128), low),
            jax.ShapeDtypeStruct((8, heads * 128), jnp.float32),
        ],
        scratch_shapes=[
            pltpu.VMEM((total, 128), low),
            pltpu.VMEM((total, 128), low),
            pltpu.VMEM((text_total, 128), low),
            pltpu.VMEM((text_total, 128), low),
            pltpu.VMEM((total, 128), jnp.float32),
            pltpu.VMEM((text_total, 128), jnp.float32),
        ],
        compiler_params=pltpu.CompilerParams(vmem_limit_bytes=56 * 1024 * 1024),
        cost_estimate=pl.CostEstimate(
            flops=pairs * 1280, bytes_accessed=12 * total * heads * 128, transcendentals=pairs
        ),
    )(q, dm, sel, msel, qf, kv, kf, tkv, tf, gates, outs, stats)


def half_means(values, lanes):
    low = jnp.sum(jnp.where(lanes < 64, values, 0.0), axis=1, keepdims=True)
    high = jnp.sum(jnp.where(lanes < 64, 0.0, values), axis=1, keepdims=True)
    return jnp.where(lanes < 64, low, high) * (1.0 / 64.0)


def swap_halves(values, lanes):
    return jnp.where(
        lax.rem(lanes, 64) < 32, pltpu.roll(values, 96, 1), pltpu.roll(values, 32, 1)
    )


def placed_at(groups, head, upper):
    values = groups[head // 2]
    return values if (head % 2 == 1) == upper else pltpu.roll(values, 64, 1)


def rope_forward_kernel(heads, qkv_ref, cos_ref, sin_ref, gains_ref, out_ref):
    width = heads * 64
    cosine, sine = cos_ref[...], sin_ref[...]
    lanes = lax.broadcasted_iota(jnp.int32, cosine.shape, 1)

    def turned(start, gain):
        groups = []
        for index in range(heads // 2):
            raw = qkv_ref[:, start + 128 * index : start + 128 * index + 128]
            normed = raw * lax.rsqrt(half_means(raw * raw, lanes) + EPS) * gain
            groups.append(normed * cosine + swap_halves(normed, lanes) * sine)
        return groups

    queries = turned(0, gains_ref[0:1, :])
    keys = turned(width, gains_ref[1:2, :])
    values = [
        qkv_ref[:, 2 * width + 128 * index : 2 * width + 128 * index + 128]
        for index in range(heads // 2)
    ]
    each = heads // SPLIT
    for part in range(SPLIT):
        first = part * each
        blocks = []
        for pair in range((each + 1) // 2):
            left = placed_at(queries, first + 2 * pair, False)
            if 2 * pair + 1 < each:
                right = placed_at(queries, first + 2 * pair + 1, True)
            else:
                right = jnp.zeros_like(left)
            blocks.append(jnp.where(lanes < 64, left, right))
        for head in range(first, first + each):
            blocks.append(
                jnp.where(lanes < 64, placed_at(keys, head, False), placed_at(values, head, True))
            )
        for index, block in enumerate(blocks):
            out_ref[part, :, 128 * index : 128 * index + 128] = block.astype(LOW)


def rope_forward(qkv, cosine, sine, gains, heads):
    rows = qkv.shape[0]
    each = heads // SPLIT
    width = 128 * ((each + 1) // 2 + each)
    return pl.pallas_call(
        functools.partial(rope_forward_kernel, heads),
        out_shape=jax.ShapeDtypeStruct((SPLIT, rows, width), LOW),
        compiler_params=pltpu.CompilerParams(vmem_limit_bytes=32 * MIB),
    )(qkv, cosine, sine, gains)


def rope_backward_kernel(heads, part_ref, qkv_ref, cos_ref, sin_ref, gains_ref, out_ref, sums_ref):
    width = heads * 64
    each = heads // SPLIT
    query_blocks = (each + 1) // 2
    cosine, sine = cos_ref[...], sin_ref[...]
    lanes = lax.broadcasted_iota(jnp.int32, cosine.shape, 1)

    def found(kind, head):
        part, index = head // each, head % each
        if kind == 0:
            block, upper = index // 2, index % 2 == 1
        else:
            block, upper = query_blocks + index, kind == 2
        values = part_ref[part, :, 128 * block : 128 * block + 128].astype(FLOAT)
        return values if upper == (head % 2 == 1) else pltpu.roll(values, 64, 1)

    def joined(kind, index):
        return jnp.where(lanes < 64, found(kind, 2 * index), found(kind, 2 * index + 1))

    for kind in range(2):
        gain = gains_ref[kind : kind + 1, :]
        total = jnp.zeros((1, 128), FLOAT)
        for index in range(heads // 2):
            spot = kind * width + 128 * index
            raw = qkv_ref[:, spot : spot + 128]
            inverse = lax.rsqrt(half_means(raw * raw, lanes) + EPS)
            unit = raw * inverse
            grad = joined(kind, index)
            back = grad * cosine - swap_halves(grad, lanes) * sine
            total = total + jnp.sum(back * unit, axis=0, keepdims=True)
            scaled = back * gain
            raw_grad = inverse * (scaled - unit * half_means(scaled * unit, lanes))
            out_ref[:, spot : spot + 128] = raw_grad.astype(LOW)
        sums_ref[kind : kind + 1, :] = total
    sums_ref[2:8, :] = jnp.zeros((6, 128), FLOAT)
    for index in range(heads // 2):
        spot = 2 * width + 128 * index
        out_ref[:, spot : spot + 128] = joined(2, index).astype(LOW)


def rope_backward(parts, qkv, cosine, sine, gains, heads):
    return pl.pallas_call(
        functools.partial(rope_backward_kernel, heads),
        out_shape=[
            jax.ShapeDtypeStruct(qkv.shape, LOW),
            jax.ShapeDtypeStruct((8, 128), FLOAT),
        ],
        compiler_params=pltpu.CompilerParams(vmem_limit_bytes=32 * MIB),
    )(parts, qkv, cosine, sine, gains)


def outer_kernel(left_ref, right_ref, out_ref):
    out_ref[...] = matmul(left_ref[0], right_ref[...], 1, 0).astype(LOW)


def outer_products(left, right, bounds, tile):
    depth, columns = left.shape[1], right.shape[1]
    return pl.pallas_call(
        outer_kernel,
        grid=(columns // tile,),
        in_specs=[
            pl.BlockSpec(
                (1, depth, left.shape[2]), lambda i: (jnp.where(i < bounds // tile, 0, 1), 0, 0)
            ),
            pl.BlockSpec((right.shape[0], tile), lambda i: (0, i)),
        ],
        out_specs=pl.BlockSpec((depth, tile), lambda i: (0, i)),
        out_shape=jax.ShapeDtypeStruct((depth, columns), LOW),
        compiler_params=pltpu.CompilerParams(vmem_limit_bytes=40 * MIB),
        cost_estimate=pl.CostEstimate(
            flops=2 * depth * columns * right.shape[0],
            bytes_accessed=2 * depth * columns,
            transcendentals=0,
        ),
    )(left, right)


def dot_float(left, right):
    return jnp.dot(left, right, preferred_element_type=FLOAT)


def dot_turned(left, right):
    return matmul(left, right, 1, 1)


def norm_rows(values, gains):
    return values * lax.rsqrt(jnp.mean(values * values, axis=-1, keepdims=True) + EPS) * gains


def modulated(values, gains, shifts, scales):
    return norm_rows(values, gains) * (1.0 + scales) + shifts


def swapped(values):
    return lax.ppermute(values, "tensor", [(0, 1), (1, 0)])


def both_rows(values):
    return jnp.concatenate([values, swapped(values)], axis=0)


def own_rows(partial):
    rows = partial.shape[0] // 2
    return partial[:rows] + swapped(partial[rows:].astype(LOW)).astype(FLOAT)


def shards(
    inputs,
    clip_ids,
    positions,
    text_tokens,
    conditioning,
    ada_weight,
    ada_bias,
    first_norm_gain,
    query_gain,
    key_gain,
    text_key_gain,
    head_gate,
    qkv_weight,
    out_weight,
    text_kv_weight,
    second_norm_gain,
    gate_up_weight,
    down_weight,
    grad_output,
):
    dp = lax.axis_size("dp")
    near = dp // SPLIT
    bits = [near >> (step + 1) for step in range(near.bit_length() - 1)]
    tensor_index = lax.axis_index("tensor")
    dp_index = lax.axis_index("dp")
    far_index, near_index = dp_index // near, dp_index % near
    row_count, width = inputs.shape
    token_count = clip_ids.shape[0]
    head_size = query_gain.shape[0]
    local_width = qkv_weight.shape[2]
    heads = local_width // head_size
    each = heads // SPLIT
    part_width = each * head_size
    clip_count = conditioning.shape[0]
    hidden_count = gate_up_weight.shape[2]
    weight_rows = qkv_weight.shape[1]

    def flip(values, bit):
        return lax.ppermute(values, "dp", [(j, j ^ bit) for j in range(dp)])

    def shift(values, steps):
        pairs = [(j, ((j // near + steps) % SPLIT) * near + j % near) for j in range(dp)]
        return lax.ppermute(values, "dp", pairs)

    def sum_dp(values):
        step = 1
        while step < dp:
            values = values + flip(values, step)
            step *= 2
        return values

    def spread(values):
        for bit in bits:
            values = jnp.concatenate([values, flip(values, bit)], axis=0)
        return values

    def collect(values):
        for bit in reversed(bits):
            half = values.shape[0] // 2
            values = values[:half].astype(FLOAT) + flip(
                values[half:].astype(LOW), bit
            ).astype(FLOAT)
        return values

    def pick(stacked, index):
        return lax.dynamic_index_in_dim(stacked, index, 0, keepdims=False)

    def send_parts(stacked):
        out = [pick(stacked, far_index)]
        for steps in range(1, SPLIT):
            out.append(shift(pick(stacked, (far_index + steps) % SPLIT), steps))
        return out

    def in_place(parts):
        doubled = jnp.stack(parts + parts)
        return lax.dynamic_slice_in_dim(doubled, (SPLIT - far_index) % SPLIT, SPLIT, 0)

    def return_parts(slots):
        return in_place(
            [slots[0]] + [shift(slots[steps], -steps) for steps in range(1, SPLIT)]
        )

    qkv_full = lax.all_gather(
        qkv_weight.transpose(1, 0, 2).reshape(weight_rows, 3 * local_width),
        "dp",
        axis=0,
        tiled=True,
    )
    rest_shard = jnp.concatenate(
        [out_weight.T, gate_up_weight[0], gate_up_weight[1], down_weight.T], axis=1
    )
    rest_shard, qkv_full = lax.optimization_barrier((rest_shard, qkv_full))
    rest_full = lax.all_gather(rest_shard, "dp", axis=0, tiled=True)
    out_full = rest_full[:, :local_width]
    gate_up_full = rest_full[:, local_width : local_width + 2 * hidden_count]
    down_full = rest_full[:, local_width + 2 * hidden_count :]

    cond_float = conditioning.astype(FLOAT)
    silu_cond = jax.nn.silu(cond_float).astype(LOW)
    cond_rows = ada_weight.shape[0]
    silu_slice = lax.dynamic_slice_in_dim(silu_cond, dp_index * cond_rows, cond_rows, axis=1)
    first_rows = jnp.sum((clip_ids == 0).astype(FLOAT))
    spots = jnp.arange(ada_weight.shape[1], dtype=jnp.int32)
    mod_part = jnp.concatenate(
        [
            dot_float(silu_slice, ada_weight),
            jnp.where(spots == dp_index, first_rows, 0.0)[None],
        ],
        axis=0,
    )
    mod_sum = sum_dp(mod_part)
    modulation = mod_sum[:clip_count] + ada_bias.astype(FLOAT)
    counts = mod_sum[clip_count, :dp].astype(jnp.int32)

    own_ids = lax.dynamic_slice_in_dim(clip_ids, tensor_index * row_count, row_count)
    row_positions = jnp.where(
        tensor_index == 0, positions, jnp.roll(positions, row_count)
    )
    other_clip = jnp.max(clip_ids)
    first_clip = (own_ids == 0)[:, None]
    mod_rows = jnp.where(
        first_clip,
        modulation[0:1],
        lax.dynamic_slice_in_dim(modulation, other_clip, 1, 0),
    )
    shift_one, scale_one, gate_one, shift_two, scale_two, gate_two = jnp.split(mod_rows, 6, axis=1)

    input_rows = inputs.astype(FLOAT)
    first_gain = first_norm_gain.astype(FLOAT)
    normed_all = both_rows(modulated(input_rows, first_gain, shift_one, scale_one).astype(LOW))
    grad_two = grad_output.astype(FLOAT)
    grad_ffn = both_rows((gate_two * grad_two).astype(LOW))

    half_size = head_size // 2
    frequency = 10000.0 ** (-(jnp.arange(half_size, dtype=FLOAT) * 2.0 / head_size))
    angles = row_positions.astype(FLOAT)[:, None] * frequency[None, :]
    cosine = jnp.cos(angles)
    sine = jnp.sin(angles)
    cosine = jnp.concatenate([cosine] * 4, axis=1)
    sine = jnp.concatenate([-sine, sine, -sine, sine], axis=1)
    gains = jnp.stack([jnp.tile(query_gain, 2), jnp.tile(key_gain, 2)]).astype(FLOAT)
    gains = jnp.concatenate([gains, jnp.zeros((6, 128), FLOAT)], axis=0)

    flips = []
    for order in range(near):
        mask = 0
        for place, bit in enumerate(bits):
            if order >> place & 1:
                mask |= bit
        flips.append(mask)

    text_rows = text_tokens.shape[0]
    group_rows = text_rows * SPLIT
    text_columns = lax.all_to_all(text_tokens, "dp", split_axis=1, concat_axis=0, tiled=True)
    text_groups = text_columns.reshape(near, group_rows, text_columns.shape[1])
    text_near = jnp.concatenate([pick(text_groups, near_index ^ mask) for mask in flips], axis=0)
    text_weight = (
        text_kv_weight.reshape(2, -1, SPLIT, part_width)
        .transpose(1, 2, 0, 3)
        .reshape(-1, 2 * local_width)
    )
    text_sum = collect(dot_float(text_near, text_weight))
    text_parts = text_sum.astype(LOW).reshape(group_rows, SPLIT, 2 * part_width).transpose(1, 0, 2)
    text_raw = sum(part.astype(FLOAT) for part in send_parts(text_parts))
    ky_gain = text_key_gain.astype(FLOAT)
    text_key_raw = text_raw[:, :part_width].reshape(group_rows, each, head_size)
    text_key = norm_rows(text_key_raw, ky_gain).astype(LOW)
    text_value = text_raw[:, part_width:].astype(LOW).reshape(group_rows, each, head_size)
    text_pairs = spread(
        jnp.concatenate([text_key, text_value], axis=-1).reshape(group_rows, 2 * part_width)
    )

    lanes = jnp.arange(128, dtype=jnp.int32)[None, :]
    text_groups_at = jnp.stack([near_index ^ mask for mask in flips])
    text_clip = (
        text_groups_at[:, None] * group_rows + jnp.arange(group_rows, dtype=jnp.int32)[None, :]
    ).reshape(-1) // TXT
    text_features = (lanes == 64 + text_clip[:, None]).astype(LOW)
    block_at = jnp.stack(
        [
            ((far_index - steps) % SPLIT) * near + (near_index ^ mask)
            for mask in flips
            for steps in range(SPLIT)
        ]
    )
    block_count = jnp.sum(
        jnp.where(block_at[:, None] == jnp.arange(dp, dtype=jnp.int32)[None, :], counts[None, :], 0),
        axis=1,
    )
    row_at = (jnp.arange(token_count, dtype=jnp.int32) + tensor_index * row_count) % token_count
    key_clip = jnp.where(
        row_at[None, :] < block_count[:, None], 0, 1 + block_at[:, None] // GROUP
    ).reshape(-1)
    key_features = (lanes == 64 + key_clip[:, None]).astype(LOW)
    group_tokens = SPLIT * token_count
    query_clip = key_clip[:group_tokens, None]
    query_features = jnp.where(
        (lanes >= 64) & (lanes < 64 + clip_count) & (lanes != 64 + query_clip), MASK, 0.0
    ).astype(LOW)
    query_width = 128 * ((each + 1) // 2)
    head_at = jnp.arange(each, dtype=jnp.int32)[:, None, None]
    lane_at = jnp.arange(128, dtype=jnp.int32)[None, None, :]

    def selector(rows, offset, scale):
        row = jnp.arange(rows, dtype=jnp.int32)[None, :, None]
        hit = (row == head_at * head_size + lane_at - offset) & (lane_at >= offset)
        hit = hit & (lane_at < offset + head_size)
        return jnp.where(hit, scale, 0.0).astype(LOW)

    query_select = selector(query_width, 0, head_size**-0.5)
    mixed_select = selector(query_width, 64, 1.0)
    gate_heads = jnp.tanh(
        lax.dynamic_slice_in_dim(
            head_gate.astype(FLOAT), tensor_index * heads + far_index * each, each
        )
    )
    gate_lanes = jnp.broadcast_to(gate_heads[:, None, None], (each, 8, 128))

    qkv_raw = dot_float(normed_all, qkv_full)
    head_parts = send_parts(rope_forward(qkv_raw, cosine, sine, gains, heads))
    arrived = jnp.concatenate(head_parts, axis=0)
    queries = arrived[:, :query_width]
    pairs = spread(arrived[:, query_width:])
    mixed_wide, head_outs, head_stats = attention_forward(
        queries,
        query_select,
        query_features,
        pairs,
        key_features,
        text_pairs,
        text_features,
        gate_lanes,
    )
    mixed_slots = mixed_wide.reshape(SPLIT, token_count, each, 128)[..., 64:].reshape(
        SPLIT, token_count, part_width
    )
    mixed = (
        return_parts([mixed_slots[index] for index in range(SPLIT)])
        .transpose(1, 0, 2)
        .reshape(token_count, local_width)
    )
    attn_rows = own_rows(dot_turned(mixed, out_full))
    after_attn = input_rows + gate_one * attn_rows
    second_gain = second_norm_gain.astype(FLOAT)
    normed_two_all = both_rows(modulated(after_attn, second_gain, shift_two, scale_two).astype(LOW))
    gate_up = dot_float(normed_two_all, gate_up_full)
    gate_values, up_values = gate_up[:, :hidden_count], gate_up[:, hidden_count:]
    sigmoid_gate = jax.nn.sigmoid(gate_values)
    hidden_low = (gate_values * sigmoid_gate * up_values).astype(LOW)
    ffn_rows = own_rows(dot_turned(hidden_low, down_full))
    output = (after_attn + gate_two * ffn_rows).astype(LOW)
    grad_gate_two = grad_two * ffn_rows
    grad_hidden = dot_float(grad_ffn, down_full)
    grad_gate_low = (
        grad_hidden * up_values * sigmoid_gate * (1.0 + gate_values * (1.0 - sigmoid_gate))
    ).astype(LOW)
    grad_up_low = (grad_hidden * gate_values * sigmoid_gate).astype(LOW)
    grad_gate_up = jnp.concatenate([grad_gate_low, grad_up_low], axis=1)
    feed_grads = outer_products(
        jnp.stack([normed_two_all.T, grad_ffn.T]),
        jnp.concatenate([grad_gate_up, hidden_low], axis=1),
        2 * hidden_count,
        512,
    )
    feed_shard = lax.psum_scatter(feed_grads, "dp", scatter_dimension=0, tiled=True).astype(FLOAT)
    grad_normed_two = own_rows(dot_turned(grad_gate_up, gate_up_full))
    _, pull_two = jax.vjp(modulated, after_attn, second_gain, shift_two, scale_two)
    back_two, grad_second_gain, grad_shift_two, grad_scale_two = pull_two(grad_normed_two)
    grad_after = grad_two + back_two
    grad_attn = both_rows((gate_one * grad_after).astype(LOW))
    grad_gate_one = grad_after * attn_rows
    grad_mixed = dot_float(grad_attn, out_full).astype(LOW)
    grad_mixed_parts = send_parts(
        grad_mixed.reshape(token_count, SPLIT, part_width).transpose(1, 0, 2)
    )
    query_grad, pair_grads, text_grads, gate_sums = attention_backward(
        queries,
        jnp.pad(
            jnp.concatenate(grad_mixed_parts, axis=0), ((0, 0), (0, query_width - part_width))
        ),
        query_select,
        mixed_select,
        query_features,
        pairs,
        key_features,
        text_pairs,
        text_features,
        gate_lanes,
        head_outs,
        head_stats,
    )
    pair_sum = collect(pair_grads).astype(LOW)
    query_packed = query_grad.reshape(group_tokens, each, 128)[..., :64].reshape(
        group_tokens, part_width
    )
    back_slots = jnp.concatenate(
        [
            query_packed,
            jnp.zeros((group_tokens, query_width - part_width), LOW),
            pair_sum,
        ],
        axis=1,
    ).reshape(SPLIT, token_count, -1)
    back_parts = return_parts([back_slots[index] for index in range(SPLIT)])
    qkv_grad, gain_sums = rope_backward(back_parts, qkv_raw, cosine, sine, gains, heads)
    grad_normed_one = own_rows(dot_turned(qkv_grad, qkv_full))
    attention_grads = outer_products(
        jnp.stack([normed_all.T, grad_attn.T]),
        jnp.concatenate([qkv_grad, mixed], axis=1),
        3 * local_width,
        local_width,
    )
    attention_shard = lax.psum_scatter(
        attention_grads, "dp", scatter_dimension=0, tiled=True
    ).astype(FLOAT)

    text_grad_sum = collect(text_grads).reshape(group_rows, each, 2 * head_size)
    text_key_low = text_grad_sum[..., :head_size].astype(LOW).astype(FLOAT)
    _, pull_text = jax.vjp(norm_rows, text_key_raw, ky_gain)
    text_raw_grad, grad_ky_gain = pull_text(text_key_low)
    text_low = jnp.concatenate(
        [
            text_raw_grad.astype(LOW).reshape(group_rows, part_width),
            text_grad_sum[..., head_size:].astype(LOW).reshape(group_rows, part_width),
        ],
        axis=1,
    )
    text_all = spread(
        in_place([text_low] + [shift(text_low, -steps) for steps in range(1, SPLIT)])
        .transpose(1, 0, 2)
        .reshape(group_rows, 2 * local_width)
    )
    grad_text_kv = (
        matmul(text_near, text_all, 0, 0)
        .reshape(-1, SPLIT, 2, part_width)
        .transpose(2, 0, 1, 3)
        .reshape(2, -1, local_width)
    )
    grad_text_part = dot_turned(text_all, text_weight).astype(LOW)
    grad_text_pair = grad_text_part.astype(FLOAT) + swapped(grad_text_part).astype(FLOAT)
    grad_text_groups = grad_text_pair.astype(LOW).reshape(near, group_rows, -1)
    orders = jnp.arange(near, dtype=jnp.int32)
    flip_at = jnp.array(flips, jnp.int32)
    grad_text_rows = jnp.concatenate(
        [
            pick(grad_text_groups, jnp.sum(jnp.where(flip_at == near_index ^ group, orders, 0)))
            for group in range(near)
        ],
        axis=0,
    )
    grad_text_all = lax.all_to_all(grad_text_rows, "dp", split_axis=0, concat_axis=1, tiled=True)
    half_text = text_tokens.shape[1] // 2
    grad_text = lax.dynamic_slice_in_dim(
        grad_text_all, tensor_index * half_text, half_text, 1
    ).astype(FLOAT)

    _, pull_one = jax.vjp(modulated, input_rows, first_gain, shift_one, scale_one)
    back_one, grad_first_gain, grad_shift_one, grad_scale_one = pull_one(grad_normed_one)
    grad_inputs = grad_after + back_one
    clip_at = jnp.arange(clip_count, dtype=jnp.int32)[:, None]

    def clip_sums(values):
        first_sum = jnp.sum(jnp.where(first_clip, values, 0.0), axis=0)[None]
        other_sum = jnp.sum(jnp.where(first_clip, 0.0, values), axis=0)[None]
        return jnp.where(clip_at == 0, first_sum, jnp.where(clip_at == other_clip, other_sum, 0.0))

    mod_grads = jnp.concatenate(
        [
            clip_sums(values)
            for values in (
                grad_shift_one,
                grad_scale_one,
                grad_gate_one,
                grad_shift_two,
                grad_scale_two,
                grad_gate_two,
            )
        ],
        axis=1,
    )
    head_sums = (1.0 - gate_heads * gate_heads) * jnp.sum(
        gate_sums.reshape(8, each, 128), axis=(0, 2)
    )
    head_row = lax.dynamic_update_slice_in_dim(
        jnp.zeros((head_gate.shape[0],), FLOAT),
        head_sums,
        tensor_index * heads + far_index * each,
        0,
    )
    gain_halves = gain_sums[:2, :head_size] + gain_sums[:2, head_size:]
    small = jnp.concatenate(
        [grad_first_gain, grad_second_gain, gain_halves.reshape(-1), grad_ky_gain, head_row]
    )
    small_row = jnp.concatenate([small, jnp.zeros((mod_grads.shape[1] - small.shape[0],), FLOAT)])
    grad_sums = jnp.concatenate([mod_grads, small_row[None]], axis=0)
    grad_sums = sum_dp(grad_sums + swapped(grad_sums))
    grad_mod_low = grad_sums[:clip_count].astype(LOW)
    sums = grad_sums[clip_count]
    first_gain_sum = sums[:width]
    second_gain_sum = sums[width : 2 * width]
    at = 2 * width
    q_gain_sum = sums[at : at + head_size]
    k_gain_sum = sums[at + head_size : at + 2 * head_size]
    ky_gain_sum = sums[at + 2 * head_size : at + 3 * head_size]
    gate_sum = sums[at + 3 * head_size : at + 3 * head_size + head_gate.shape[0]]
    grad_ada_bias = jnp.sum(grad_mod_low.astype(FLOAT), axis=0)
    grad_ada = matmul(silu_slice, grad_mod_low, 0, 0)
    cond_part = lax.dynamic_update_slice_in_dim(
        jnp.zeros(cond_float.shape, FLOAT),
        dot_turned(grad_mod_low, ada_weight),
        dp_index * cond_rows,
        1,
    )
    cond_sigmoid = jax.nn.sigmoid(cond_float)
    grad_conditioning = (
        sum_dp(cond_part) * cond_sigmoid * (1.0 + cond_float * (1.0 - cond_sigmoid))
    )
    qkv_shard = (
        attention_shard[:, : 3 * local_width]
        .reshape(weight_rows, 3, local_width)
        .transpose(1, 0, 2)
    )
    out_shard = attention_shard[:, 3 * local_width :].T
    gate_up_shard = jnp.stack(
        [feed_shard[:, :hidden_count], feed_shard[:, hidden_count : 2 * hidden_count]]
    )
    down_shard = feed_shard[:, 2 * hidden_count :].T
    return (
        output,
        grad_inputs,
        grad_text,
        grad_conditioning,
        grad_ada,
        grad_ada_bias,
        first_gain_sum,
        q_gain_sum,
        k_gain_sum,
        ky_gain_sum,
        gate_sum,
        qkv_shard,
        out_shard,
        grad_text_kv,
        second_gain_sum,
        gate_up_shard,
        down_shard,
    )


def solution(mesh):
    placed = (
        P(("dp", "tensor"), None),
        P("dp"),
        P("dp"),
        P("dp", None),
        P(),
        P("dp", None),
        P(),
        P(),
        P(),
        P(),
        P(),
        P(),
        P(None, "dp", "tensor"),
        P("tensor", "dp"),
        P(None, "dp", "tensor"),
        P(),
        P(None, "dp", "tensor"),
        P("tensor", "dp"),
        P(("dp", "tensor"), None),
    )
    return jax.shard_map(
        shards,
        mesh=mesh,
        in_specs=placed,
        out_specs=(
            P(("dp", "tensor"), None),
            P(("dp", "tensor"), None),
            P("dp", "tensor"),
            P(),
            P("dp", None),
            P(),
            P(),
            P(),
            P(),
            P(),
            P(),
            P(None, "dp", "tensor"),
            P("tensor", "dp"),
            P(None, "dp", "tensor"),
            P(),
            P(None, "dp", "tensor"),
            P("tensor", "dp"),
        ),
        check_vma=False,
    )
```

time: 2670 us -> 918 us (0.34)
  waiting for transfers between devices: 1480 us -> 427 us
  local copies, waits for them, and re-layouts: 654 us -> 94.9 us
  matrix products: 283 us -> 50.1 us
  Pallas kernels: 0 us -> 137 us
  blocking collectives: 112 us -> 0 us
  starting transfers between devices: 1.65 us -> 85.1 us
    reduce_scatter x14 -> x2, waiting for transfers between devices: 1010 us -> 117 us  [the longest x1 117 us: shards(): lax.psum_scatter(feed_grads, 'dp', scatter_dimension=0, tiled=True)]
    dynamic_update_slice x20 -> x1, local copies, waits for them, and re-layouts: 504 us -> 0.11 us  [shards(): lax.dynamic_update_slice_in_dim(jnp.zeros(cond_float.shape, FLOAT), dot_t...]
    all_gather x10 -> x2, waiting for transfers between devices: 470 us -> 68.6 us  [the longest x1 68.6 us: shards(): lax.all_gather(qkv_weight.transpose(1, 0, 2).reshape(weight_rows, 3 * loc...]
    ppermute x0 -> x52, waiting for transfers between devices: none -> 242 us  [the longest x18 99.7 us: shift(): return lax.ppermute(values, 'dp', pairs)]
    dot_general x65 -> x14, matrix products: 277 us -> 50.1 us  [the longest x8 30.1 us: matmul(): lax.dot_general(left, right, (((left_dim,), (right_dim,)), ((), ())), pre...]
    pallas_call x0 -> x6, Pallas kernels: none -> 137 us  [the longest x1 70.6 us: attention_backward(): pl.pallas_call(functools.partial(backward_kernel, chunk), grid=(heads, ro...]
    all_gather x5 -> x0, blocking collectives: 65 us -> none  [the longest x2 23.2 us: gather_grads(): return lax.all_gather(values, 'tensor', axis=0, tiled=True)]
    ppermute x0 -> x52, starting transfers between devices: none -> 64.3 us  [the longest x18 32.6 us: shift(): return lax.ppermute(values, 'dp', pairs)]
  transfers between devices with their start and end apart: 24 -> 58, of which waited for: 18 -> 36; matrix products, arithmetic and copies ran while one was open for 37% -> 18% of each run, Pallas kernels for 0% -> 6%
where the time goes in v1:
time: 918 us; the launch traced here: 906 us
  waiting for transfers between devices  427 us (47%)
  Pallas kernels  137 us (15%)
  local copies, waits for them, and re-layouts  94.9 us (10%)
  other arithmetic  86.4 us (9%)
  starting transfers between devices  85.1 us (9%)
  matrix products  50.1 us (5%)
  between operations  26 us (3%)
    reduce_scatter x1, waiting for transfers between devices, shards(): lax.psum_scatter(feed_grads, 'dp', scatter_dimension=0, tiled=True)  117 us
    ppermute x18, waiting for transfers between devices, shift(): return lax.ppermute(values, 'dp', pairs)  99.7 us
    ppermute x24, waiting for transfers between devices, flip(): return lax.ppermute(values, 'dp', [(j, j ^ bit) for j in range(dp)])  91 us
    pallas_call x1, Pallas kernels, attention_backward(): pl.pallas_call(functools.partial(backward_kernel, chunk), grid=(heads, ro...  70.6 us
    all_gather x1, waiting for transfers between devices, shards(): lax.all_gather(qkv_weight.transpose(1, 0, 2).reshape(weight_rows, 3 * loc...  68.6 us
    ppermute x10, waiting for transfers between devices, swapped(): return lax.ppermute(values, 'tensor', [(0, 1), (1, 0)])  51.1 us
    pallas_call x1, Pallas kernels, attention_forward(): pl.pallas_call(functools.partial(forward_kernel, chunk), grid=(heads, row...  43.9 us
    ppermute x18, starting transfers between devices, shift(): return lax.ppermute(values, 'dp', pairs)  32.6 us
  transfers between devices with their start and end apart: 58, of which 36 were waited for; matrix products, arithmetic and copies ran while one was open for 18% of the time, Pallas kernels for 6%

profile of v1, /device:TPU:0, one launch (start us, length us, event | category | flops | bytes accessed | tf_op | source)
XLA Modules:
  0.0 906.4 jit_solution(11103001159316095387)
XLA Ops:
  11.6 68.6 %all-gather.3.cloned.1.call-done = bf16[1536,2304]{1,0:T(8,128)(2,1)} async-done(((bf16[96,2304]{1,0:T(8,128)(2,1)}), bf16[1536,2304]{1,0:T(8,128)(2,1)}) %all-gather.3.cloned.1.call-update) | async-done | bytes 7077904 | tf_op jit(solution)/shard_map/all_gather | solution.py:512
  83.8 3.7 all-to-all-start
  97.5 8.0 collective-permute-done.1
  106.6 8.4 collective-permute-done.2
  123.1 2.3 pad_maximum_fusion.33
  125.4 3.3 collective-permute-done.3
  131.9 4.8 broadcast_select_fusion
  143.5 7.3 collective-permute-done.4
  152.9 2.9 shard_map.323
  156.9 3.2 collective-permute-start.7
  160.2 10.4 %collective-permute-done.11 = bf16[192,1536]{1,0:T(8,128)(2,1)S(1)} collective-permute-done((bf16[192,1536]{1,0:T(8,128)(2,1)S(1)}, bf16[192,1536]{1,0:T(8,128)(2,1)S(1)}, u32[]{:S(2)}, u32[]{:S(2)}) %collective-permute-start.11) | collective-permute-done | bytes 589856 | tf_op jit(solution)/shard_map/ppermute | solution.py:468
  171.5 2.3 reshape.897
  173.9 3.6 collective-permute-start.5
  177.5 3.1 constant_dynamic-slice_fusion.12
  184.3 21.7 %collective-permute-done.6 = bf16[256,640]{1,0:T(8,128)(2,1)S(1)} collective-permute-done((bf16[256,640]{1,0:T(8,128)(2,1)}, bf16[256,640]{1,0:T(8,128)(2,1)S(1)}, u32[]{:S(2)}, u32[]{:S(2)}) %collective-permute-start.6) | collective-permute-done | bytes 327712 | tf_op jit(solution)/shard_map/ppermute | solution.py:472
  210.2 14.3 %collective-permute-done.13 = bf16[192,384]{1,0:T(8,128)(2,1)S(1)} collective-permute-done((bf16[192,384]{1,0:T(8,128)(2,1)S(1)}, bf16[192,384]{1,0:T(8,128)(2,1)S(1)}, u32[]{:S(2)}, u32[]{:S(2)}) %collective-permute-start.13) | collective-permute-done | bytes 147488 | tf_op jit(solution)/shard_map/ppermute | solution.py:472
  244.4 3.6 pad_maximum_fusion.kv_ref
  248.1 43.9 %shard_map.324 = (bf16[1024,384]{1,0:T(8,128)(2,1)S(1)}, f32[1024,384]{1,0:T(8,128)S(1)}, f32[1024,384]{1,0:T(8,128)}) custom-call(bf16[1024,256]{1,0:T(8,128)(2,1)S(1)} %pad_maximum_fusion.21.q_ref, bf16[3,256,128]{2,1,0:T(8,128)(2,1)S(1)} %copy-done.13, bf16[1024,128]{1,0:T(8,128)(2,1)S(1)} %select_convert_fusion.qf_ref, ...), custom_call_target="tpu_custom_call" | custom-call | flops 7650410496 | bytes 12582912 | tf_op jit(solution)/shard_map/pallas_call | solution.py:96
  296.3 2.6 reshape.901
  299.0 2.5 fusion.100
  301.5 2.7 collective-permute-start.17
  304.2 5.3 collective-permute-start.18
  309.6 2.5 collective-permute-start.19
  312.1 6.8 collective-permute-done.18
  319.8 2.5 fusion.14
  327.1 8.1 collective-permute-done.20
  341.4 10.0 %collective-permute-done.21 = bf16[128,1536]{0,1:T(8,128)(2,1)S(1)} collective-permute-done((bf16[128,1536]{0,1:T(8,128)(2,1)S(1)}, bf16[128,1536]{0,1:T(8,128)(2,1)S(1)}, u32[]{:S(2)}, u32[]{:S(2)}) %collective-permute-start.21) | collective-permute-done | bytes 393248 | tf_op jit(solution)/shard_map/ppermute | solution.py:417
  351.4 6.7 fusion.2
  358.1 7.0 multiply_convert_fusion.1
  365.1 10.0 %fusion = f32[256,1536]{0,1:T(8,128)} fusion(bf16[1536,6912]{1,0:T(8,128)(2,1)} %all-gather.5.cloned.1.call-done, bf16[256,2048]{1,0:T(8,128)(2,1)} %get-tuple-element.185, bf16[256,2048]{1,0:T(8,128)(2,1)S(1)} %get-tuple-element.184), kind=kOutput, calls=%fused_computation | convolution fusion | flops 3225419776 | bytes 16252928 | tf_op jit(solution)/shard_map/dot_general | solution.py:28
  377.4 7.2 collective-permute-done.24
  384.5 3.2 select_reduce_fusion.3
  390.6 6.1 collective-permute-done.25
  397.5 3.2 fusion.17
  421.0 70.6 %shard_map.325 = (bf16[1024,384]{1,0:T(8,128)(2,1)}, bf16[4096,384]{1,0:T(8,128)(2,1)}, bf16[768,384]{1,0:T(8,128)(2,1)}, f32[8,384]{1,0:T(8,128)}) custom-call(bf16[1024,256]{1,0:T(8,128)(2,1)} %copy-done.11, bf16[1024,256]{1,0:T(8,128)(2,1)} %fusion.42.dm_ref, bf16[3,256,128]{2,1,0:T(8,128)(2,1)} %select_convert_fusion.2.sel_ref, ...), custom_call_target="tpu_custom_call" | custom-call | flops 19126026240 | bytes 18874368 | tf_op jit(solution)/shard_map/pallas_call | solution.py:213
  493.4 3.4 collective-permute-done.29
  512.3 7.3 collective-permute-done.30
  525.3 6.4 collective-permute-done.31
  531.8 19.6 %collective-permute-done.32 = bf16[256,640]{1,0:T(8,128)(2,1)S(1)} collective-permute-done((bf16[256,640]{1,0:T(8,128)(2,1)S(1)}, bf16[256,640]{1,0:T(8,128)(2,1)S(1)}, u32[]{:S(2)}, u32[]{:S(2)}) %collective-permute-start.32) | collective-permute-done | bytes 327712 | tf_op jit(solution)/shard_map/ppermute | solution.py:472
  552.6 3.9 shard_map.326
  557.7 3.9 shard_map.327
  561.6 3.6 copy-done.1
  568.7 11.5 %shard_map.328 = bf16[1536,6144]{1,0:T(8,128)(2,1)} custom-call(bf16[2,1536,256]{2,1,0:T(8,128)(2,1)S(1)} %pad_maximum_fusion.6.left_ref, bf16[256,6144]{1,0:T(8,128)(2,1)S(1)} %pad_maximum_fusion.1.right_ref), custom_call_target="tpu_custom_call" | custom-call | flops 4831838208 | bytes 18874368 | tf_op jit(solution)/shard_map/pallas_call | solution.py:380
  584.8 4.4 collective-permute-done.36
  590.6 3.0 collective-permute-start.38
  596.9 26.1 %collective-permute-done.38 = bf16[192,384]{0,1:T(8,128)(2,1)S(1)} collective-permute-done((bf16[192,384]{0,1:T(8,128)(2,1)S(1)}, bf16[192,384]{0,1:T(8,128)(2,1)S(1)}, u32[]{:S(2)}, u32[]{:S(2)}) %collective-permute-start.38) | collective-permute-done | bytes 147488 | tf_op jit(solution)/shard_map/ppermute | solution.py:472
  625.1 8.4 collective-permute-done.40
  644.1 5.1 fusion.6
  652.8 2.8 convolution_convert_fusion
  656.9 5.1 fusion.105
  663.6 2.3 fusion.25
  667.3 3.2 copy.253
  671.2 8.8 collective-permute-done.34
  680.0 5.9 select_reduce_fusion.1
  693.6 3.6 collective-permute-done.43
  698.2 16.7 %all-to-all-start.1 = ((bf16[16,48,256]{2,1,0:T(8,128)(2,1)}), bf16[16,48,256]{2,1,0:T(8,128)(2,1)}, u32[]{:S(2)}, u32[]{:S(2)}) async-start(bf16[16,48,256]{2,1,0:T(8,128)(2,1)} %bitcast.79), calls=%async_computation.1 | async-start | bytes 786432 | tf_op jit(solution)/shard_map/all_to_all | solution.py:780
  717.6 6.9 collective-permute-done.45
  730.2 2.5 copy.251
  734.8 2.7 collective-permute-start.47
  738.3 15.4 %collective-permute-done.47 = f32[4,9216]{1,0:T(4,128)S(1)} collective-permute-done((f32[4,9216]{1,0:T(4,128)S(1)}, f32[4,9216]{1,0:T(4,128)S(1)}, u32[]{:S(2)}, u32[]{:S(2)}) %collective-permute-start.47) | collective-permute-done | bytes 147488 | tf_op jit(solution)/shard_map/ppermute | solution.py:468
  758.4 2.4 collective-permute-done.49
  761.8 5.2 collective-permute-done.50
  767.6 5.2 collective-permute-done.51
  779.0 116.6 %reduce-scatter.5.cloned.1.call-done = bf16[96,6144]{1,0:T(8,128)(2,1)} async-done(((bf16[1536,6144]{1,0:T(8,128)(2,1)}), bf16[96,6144]{1,0:T(8,128)(2,1)}) %reduce-scatter.5.cloned.1.call-update) | async-done | bytes 1179664 | tf_op jit(solution)/shard_map/reduce_scatter | solution.py:694
  (549 shorter events, 195.9 us)
Async XLA Ops:
  7.2 73.9 %copy-start = (bf16[64,9216]{1,0:T(8,128)(2,1)S(1)}, bf16[64,9216]{1,0:T(8,128)(2,1)}, u32[]{:S(2)}) copy-start(bf16[64,9216]{1,0:T(8,128)(2,1)} %param.25) | copy-start | bytes 3538948
  7.2 73.0 %all-gather.3.cloned.1.call-start = ((), (), s32[]{:S(2)}) async-start(), calls=%async_computation.4 | async-start | bytes 7520256 | tf_op jit(solution)/shard_map/all_gather | solution.py:512
  9.2 310.5 %all-gather.5.cloned.1.call-start = ((), (), s32[]{:S(2)}) async-start(), calls=%async_computation.5 | async-start | bytes 22560768 | tf_op jit(solution)/shard_map/all_gather | solution.py:522
  10.4 69.9 %copy-start.79 = (bf16[3,1024]{1,0:T(4,128)(2,1)S(1)}, bf16[3,1024]{1,0:T(4,128)(2,1)}, u32[]{:S(2)}) copy-start(bf16[3,1024]{1,0:T(4,128)(2,1)} %param.24) | copy-start | bytes 18436
  10.4 70.0 %copy-start.101 = (s32[256]{0:T(256)S(1)}, s32[256]{0:T(256)}, u32[]{:S(2)}) copy-start(s32[256]{0:T(256)} %param.21) | copy-start | bytes 3076
  11.6 71.4 %copy-start.62 = (bf16[48,4096]{1,0:T(8,128)(2,1)S(1)}, bf16[48,4096]{1,0:T(8,128)(2,1)}, u32[]{:S(2)}) copy-start(bf16[48,4096]{1,0:T(8,128)(2,1)} %param.23) | copy-start | bytes 1179652
  11.6 76.0 %copy-start.63 = (bf16[128,1536]{1,0:T(8,128)(2,1)S(1)}, bf16[128,1536]{1,0:T(8,128)(2,1)}, u32[]{:S(2)}) copy-start(bf16[128,1536]{1,0:T(8,128)(2,1)} %param.20) | copy-start | bytes 1179652
  82.7 11.7 %collective-permute-start = (f32[4,9216]{1,0:T(4,128)}, f32[4,9216]{1,0:T(4,128)S(1)}, u32[]{:S(2)}, u32[]{:S(2)}) collective-permute-start(f32[4,9216]{1,0:T(4,128)} %pad_maximum_fusion.31), channel_id=1, source_target_pairs={{0,2},{2,0},{4,6},{6,4},{8,10},{10,8},{12,14},{14,12},{16,18},{18,... | collective-permute-start | bytes 442376 | tf_op jit(solution)/shard_map/ppermute | solution.py:468
  83.8 46.9 %all-to-all-start = ((bf16[48,16,256]{2,0,1:T(8,128)(2,1)}), bf16[48,16,256]{2,0,1:T(8,128)(2,1)S(1)}, u32[]{:S(2)}, u32[]{:S(2)}) async-start(bf16[48,16,256]{2,0,1:T(8,128)(2,1)} %bitcast.200), calls=%async_computation | async-start | bytes 786432 | tf_op jit(solution)/shard_map/all_to_all | solution.py:583
  87.5 685.9 %reduce-scatter.3.cloned.1.call-start = ((), (), s32[]{:S(2)}) async-start(), calls=%async_computation.6 | async-start | bytes 10027008 | tf_op jit(solution)/shard_map/reduce_scatter | solution.py:742
  94.5 11.0 %collective-permute-start.1 = (f32[4,9216]{1,0:T(4,128)S(1)}, f32[4,9216]{1,0:T(4,128)S(1)}, u32[]{:S(2)}, u32[]{:S(2)}) collective-permute-start(f32[4,9216]{1,0:T(4,128)S(1)} %fusion.118), channel_id=1, source_target_pairs={{0,4},{2,6},{4,0},{6,2},{8,12},{10,14},{12,8},{14,10},{16,20},{18,... | collective-permute-start | bytes 442376 | tf_op jit(solution)/shard_map/ppermute | solution.py:468
  105.5 9.4 %collective-permute-start.2 = (f32[4,9216]{1,0:T(4,128)S(1)}, f32[4,9216]{1,0:T(4,128)S(1)}, u32[]{:S(2)}, u32[]{:S(2)}) collective-permute-start(f32[4,9216]{1,0:T(4,128)S(1)} %add.512), channel_id=1, source_target_pairs={{0,8},{2,10},{4,12},{6,14},{8,0},{10,2},{12,4},{14,6},{16,24},{18,... | collective-permute-start | bytes 442376 | tf_op jit(solution)/shard_map/ppermute | solution.py:468
  115.6 13.1 %collective-permute-start.3 = (f32[4,9216]{1,0:T(4,128)}, f32[4,9216]{1,0:T(4,128)}, u32[]{:S(2)}, u32[]{:S(2)}) collective-permute-start(f32[4,9216]{1,0:T(4,128)} %add.513), channel_id=1, source_target_pairs={{0,16},{2,18},{4,20},{6,22},{8,24},{10,26},{12,28},{14,30},{16,0},... | collective-permute-start | bytes 442376 | tf_op jit(solution)/shard_map/ppermute | solution.py:468
  131.7 9.8 %collective-permute-start.10 = (bf16[384,1536]{1,0:T(8,128)(2,1)S(1)}, bf16[384,1536]{1,0:T(8,128)(2,1)S(1)}, u32[]{:S(2)}, u32[]{:S(2)}) collective-permute-start(bf16[384,1536]{1,0:T(8,128)(2,1)S(1)} %slice.452), channel_id=1, source_target_pairs={{0,2},{2,0},{4,6},{6,4},{8,10},{10,8},{12,14},{14,12},{16,18},{18,... | collective-permute-start | bytes 3538952 | tf_op jit(solution)/shard_map/ppermute | solution.py:468
  139.3 11.5 %collective-permute-start.4 = (bf16[128,1536]{0,1:T(8,128)(2,1)S(1)}, bf16[128,1536]{0,1:T(8,128)(2,1)S(1)}, u32[]{:S(2)}, u32[]{:S(2)}) collective-permute-start(bf16[128,1536]{0,1:T(8,128)(2,1)S(1)} %fusion.31), channel_id=1, source_target_pairs={{0,1},{1,0},{2,3},{3,2},{4,5},{5,4},{6,7},{7,6},{8,9},{9,8},{10,11... | collective-permute-start | bytes 1179656 | tf_op jit(solution)/shard_map/ppermute | solution.py:417
  141.9 28.6 %collective-permute-start.11 = (bf16[192,1536]{1,0:T(8,128)(2,1)S(1)}, bf16[192,1536]{1,0:T(8,128)(2,1)S(1)}, u32[]{:S(2)}, u32[]{:S(2)}) collective-permute-start(bf16[192,1536]{1,0:T(8,128)(2,1)S(1)} %slice.454), channel_id=1, source_target_pairs={{0,4},{2,6},{4,0},{6,2},{8,12},{10,14},{12,8},{14,10},{16,20},{18,... | collective-permute-start | bytes 1769480 | tf_op jit(solution)/shard_map/ppermute | solution.py:468
  156.9 25.4 %collective-permute-start.7 = (bf16[256,640]{1,0:T(8,128)(2,1)}, bf16[256,640]{1,0:T(8,128)(2,1)}, u32[]{:S(2)}, u32[]{:S(2)}) collective-permute-start(bf16[256,640]{1,0:T(8,128)(2,1)} %get-tuple-element.196), channel_id=1, source_target_pairs={{0,24},{2,26},{4,28},{6,30},{8,0},{10,2},{12,4},{14,6},{16,8},{18,... | collective-permute-start | bytes 983048 | tf_op jit(solution)/shard_map/ppermute | solution.py:472
  173.8 32.2 %collective-permute-start.6 = (bf16[256,640]{1,0:T(8,128)(2,1)}, bf16[256,640]{1,0:T(8,128)(2,1)S(1)}, u32[]{:S(2)}, u32[]{:S(2)}) collective-permute-start(bf16[256,640]{1,0:T(8,128)(2,1)} %get-tuple-element.197), channel_id=1, source_target_pairs={{0,16},{2,18},{4,20},{6,22},{8,24},{10,26},{12,28},{14,30},{16,0},... | collective-permute-start | bytes 983048 | tf_op jit(solution)/shard_map/ppermute | solution.py:472
  173.9 32.9 %collective-permute-start.5 = (bf16[256,640]{1,0:T(8,128)(2,1)}, bf16[256,640]{1,0:T(8,128)(2,1)S(1)}, u32[]{:S(2)}, u32[]{:S(2)}) collective-permute-start(bf16[256,640]{1,0:T(8,128)(2,1)} %get-tuple-element.198), channel_id=1, source_target_pairs={{0,8},{2,10},{4,12},{6,14},{8,16},{10,18},{12,20},{14,22},{16,24},... | collective-permute-start | bytes 983048 | tf_op jit(solution)/shard_map/ppermute | solution.py:472
  180.7 29.6 %collective-permute-start.14 = (bf16[192,384]{1,0:T(8,128)(2,1)S(1)}, bf16[192,384]{1,0:T(8,128)(2,1)S(1)}, u32[]{:S(2)}, u32[]{:S(2)}) collective-permute-start(bf16[192,384]{1,0:T(8,128)(2,1)S(1)} %bitcast.246), channel_id=1, source_target_pairs={{0,24},{2,26},{4,28},{6,30},{8,0},{10,2},{12,4},{14,6},{16,8},{18,... | collective-permute-start | bytes 442376 | tf_op jit(solution)/shard_map/ppermute | solution.py:472
  181.0 43.5 %collective-permute-start.13 = (bf16[192,384]{1,0:T(8,128)(2,1)S(1)}, bf16[192,384]{1,0:T(8,128)(2,1)S(1)}, u32[]{:S(2)}, u32[]{:S(2)}) collective-permute-start(bf16[192,384]{1,0:T(8,128)(2,1)S(1)} %bitcast.247), channel_id=1, source_target_pairs={{0,16},{2,18},{4,20},{6,22},{8,24},{10,26},{12,28},{14,30},{16,0},... | collective-permute-start | bytes 442376 | tf_op jit(solution)/shard_map/ppermute | solution.py:472
  182.3 43.0 %collective-permute-start.12 = (bf16[192,384]{1,0:T(8,128)(2,1)S(1)}, bf16[192,384]{1,0:T(8,128)(2,1)S(1)}, u32[]{:S(2)}, u32[]{:S(2)}) collective-permute-start(bf16[192,384]{1,0:T(8,128)(2,1)S(1)} %bitcast.248), channel_id=1, source_target_pairs={{0,8},{2,10},{4,12},{6,14},{8,16},{10,18},{12,20},{14,22},{16,24},... | collective-permute-start | bytes 442376 | tf_op jit(solution)/shard_map/ppermute | solution.py:472
  208.7 28.8 %collective-permute-start.8 = (bf16[1024,384]{1,0:T(8,128)(2,1)}, bf16[1024,384]{1,0:T(8,128)(2,1)}, u32[]{:S(2)}, u32[]{:S(2)}) collective-permute-start(bf16[1024,384]{1,0:T(8,128)(2,1)} %pad_maximum_fusion.13), channel_id=1, source_target_pairs={{0,4},{2,6},{4,0},{6,2},{8,12},{10,14},{12,8},{14,10},{16,20},{18,... | collective-permute-start | bytes 2359304 | tf_op jit(solution)/shard_map/ppermute | solution.py:468
  236.1 5.4 collective-permute-start.15
  239.1 5.2 collective-permute-start.9
  241.5 1.6 collective-permute-start.16
  301.5 10.6 %collective-permute-start.17 = (bf16[256,192]{0,1:T(8,128)(2,1)S(1)}, bf16[256,192]{0,1:T(8,128)(2,1)S(1)}, u32[]{:S(2)}, u32[]{:S(2)}) collective-permute-start(bf16[256,192]{0,1:T(8,128)(2,1)S(1)} %bitcast.253), channel_id=1, source_target_pairs={{0,24},{2,26},{4,28},{6,30},{8,0},{10,2},{12,4},{14,6},{16,8},{18,... | collective-permute-start | bytes 294920 | tf_op jit(solution)/shard_map/ppermute | solution.py:472
  304.2 14.7 %collective-permute-start.18 = (bf16[256,192]{0,1:T(8,128)(2,1)S(1)}, bf16[256,192]{0,1:T(8,128)(2,1)S(1)}, u32[]{:S(2)}, u32[]{:S(2)}) collective-permute-start(bf16[256,192]{0,1:T(8,128)(2,1)S(1)} %bitcast.254), channel_id=1, source_target_pairs={{0,16},{2,18},{4,20},{6,22},{8,24},{10,26},{12,28},{14,30},{16,0},... | collective-permute-start | bytes 294920 | tf_op jit(solution)/shard_map/ppermute | solution.py:472
  309.6 9.3 %collective-permute-start.19 = (bf16[256,192]{0,1:T(8,128)(2,1)S(1)}, bf16[256,192]{0,1:T(8,128)(2,1)S(1)}, u32[]{:S(2)}, u32[]{:S(2)}) collective-permute-start(bf16[256,192]{0,1:T(8,128)(2,1)S(1)} %bitcast.255), channel_id=1, source_target_pairs={{0,8},{2,10},{4,12},{6,14},{8,16},{10,18},{12,20},{14,22},{16,24},... | collective-permute-start | bytes 294920 | tf_op jit(solution)/shard_map/ppermute | solution.py:472
  324.2 11.0 %collective-permute-start.20 = (bf16[128,1536]{0,1:T(8,128)(2,1)}, bf16[128,1536]{0,1:T(8,128)(2,1)}, u32[]{:S(2)}, u32[]{:S(2)}) collective-permute-start(bf16[128,1536]{0,1:T(8,128)(2,1)} %slice.458), channel_id=1, source_target_pairs={{0,1},{1,0},{2,3},{3,2},{4,5},{5,4},{6,7},{7,6},{8,9},{9,8},{10,11... | collective-permute-start | bytes 1179656 | tf_op jit(solution)/shard_map/ppermute | solution.py:417
  337.0 50.7 %copy-start.18 = (f32[128,1536]{0,1:T(8,128)}, f32[128,1536]{0,1:T(8,128)S(1)}, u32[]{:S(2)}) copy-start(f32[128,1536]{0,1:T(8,128)S(1)} %get-tuple-element.182) | copy-start | bytes 2359300
  339.3 12.1 %collective-permute-start.21 = (bf16[128,1536]{0,1:T(8,128)(2,1)S(1)}, bf16[128,1536]{0,1:T(8,128)(2,1)S(1)}, u32[]{:S(2)}, u32[]{:S(2)}) collective-permute-start(bf16[128,1536]{0,1:T(8,128)(2,1)S(1)} %get-tuple-element.187), channel_id=1, source_target_pairs={{0,1},{1,0},{2,3},{3,2},{4,5},{5,4},{6,7},{7,6},{8,9},{9,8},{10,11... | collective-permute-start | bytes 1179656 | tf_op jit(solution)/shard_map/ppermute | solution.py:417
  340.4 17.7 %collective-permute-start.23 = (bf16[128,1536]{0,1:T(8,128)(2,1)S(1)}, bf16[128,1536]{0,1:T(8,128)(2,1)S(1)}, u32[]{:S(2)}, u32[]{:S(2)}) collective-permute-start(bf16[128,1536]{0,1:T(8,128)(2,1)S(1)} %get-tuple-element.186), channel_id=1, source_target_pairs={{0,1},{1,0},{2,3},{3,2},{4,5},{5,4},{6,7},{7,6},{8,9},{9,8},{10,11... | collective-permute-start | bytes 1179656 | tf_op jit(solution)/shard_map/ppermute | solution.py:417
  376.3 8.3 collective-permute-start.24
  388.9 7.8 collective-permute-start.25
  406.1 10.9 %collective-permute-start.28 = (bf16[256,192]{1,0:T(8,128)(2,1)}, bf16[256,192]{1,0:T(8,128)(2,1)}, u32[]{:S(2)}, u32[]{:S(2)}) collective-permute-start(bf16[256,192]{1,0:T(8,128)(2,1)} %bitcast.250), channel_id=1, source_target_pairs={{0,24},{2,26},{4,28},{6,30},{8,0},{10,2},{12,4},{14,6},{16,8},{18,... | collective-permute-start | bytes 294920 | tf_op jit(solution)/shard_map/ppermute | solution.py:472
  408.6 8.5 collective-permute-start.27
  411.8 7.1 collective-permute-start.26
  493.3 3.5 collective-permute-start.29
  499.7 19.9 %collective-permute-start.30 = (bf16[1024,384]{1,0:T(8,128)(2,1)}, bf16[1024,384]{1,0:T(8,128)(2,1)}, u32[]{:S(2)}, u32[]{:S(2)}) collective-permute-start(bf16[1024,384]{1,0:T(8,128)(2,1)} %slice.453), channel_id=1, source_target_pairs={{0,4},{2,6},{4,0},{6,2},{8,12},{10,14},{12,8},{14,10},{16,20},{18,... | collective-permute-start | bytes 2359304 | tf_op jit(solution)/shard_map/ppermute | solution.py:468
  521.7 10.0 %collective-permute-start.31 = (bf16[256,640]{1,0:T(8,128)(2,1)S(1)}, bf16[256,640]{1,0:T(8,128)(2,1)S(1)}, u32[]{:S(2)}, u32[]{:S(2)}) collective-permute-start(bf16[256,640]{1,0:T(8,128)(2,1)S(1)} %get-tuple-element.194), channel_id=1, source_target_pairs={{0,24},{2,26},{4,28},{6,30},{8,0},{10,2},{12,4},{14,6},{16,8},{18,... | collective-permute-start | bytes 983048 | tf_op jit(solution)/shard_map/ppermute | solution.py:472
  523.5 28.0 %collective-permute-start.32 = (bf16[256,640]{1,0:T(8,128)(2,1)S(1)}, bf16[256,640]{1,0:T(8,128)(2,1)S(1)}, u32[]{:S(2)}, u32[]{:S(2)}) collective-permute-start(bf16[256,640]{1,0:T(8,128)(2,1)S(1)} %get-tuple-element.193), channel_id=1, source_target_pairs={{0,16},{2,18},{4,20},{6,22},{8,24},{10,26},{12,28},{14,30},{16,0},... | collective-permute-start | bytes 983048 | tf_op jit(solution)/shard_map/ppermute | solution.py:472
  524.2 27.3 %collective-permute-start.33 = (bf16[256,640]{1,0:T(8,128)(2,1)S(1)}, bf16[256,640]{1,0:T(8,128)(2,1)S(1)}, u32[]{:S(2)}, u32[]{:S(2)}) collective-permute-start(bf16[256,640]{1,0:T(8,128)(2,1)S(1)} %get-tuple-element.192), channel_id=1, source_target_pairs={{0,8},{2,10},{4,12},{6,14},{8,16},{10,18},{12,20},{14,22},{16,24},... | collective-permute-start | bytes 983048 | tf_op jit(solution)/shard_map/ppermute | solution.py:472
  565.2 330.4 %reduce-scatter.5.cloned.1.call-start = ((), (), s32[]{:S(2)}) async-start(), calls=%async_computation.7 | async-start | bytes 20054016 | tf_op jit(solution)/shard_map/reduce_scatter | solution.py:694
  581.4 1.6 collective-permute-start.35
  583.1 6.0 collective-permute-start.36
  590.5 6.4 collective-permute-start.37
  590.6 32.4 %collective-permute-start.38 = (bf16[192,384]{0,1:T(8,128)(2,1)S(1)}, bf16[192,384]{0,1:T(8,128)(2,1)S(1)}, u32[]{:S(2)}, u32[]{:S(2)}) collective-permute-start(bf16[192,384]{0,1:T(8,128)(2,1)S(1)} %pad_maximum_fusion.30), channel_id=1, source_target_pairs={{0,16},{2,18},{4,20},{6,22},{8,24},{10,26},{12,28},{14,30},{16,0},... | collective-permute-start | bytes 442376 | tf_op jit(solution)/shard_map/ppermute | solution.py:472
  593.6 29.4 %collective-permute-start.39 = (bf16[192,384]{0,1:T(8,128)(2,1)S(1)}, bf16[192,384]{0,1:T(8,128)(2,1)S(1)}, u32[]{:S(2)}, u32[]{:S(2)}) collective-permute-start(bf16[192,384]{0,1:T(8,128)(2,1)S(1)} %pad_maximum_fusion.30), channel_id=1, source_target_pairs={{0,8},{2,10},{4,12},{6,14},{8,16},{10,18},{12,20},{14,22},{16,24},... | collective-permute-start | bytes 442376 | tf_op jit(solution)/shard_map/ppermute | solution.py:472
  623.5 9.9 %collective-permute-start.40 = (bf16[192,1536]{1,0:T(8,128)(2,1)S(1)}, bf16[192,1536]{1,0:T(8,128)(2,1)S(1)}, u32[]{:S(2)}, u32[]{:S(2)}) collective-permute-start(bf16[192,1536]{1,0:T(8,128)(2,1)S(1)} %copy.260), channel_id=1, source_target_pairs={{0,4},{2,6},{4,0},{6,2},{8,12},{10,14},{12,8},{14,10},{16,20},{18,... | collective-permute-start | bytes 1769480 | tf_op jit(solution)/shard_map/ppermute | solution.py:468
  634.6 17.6 %collective-permute-start.41 = (bf16[384,1536]{1,0:T(8,128)(2,1)}, bf16[384,1536]{1,0:T(8,128)(2,1)}, u32[]{:S(2)}, u32[]{:S(2)}) collective-permute-start(bf16[384,1536]{1,0:T(8,128)(2,1)} %pad_maximum_fusion.10), channel_id=1, source_target_pairs={{0,2},{2,0},{4,6},{6,4},{8,10},{10,8},{12,14},{14,12},{16,18},{18,... | collective-permute-start | bytes 3538952 | tf_op jit(solution)/shard_map/ppermute | solution.py:468
  651.2 20.0 %collective-permute-start.22 = (bf16[128,1536]{0,1:T(8,128)(2,1)}, bf16[128,1536]{0,1:T(8,128)(2,1)}, u32[]{:S(2)}, u32[]{:S(2)}) collective-permute-start(bf16[128,1536]{0,1:T(8,128)(2,1)} %slice.457), channel_id=1, source_target_pairs={{0,1},{1,0},{2,3},{3,2},{4,5},{5,4},{6,7},{7,6},{8,9},{9,8},{10,11... | collective-permute-start | bytes 1179656 | tf_op jit(solution)/shard_map/ppermute | solution.py:417
  655.6 36.8 %collective-permute-start.42 = (bf16[768,256]{1,0:T(8,128)(2,1)}, bf16[768,256]{1,0:T(8,128)(2,1)}, u32[]{:S(2)}, u32[]{:S(2)}) collective-permute-start(bf16[768,256]{1,0:T(8,128)(2,1)} %convolution_convert_fusion), channel_id=1, source_target_pairs={{0,1},{1,0},{2,3},{3,2},{4,5},{5,4},{6,7},{7,6},{8,9},{9,8},{10,11... | collective-permute-start | bytes 1179656 | tf_op jit(solution)/shard_map/ppermute | solution.py:417
  662.9 17.0 %collective-permute-start.34 = (bf16[128,1536]{0,1:T(8,128)(2,1)}, bf16[128,1536]{0,1:T(8,128)(2,1)}, u32[]{:S(2)}, u32[]{:S(2)}) collective-permute-start(bf16[128,1536]{0,1:T(8,128)(2,1)} %slice.455), channel_id=1, source_target_pairs={{0,1},{1,0},{2,3},{3,2},{4,5},{5,4},{6,7},{7,6},{8,9},{9,8},{10,11... | collective-permute-start | bytes 1179656 | tf_op jit(solution)/shard_map/ppermute | solution.py:417
  691.6 5.6 collective-permute-start.43
  697.3 17.6 %collective-permute-start.44 = (f32[4,9216]{1,0:T(4,128)S(1)}, f32[4,9216]{1,0:T(4,128)S(1)}, u32[]{:S(2)}, u32[]{:S(2)}) collective-permute-start(f32[4,9216]{1,0:T(4,128)S(1)} %fusion.117), channel_id=1, source_target_pairs={{0,2},{2,0},{4,6},{6,4},{8,10},{10,8},{12,14},{14,12},{16,18},{18,... | collective-permute-start | bytes 442376 | tf_op jit(solution)/shard_map/ppermute | solution.py:468
  698.2 34.6 %all-to-all-start.1 = ((bf16[16,48,256]{2,1,0:T(8,128)(2,1)}), bf16[16,48,256]{2,1,0:T(8,128)(2,1)}, u32[]{:S(2)}, u32[]{:S(2)}) async-start(bf16[16,48,256]{2,1,0:T(8,128)(2,1)} %bitcast.79), calls=%async_computation.1 | async-start | bytes 786432 | tf_op jit(solution)/shard_map/all_to_all | solution.py:780
  715.0 9.5 %collective-permute-start.45 = (f32[4,9216]{1,0:T(4,128)S(1)}, f32[4,9216]{1,0:T(4,128)S(1)}, u32[]{:S(2)}, u32[]{:S(2)}) collective-permute-start(f32[4,9216]{1,0:T(4,128)S(1)} %add.610), channel_id=1, source_target_pairs={{0,4},{2,6},{4,0},{6,2},{8,12},{10,14},{12,8},{14,10},{16,20},{18,... | collective-permute-start | bytes 442376 | tf_op jit(solution)/shard_map/ppermute | solution.py:468
  725.2 8.6 collective-permute-start.46
  734.8 18.9 %collective-permute-start.47 = (f32[4,9216]{1,0:T(4,128)S(1)}, f32[4,9216]{1,0:T(4,128)S(1)}, u32[]{:S(2)}, u32[]{:S(2)}) collective-permute-start(f32[4,9216]{1,0:T(4,128)S(1)} %add.612), channel_id=1, source_target_pairs={{0,16},{2,18},{4,20},{6,22},{8,24},{10,26},{12,28},{14,30},{16,0},... | collective-permute-start | bytes 442376 | tf_op jit(solution)/shard_map/ppermute | solution.py:468
  754.3 2.6 collective-permute-start.48
  757.1 3.8 collective-permute-start.49
  760.9 6.1 collective-permute-start.50
  766.9 5.8 collective-permute-start.51
  (114 other events, 1113.6 us)
Sparse Core Ops, SparseCore 0:
  10.9 69.3 all-gather.2
  82.4 155.9 all-gather.4
  565.3 122.7 reduce-scatter.2
  692.7 202.8 reduce-scatter.4

commit v2 on v1

--- a/solution.py
+++ b/solution.py
@@ -15,6 +15,7 @@
 LOW = jnp.bfloat16
 FLOAT = jnp.float32
 MIB = 1024 * 1024
+SMALL = pl.CostEstimate(flops=1024, bytes_accessed=1024, transcendentals=0)
 
 
 def pick_tile(total, most):
@@ -92,7 +93,6 @@
     chunk = pick_tile(total, 512)
     head_block = lambda h, i: (i, h)
     out = jax.ShapeDtypeStruct((rows, heads * 128), jnp.float32)
-    pairs = rows * heads * (total + text_total)
     return pl.pallas_call(
         functools.partial(forward_kernel, chunk),
         grid=(heads, rows // tile),
@@ -115,9 +115,7 @@
             pltpu.VMEM((text_total, 128), jnp.bfloat16),
         ],
         compiler_params=pltpu.CompilerParams(vmem_limit_bytes=48 * 1024 * 1024),
-        cost_estimate=pl.CostEstimate(
-            flops=pairs * 512, bytes_accessed=8 * total * heads * 128, transcendentals=pairs
-        ),
+        cost_estimate=SMALL,
     )(q, sel, qf, kv, kf, tkv, tf, gates)
 
 
@@ -209,7 +207,6 @@
     tile = pick_tile(rows, 256)
     chunk = pick_tile(total, 512)
     low = jnp.bfloat16
-    pairs = rows * heads * (total + text_total)
     return pl.pallas_call(
         functools.partial(backward_kernel, chunk),
         grid=(heads, rows // tile),
@@ -248,9 +245,7 @@
             pltpu.VMEM((text_total, 128), jnp.float32),
         ],
         compiler_params=pltpu.CompilerParams(vmem_limit_bytes=56 * 1024 * 1024),
-        cost_estimate=pl.CostEstimate(
-            flops=pairs * 1280, bytes_accessed=12 * total * heads * 128, transcendentals=pairs
-        ),
+        cost_estimate=SMALL,
     )(q, dm, sel, msel, qf, kv, kf, tkv, tf, gates, outs, stats)
 
 
@@ -371,30 +366,33 @@
     )(parts, qkv, cosine, sine, gains)
 
 
-def outer_kernel(left_ref, right_ref, out_ref):
-    out_ref[...] = matmul(left_ref[0], right_ref[...], 1, 0).astype(LOW)
-
-
-def outer_products(left, right, bounds, tile):
-    depth, columns = left.shape[1], right.shape[1]
+def outer_kernel(left_ref, *refs):
+    out_ref = refs[-1]
+    total = None
+    for index, right_ref in enumerate(refs[:-1]):
+        rows = right_ref.shape[0]
+        term = matmul(left_ref[:, rows * index : rows * index + rows], right_ref[...], 1, 0)
+        total = term if total is None else total + term
+    out_ref[...] = total.astype(LOW)
+
+
+def outer_products(left, rights, tile):
+    depth = left.shape[0]
+    rows, columns = rights[0].shape
     return pl.pallas_call(
         outer_kernel,
         grid=(columns // tile,),
-        in_specs=[
-            pl.BlockSpec(
-                (1, depth, left.shape[2]), lambda i: (jnp.where(i < bounds // tile, 0, 1), 0, 0)
-            ),
-            pl.BlockSpec((right.shape[0], tile), lambda i: (0, i)),
-        ],
+        in_specs=[pl.BlockSpec(left.shape, lambda i: (0, 0))]
+        + [pl.BlockSpec((rows, tile), lambda i: (0, i)) for _ in rights],
         out_specs=pl.BlockSpec((depth, tile), lambda i: (0, i)),
         out_shape=jax.ShapeDtypeStruct((depth, columns), LOW),
         compiler_params=pltpu.CompilerParams(vmem_limit_bytes=40 * MIB),
-        cost_estimate=pl.CostEstimate(
-            flops=2 * depth * columns * right.shape[0],
-            bytes_accessed=2 * depth * columns,
-            transcendentals=0,
-        ),
-    )(left, right)
+        cost_estimate=SMALL,
+    )(left, *rights)
+
+
+def tie(*values):
+    return lax.optimization_barrier(values)
 
 
 def dot_float(left, right):
@@ -483,6 +481,12 @@
             values = jnp.concatenate([values, flip(values, bit)], axis=0)
         return values
 
+    def spread_list(values):
+        values = [values]
+        for bit in bits:
+            values = values + [flip(value, bit) for value in values]
+        return values
+
     def collect(values):
         for bit in reversed(bits):
             half = values.shape[0] // 2
@@ -509,37 +513,53 @@
             [slots[0]] + [shift(slots[steps], -steps) for steps in range(1, SPLIT)]
         )
 
+    flips = []
+    for order in range(near):
+        mask = 0
+        for place, bit in enumerate(bits):
+            if order >> place & 1:
+                mask |= bit
+        flips.append(mask)
+
+    def own_columns(values):
+        blocks = (
+            values.T.reshape(SPLIT, near, weight_rows, token_count)
+            .transpose(1, 0, 2, 3)
+            .reshape(near, SPLIT * weight_rows, token_count)
+        )
+        parts = [pick(blocks, near_index ^ mask) for mask in flips]
+        return jnp.concatenate(
+            [part if mask == 0 else flip(part, mask) for part, mask in zip(parts, flips)], axis=1
+        )
+
+    def weight_shard(partial):
+        parts = send_parts(partial.reshape(SPLIT, weight_rows, -1))
+        return sum(part.astype(FLOAT) for part in parts)
+
     qkv_full = lax.all_gather(
         qkv_weight.transpose(1, 0, 2).reshape(weight_rows, 3 * local_width),
         "dp",
         axis=0,
         tiled=True,
     )
-    rest_shard = jnp.concatenate(
-        [out_weight.T, gate_up_weight[0], gate_up_weight[1], down_weight.T], axis=1
-    )
-    rest_shard, qkv_full = lax.optimization_barrier((rest_shard, qkv_full))
-    rest_full = lax.all_gather(rest_shard, "dp", axis=0, tiled=True)
-    out_full = rest_full[:, :local_width]
-    gate_up_full = rest_full[:, local_width : local_width + 2 * hidden_count]
-    down_full = rest_full[:, local_width + 2 * hidden_count :]
-
     cond_float = conditioning.astype(FLOAT)
     silu_cond = jax.nn.silu(cond_float).astype(LOW)
     cond_rows = ada_weight.shape[0]
     silu_slice = lax.dynamic_slice_in_dim(silu_cond, dp_index * cond_rows, cond_rows, axis=1)
     first_rows = jnp.sum((clip_ids == 0).astype(FLOAT))
     spots = jnp.arange(ada_weight.shape[1], dtype=jnp.int32)
-    mod_part = jnp.concatenate(
+    early = 2 * width
+    early_part = jnp.concatenate(
         [
-            dot_float(silu_slice, ada_weight),
-            jnp.where(spots == dp_index, first_rows, 0.0)[None],
+            dot_float(silu_slice, ada_weight[:, :early]),
+            jnp.where(spots[:early] == dp_index, first_rows, 0.0)[None],
         ],
         axis=0,
     )
-    mod_sum = sum_dp(mod_part)
-    modulation = mod_sum[:clip_count] + ada_bias.astype(FLOAT)
-    counts = mod_sum[clip_count, :dp].astype(jnp.int32)
+    early_sum = sum_dp(early_part)
+    bias = ada_bias.astype(FLOAT)
+    early_mod = early_sum[:clip_count] + bias[:early]
+    counts = early_sum[clip_count, :dp].astype(jnp.int32)
 
     own_ids = lax.dynamic_slice_in_dim(clip_ids, tensor_index * row_count, row_count)
     row_positions = jnp.where(
@@ -547,18 +567,22 @@
     )
     other_clip = jnp.max(clip_ids)
     first_clip = (own_ids == 0)[:, None]
-    mod_rows = jnp.where(
-        first_clip,
-        modulation[0:1],
-        lax.dynamic_slice_in_dim(modulation, other_clip, 1, 0),
-    )
-    shift_one, scale_one, gate_one, shift_two, scale_two, gate_two = jnp.split(mod_rows, 6, axis=1)
-
+
+    def mod_blocks(modulation):
+        rows = jnp.where(
+            first_clip,
+            modulation[0:1],
+            lax.dynamic_slice_in_dim(modulation, other_clip, 1, 0),
+        )
+        return jnp.split(rows, rows.shape[1] // width, axis=1)
+
+    shift_one, scale_one = mod_blocks(early_mod)
     input_rows = inputs.astype(FLOAT)
     first_gain = first_norm_gain.astype(FLOAT)
-    normed_all = both_rows(modulated(input_rows, first_gain, shift_one, scale_one).astype(LOW))
-    grad_two = grad_output.astype(FLOAT)
-    grad_ffn = both_rows((gate_two * grad_two).astype(LOW))
+    normed_one = modulated(input_rows, first_gain, shift_one, scale_one).astype(LOW)
+    normed_one, text_tokens, silu_late = tie(normed_one, text_tokens, silu_slice)
+    normed_all = both_rows(normed_one)
+    late_sum = sum_dp(dot_float(silu_late, ada_weight[:, early:]))
 
     half_size = head_size // 2
     frequency = 10000.0 ** (-(jnp.arange(half_size, dtype=FLOAT) * 2.0 / head_size))
@@ -570,14 +594,6 @@
     gains = jnp.stack([jnp.tile(query_gain, 2), jnp.tile(key_gain, 2)]).astype(FLOAT)
     gains = jnp.concatenate([gains, jnp.zeros((6, 128), FLOAT)], axis=0)
 
-    flips = []
-    for order in range(near):
-        mask = 0
-        for place, bit in enumerate(bits):
-            if order >> place & 1:
-                mask |= bit
-        flips.append(mask)
-
     text_rows = text_tokens.shape[0]
     group_rows = text_rows * SPLIT
     text_columns = lax.all_to_all(text_tokens, "dp", split_axis=1, concat_axis=0, tiled=True)
@@ -590,6 +606,10 @@
     )
     text_sum = collect(dot_float(text_near, text_weight))
     text_parts = text_sum.astype(LOW).reshape(group_rows, SPLIT, 2 * part_width).transpose(1, 0, 2)
+    out_part, qkv_full, normed_all, text_parts, late_sum = tie(
+        out_weight.T, qkv_full, normed_all, text_parts, late_sum
+    )
+    out_full = lax.all_gather(out_part, "dp", axis=0, tiled=True)
     text_raw = sum(part.astype(FLOAT) for part in send_parts(text_parts))
     ky_gain = text_key_gain.astype(FLOAT)
     text_key_raw = text_raw[:, :part_width].reshape(group_rows, each, head_size)
@@ -646,10 +666,19 @@
     gate_lanes = jnp.broadcast_to(gate_heads[:, None, None], (each, 8, 128))
 
     qkv_raw = dot_float(normed_all, qkv_full)
+    gate_one, shift_two, scale_two, gate_two = mod_blocks(late_sum + bias[early:])
+    grad_two = grad_output.astype(FLOAT)
+    grad_ffn = both_rows((gate_two * grad_two).astype(LOW))
     head_parts = send_parts(rope_forward(qkv_raw, cosine, sine, gains, heads))
     arrived = jnp.concatenate(head_parts, axis=0)
+    feed_weights, arrived = tie(
+        jnp.concatenate([gate_up_weight[0], gate_up_weight[1], down_weight.T], axis=1), arrived
+    )
     queries = arrived[:, :query_width]
     pairs = spread(arrived[:, query_width:])
+    feed_full = lax.all_gather(feed_weights, "dp", axis=0, tiled=True)
+    gate_up_full = feed_full[:, : 2 * hidden_count]
+    down_full = feed_full[:, 2 * hidden_count :]
     mixed_wide, head_outs, head_stats = attention_forward(
         queries,
         query_select,
@@ -668,6 +697,8 @@
         .transpose(1, 0, 2)
         .reshape(token_count, local_width)
     )
+    mixed_all = spread_list(mixed)
+    normed_columns = own_columns(normed_all)
     attn_rows = own_rows(dot_turned(mixed, out_full))
     after_attn = input_rows + gate_one * attn_rows
     second_gain = second_norm_gain.astype(FLOAT)
@@ -676,6 +707,9 @@
     gate_values, up_values = gate_up[:, :hidden_count], gate_up[:, hidden_count:]
     sigmoid_gate = jax.nn.sigmoid(gate_values)
     hidden_low = (gate_values * sigmoid_gate * up_values).astype(LOW)
+    down_grads = outer_products(grad_ffn.T, [hidden_low], 512)
+    hidden_low, down_grads = tie(hidden_low, down_grads)
+    down_low = lax.psum_scatter(down_grads, "dp", scatter_dimension=0, tiled=True)
     ffn_rows = own_rows(dot_turned(hidden_low, down_full))
     output = (after_attn + gate_two * ffn_rows).astype(LOW)
     grad_gate_two = grad_two * ffn_rows
@@ -685,28 +719,29 @@
     ).astype(LOW)
     grad_up_low = (grad_hidden * gate_values * sigmoid_gate).astype(LOW)
     grad_gate_up = jnp.concatenate([grad_gate_low, grad_up_low], axis=1)
-    feed_grads = outer_products(
-        jnp.stack([normed_two_all.T, grad_ffn.T]),
-        jnp.concatenate([grad_gate_up, hidden_low], axis=1),
-        2 * hidden_count,
-        512,
-    )
-    feed_shard = lax.psum_scatter(feed_grads, "dp", scatter_dimension=0, tiled=True).astype(FLOAT)
+    gate_up_grads = outer_products(normed_two_all.T, [grad_gate_up], 512)
     grad_normed_two = own_rows(dot_turned(grad_gate_up, gate_up_full))
     _, pull_two = jax.vjp(modulated, after_attn, second_gain, shift_two, scale_two)
     back_two, grad_second_gain, grad_shift_two, grad_scale_two = pull_two(grad_normed_two)
     grad_after = grad_two + back_two
     grad_attn = both_rows((gate_one * grad_after).astype(LOW))
     grad_gate_one = grad_after * attn_rows
+    out_partial = outer_products(own_columns(grad_attn), mixed_all, local_width)
     grad_mixed = dot_float(grad_attn, out_full).astype(LOW)
     grad_mixed_parts = send_parts(
         grad_mixed.reshape(token_count, SPLIT, part_width).transpose(1, 0, 2)
     )
+    grad_mixed_slots = jnp.pad(
+        jnp.concatenate(grad_mixed_parts, axis=0), ((0, 0), (0, query_width - part_width))
+    )
+    grad_mixed_slots, gate_up_grads, out_partial, normed_columns = tie(
+        grad_mixed_slots, gate_up_grads, out_partial, normed_columns
+    )
+    gate_up_low = lax.psum_scatter(gate_up_grads, "dp", scatter_dimension=0, tiled=True)
+    out_shard = weight_shard(out_partial)
     query_grad, pair_grads, text_grads, gate_sums = attention_backward(
         queries,
-        jnp.pad(
-            jnp.concatenate(grad_mixed_parts, axis=0), ((0, 0), (0, query_width - part_width))
-        ),
+        grad_mixed_slots,
         query_select,
         mixed_select,
         query_features,
@@ -718,7 +753,30 @@
         head_outs,
         head_stats,
     )
+    clip_at = jnp.arange(clip_count, dtype=jnp.int32)[:, None]
+
+    def clip_sums(values):
+        first_sum = jnp.sum(jnp.where(first_clip, values, 0.0), axis=0)[None]
+        other_sum = jnp.sum(jnp.where(first_clip, 0.0, values), axis=0)[None]
+        return jnp.where(clip_at == 0, first_sum, jnp.where(clip_at == other_clip, other_sum, 0.0))
+
+    def pair_sums(blocks, gains_row):
+        wide = jnp.concatenate([clip_sums(values) for values in blocks], axis=1)
+        gains_row = jnp.concatenate(
+            [gains_row, jnp.zeros((wide.shape[1] - gains_row.shape[0],), FLOAT)]
+        )
+        wide = jnp.concatenate([wide, gains_row[None]], axis=0)
+        return wide + swapped(wide)
+
+    late_pairs = pair_sums(
+        (grad_gate_one, grad_shift_two, grad_scale_two, grad_gate_two), grad_second_gain
+    )
+
     pair_sum = collect(pair_grads).astype(LOW)
+    pair_sum, text_grads, late_pairs = tie(pair_sum, text_grads, late_pairs)
+    late_total = sum_dp(late_pairs)
+    late_grads = late_total[:clip_count].astype(LOW)
+    second_gain_sum = late_total[clip_count, :width]
     query_packed = query_grad.reshape(group_tokens, each, 128)[..., :64].reshape(
         group_tokens, part_width
     )
@@ -731,18 +789,6 @@
         axis=1,
     ).reshape(SPLIT, token_count, -1)
     back_parts = return_parts([back_slots[index] for index in range(SPLIT)])
-    qkv_grad, gain_sums = rope_backward(back_parts, qkv_raw, cosine, sine, gains, heads)
-    grad_normed_one = own_rows(dot_turned(qkv_grad, qkv_full))
-    attention_grads = outer_products(
-        jnp.stack([normed_all.T, grad_attn.T]),
-        jnp.concatenate([qkv_grad, mixed], axis=1),
-        3 * local_width,
-        local_width,
-    )
-    attention_shard = lax.psum_scatter(
-        attention_grads, "dp", scatter_dimension=0, tiled=True
-    ).astype(FLOAT)
-
     text_grad_sum = collect(text_grads).reshape(group_rows, each, 2 * head_size)
     text_key_low = text_grad_sum[..., :head_size].astype(LOW).astype(FLOAT)
     _, pull_text = jax.vjp(norm_rows, text_key_raw, ky_gain)
@@ -754,11 +800,44 @@
         ],
         axis=1,
     )
-    text_all = spread(
+    back_parts, text_low, late_grads = tie(back_parts, text_low, late_grads)
+    qkv_grad, gain_sums = rope_backward(back_parts, qkv_raw, cosine, sine, gains, heads)
+    qkv_partial = outer_products(normed_columns, spread_list(qkv_grad), local_width)
+    grad_normed_one = own_rows(dot_turned(qkv_grad, qkv_full))
+    _, pull_one = jax.vjp(modulated, input_rows, first_gain, shift_one, scale_one)
+    back_one, grad_first_gain, grad_shift_one, grad_scale_one = pull_one(grad_normed_one)
+    grad_inputs = grad_after + back_one
+    head_sums = (1.0 - gate_heads * gate_heads) * jnp.sum(
+        gate_sums.reshape(8, each, 128), axis=(0, 2)
+    )
+    head_row = lax.dynamic_update_slice_in_dim(
+        jnp.zeros((head_gate.shape[0],), FLOAT),
+        head_sums,
+        tensor_index * heads + far_index * each,
+        0,
+    )
+    gain_halves = gain_sums[:2, :head_size] + gain_sums[:2, head_size:]
+    early_pairs = pair_sums(
+        (grad_shift_one, grad_scale_one),
+        jnp.concatenate([grad_first_gain, gain_halves.reshape(-1), grad_ky_gain, head_row]),
+    )
+    text_wide = (
         in_place([text_low] + [shift(text_low, -steps) for steps in range(1, SPLIT)])
         .transpose(1, 0, 2)
         .reshape(group_rows, 2 * local_width)
     )
+    early_pairs, text_wide, qkv_partial = tie(early_pairs, text_wide, qkv_partial)
+    qkv_shard = weight_shard(qkv_partial)
+    early_total = sum_dp(early_pairs)
+    early_grads, sums = early_total[:clip_count].astype(LOW), early_total[clip_count]
+    grad_mod_low = jnp.concatenate([early_grads, late_grads], axis=1)
+    first_gain_sum = sums[:width]
+    at = width
+    q_gain_sum = sums[at : at + head_size]
+    k_gain_sum = sums[at + head_size : at + 2 * head_size]
+    ky_gain_sum = sums[at + 2 * head_size : at + 3 * head_size]
+    gate_sum = sums[at + 3 * head_size : at + 3 * head_size + head_gate.shape[0]]
+    text_all = spread(text_wide)
     grad_text_kv = (
         matmul(text_near, text_all, 0, 0)
         .reshape(-1, SPLIT, 2, part_width)
@@ -782,56 +861,6 @@
     grad_text = lax.dynamic_slice_in_dim(
         grad_text_all, tensor_index * half_text, half_text, 1
     ).astype(FLOAT)
-
-    _, pull_one = jax.vjp(modulated, input_rows, first_gain, shift_one, scale_one)
-    back_one, grad_first_gain, grad_shift_one, grad_scale_one = pull_one(grad_normed_one)
-    grad_inputs = grad_after + back_one
-    clip_at = jnp.arange(clip_count, dtype=jnp.int32)[:, None]
-
-    def clip_sums(values):
-        first_sum = jnp.sum(jnp.where(first_clip, values, 0.0), axis=0)[None]
-        other_sum = jnp.sum(jnp.where(first_clip, 0.0, values), axis=0)[None]
-        return jnp.where(clip_at == 0, first_sum, jnp.where(clip_at == other_clip, other_sum, 0.0))
-
-    mod_grads = jnp.concatenate(
-        [
-            clip_sums(values)
-            for values in (
-                grad_shift_one,
-                grad_scale_one,
-                grad_gate_one,
-                grad_shift_two,
-                grad_scale_two,
-                grad_gate_two,
-            )
-        ],
-        axis=1,
-    )
-    head_sums = (1.0 - gate_heads * gate_heads) * jnp.sum(
-        gate_sums.reshape(8, each, 128), axis=(0, 2)
-    )
-    head_row = lax.dynamic_update_slice_in_dim(
-        jnp.zeros((head_gate.shape[0],), FLOAT),
-        head_sums,
-        tensor_index * heads + far_index * each,
-        0,
-    )
-    gain_halves = gain_sums[:2, :head_size] + gain_sums[:2, head_size:]
-    small = jnp.concatenate(
-        [grad_first_gain, grad_second_gain, gain_halves.reshape(-1), grad_ky_gain, head_row]
-    )
-    small_row = jnp.concatenate([small, jnp.zeros((mod_grads.shape[1] - small.shape[0],), FLOAT)])
-    grad_sums = jnp.concatenate([mod_grads, small_row[None]], axis=0)
-    grad_sums = sum_dp(grad_sums + swapped(grad_sums))
-    grad_mod_low = grad_sums[:clip_count].astype(LOW)
-    sums = grad_sums[clip_count]
-    first_gain_sum = sums[:width]
-    second_gain_sum = sums[width : 2 * width]
-    at = 2 * width
-    q_gain_sum = sums[at : at + head_size]
-    k_gain_sum = sums[at + head_size : at + 2 * head_size]
-    ky_gain_sum = sums[at + 2 * head_size : at + 3 * head_size]
-    gate_sum = sums[at + 3 * head_size : at + 3 * head_size + head_gate.shape[0]]
     grad_ada_bias = jnp.sum(grad_mod_low.astype(FLOAT), axis=0)
     grad_ada = matmul(silu_slice, grad_mod_low, 0, 0)
     cond_part = lax.dynamic_update_slice_in_dim(
@@ -844,16 +873,10 @@
     grad_conditioning = (
         sum_dp(cond_part) * cond_sigmoid * (1.0 + cond_float * (1.0 - cond_sigmoid))
     )
-    qkv_shard = (
-        attention_shard[:, : 3 * local_width]
-        .reshape(weight_rows, 3, local_width)
-        .transpose(1, 0, 2)
-    )
-    out_shard = attention_shard[:, 3 * local_width :].T
-    gate_up_shard = jnp.stack(
-        [feed_shard[:, :hidden_count], feed_shard[:, hidden_count : 2 * hidden_count]]
-    )
-    down_shard = feed_shard[:, 2 * hidden_count :].T
+    qkv_shard = qkv_shard.reshape(weight_rows, 3, local_width).transpose(1, 0, 2)
+    gate_up_low = gate_up_low.astype(FLOAT)
+    gate_up_shard = jnp.stack([gate_up_low[:, :hidden_count], gate_up_low[:, hidden_count:]])
+    down_shard = down_low.astype(FLOAT)
     return (
         output,
         grad_inputs,
@@ -867,11 +890,11 @@
         ky_gain_sum,
         gate_sum,
         qkv_shard,
-        out_shard,
+        out_shard.T,
         grad_text_kv,
         second_gain_sum,
         gate_up_shard,
-        down_shard,
+        down_shard.T,
     )
 
 

time: 918 us -> 827 us (0.901)
  waiting for transfers between devices: 427 us -> 262 us
  starting transfers between devices: 85.1 us -> 143 us
  local copies, waits for them, and re-layouts: 94.9 us -> 111 us
    reduce_scatter x2, waiting for transfers between devices: 117 us -> 0.01 us  [the longest x1 0.01 us: shards(): lax.psum_scatter(gate_up_grads, 'dp', scatter_dimension=0, tiled=True)]
    all_gather x1, waiting for transfers between devices: 68.6 us -> 0.01 us  [shards(): lax.all_gather(qkv_weight.transpose(1, 0, 2).reshape(weight_rows, 3 * loc...]
    ppermute x24 -> x44, starting transfers between devices: 21.4 us -> 56.3 us  [flip(): return lax.ppermute(values, 'dp', [(j, j ^ bit) for j in range(dp)])]
    ppermute x18 -> x24, starting transfers between devices: 32.6 us -> 60.7 us  [shift(): return lax.ppermute(values, 'dp', pairs)]
    all_to_all x1, waiting for transfers between devices: 0.01 us -> 15.2 us  [shards(): lax.all_to_all(text_tokens, 'dp', split_axis=1, concat_axis=0, tiled=True)]
    all_to_all x1, starting transfers between devices: 16.7 us -> 3.55 us  [shards(): lax.all_to_all(grad_text_rows, 'dp', split_axis=0, concat_axis=1, tiled=T...]
    ppermute x10 -> x11, waiting for transfers between devices: 51.1 us -> 41 us  [swapped(): return lax.ppermute(values, 'tensor', [(0, 1), (1, 0)])]
    unnamed x276 -> x313, local copies, waits for them, and re-layouts: 31.5 us -> 40.9 us
  transfers between devices with their start and end apart: 58 -> 86, of which waited for: 36 -> 43; matrix products, arithmetic and copies ran while one was open for 18% -> 26% of each run, Pallas kernels for 6% -> 17%
where the time goes in v2:
time: 827 us; the launch traced here: 816 us
  waiting for transfers between devices  262 us (32%)
  starting transfers between devices  143 us (17%)
  Pallas kernels  140 us (17%)
  local copies, waits for them, and re-layouts  111 us (13%)
  other arithmetic  83.2 us (10%)
  matrix products  51.3 us (6%)
  between operations  26.4 us (3%)
    ppermute x24, waiting for transfers between devices, shift(): return lax.ppermute(values, 'dp', pairs)  107 us
    ppermute x44, waiting for transfers between devices, flip(): return lax.ppermute(values, 'dp', [(j, j ^ bit) for j in range(dp)])  93.7 us
    pallas_call x1, Pallas kernels, attention_backward(): pl.pallas_call(functools.partial(backward_kernel, chunk), grid=(heads, ro...  71 us
    ppermute x24, starting transfers between devices, shift(): return lax.ppermute(values, 'dp', pairs)  60.7 us
    ppermute x44, starting transfers between devices, flip(): return lax.ppermute(values, 'dp', [(j, j ^ bit) for j in range(dp)])  56.3 us
    pallas_call x1, Pallas kernels, attention_forward(): pl.pallas_call(functools.partial(forward_kernel, chunk), grid=(heads, row...  44.2 us
    ppermute x11, waiting for transfers between devices, swapped(): return lax.ppermute(values, 'tensor', [(0, 1), (1, 0)])  41 us
    unnamed x313, local copies, waits for them, and re-layouts  40.9 us
  transfers between devices with their start and end apart: 86, of which 43 were waited for; matrix products, arithmetic and copies ran while one was open for 26% of the time, Pallas kernels for 17%

profile of v2, /device:TPU:0, one launch (start us, length us, event | category | flops | bytes accessed | tf_op | source)
XLA Modules:
  0.0 815.8 jit_solution(5790493427891212673)
XLA Ops:
  15.2 2.9 collective-permute-start.1
  24.8 3.9 collective-permute-start.3
  36.6 7.0 all-to-all-start
  45.1 15.2 %all-to-all-done = bf16[48,16,256]{2,0,1:T(8,128)(2,1)S(1)} async-done(((bf16[48,16,256]{2,0,1:T(8,128)(2,1)}), bf16[48,16,256]{2,0,1:T(8,128)(2,1)S(1)}, u32[]{:S(2)}, u32[]{:S(2)}) %all-to-all-start) | async-done | bytes 393248 | tf_op jit(solution)/shard_map/all_to_all | solution.py:599
  64.7 2.6 collective-permute-start.6
  69.1 15.6 %collective-permute-done.8 = f32[3,6144]{1,0:T(4,128)S(1)} collective-permute-done((f32[3,6144]{1,0:T(4,128)S(1)}, f32[3,6144]{1,0:T(4,128)S(1)}, u32[]{:S(2)}, u32[]{:S(2)}) %collective-permute-start.8) | collective-permute-done | bytes 73760 | tf_op jit(solution)/shard_map/ppermute | solution.py:466
  87.2 2.6 collective-permute-done.9
  89.8 4.5 collective-permute-start.10
  94.3 3.6 collective-permute-done.10
  102.9 5.1 fusion.98.qkv_ref
  108.0 3.0 shard_map.323
  113.9 2.9 collective-permute-start.13
  117.9 8.5 %collective-permute-done.11 = bf16[256,640]{1,0:T(8,128)(2,1)} collective-permute-done((bf16[256,640]{1,0:T(8,128)(2,1)}, bf16[256,640]{1,0:T(8,128)(2,1)}, u32[]{:S(2)}, u32[]{:S(2)}) %collective-permute-start.11) | collective-permute-done | bytes 327712 | tf_op jit(solution)/shard_map/ppermute | solution.py:470
  126.4 12.1 %collective-permute-done.12 = bf16[256,640]{1,0:T(8,128)(2,1)} collective-permute-done((bf16[256,640]{1,0:T(8,128)(2,1)}, bf16[256,640]{1,0:T(8,128)(2,1)}, u32[]{:S(2)}, u32[]{:S(2)}) %collective-permute-start.12) | collective-permute-done | bytes 327712 | tf_op jit(solution)/shard_map/ppermute | solution.py:470
  152.9 16.4 %collective-permute-start.16 = (bf16[192,384]{1,0:T(8,128)(2,1)S(1)}, bf16[192,384]{1,0:T(8,128)(2,1)S(1)}, u32[]{:S(2)}, u32[]{:S(2)}) collective-permute-start(bf16[192,384]{1,0:T(8,128)(2,1)S(1)} %get-tuple-element.255), channel_id=1, source_target_pairs={{0,8},{2,10},{4,12},{6,14},{8,16},{10,18},{12,20},{14,22},{16,24},... | collective-permute-start | bytes 442376 | tf_op jit(solution)/shard_map/ppermute | solution.py:470
  174.8 2.8 collective-permute-done.16
  177.5 5.7 collective-permute-done.17
  183.2 5.3 collective-permute-done.18
  199.5 11.3 %collective-permute-done.14 = bf16[1024,384]{1,0:T(8,128)(2,1)} collective-permute-done((bf16[1024,384]{1,0:T(8,128)(2,1)}, bf16[1024,384]{1,0:T(8,128)(2,1)}, u32[]{:S(2)}, u32[]{:S(2)}) %collective-permute-start.14) | collective-permute-done | bytes 786464 | tf_op jit(solution)/shard_map/ppermute | solution.py:466
  212.5 3.6 collective-permute-done.19
  218.3 3.7 pad_maximum_fusion.kv_ref
  222.1 44.2 %shard_map.324 = (bf16[1024,384]{1,0:T(8,128)(2,1)S(1)}, f32[1024,384]{1,0:T(8,128)S(1)}, f32[1024,384]{1,0:T(8,128)}) custom-call(bf16[1024,256]{1,0:T(8,128)(2,1)S(1)} %slice.265.q_ref, bf16[3,256,128]{2,1,0:T(8,128)(2,1)S(1)} %copy-done.10, bf16[1024,128]{1,0:T(8,128)(2,1)S(1)} %copy-done.8, bf16[4096,384]{1,0:T(8,128)(2,1)} %pad_maximum_fusion.kv_ref, ...), custom_call_target="tpu_custom_call" | custom-call | flops 1024 | bytes 1024 | tf_op jit(solution)/shard_map/pallas_call | solution.py:96
  278.5 6.5 collective-permute-done.22
  285.1 2.6 fusion.100
  291.1 7.9 collective-permute-done.24
  302.4 10.0 %collective-permute-done.26 = bf16[128,1536]{0,1:T(8,128)(2,1)S(1)} collective-permute-done((bf16[128,1536]{0,1:T(8,128)(2,1)S(1)}, bf16[128,1536]{0,1:T(8,128)(2,1)S(1)}, u32[]{:S(2)}, u32[]{:S(2)}) %collective-permute-start.26) | collective-permute-done | bytes 393248 | tf_op jit(solution)/shard_map/ppermute | solution.py:415
  313.1 5.9 collective-permute-done.25
  319.1 6.6 fusion.2
  325.7 6.8 multiply_convert_fusion.1
  332.6 2.8 shard_map.325
  335.4 2.6 copy-done
  348.2 8.2 %fusion = f32[256,1536]{0,1:T(8,128)S(1)} fusion(bf16[1536,6144]{1,0:T(8,128)(2,1)} %all-gather.8.cloned.1.call-done, bf16[256,2048]{1,0:T(8,128)(2,1)} %get-tuple-element.221, bf16[256,2048]{1,0:T(8,128)(2,1)} %get-tuple-element.220), kind=kOutput, calls=%fused_computation | convolution fusion | flops 3225419776 | bytes 16252928 | tf_op jit(solution)/shard_map/dot_general | solution.py:29
  358.0 4.7 fusion.6
  362.8 4.5 collective-permute-done.28
  370.7 6.5 collective-permute-done.27
  382.8 6.2 collective-permute-done.29
  400.5 3.0 collective-permute-start.32
  404.4 3.4 collective-permute-done.30
  408.4 8.5 %collective-permute-done.31 = bf16[256,192]{1,0:T(8,128)(2,1)S(1)} collective-permute-done((bf16[256,192]{1,0:T(8,128)(2,1)}, bf16[256,192]{1,0:T(8,128)(2,1)S(1)}, u32[]{:S(2)}, u32[]{:S(2)}) %collective-permute-start.31) | collective-permute-done | bytes 98336 | tf_op jit(solution)/shard_map/ppermute | solution.py:470
  420.2 7.9 shard_map.326
  435.9 71.0 %shard_map.328 = (bf16[1024,384]{1,0:T(8,128)(2,1)}, bf16[4096,384]{1,0:T(8,128)(2,1)}, bf16[768,384]{1,0:T(8,128)(2,1)}, f32[8,384]{1,0:T(8,128)}) custom-call(bf16[1024,256]{1,0:T(8,128)(2,1)} %copy-done.5, bf16[1024,256]{1,0:T(8,128)(2,1)} %fusion.35.dm_ref, bf16[3,256,128]{2,1,0:T(8,128)(2,1)} %get-tuple-element.297.sel_ref, ...), custom_call_target="tpu_custom_call" | custom-call | flops 1024 | bytes 1024 | tf_op jit(solution)/shard_map/pallas_call | solution.py:210
  507.0 2.7 slice.288
  540.3 8.9 %collective-permute-start.76 = (bf16[96,768]{1,0:T(8,128)(2,1)S(1)}, bf16[96,768]{1,0:T(8,128)(2,1)S(1)}, u32[]{:S(2)}, u32[]{:S(2)}) collective-permute-start(bf16[96,768]{1,0:T(8,128)(2,1)S(1)} %get-tuple-element.252), channel_id=1, source_target_pairs={{0,8},{2,10},{4,12},{6,14},{8,16},{10,18},{12,20},{14,22},{16,24},... | collective-permute-start | bytes 442376 | tf_op jit(solution)/shard_map/ppermute | solution.py:470
  553.6 4.7 collective-permute-done.77
  564.6 6.3 collective-permute-start.45
  571.3 3.0 collective-permute-start.52
  574.3 3.3 collective-permute-start.46
  577.8 18.6 %collective-permute-done.52 = f32[4,6144]{1,0:T(4,128)S(1)} collective-permute-done((f32[4,6144]{1,0:T(4,128)S(1)}, f32[4,6144]{1,0:T(4,128)S(1)}, u32[]{:S(2)}, u32[]{:S(2)}) %collective-permute-start.52) | collective-permute-done | bytes 98336 | tf_op jit(solution)/shard_map/ppermute | solution.py:466
  597.9 34.9 %collective-permute-done.46 = bf16[256,640]{1,0:T(8,128)(2,1)S(1)} collective-permute-done((bf16[256,640]{1,0:T(8,128)(2,1)S(1)}, bf16[256,640]{1,0:T(8,128)(2,1)S(1)}, u32[]{:S(2)}, u32[]{:S(2)}) %collective-permute-start.46) | collective-permute-done | bytes 327712 | tf_op jit(solution)/shard_map/ppermute | solution.py:470
  634.3 6.8 collective-permute-done.53
  655.1 4.9 shard_map.329
  661.4 4.1 collective-permute-start.56
  666.1 6.0 fusion.99
  679.7 10.8 %collective-permute-done.57 = bf16[192,384]{0,1:T(8,128)(2,1)} collective-permute-done((bf16[192,384]{0,1:T(8,128)(2,1)}, bf16[192,384]{0,1:T(8,128)(2,1)}, u32[]{:S(2)}, u32[]{:S(2)}) %collective-permute-start.57) | collective-permute-done | bytes 147488 | tf_op jit(solution)/shard_map/ppermute | solution.py:470
  700.3 3.2 select_reduce_fusion.1
  718.5 4.1 shard_map.330
  729.9 7.9 collective-permute-start.67
  739.8 5.2 collective-permute-start.68
  745.9 4.1 collective-permute-start.75
  766.5 8.8 %collective-permute-done.71 = f32[3,1024]{1,0:T(4,128)S(1)} collective-permute-done((f32[3,1024]{1,0:T(4,128)S(1)}, f32[3,1024]{1,0:T(4,128)S(1)}, u32[]{:S(2)}, u32[]{:S(2)}) %collective-permute-start.71) | collective-permute-done | bytes 12320 | tf_op jit(solution)/shard_map/ppermute | solution.py:466
  779.2 6.9 collective-permute-done.72
  787.6 3.6 all-to-all-start.1
  794.3 2.7 fusion.59
  798.8 4.6 all-to-all-done.1
  (665 shorter events, 265.3 us)
Async XLA Ops:
  7.2 92.5 %all-gather.4.cloned.1.call-start = ((), (), s32[]{:S(2)}) async-start(), calls=%async_computation.4 | async-start | bytes 7520256 | tf_op jit(solution)/shard_map/all_gather | solution.py:539
  36.6 23.8 %all-to-all-start = ((bf16[48,16,256]{2,0,1:T(8,128)(2,1)}), bf16[48,16,256]{2,0,1:T(8,128)(2,1)S(1)}, u32[]{:S(2)}, u32[]{:S(2)}) async-start(bf16[48,16,256]{2,0,1:T(8,128)(2,1)} %bitcast.250), calls=%async_computation | async-start | bytes 786432 | tf_op jit(solution)/shard_map/all_to_all | solution.py:599
  43.5 241.6 %all-gather.6.cloned.1.call-start = ((), (), s32[]{:S(2)}) async-start(), calls=%async_computation.5 | async-start | bytes 2506752 | tf_op jit(solution)/shard_map/all_gather | solution.py:612
  61.5 37.1 %collective-permute-start.4 = (bf16[128,1536]{0,1:T(8,128)(2,1)S(1)}, bf16[128,1536]{0,1:T(8,128)(2,1)S(1)}, u32[]{:S(2)}, u32[]{:S(2)}) collective-permute-start(bf16[128,1536]{0,1:T(8,128)(2,1)S(1)} %fusion.22), channel_id=1, source_target_pairs={{0,1},{1,0},{2,3},{3,2},{4,5},{5,4},{6,7},{7,6},{8,9},{9,8},{10,11... | collective-permute-start | bytes 1179656 | tf_op jit(solution)/shard_map/ppermute | solution.py:415
  64.7 34.0 %collective-permute-start.6 = (bf16[192,1536]{1,0:T(8,128)(2,1)S(1)}, bf16[192,1536]{1,0:T(8,128)(2,1)S(1)}, u32[]{:S(2)}, u32[]{:S(2)}) collective-permute-start(bf16[192,1536]{1,0:T(8,128)(2,1)S(1)} %slice.455), channel_id=1, source_target_pairs={{0,4},{2,6},{4,0},{6,2},{8,12},{10,14},{12,8},{14,10},{16,20},{18,... | collective-permute-start | bytes 1769480 | tf_op jit(solution)/shard_map/ppermute | solution.py:466
  69.0 15.7 %collective-permute-start.8 = (f32[3,6144]{1,0:T(4,128)S(1)}, f32[3,6144]{1,0:T(4,128)S(1)}, u32[]{:S(2)}, u32[]{:S(2)}) collective-permute-start(f32[3,6144]{1,0:T(4,128)S(1)} %add.615), channel_id=1, source_target_pairs={{0,4},{2,6},{4,0},{6,2},{8,12},{10,14},{12,8},{14,10},{16,20},{18,... | collective-permute-start | bytes 221192 | tf_op jit(solution)/shard_map/ppermute | solution.py:466
  99.8 219.3 %all-gather.8.cloned.1.call-start = ((), (), s32[]{:S(2)}) async-start(), calls=%async_computation.6 | async-start | bytes 20054016 | tf_op jit(solution)/shard_map/all_gather | solution.py:679
  112.0 14.5 %collective-permute-start.11 = (bf16[256,640]{1,0:T(8,128)(2,1)}, bf16[256,640]{1,0:T(8,128)(2,1)}, u32[]{:S(2)}, u32[]{:S(2)}) collective-permute-start(bf16[256,640]{1,0:T(8,128)(2,1)} %get-tuple-element.237), channel_id=1, source_target_pairs={{0,8},{2,10},{4,12},{6,14},{8,16},{10,18},{12,20},{14,22},{16,24},... | collective-permute-start | bytes 983048 | tf_op jit(solution)/shard_map/ppermute | solution.py:470
  112.0 26.6 %collective-permute-start.12 = (bf16[256,640]{1,0:T(8,128)(2,1)}, bf16[256,640]{1,0:T(8,128)(2,1)}, u32[]{:S(2)}, u32[]{:S(2)}) collective-permute-start(bf16[256,640]{1,0:T(8,128)(2,1)} %get-tuple-element.236), channel_id=1, source_target_pairs={{0,16},{2,18},{4,20},{6,22},{8,24},{10,26},{12,28},{14,30},{16,0},... | collective-permute-start | bytes 983048 | tf_op jit(solution)/shard_map/ppermute | solution.py:470
  113.9 24.6 %collective-permute-start.13 = (bf16[256,640]{1,0:T(8,128)(2,1)S(1)}, bf16[256,640]{1,0:T(8,128)(2,1)}, u32[]{:S(2)}, u32[]{:S(2)}) collective-permute-start(bf16[256,640]{1,0:T(8,128)(2,1)S(1)} %get-tuple-element.235), channel_id=1, source_target_pairs={{0,24},{2,26},{4,28},{6,30},{8,0},{10,2},{12,4},{14,6},{16,8},{18,... | collective-permute-start | bytes 983048 | tf_op jit(solution)/shard_map/ppermute | solution.py:470
  140.9 663.2 %reduce-scatter.5.cloned.1.call-start = ((), (), s32[]{:S(2)}) async-start(), calls=%async_computation.8 | async-start | bytes 6684672 | tf_op jit(solution)/shard_map/reduce_scatter | solution.py:712
  152.9 24.7 %collective-permute-start.16 = (bf16[192,384]{1,0:T(8,128)(2,1)S(1)}, bf16[192,384]{1,0:T(8,128)(2,1)S(1)}, u32[]{:S(2)}, u32[]{:S(2)}) collective-permute-start(bf16[192,384]{1,0:T(8,128)(2,1)S(1)} %get-tuple-element.255), channel_id=1, source_target_pairs={{0,8},{2,10},{4,12},{6,14},{8,16},{10,18},{12,20},{14,22},{16,24},... | collective-permute-start | bytes 442376 | tf_op jit(solution)/shard_map/ppermute | solution.py:470
  169.2 14.0 %collective-permute-start.17 = (bf16[192,384]{1,0:T(8,128)(2,1)S(1)}, bf16[192,384]{1,0:T(8,128)(2,1)S(1)}, u32[]{:S(2)}, u32[]{:S(2)}) collective-permute-start(bf16[192,384]{1,0:T(8,128)(2,1)S(1)} %get-tuple-element.257), channel_id=1, source_target_pairs={{0,16},{2,18},{4,20},{6,22},{8,24},{10,26},{12,28},{14,30},{16,0},... | collective-permute-start | bytes 442376 | tf_op jit(solution)/shard_map/ppermute | solution.py:470
  170.3 18.2 %collective-permute-start.18 = (bf16[192,384]{1,0:T(8,128)(2,1)S(1)}, bf16[192,384]{1,0:T(8,128)(2,1)S(1)}, u32[]{:S(2)}, u32[]{:S(2)}) collective-permute-start(bf16[192,384]{1,0:T(8,128)(2,1)S(1)} %get-tuple-element.256), channel_id=1, source_target_pairs={{0,24},{2,26},{4,28},{6,30},{8,0},{10,2},{12,4},{14,6},{16,8},{18,... | collective-permute-start | bytes 442376 | tf_op jit(solution)/shard_map/ppermute | solution.py:470
  173.3 37.5 %collective-permute-start.14 = (bf16[1024,384]{1,0:T(8,128)(2,1)}, bf16[1024,384]{1,0:T(8,128)(2,1)}, u32[]{:S(2)}, u32[]{:S(2)}) collective-permute-start(bf16[1024,384]{1,0:T(8,128)(2,1)} %slice.268), channel_id=1, source_target_pairs={{0,4},{2,6},{4,0},{6,2},{8,12},{10,14},{12,8},{14,10},{16,20},{18,... | collective-permute-start | bytes 2359304 | tf_op jit(solution)/shard_map/ppermute | solution.py:466
  198.1 18.0 %collective-permute-start.19 = (bf16[192,384]{1,0:T(8,128)(2,1)}, bf16[192,384]{1,0:T(8,128)(2,1)S(1)}, u32[]{:S(2)}, u32[]{:S(2)}) collective-permute-start(bf16[192,384]{1,0:T(8,128)(2,1)} %copy.265), channel_id=1, source_target_pairs={{0,4},{2,6},{4,0},{6,2},{8,12},{10,14},{12,8},{14,10},{16,20},{18,... | collective-permute-start | bytes 442376 | tf_op jit(solution)/shard_map/ppermute | solution.py:466
  275.3 9.7 %collective-permute-start.22 = (bf16[256,192]{0,1:T(8,128)(2,1)S(1)}, bf16[256,192]{0,1:T(8,128)(2,1)S(1)}, u32[]{:S(2)}, u32[]{:S(2)}) collective-permute-start(bf16[256,192]{0,1:T(8,128)(2,1)S(1)} %bitcast.306), channel_id=1, source_target_pairs={{0,16},{2,18},{4,20},{6,22},{8,24},{10,26},{12,28},{14,30},{16,0},... | collective-permute-start | bytes 294920 | tf_op jit(solution)/shard_map/ppermute | solution.py:470
  275.4 9.6 %collective-permute-start.23 = (bf16[256,192]{0,1:T(8,128)(2,1)S(1)}, bf16[256,192]{0,1:T(8,128)(2,1)S(1)}, u32[]{:S(2)}, u32[]{:S(2)}) collective-permute-start(bf16[256,192]{0,1:T(8,128)(2,1)S(1)} %bitcast.307), channel_id=1, source_target_pairs={{0,8},{2,10},{4,12},{6,14},{8,16},{10,18},{12,20},{14,22},{16,24},... | collective-permute-start | bytes 294920 | tf_op jit(solution)/shard_map/ppermute | solution.py:470
  287.8 11.1 %collective-permute-start.24 = (bf16[128,1536]{0,1:T(8,128)(2,1)S(1)}, bf16[128,1536]{0,1:T(8,128)(2,1)S(1)}, u32[]{:S(2)}, u32[]{:S(2)}) collective-permute-start(bf16[128,1536]{0,1:T(8,128)(2,1)S(1)} %slice.459), channel_id=1, source_target_pairs={{0,1},{1,0},{2,3},{3,2},{4,5},{5,4},{6,7},{7,6},{8,9},{9,8},{10,11... | collective-permute-start | bytes 1179656 | tf_op jit(solution)/shard_map/ppermute | solution.py:415
  300.3 12.1 %collective-permute-start.26 = (bf16[128,1536]{0,1:T(8,128)(2,1)S(1)}, bf16[128,1536]{0,1:T(8,128)(2,1)S(1)}, u32[]{:S(2)}, u32[]{:S(2)}) collective-permute-start(bf16[128,1536]{0,1:T(8,128)(2,1)S(1)} %get-tuple-element.224), channel_id=1, source_target_pairs={{0,1},{1,0},{2,3},{3,2},{4,5},{5,4},{6,7},{7,6},{8,9},{9,8},{10,11... | collective-permute-start | bytes 1179656 | tf_op jit(solution)/shard_map/ppermute | solution.py:415
  301.8 17.3 %collective-permute-start.25 = (bf16[128,1536]{0,1:T(8,128)(2,1)S(1)}, bf16[128,1536]{0,1:T(8,128)(2,1)}, u32[]{:S(2)}, u32[]{:S(2)}) collective-permute-start(bf16[128,1536]{0,1:T(8,128)(2,1)S(1)} %get-tuple-element.225), channel_id=1, source_target_pairs={{0,1},{1,0},{2,3},{3,2},{4,5},{5,4},{6,7},{7,6},{8,9},{9,8},{10,11... | collective-permute-start | bytes 1179656 | tf_op jit(solution)/shard_map/ppermute | solution.py:415
  339.1 467.0 %reduce-scatter.3.cloned.1.call-start = ((), (), s32[]{:S(2)}) async-start(), calls=%async_computation.7 | async-start | bytes 13369344 | tf_op jit(solution)/shard_map/reduce_scatter | solution.py:740
  341.2 58.2 %collective-permute-start.39 = (bf16[384,256]{1,0:T(8,128)(2,1)}, bf16[384,256]{1,0:T(8,128)(2,1)}, u32[]{:S(2)}, u32[]{:S(2)}) collective-permute-start(bf16[384,256]{1,0:T(8,128)(2,1)} %get-tuple-element.241), channel_id=1, source_target_pairs={{0,4},{2,6},{4,0},{6,2},{8,12},{10,14},{12,8},{14,10},{16,20},{18,... | collective-permute-start | bytes 589832 | tf_op jit(solution)/shard_map/ppermute | solution.py:466
  342.7 56.7 %collective-permute-start.40 = (bf16[384,256]{1,0:T(8,128)(2,1)}, bf16[384,256]{1,0:T(8,128)(2,1)}, u32[]{:S(2)}, u32[]{:S(2)}) collective-permute-start(bf16[384,256]{1,0:T(8,128)(2,1)} %get-tuple-element.240), channel_id=1, source_target_pairs={{0,2},{2,0},{4,6},{6,4},{8,10},{10,8},{12,14},{14,12},{16,18},{18,... | collective-permute-start | bytes 589832 | tf_op jit(solution)/shard_map/ppermute | solution.py:466
  342.7 57.8 %collective-permute-start.41 = (bf16[384,256]{1,0:T(8,128)(2,1)}, bf16[384,256]{1,0:T(8,128)(2,1)}, u32[]{:S(2)}, u32[]{:S(2)}) collective-permute-start(bf16[384,256]{1,0:T(8,128)(2,1)} %get-tuple-element.239), channel_id=1, source_target_pairs={{0,6},{2,4},{4,2},{6,0},{8,14},{10,12},{12,10},{14,8},{16,22},{18,... | collective-permute-start | bytes 589832 | tf_op jit(solution)/shard_map/ppermute | solution.py:466
  344.5 38.3 %collective-permute-start.36 = (bf16[256,768]{1,0:T(8,128)(2,1)S(1)}, bf16[256,768]{1,0:T(8,128)(2,1)}, u32[]{:S(2)}, u32[]{:S(2)}) collective-permute-start(bf16[256,768]{1,0:T(8,128)(2,1)S(1)} %copy.244.refs_0_), channel_id=1, source_target_pairs={{0,4},{2,6},{4,0},{6,2},{8,12},{10,14},{12,8},{14,10},{16,20},{18,... | collective-permute-start | bytes 1179656 | tf_op jit(solution)/shard_map/ppermute | solution.py:466
  356.5 10.8 %collective-permute-start.28 = (bf16[128,1536]{0,1:T(8,128)(2,1)S(1)}, bf16[128,1536]{0,1:T(8,128)(2,1)S(1)}, u32[]{:S(2)}, u32[]{:S(2)}) collective-permute-start(bf16[128,1536]{0,1:T(8,128)(2,1)S(1)} %slice.457), channel_id=1, source_target_pairs={{0,1},{1,0},{2,3},{3,2},{4,5},{5,4},{6,7},{7,6},{8,9},{9,8},{10,11... | collective-permute-start | bytes 1179656 | tf_op jit(solution)/shard_map/ppermute | solution.py:415
  367.3 9.9 %collective-permute-start.27 = (bf16[128,1536]{0,1:T(8,128)(2,1)S(1)}, bf16[128,1536]{0,1:T(8,128)(2,1)S(1)}, u32[]{:S(2)}, u32[]{:S(2)}) collective-permute-start(bf16[128,1536]{0,1:T(8,128)(2,1)S(1)} %slice.458), channel_id=1, source_target_pairs={{0,1},{1,0},{2,3},{3,2},{4,5},{5,4},{6,7},{7,6},{8,9},{9,8},{10,11... | collective-permute-start | bytes 1179656 | tf_op jit(solution)/shard_map/ppermute | solution.py:415
  379.9 9.1 %collective-permute-start.29 = (bf16[128,1536]{0,1:T(8,128)(2,1)S(1)}, bf16[128,1536]{0,1:T(8,128)(2,1)S(1)}, u32[]{:S(2)}, u32[]{:S(2)}) collective-permute-start(bf16[128,1536]{0,1:T(8,128)(2,1)S(1)} %multiply_convert_fusion.3), channel_id=1, source_target_pairs={{0,1},{1,0},{2,3},{3,2},{4,5},{5,4},{6,7},{7,6},{8,9},{9,8},{10,11... | collective-permute-start | bytes 1179656 | tf_op jit(solution)/shard_map/ppermute | solution.py:415
  382.8 50.3 %collective-permute-start.37 = (bf16[256,768]{1,0:T(8,128)(2,1)S(1)}, bf16[256,768]{1,0:T(8,128)(2,1)}, u32[]{:S(2)}, u32[]{:S(2)}) collective-permute-start(bf16[256,768]{1,0:T(8,128)(2,1)S(1)} %copy.244.refs_0_), channel_id=1, source_target_pairs={{0,2},{2,0},{4,6},{6,4},{8,10},{10,8},{12,14},{14,12},{16,18},{18,... | collective-permute-start | bytes 1179656 | tf_op jit(solution)/shard_map/ppermute | solution.py:466
  389.0 44.1 %collective-permute-start.38 = (bf16[256,768]{1,0:T(8,128)(2,1)}, bf16[256,768]{1,0:T(8,128)(2,1)}, u32[]{:S(2)}, u32[]{:S(2)}) collective-permute-start(bf16[256,768]{1,0:T(8,128)(2,1)} %collective-permute-done.36.refs_1_), channel_id=1, source_target_pairs={{0,2},{2,0},{4,6},{6,4},{8,10},{10,8},{12,14},{14,12},{16,18},{18,... | collective-permute-start | bytes 1179656 | tf_op jit(solution)/shard_map/ppermute | solution.py:466
  399.4 17.5 %collective-permute-start.31 = (bf16[256,192]{1,0:T(8,128)(2,1)}, bf16[256,192]{1,0:T(8,128)(2,1)S(1)}, u32[]{:S(2)}, u32[]{:S(2)}) collective-permute-start(bf16[256,192]{1,0:T(8,128)(2,1)} %bitcast.297), channel_id=1, source_target_pairs={{0,16},{2,18},{4,20},{6,22},{8,24},{10,26},{12,28},{14,30},{16,0},... | collective-permute-start | bytes 294920 | tf_op jit(solution)/shard_map/ppermute | solution.py:470
  400.5 16.4 %collective-permute-start.32 = (bf16[256,192]{1,0:T(8,128)(2,1)}, bf16[256,192]{1,0:T(8,128)(2,1)S(1)}, u32[]{:S(2)}, u32[]{:S(2)}) collective-permute-start(bf16[256,192]{1,0:T(8,128)(2,1)} %bitcast.296), channel_id=1, source_target_pairs={{0,24},{2,26},{4,28},{6,30},{8,0},{10,2},{12,4},{14,6},{16,8},{18,... | collective-permute-start | bytes 294920 | tf_op jit(solution)/shard_map/ppermute | solution.py:470
  407.8 23.9 %collective-permute-start.33 = (bf16[384,256]{1,0:T(8,128)(2,1)}, bf16[384,256]{1,0:T(8,128)(2,1)}, u32[]{:S(2)}, u32[]{:S(2)}) collective-permute-start(bf16[384,256]{1,0:T(8,128)(2,1)} %get-tuple-element.245), channel_id=1, source_target_pairs={{0,4},{2,6},{4,0},{6,2},{8,12},{10,14},{12,8},{14,10},{16,20},{18,... | collective-permute-start | bytes 589832 | tf_op jit(solution)/shard_map/ppermute | solution.py:466
  416.9 14.8 %collective-permute-start.34 = (bf16[384,256]{1,0:T(8,128)(2,1)}, bf16[384,256]{1,0:T(8,128)(2,1)}, u32[]{:S(2)}, u32[]{:S(2)}) collective-permute-start(bf16[384,256]{1,0:T(8,128)(2,1)} %get-tuple-element.244), channel_id=1, source_target_pairs={{0,2},{2,0},{4,6},{6,4},{8,10},{10,8},{12,14},{14,12},{16,18},{18,... | collective-permute-start | bytes 589832 | tf_op jit(solution)/shard_map/ppermute | solution.py:466
  416.9 14.8 %collective-permute-start.35 = (bf16[384,256]{1,0:T(8,128)(2,1)}, bf16[384,256]{1,0:T(8,128)(2,1)}, u32[]{:S(2)}, u32[]{:S(2)}) collective-permute-start(bf16[384,256]{1,0:T(8,128)(2,1)} %get-tuple-element.243), channel_id=1, source_target_pairs={{0,6},{2,4},{4,2},{6,0},{8,14},{10,12},{12,10},{14,8},{16,22},{18,... | collective-permute-start | bytes 589832 | tf_op jit(solution)/shard_map/ppermute | solution.py:466
  509.7 16.6 %collective-permute-start.42 = (bf16[2048,384]{1,0:T(8,128)(2,1)}, bf16[2048,384]{1,0:T(8,128)(2,1)}, u32[]{:S(2)}, u32[]{:S(2)}) collective-permute-start(bf16[2048,384]{1,0:T(8,128)(2,1)} %slice.288), channel_id=1, source_target_pairs={{0,2},{2,0},{4,6},{6,4},{8,10},{10,8},{12,14},{14,12},{16,18},{18,... | collective-permute-start | bytes 4718600 | tf_op jit(solution)/shard_map/ppermute | solution.py:466
  531.1 28.9 %collective-permute-start.43 = (bf16[1024,384]{1,0:T(8,128)(2,1)}, bf16[1024,384]{1,0:T(8,128)(2,1)}, u32[]{:S(2)}, u32[]{:S(2)}) collective-permute-start(bf16[1024,384]{1,0:T(8,128)(2,1)} %slice.454), channel_id=1, source_target_pairs={{0,4},{2,6},{4,0},{6,2},{8,12},{10,14},{12,8},{14,10},{16,20},{18,... | collective-permute-start | bytes 2359304 | tf_op jit(solution)/shard_map/ppermute | solution.py:466
  540.3 13.3 %collective-permute-start.76 = (bf16[96,768]{1,0:T(8,128)(2,1)S(1)}, bf16[96,768]{1,0:T(8,128)(2,1)S(1)}, u32[]{:S(2)}, u32[]{:S(2)}) collective-permute-start(bf16[96,768]{1,0:T(8,128)(2,1)S(1)} %get-tuple-element.252), channel_id=1, source_target_pairs={{0,8},{2,10},{4,12},{6,14},{8,16},{10,18},{12,20},{14,22},{16,24},... | collective-permute-start | bytes 442376 | tf_op jit(solution)/shard_map/ppermute | solution.py:470
  549.3 9.1 %collective-permute-start.77 = (bf16[96,768]{1,0:T(8,128)(2,1)S(1)}, bf16[96,768]{1,0:T(8,128)(2,1)S(1)}, u32[]{:S(2)}, u32[]{:S(2)}) collective-permute-start(bf16[96,768]{1,0:T(8,128)(2,1)S(1)} %get-tuple-element.254), channel_id=1, source_target_pairs={{0,16},{2,18},{4,20},{6,22},{8,24},{10,26},{12,28},{14,30},{16,0},... | collective-permute-start | bytes 442376 | tf_op jit(solution)/shard_map/ppermute | solution.py:470
  562.5 34.1 %collective-permute-start.48 = (bf16[384,384]{1,0:T(8,128)(2,1)S(1)}, bf16[384,384]{1,0:T(8,128)(2,1)S(1)}, u32[]{:S(2)}, u32[]{:S(2)}) collective-permute-start(bf16[384,384]{1,0:T(8,128)(2,1)S(1)} %slice.297), channel_id=1, source_target_pairs={{0,2},{2,0},{4,6},{6,4},{8,10},{10,8},{12,14},{14,12},{16,18},{18,... | collective-permute-start | bytes 884744 | tf_op jit(solution)/shard_map/ppermute | solution.py:466
  564.6 33.3 %collective-permute-start.45 = (bf16[256,640]{1,0:T(8,128)(2,1)S(1)}, bf16[256,640]{1,0:T(8,128)(2,1)S(1)}, u32[]{:S(2)}, u32[]{:S(2)}) collective-permute-start(bf16[256,640]{1,0:T(8,128)(2,1)S(1)} %get-tuple-element.233), channel_id=1, source_target_pairs={{0,24},{2,26},{4,28},{6,30},{8,0},{10,2},{12,4},{14,6},{16,8},{18,... | collective-permute-start | bytes 983048 | tf_op jit(solution)/shard_map/ppermute | solution.py:470
  571.3 25.1 %collective-permute-start.52 = (f32[4,6144]{1,0:T(4,128)S(1)}, f32[4,6144]{1,0:T(4,128)S(1)}, u32[]{:S(2)}, u32[]{:S(2)}) collective-permute-start(f32[4,6144]{1,0:T(4,128)S(1)} %add.695), channel_id=1, source_target_pairs={{0,8},{2,10},{4,12},{6,14},{8,0},{10,2},{12,4},{14,6},{16,24},{18,... | collective-permute-start | bytes 294920 | tf_op jit(solution)/shard_map/ppermute | solution.py:466
  574.3 58.5 %collective-permute-start.46 = (bf16[256,640]{1,0:T(8,128)(2,1)S(1)}, bf16[256,640]{1,0:T(8,128)(2,1)S(1)}, u32[]{:S(2)}, u32[]{:S(2)}) collective-permute-start(bf16[256,640]{1,0:T(8,128)(2,1)S(1)} %get-tuple-element.232), channel_id=1, source_target_pairs={{0,16},{2,18},{4,20},{6,22},{8,24},{10,26},{12,28},{14,30},{16,0},... | collective-permute-start | bytes 983048 | tf_op jit(solution)/shard_map/ppermute | solution.py:470
  577.6 55.2 %collective-permute-start.47 = (bf16[256,640]{1,0:T(8,128)(2,1)S(1)}, bf16[256,640]{1,0:T(8,128)(2,1)S(1)}, u32[]{:S(2)}, u32[]{:S(2)}) collective-permute-start(bf16[256,640]{1,0:T(8,128)(2,1)S(1)} %get-tuple-element.231), channel_id=1, source_target_pairs={{0,8},{2,10},{4,12},{6,14},{8,16},{10,18},{12,20},{14,22},{16,24},... | collective-permute-start | bytes 983048 | tf_op jit(solution)/shard_map/ppermute | solution.py:470
  596.4 44.6 %collective-permute-start.53 = (f32[4,6144]{1,0:T(4,128)S(1)}, f32[4,6144]{1,0:T(4,128)S(1)}, u32[]{:S(2)}, u32[]{:S(2)}) collective-permute-start(f32[4,6144]{1,0:T(4,128)S(1)} %add.696), channel_id=1, source_target_pairs={{0,16},{2,18},{4,20},{6,22},{8,24},{10,26},{12,28},{14,30},{16,0},... | collective-permute-start | bytes 294920 | tf_op jit(solution)/shard_map/ppermute | solution.py:466
  596.6 45.7 %collective-permute-start.49 = (bf16[192,384]{1,0:T(8,128)(2,1)S(1)}, bf16[192,384]{1,0:T(8,128)(2,1)S(1)}, u32[]{:S(2)}, u32[]{:S(2)}) collective-permute-start(bf16[192,384]{1,0:T(8,128)(2,1)S(1)} %slice.460), channel_id=1, source_target_pairs={{0,4},{2,6},{4,0},{6,2},{8,12},{10,14},{12,8},{14,10},{16,20},{18,... | collective-permute-start | bytes 442376 | tf_op jit(solution)/shard_map/ppermute | solution.py:466
  660.0 43.5 %collective-permute-start.59 = (bf16[256,2304]{1,0:T(8,128)(2,1)}, bf16[256,2304]{1,0:T(8,128)(2,1)S(1)}, u32[]{:S(2)}, u32[]{:S(2)}) collective-permute-start(bf16[256,2304]{1,0:T(8,128)(2,1)} %get-tuple-element.73.refs_0_), channel_id=1, source_target_pairs={{0,4},{2,6},{4,0},{6,2},{8,12},{10,14},{12,8},{14,10},{16,20},{18,... | collective-permute-start | bytes 3538952 | tf_op jit(solution)/shard_map/ppermute | solution.py:466
  661.4 53.5 %collective-permute-start.60 = (bf16[256,2304]{1,0:T(8,128)(2,1)}, bf16[256,2304]{1,0:T(8,128)(2,1)S(1)}, u32[]{:S(2)}, u32[]{:S(2)}) collective-permute-start(bf16[256,2304]{1,0:T(8,128)(2,1)} %get-tuple-element.73.refs_0_), channel_id=1, source_target_pairs={{0,2},{2,0},{4,6},{6,4},{8,10},{10,8},{12,14},{14,12},{16,18},{18,... | collective-permute-start | bytes 3538952 | tf_op jit(solution)/shard_map/ppermute | solution.py:466
  661.4 16.3 %collective-permute-start.56 = (bf16[192,384]{0,1:T(8,128)(2,1)}, bf16[192,384]{0,1:T(8,128)(2,1)}, u32[]{:S(2)}, u32[]{:S(2)}) collective-permute-start(bf16[192,384]{0,1:T(8,128)(2,1)} %pad_maximum_fusion.21), channel_id=1, source_target_pairs={{0,24},{2,26},{4,28},{6,30},{8,0},{10,2},{12,4},{14,6},{16,8},{18,... | collective-permute-start | bytes 442376 | tf_op jit(solution)/shard_map/ppermute | solution.py:470
  665.5 25.0 %collective-permute-start.57 = (bf16[192,384]{0,1:T(8,128)(2,1)}, bf16[192,384]{0,1:T(8,128)(2,1)}, u32[]{:S(2)}, u32[]{:S(2)}) collective-permute-start(bf16[192,384]{0,1:T(8,128)(2,1)} %pad_maximum_fusion.21), channel_id=1, source_target_pairs={{0,16},{2,18},{4,20},{6,22},{8,24},{10,26},{12,28},{14,30},{16,0},... | collective-permute-start | bytes 442376 | tf_op jit(solution)/shard_map/ppermute | solution.py:470
  665.5 26.6 %collective-permute-start.58 = (bf16[192,384]{0,1:T(8,128)(2,1)}, bf16[192,384]{0,1:T(8,128)(2,1)}, u32[]{:S(2)}, u32[]{:S(2)}) collective-permute-start(bf16[192,384]{0,1:T(8,128)(2,1)} %pad_maximum_fusion.21), channel_id=1, source_target_pairs={{0,8},{2,10},{4,12},{6,14},{8,16},{10,18},{12,20},{14,22},{16,24},... | collective-permute-start | bytes 442376 | tf_op jit(solution)/shard_map/ppermute | solution.py:470
  677.7 22.5 %collective-permute-start.54 = (bf16[128,1536]{0,1:T(8,128)(2,1)}, bf16[128,1536]{0,1:T(8,128)(2,1)S(1)}, u32[]{:S(2)}, u32[]{:S(2)}) collective-permute-start(bf16[128,1536]{0,1:T(8,128)(2,1)} %slice.456), channel_id=1, source_target_pairs={{0,1},{1,0},{2,3},{3,2},{4,5},{5,4},{6,7},{7,6},{8,9},{9,8},{10,11... | collective-permute-start | bytes 1179656 | tf_op jit(solution)/shard_map/ppermute | solution.py:415
  703.5 12.5 %collective-permute-start.61 = (bf16[256,2304]{1,0:T(8,128)(2,1)S(1)}, bf16[256,2304]{1,0:T(8,128)(2,1)}, u32[]{:S(2)}, u32[]{:S(2)}) collective-permute-start(bf16[256,2304]{1,0:T(8,128)(2,1)S(1)} %collective-permute-done.59.refs_1_), channel_id=1, source_target_pairs={{0,2},{2,0},{4,6},{6,4},{8,10},{10,8},{12,14},{14,12},{16,18},{18,... | collective-permute-start | bytes 3538952 | tf_op jit(solution)/shard_map/ppermute | solution.py:466
  726.0 24.0 %collective-permute-start.62 = (bf16[192,1536]{1,0:T(8,128)(2,1)S(1)}, bf16[192,1536]{1,0:T(8,128)(2,1)S(1)}, u32[]{:S(2)}, u32[]{:S(2)}) collective-permute-start(bf16[192,1536]{1,0:T(8,128)(2,1)S(1)} %copy-done.42), channel_id=1, source_target_pairs={{0,4},{2,6},{4,0},{6,2},{8,12},{10,14},{12,8},{14,10},{16,20},{18,... | collective-permute-start | bytes 1769480 | tf_op jit(solution)/shard_map/ppermute | solution.py:466
  729.9 10.0 %collective-permute-start.67 = (f32[4,3072]{1,0:T(4,128)S(1)}, f32[4,3072]{1,0:T(4,128)S(1)}, u32[]{:S(2)}, u32[]{:S(2)}) collective-permute-start(f32[4,3072]{1,0:T(4,128)S(1)} %add.709), channel_id=1, source_target_pairs={{0,8},{2,10},{4,12},{6,14},{8,0},{10,2},{12,4},{14,6},{16,24},{18,... | collective-permute-start | bytes 147464 | tf_op jit(solution)/shard_map/ppermute | solution.py:466
  739.8 10.2 %collective-permute-start.68 = (f32[4,3072]{1,0:T(4,128)S(1)}, f32[4,3072]{1,0:T(4,128)S(1)}, u32[]{:S(2)}, u32[]{:S(2)}) collective-permute-start(f32[4,3072]{1,0:T(4,128)S(1)} %add.710), channel_id=1, source_target_pairs={{0,16},{2,18},{4,20},{6,22},{8,24},{10,26},{12,28},{14,30},{16,0},... | collective-permute-start | bytes 147464 | tf_op jit(solution)/shard_map/ppermute | solution.py:466
  745.9 45.3 %collective-permute-start.73 = (bf16[96,2304]{1,0:T(8,128)(2,1)}, bf16[96,2304]{1,0:T(8,128)(2,1)}, u32[]{:S(2)}, u32[]{:S(2)}) collective-permute-start(bf16[96,2304]{1,0:T(8,128)(2,1)} %get-tuple-element.226), channel_id=1, source_target_pairs={{0,8},{2,10},{4,12},{6,14},{8,16},{10,18},{12,20},{14,22},{16,24},... | collective-permute-start | bytes 1327112 | tf_op jit(solution)/shard_map/ppermute | solution.py:470
  745.9 45.3 %collective-permute-start.74 = (bf16[96,2304]{1,0:T(8,128)(2,1)}, bf16[96,2304]{1,0:T(8,128)(2,1)}, u32[]{:S(2)}, u32[]{:S(2)}) collective-permute-start(bf16[96,2304]{1,0:T(8,128)(2,1)} %get-tuple-element.228), channel_id=1, source_target_pairs={{0,16},{2,18},{4,20},{6,22},{8,24},{10,26},{12,28},{14,30},{16,0},... | collective-permute-start | bytes 1327112 | tf_op jit(solution)/shard_map/ppermute | solution.py:470
  745.9 45.3 %collective-permute-start.75 = (bf16[96,2304]{1,0:T(8,128)(2,1)}, bf16[96,2304]{1,0:T(8,128)(2,1)}, u32[]{:S(2)}, u32[]{:S(2)}) collective-permute-start(bf16[96,2304]{1,0:T(8,128)(2,1)} %get-tuple-element.227), channel_id=1, source_target_pairs={{0,24},{2,26},{4,28},{6,30},{8,0},{10,2},{12,4},{14,6},{16,8},{18,... | collective-permute-start | bytes 1327112 | tf_op jit(solution)/shard_map/ppermute | solution.py:470
  758.4 16.9 %collective-permute-start.71 = (f32[3,1024]{1,0:T(4,128)S(1)}, f32[3,1024]{1,0:T(4,128)S(1)}, u32[]{:S(2)}, u32[]{:S(2)}) collective-permute-start(f32[3,1024]{1,0:T(4,128)S(1)} %add.713), channel_id=1, source_target_pairs={{0,8},{2,10},{4,12},{6,14},{8,0},{10,2},{12,4},{14,6},{16,24},{18,... | collective-permute-start | bytes 36872 | tf_op jit(solution)/shard_map/ppermute | solution.py:466
  764.7 21.9 %collective-permute-start.64 = (bf16[768,256]{1,0:T(8,128)(2,1)S(1)}, bf16[768,256]{1,0:T(8,128)(2,1)S(1)}, u32[]{:S(2)}, u32[]{:S(2)}) collective-permute-start(bf16[768,256]{1,0:T(8,128)(2,1)S(1)} %convolution_convert_fusion), channel_id=1, source_target_pairs={{0,1},{1,0},{2,3},{3,2},{4,5},{5,4},{6,7},{7,6},{8,9},{9,8},{10,11... | collective-permute-start | bytes 1179656 | tf_op jit(solution)/shard_map/ppermute | solution.py:415
  775.3 10.7 %collective-permute-start.72 = (f32[3,1024]{1,0:T(4,128)S(1)}, f32[3,1024]{1,0:T(4,128)S(1)}, u32[]{:S(2)}, u32[]{:S(2)}) collective-permute-start(f32[3,1024]{1,0:T(4,128)S(1)} %add.714), channel_id=1, source_target_pairs={{0,16},{2,18},{4,20},{6,22},{8,24},{10,26},{12,28},{14,30},{16,0},... | collective-permute-start | bytes 36872 | tf_op jit(solution)/shard_map/ppermute | solution.py:466
  787.6 15.7 %all-to-all-start.1 = ((bf16[16,48,256]{2,1,0:T(8,128)(2,1)}), bf16[16,48,256]{2,1,0:T(8,128)(2,1)S(1)}, u32[]{:S(2)}, u32[]{:S(2)}) async-start(bf16[16,48,256]{2,1,0:T(8,128)(2,1)} %bitcast.104), calls=%async_computation.1 | async-start | bytes 786432 | tf_op jit(solution)/shard_map/all_to_all | solution.py:859
  (160 other events, 1471.1 us)
Sparse Core Ops, SparseCore 0:
  10.9 75.3 all-gather.3
  99.9 55.4 all-gather.5
  157.6 117.3 all-gather.7
  339.2 89.1 reduce-scatter.4
  521.0 187.5 reduce-scatter.2

commit v3 on v2

v3 whole, which is shorter than its diff:
```python
import functools

import jax
import jax.numpy as jnp
from jax import lax
from jax.experimental import pallas as pl
from jax.experimental.pallas import tpu as pltpu
from jax.sharding import PartitionSpec as P

TXT = 256
GROUP = 8
SPLIT = 4
EPS = 1e-06
MASK = -1e4
FORWARD_SLOTS = 4
BACKWARD_SLOTS = 4
LOW = jnp.bfloat16
FLOAT = jnp.float32
MIB = 1024 * 1024
SMALL = pl.CostEstimate(flops=1024, bytes_accessed=1024, transcendentals=0)


def pick_tile(total, most):
    size = most
    while total % size:
        size //= 2
    return size


def matmul(left, right, left_dim, right_dim):
    return lax.dot_general(
        left, right, (((left_dim,), (right_dim,)), ((), ())), preferred_element_type=jnp.float32
    )


def lane_ids(shape):
    return lax.broadcasted_iota(jnp.int32, shape, len(shape) - 1)


def turn(values):
    return pltpu.roll(values, 64, 1)


def fold_low(values):
    half = values.shape[0] // 2
    top, bottom = values[:half], turn(values)[half:]
    return jnp.where(lane_ids(top.shape) < 64, top, bottom).astype(LOW)


def fold_high(values):
    half = values.shape[0] // 2
    top, bottom = turn(values)[:half], values[half:]
    return jnp.where(lane_ids(top.shape) < 64, top, bottom).astype(LOW)


def unfold_low(packed):
    wide = packed.astype(FLOAT)
    return jnp.concatenate([wide, turn(wide)], axis=0)


def unfold_high(packed):
    wide = packed.astype(FLOAT)
    return jnp.concatenate([turn(wide), wide], axis=0)


def build_pair(pair, features, spot, keys, values):
    lanes = lane_ids(pair.shape)
    rows = pl.ds(spot, pair.shape[0])
    keys[rows, :] = jnp.where(lanes < 64, pair, features)
    values[rows, :] = jnp.where(
        lanes < 64, jnp.where(lanes < 3, 1.0, 0.0).astype(LOW), pair
    )


def build_inputs(head, near_refs, query_ref, qf_ref, kf_ref, tf_ref, queries, keys, values, text_keys, text_values):
    rows = query_ref.shape[0]
    queries[...] = query_ref[...] + qf_ref[...]
    each = pl.cdiv(near_refs[0].shape[0], rows) - 1
    text_rows = (near_refs[0].shape[0] - each * rows) // each
    for index, ref in enumerate(near_refs):
        spot = pl.ds(pl.multiple_of(head * rows, rows), rows)
        build_pair(ref[spot, :], kf_ref[rows * index : rows * index + rows, :], rows * index, keys, values)
        spot = pl.ds(pl.multiple_of(each * rows + head * text_rows, 16), text_rows)
        first = text_rows * index
        build_pair(
            ref[spot, :], tf_ref[first : first + text_rows, :], first, text_keys, text_values
        )


def forward_kernel(near, chunk, *refs):
    near_refs, refs = refs[:near], refs[near:]
    query_ref, qf_ref, kf_ref, tf_ref, gate_ref = refs[:5]
    mixed_refs, refs = refs[5 : 5 + SPLIT], refs[5 + SPLIT :]
    outs_ref, stats_ref, queries, keys, values, text_keys, text_values, hold = refs
    build_inputs(
        pl.program_id(0), near_refs, query_ref, qf_ref, kf_ref, tf_ref,
        queries, keys, values, text_keys, text_values,
    )
    rows = queries.shape[0] // SPLIT * FORWARD_SLOTS
    text_chunk = pick_tile(text_keys.shape[0], 256)

    def tile_step(tile, carry):
        spot = pl.ds(pl.multiple_of(tile * rows, rows), rows)
        query = queries[spot, :]

        def attend(key_part, value_part):
            scores = matmul(query, key_part, 1, 1)
            return matmul(jnp.exp(scores).astype(LOW), value_part, 1, 0)

        def step(index, total):
            part = pl.ds(pl.multiple_of(index * chunk, chunk), chunk)
            return total + attend(keys[part, :], values[part, :])

        def text_step(index, total):
            part = pl.ds(pl.multiple_of(index * text_chunk, text_chunk), text_chunk)
            return total + attend(text_keys[part, :], text_values[part, :])

        blank = jnp.zeros((rows, 128), FLOAT)
        own = lax.fori_loop(0, keys.shape[0] // chunk, step, blank)
        cross = lax.fori_loop(0, text_keys.shape[0] // text_chunk, text_step, blank, unroll=True)
        own_inverse = 1.0 / own[:, 0:1]
        cross_inverse = 1.0 / cross[:, 0:1]
        own = own * own_inverse
        cross = cross * cross_inverse
        lanes = lane_ids(own.shape)
        mixed = own + gate_ref[0, 0:1, :] * cross
        each = rows // FORWARD_SLOTS
        for slot in range(FORWARD_SLOTS):
            hold[tile * FORWARD_SLOTS + slot] = fold_high(mixed[each * slot : each * slot + each])
        outs_ref[spot, :] = jnp.where(lanes < 64, turn(cross), own)
        stats_ref[spot, :] = jnp.where(lanes == 0, own_inverse, cross_inverse)
        return carry

    lax.fori_loop(0, SPLIT // FORWARD_SLOTS, tile_step, 0)
    for index, ref in enumerate(mixed_refs):
        ref[...] = hold[index]


def whole(shape):
    return pl.BlockSpec(shape, lambda i: (0,) * len(shape))


def attention_specs(pairs, queries, qf, kf, tf):
    return [whole(value.shape) for value in pairs] + [
        pl.BlockSpec(qf.shape, lambda i: (i, 0)),
        whole(qf.shape),
        whole(kf.shape),
        whole(tf.shape),
        pl.BlockSpec((1, 8, 128), lambda i: (i, 0, 0)),
    ]


def attention_scratch(qf, kf, tf):
    return [
        pltpu.VMEM(qf.shape, LOW),
        pltpu.VMEM(kf.shape, LOW),
        pltpu.VMEM(kf.shape, LOW),
        pltpu.VMEM(tf.shape, LOW),
        pltpu.VMEM(tf.shape, LOW),
    ]


def attention_forward(pairs, queries, qf, kf, tf, gates):
    rows = qf.shape[0]
    heads = gates.shape[0]
    half = rows // SPLIT // 2
    folded = jax.ShapeDtypeStruct((heads * half, 128), LOW)
    wide = jax.ShapeDtypeStruct((heads * rows, 128), FLOAT)
    out = pl.pallas_call(
        functools.partial(forward_kernel, len(pairs), pick_tile(kf.shape[0], 1024)),
        grid=(heads,),
        in_specs=attention_specs(pairs, queries, qf, kf, tf),
        out_specs=[pl.BlockSpec((half, 128), lambda i: (i, 0))] * SPLIT
        + [pl.BlockSpec((rows, 128), lambda i: (i, 0))] * 2,
        out_shape=[folded] * SPLIT + [wide] * 2,
        scratch_shapes=attention_scratch(qf, kf, tf) + [pltpu.VMEM((SPLIT, half, 128), LOW)],
        compiler_params=pltpu.CompilerParams(vmem_limit_bytes=60 * MIB),
        cost_estimate=SMALL,
    )(*pairs, queries, qf, kf, tf, gates)
    return out[:SPLIT], out[SPLIT], out[SPLIT + 1]


def backward_kernel(near, chunk, *refs):
    near_refs, refs = refs[:near], refs[near:]
    query_ref, qf_ref, kf_ref, tf_ref, gate_ref = refs[:5]
    refs = refs[5:]
    grad_refs, refs = refs[:SPLIT], refs[SPLIT:]
    outs_ref, stats_ref, refs = refs[0], refs[1], refs[2:]
    dq_refs, refs = refs[:SPLIT], refs[SPLIT:]
    dkv_refs, dt_refs, dg_ref = refs[:2], refs[2:4], refs[4]
    queries, keys, values, text_keys, text_values, hold, grad_hold, acc, text_acc = refs[5:]
    build_inputs(
        pl.program_id(0), near_refs, query_ref, qf_ref, kf_ref, tf_ref,
        queries, keys, values, text_keys, text_values,
    )
    for index, ref in enumerate(grad_refs):
        grad_hold[index] = ref[...]
    acc[...] = jnp.zeros_like(acc)
    text_acc[...] = jnp.zeros_like(text_acc)
    dg_ref[...] = jnp.zeros_like(dg_ref)
    rows = queries.shape[0] // SPLIT * BACKWARD_SLOTS
    text_chunk = pick_tile(text_keys.shape[0], 256)
    gate = gate_ref[0, 0:1, :]

    def tile_step(tile, carry):
        spot = pl.ds(pl.multiple_of(tile * rows, rows), rows)
        query = queries[spot, :]
        lanes = lane_ids(query.shape)
        query_low = jnp.where(lanes < 64, query, jnp.zeros_like(query))
        grads = jnp.concatenate(
            [unfold_high(grad_hold[tile * BACKWARD_SLOTS + slot]) for slot in range(BACKWARD_SLOTS)],
            axis=0,
        )
        grads = jnp.where(lanes < 64, 0.0, grads)
        outs = outs_ref[spot, :]
        cross_out = jnp.where(lanes < 64, 0.0, turn(outs))
        dg_ref[0] += jnp.sum((grads * cross_out).reshape(rows // 8, 8, 128), axis=0)
        cross_grads = (gate * grads).astype(LOW).astype(FLOAT)

        def widen(grad, out, inverse):
            delta = -jnp.sum(grad * out, axis=1, keepdims=True) * inverse
            first = delta.astype(LOW).astype(FLOAT)
            second = (delta - first).astype(LOW).astype(FLOAT)
            third = delta - first - second
            features = jnp.where(lanes == 0, first, jnp.where(lanes == 1, second, third))
            scaled = grad * inverse
            return jnp.where(lanes < 3, features, scaled).astype(LOW), scaled.astype(LOW)

        stats = stats_ref[spot, :]
        own_wide, own_low = widen(grads, outs, stats[:, 0:1])
        cross_wide, cross_low = widen(cross_grads, cross_out, stats[:, 1:2])
        own_pair = jnp.concatenate([query_low, own_low], axis=0)
        cross_pair = jnp.concatenate([query_low, cross_low], axis=0)

        def attend(key_part, value_part, wide, pair):
            weights = jnp.exp(matmul(key_part, query, 1, 1))
            grad_scores = (weights * matmul(value_part, wide, 1, 1)).astype(LOW)
            low = weights.astype(LOW)
            grad_pair = matmul(jnp.concatenate([grad_scores, low], axis=1), pair, 1, 0)
            return grad_pair, matmul(grad_scores, key_part, 0, 0)

        def step(index, total):
            part = pl.ds(pl.multiple_of(index * chunk, chunk), chunk)
            grad_pair, grad_query = attend(keys[part, :], values[part, :], own_wide, own_pair)
            acc[part, :] += grad_pair
            return total + grad_query

        def text_step(index, total):
            part = pl.ds(pl.multiple_of(index * text_chunk, text_chunk), text_chunk)
            grad_pair, grad_query = attend(
                text_keys[part, :], text_values[part, :], cross_wide, cross_pair
            )
            text_acc[part, :] += grad_pair
            return total + grad_query

        blank = jnp.zeros((rows, 128), FLOAT)
        total = lax.fori_loop(0, keys.shape[0] // chunk, step, blank, unroll=2)
        total = lax.fori_loop(0, text_keys.shape[0] // text_chunk, text_step, total, unroll=True)
        total = total * 0.125
        each = rows // BACKWARD_SLOTS
        for slot in range(BACKWARD_SLOTS):
            hold[tile * BACKWARD_SLOTS + slot] = fold_low(total[each * slot : each * slot + each])
        return carry

    lax.fori_loop(0, SPLIT // BACKWARD_SLOTS, tile_step, 0)
    for index, ref in enumerate(dq_refs):
        ref[...] = hold[index]
    for values, refs in ((acc, dkv_refs), (text_acc, dt_refs)):
        size = refs[0].shape[1]
        refs[0][0] = values[:size, :].astype(LOW)
        refs[1][0] = values[size:, :].astype(LOW)


def attention_backward(pairs, queries, qf, kf, tf, gates, grads, outs, stats):
    rows = qf.shape[0]
    heads = gates.shape[0]
    half = rows // SPLIT // 2
    folded = jax.ShapeDtypeStruct((heads * half, 128), LOW)
    piece = jax.ShapeDtypeStruct((heads, kf.shape[0] // 2, 128), LOW)
    text = jax.ShapeDtypeStruct((heads, tf.shape[0] // 2, 128), LOW)
    sums = jax.ShapeDtypeStruct((heads, 8, 128), FLOAT)
    out = pl.pallas_call(
        functools.partial(backward_kernel, len(pairs), pick_tile(kf.shape[0], 512)),
        grid=(heads,),
        in_specs=attention_specs(pairs, queries, qf, kf, tf)
        + [pl.BlockSpec((half, 128), lambda i: (i, 0))] * SPLIT
        + [pl.BlockSpec((rows, 128), lambda i: (i, 0))] * 2,
        out_specs=[pl.BlockSpec((half, 128), lambda i: (i, 0))] * SPLIT
        + [
            pl.BlockSpec((1,) + value.shape[1:], lambda i: (i, 0, 0))
            for value in (piece, piece, text, text, sums)
        ],
        out_shape=[folded] * SPLIT + [piece, piece, text, text, sums],
        scratch_shapes=attention_scratch(qf, kf, tf)
        + [
            pltpu.VMEM((SPLIT, half, 128), LOW),
            pltpu.VMEM((SPLIT, half, 128), LOW),
            pltpu.VMEM(kf.shape, FLOAT),
            pltpu.VMEM(tf.shape, FLOAT),
        ],
        compiler_params=pltpu.CompilerParams(vmem_limit_bytes=60 * MIB),
        cost_estimate=SMALL,
    )(*pairs, queries, qf, kf, tf, gates, *grads, outs, stats)
    return (out[:SPLIT],) + tuple(out[SPLIT:])


def half_means(values, lanes):
    low = jnp.sum(jnp.where(lanes < 64, values, 0.0), axis=1, keepdims=True)
    high = jnp.sum(jnp.where(lanes < 64, 0.0, values), axis=1, keepdims=True)
    return jnp.where(lanes < 64, low, high) * (1.0 / 64.0)


def swap_halves(values, lanes):
    return jnp.where(
        lax.rem(lanes, 64) < 32, pltpu.roll(values, 96, 1), pltpu.roll(values, 32, 1)
    )


def placed_at(groups, head, upper):
    values = groups[head // 2]
    return values if (head % 2 == 1) == upper else turn(values)


def rope_forward_kernel(heads, far_ref, qkv_ref, cos_ref, sin_ref, gains_ref, *refs):
    outs, hold = refs[:-1], refs[-1]
    width = heads * 64
    each = heads // SPLIT
    rows = qkv_ref.shape[0]
    cosine, sine = cos_ref[...], sin_ref[...]
    lanes = lane_ids(cosine.shape)

    def turned(start, gain):
        groups = []
        for index in range(heads // 2):
            raw = qkv_ref[:, start + 128 * index : start + 128 * index + 128]
            normed = raw * lax.rsqrt(half_means(raw * raw, lanes) + EPS) * gain
            groups.append(normed * cosine + swap_halves(normed, lanes) * sine)
        return groups

    queries = turned(0, gains_ref[0:1, :])
    keys = turned(width, gains_ref[1:2, :])
    values = [
        qkv_ref[:, 2 * width + 128 * index : 2 * width + 128 * index + 128]
        for index in range(heads // 2)
    ]
    for head in range(heads):
        group, index = head // each, head % each
        slot = lax.rem(group - far_ref[0] + SPLIT, SPLIT)
        pair = jnp.where(
            lanes < 64, placed_at(keys, head, False), placed_at(values, head, True)
        )
        hold[slot, index, :rows, :] = pair.astype(LOW)
        hold[slot, index, rows:, :] = fold_low(placed_at(queries, head, False))
    size = rows * 3 // 2
    for slot in range(SPLIT):
        for index in range(each):
            outs[slot][size * index : size * index + size, :] = hold[slot, index]


def small_call(kernel, operands, shapes, scratch):
    out = pl.pallas_call(
        kernel,
        in_specs=[pl.BlockSpec(memory_space=pltpu.SMEM)]
        + [pl.BlockSpec(memory_space=pltpu.VMEM)] * (len(operands) - 1),
        out_specs=[pl.BlockSpec(memory_space=pltpu.VMEM)] * len(shapes),
        out_shape=shapes,
        scratch_shapes=scratch,
        compiler_params=pltpu.CompilerParams(vmem_limit_bytes=32 * MIB),
        cost_estimate=SMALL,
    )(*operands)
    return out


def rope_forward(far, qkv, cosine, sine, gains, heads):
    rows = qkv.shape[0] * 3 // 2
    each = heads // SPLIT
    out = small_call(
        functools.partial(rope_forward_kernel, heads),
        (far, qkv, cosine, sine, gains),
        [jax.ShapeDtypeStruct((each * rows, 128), LOW)] * SPLIT,
        [pltpu.VMEM((SPLIT, each, rows, 128), LOW)],
    )
    return list(out)


def rope_backward_kernel(heads, far_ref, *refs):
    parts, refs = refs[:SPLIT], refs[SPLIT:]
    qkv_ref, cos_ref, sin_ref, gains_ref, out_ref, sums_ref, hold = refs
    width = heads * 64
    each = heads // SPLIT
    rows = qkv_ref.shape[0]
    for slot in range(SPLIT):
        group = lax.rem(far_ref[0] + slot, SPLIT)
        size = hold.shape[2]
        for index in range(each):
            hold[group, index] = parts[slot][size * index : size * index + size, :]
    cosine, sine = cos_ref[...], sin_ref[...]
    lanes = lane_ids(cosine.shape)

    def found(kind, head):
        group, index, upper = head // each, head % each, head % 2 == 1
        if kind == 0:
            packed = hold[group, index, rows:, :]
            return unfold_high(packed) if upper else unfold_low(packed)
        values = hold[group, index, :rows, :].astype(FLOAT)
        return values if upper == (kind == 2) else turn(values)

    def joined(kind, index):
        return jnp.where(lanes < 64, found(kind, 2 * index), found(kind, 2 * index + 1))

    for kind in range(2):
        gain = gains_ref[kind : kind + 1, :]
        total = jnp.zeros((1, 128), FLOAT)
        for index in range(heads // 2):
            spot = kind * width + 128 * index
            raw = qkv_ref[:, spot : spot + 128]
            inverse = lax.rsqrt(half_means(raw * raw, lanes) + EPS)
            unit = raw * inverse
            grad = joined(kind, index)
            back = grad * cosine - swap_halves(grad, lanes) * sine
            total = total + jnp.sum(back * unit, axis=0, keepdims=True)
            scaled = back * gain
            raw_grad = inverse * (scaled - unit * half_means(scaled * unit, lanes))
            out_ref[:, spot : spot + 128] = raw_grad.astype(LOW)
        sums_ref[kind : kind + 1, :] = total
    sums_ref[2:8, :] = jnp.zeros((6, 128), FLOAT)
    for index in range(heads // 2):
        spot = 2 * width + 128 * index
        out_ref[:, spot : spot + 128] = joined(2, index).astype(LOW)


def rope_backward(far, parts, qkv, cosine, sine, gains, heads):
    each = heads // SPLIT
    return small_call(
        functools.partial(rope_backward_kernel, heads),
        (far, *parts, qkv, cosine, sine, gains),
        [jax.ShapeDtypeStruct(qkv.shape, LOW), jax.ShapeDtypeStruct((8, 128), FLOAT)],
        [pltpu.VMEM((SPLIT, each, parts[0].shape[0] // each, 128), LOW)],
    )


def join_kernel(heads, far_ref, *refs):
    parts, out_ref, hold = refs[:SPLIT], refs[SPLIT], refs[SPLIT + 1]
    each = heads // SPLIT
    half = hold.shape[2]
    for slot in range(SPLIT):
        group = lax.rem(far_ref[0] + slot, SPLIT)
        for index in range(each):
            hold[group, index] = parts[slot][half * index : half * index + half, :]
    for pair in range(heads // 2):
        low = unfold_low(hold[2 * pair // each, 2 * pair % each])
        high = unfold_high(hold[(2 * pair + 1) // each, (2 * pair + 1) % each])
        out_ref[:, 128 * pair : 128 * pair + 128] = jnp.where(
            lane_ids(low.shape) < 64, low, high
        ).astype(LOW)


def join_heads(far, parts, heads):
    each = heads // SPLIT
    half = parts[0].shape[0] // each
    return small_call(
        functools.partial(join_kernel, heads),
        (far, *parts),
        [jax.ShapeDtypeStruct((2 * half, heads * 64), LOW)],
        [pltpu.VMEM((SPLIT, each, half, 128), LOW)],
    )[0]


def split_kernel(heads, far_ref, grad_ref, *refs):
    outs, hold = refs[:-1], refs[-1]
    each = heads // SPLIT
    half = hold.shape[2]
    for head in range(heads):
        group, index = head // each, head % each
        slot = lax.rem(group - far_ref[0] + SPLIT, SPLIT)
        values = grad_ref[:, 128 * (head // 2) : 128 * (head // 2) + 128]
        hold[slot, index] = fold_high(values) if head % 2 else fold_low(values)
    for slot in range(SPLIT):
        for index in range(each):
            outs[slot][half * index : half * index + half, :] = hold[slot, index]


def split_heads(far, grads, heads):
    each = heads // SPLIT
    half = grads.shape[0] // 2
    return small_call(
        functools.partial(split_kernel, heads),
        (far, grads),
        [jax.ShapeDtypeStruct((each * half, 128), LOW)] * SPLIT,
        [pltpu.VMEM((SPLIT, each, half, 128), LOW)],
    )


def local_call(kernel, operands, shapes):
    return pl.pallas_call(
        kernel,
        out_shape=shapes,
        compiler_params=pltpu.CompilerParams(vmem_limit_bytes=40 * MIB),
        cost_estimate=SMALL,
    )(*operands)


def gather_kernel(each, *refs):
    slots, text_ref, pairs_ref, queries_ref = refs[:SPLIT], refs[SPLIT], refs[-2], refs[-1]
    size = slots[0].shape[0] // each
    rows = size * 2 // 3
    for head in range(each):
        for index, slot in enumerate(slots):
            spot = (head * SPLIT + index) * rows
            first = head * size
            pairs_ref[spot : spot + rows, :] = slot[first : first + rows, :]
            query = unfold_low(slot[first + rows : first + size, :])
            query = jnp.where(lane_ids(query.shape) < 64, query * 0.125, 0.0)
            queries_ref[spot : spot + rows, :] = query.astype(LOW)
    pairs_ref[each * SPLIT * rows :, :] = text_ref[...]


def gather_slots(slots, text, each):
    rows = slots[0].shape[0] * 2 // 3 * SPLIT
    return local_call(
        functools.partial(gather_kernel, each),
        (*slots, text),
        [
            jax.ShapeDtypeStruct((rows + text.shape[0], 128), LOW),
            jax.ShapeDtypeStruct((rows, 128), LOW),
        ],
    )


def pack_kernel(terms, *refs):
    inputs, folded, outs = refs[:terms], refs[terms : terms + SPLIT], refs[terms + SPLIT :]
    each = inputs[0].shape[0]
    size = outs[0].shape[0] // each
    rows = size * 2 // 3
    half = size - rows
    for head in range(each):
        for slot in range(SPLIT):
            total = sum(
                term[head, rows * slot : rows * slot + rows, :].astype(FLOAT) for term in inputs
            )
            spot = size * head
            outs[slot][spot : spot + rows, :] = total.astype(LOW)
            outs[slot][spot + rows : spot + size, :] = folded[slot][
                half * head : half * head + half, :
            ]


def pack_slots(terms, folded):
    return local_call(
        functools.partial(pack_kernel, len(terms)),
        (*terms, *folded),
        [jax.ShapeDtypeStruct((3 * folded[0].shape[0], 128), LOW)] * SPLIT,
    )


def text_split_kernel(far_ref, text_ref, *outs):
    size = outs[0].shape[1]
    for slot in range(SPLIT):
        group = lax.rem(far_ref[0] + slot, SPLIT)
        spot = pl.ds(pl.multiple_of(group * size, 128), size)
        outs[slot][...] = text_ref[:, spot].astype(LOW)


def text_join_kernel(far_ref, *refs):
    parts, out_ref = refs[:SPLIT], refs[SPLIT]
    size = parts[0].shape[1]
    for slot in range(SPLIT):
        group = lax.rem(far_ref[0] + slot, SPLIT)
        out_ref[:, pl.ds(pl.multiple_of(group * size, 128), size)] = parts[slot][...]


def low_means(values, lanes):
    return jnp.sum(jnp.where(lanes < 64, values, 0.0), axis=1, keepdims=True) * (1.0 / 64.0)


def text_norm_kernel(*refs):
    parts, gain_ref, raw_ref, out_ref = refs[:SPLIT], refs[SPLIT], refs[-2], refs[-1]
    rows = raw_ref.shape[0]
    raw = sum(part[...].astype(FLOAT) for part in parts)
    raw_ref[...] = raw
    for head in range(raw.shape[1] // 128):
        values = raw[:, 128 * head : 128 * head + 128]
        lanes = lane_ids(values.shape)
        normed = values * lax.rsqrt(low_means(values * values, lanes) + EPS) * gain_ref[0:1, :]
        out_ref[rows * head : rows * head + rows, :] = jnp.where(
            lanes < 64, normed, values
        ).astype(LOW)


def text_back_kernel(terms, *refs):
    inputs, refs = refs[:terms], refs[terms:]
    raw_ref, gain_ref, out_ref, sums_ref = refs
    rows = raw_ref.shape[0]
    total_gain = jnp.zeros((1, 128), FLOAT)
    for head in range(inputs[0].shape[0]):
        grad = sum(term[head, :rows, :].astype(FLOAT) for term in inputs)
        grad = grad.astype(LOW).astype(FLOAT)
        raw = raw_ref[:, 128 * head : 128 * head + 128]
        lanes = lane_ids(raw.shape)
        inverse = lax.rsqrt(low_means(raw * raw, lanes) + EPS)
        unit = raw * inverse
        total_gain = total_gain + jnp.sum(grad * unit, axis=0, keepdims=True)
        scaled = grad * gain_ref[0:1, :]
        back = inverse * (scaled - unit * low_means(scaled * unit, lanes))
        out_ref[:, 128 * head : 128 * head + 128] = jnp.where(lanes < 64, back, grad).astype(LOW)
    sums_ref[...] = jnp.broadcast_to(total_gain, sums_ref.shape)


def tie(*values):
    return lax.optimization_barrier(values)


def stacked_kernel(left_ref, own_ref, other_ref, out_ref):
    rows = own_ref.shape[1]
    out_ref[...] = (
        matmul(left_ref[:, :rows], own_ref[0], 1, 0)
        + matmul(left_ref[:, rows:], other_ref[0], 1, 0)
    ).astype(LOW)


def stacked_outer(left, own, other, tile):
    depth = left.shape[0]
    count, rows, columns = own.shape
    tiles = columns // tile
    part = pl.BlockSpec((1, rows, tile), lambda i: (i // tiles, 0, i % tiles))
    return pl.pallas_call(
        stacked_kernel,
        grid=(count * tiles,),
        in_specs=[pl.BlockSpec(left.shape, lambda i: (0, 0)), part, part],
        out_specs=pl.BlockSpec((depth, tile), lambda i: (0, i)),
        out_shape=jax.ShapeDtypeStruct((depth, count * columns), LOW),
        compiler_params=pltpu.CompilerParams(vmem_limit_bytes=40 * MIB),
        cost_estimate=SMALL,
    )(left, own, other)


def joint_kernel(count, left_ref, own_ref, other_ref, own_last_ref, other_last_ref, out_ref):
    step = pl.program_id(0)
    rows = own_ref.shape[1]

    @pl.when(step < count)
    def _():
        out_ref[...] = (
            matmul(left_ref[0, :, :rows], own_ref[0], 1, 0)
            + matmul(left_ref[0, :, rows:], other_ref[0], 1, 0)
        ).astype(LOW)

    @pl.when(step >= count)
    def _():
        out_ref[...] = (
            matmul(left_ref[0, :, :rows], own_last_ref[...], 1, 0)
            + matmul(left_ref[0, :, rows:], other_last_ref[...], 1, 0)
        ).astype(LOW)


def joint_outer(left, own, other, own_last, other_last, tile):
    depth, tokens = left.shape[1:]
    rows, columns = own.shape[1:]
    tiles = columns // tile
    count = own.shape[0] * tiles
    extra = own_last.shape[1] // tile

    def right_at(i):
        at = jnp.minimum(i, count - 1)
        return (at // tiles, 0, at % tiles)

    right = pl.BlockSpec((1, rows, tile), right_at)
    last = pl.BlockSpec((rows, tile), lambda i: (0, jnp.maximum(i - count, 0)))
    return pl.pallas_call(
        functools.partial(joint_kernel, count),
        grid=(count + extra,),
        in_specs=[
            pl.BlockSpec((1, depth, tokens), lambda i: (jnp.where(i < count, 0, 1), 0, 0)),
            right,
            right,
            last,
            last,
        ],
        out_specs=pl.BlockSpec((depth, tile), lambda i: (0, i)),
        out_shape=jax.ShapeDtypeStruct((depth, (count + extra) * tile), LOW),
        compiler_params=pltpu.CompilerParams(vmem_limit_bytes=40 * MIB),
        cost_estimate=SMALL,
    )(left, own, other, own_last, other_last)


def feed_kernel(
    normed_ref, grad_ref, gate_ref, up_ref, down_ref,
    hidden_ref, grads_ref, feed_own_ref, feed_other_ref, norm_own_ref, norm_other_ref,
    feed_acc, norm_acc,
):
    step = pl.program_id(0)

    @pl.when(step == 0)
    def _():
        feed_acc[...] = jnp.zeros_like(feed_acc)
        norm_acc[...] = jnp.zeros_like(norm_acc)

    normed = normed_ref[...]
    gate = matmul(normed, gate_ref[...], 1, 0)
    up = matmul(normed, up_ref[...], 1, 0)
    grad_hidden = matmul(grad_ref[...], down_ref[...], 1, 0)
    sigmoid = 1.0 / (1.0 + jnp.exp(-gate))
    silu = gate * sigmoid
    hidden = (silu * up).astype(LOW)
    grad_gate = (grad_hidden * up * sigmoid * (1.0 + gate * (1.0 - sigmoid))).astype(LOW)
    grad_up = (grad_hidden * silu).astype(LOW)
    hidden_ref[0] = hidden
    grads_ref[0] = grad_gate
    grads_ref[1] = grad_up
    feed_acc[...] += matmul(hidden, down_ref[...], 1, 1)
    norm_acc[...] += matmul(grad_gate, gate_ref[...], 1, 1) + matmul(grad_up, up_ref[...], 1, 1)

    @pl.when(step == pl.num_programs(0) - 1)
    def _():
        half = feed_own_ref.shape[0]
        feed_own_ref[...] = feed_acc[:half, :]
        feed_other_ref[...] = feed_acc[half:, :].astype(LOW)
        norm_own_ref[...] = norm_acc[:half, :]
        norm_other_ref[...] = norm_acc[half:, :].astype(LOW)


def feed_forward(normed, grads, weights, tile):
    rows, width = normed.shape
    columns = weights.shape[1] // 3
    tiles = columns // tile
    own = jax.ShapeDtypeStruct((rows // 2, width), FLOAT)
    other = jax.ShapeDtypeStruct((rows // 2, width), LOW)
    return pl.pallas_call(
        feed_kernel,
        grid=(tiles,),
        in_specs=[whole(normed.shape), whole(grads.shape)]
        + [
            pl.BlockSpec((width, tile), lambda i, part=part: (0, part * tiles + i))
            for part in range(3)
        ],
        out_specs=[
            pl.BlockSpec((1, rows, tile), lambda i: (0, 0, i)),
            pl.BlockSpec((2, rows, tile), lambda i: (0, 0, i)),
        ]
        + [whole(own.shape)] * 4,
        out_shape=[
            jax.ShapeDtypeStruct((1, rows, columns), LOW),
            jax.ShapeDtypeStruct((2, rows, columns), LOW),
            own,
            other,
            own,
            other,
        ],
        scratch_shapes=[pltpu.VMEM((rows, width), FLOAT)] * 2,
        compiler_params=pltpu.CompilerParams(vmem_limit_bytes=48 * MIB),
        cost_estimate=SMALL,
    )(normed, grads, weights, weights, weights)


def dot_float(left, right):
    return jnp.dot(left, right, preferred_element_type=FLOAT)


def dot_turned(left, right):
    return matmul(left, right, 1, 1)


def norm_rows(values, gains):
    return values * lax.rsqrt(jnp.mean(values * values, axis=-1, keepdims=True) + EPS) * gains


def modulated(values, gains, shifts, scales):
    return norm_rows(values, gains) * (1.0 + scales) + shifts


def swapped(values):
    return lax.ppermute(values, "tensor", [(0, 1), (1, 0)])


def both_rows(values):
    return jnp.concatenate([values, swapped(values)], axis=0)


def own_rows(partial):
    rows = partial.shape[0] // 2
    return partial[:rows] + swapped(partial[rows:].astype(LOW)).astype(FLOAT)


def shards(
    inputs,
    clip_ids,
    positions,
    text_tokens,
    conditioning,
    ada_weight,
    ada_bias,
    first_norm_gain,
    query_gain,
    key_gain,
    text_key_gain,
    head_gate,
    qkv_weight,
    out_weight,
    text_kv_weight,
    second_norm_gain,
    gate_up_weight,
    down_weight,
    grad_output,
):
    dp = lax.axis_size("dp")
    near = dp // SPLIT
    bits = [near >> (step + 1) for step in range(near.bit_length() - 1)]
    tensor_index = lax.axis_index("tensor")
    dp_index = lax.axis_index("dp")
    far_index, near_index = dp_index // near, dp_index % near
    row_count, width = inputs.shape
    token_count = clip_ids.shape[0]
    head_size = query_gain.shape[0]
    local_width = qkv_weight.shape[2]
    heads = local_width // head_size
    each = heads // SPLIT
    part_width = each * head_size
    clip_count = conditioning.shape[0]
    hidden_count = gate_up_weight.shape[2]
    weight_rows = qkv_weight.shape[1]

    def flip(values, bit):
        return lax.ppermute(values, "dp", [(j, j ^ bit) for j in range(dp)])

    def shift(values, steps):
        pairs = [(j, ((j // near + steps) % SPLIT) * near + j % near) for j in range(dp)]
        return lax.ppermute(values, "dp", pairs)

    def sum_dp(values):
        step = 1
        while step < dp:
            values = values + flip(values, step)
            step *= 2
        return values

    def spread(values):
        for bit in bits:
            values = jnp.concatenate([values, flip(values, bit)], axis=0)
        return values

    def spread_list(values):
        values = [values]
        for bit in bits:
            values = values + [flip(value, bit) for value in values]
        return values

    def collect(values):
        for bit in reversed(bits):
            half = values.shape[0] // 2
            values = values[:half].astype(FLOAT) + flip(
                values[half:].astype(LOW), bit
            ).astype(FLOAT)
        return values

    def pick(stacked, index):
        return lax.dynamic_index_in_dim(stacked, index, 0, keepdims=False)

    def send_parts(stacked):
        out = [pick(stacked, far_index)]
        for steps in range(1, SPLIT):
            out.append(shift(pick(stacked, (far_index + steps) % SPLIT), steps))
        return out

    def send_slots(slots):
        return [slots[0]] + [shift(slots[steps], steps) for steps in range(1, SPLIT)]

    def return_slots(slots):
        return [slots[0]] + [shift(slots[steps], -steps) for steps in range(1, SPLIT)]

    flips = []
    for order in range(near):
        mask = 0
        for place, bit in enumerate(bits):
            if order >> place & 1:
                mask |= bit
        flips.append(mask)

    core = dp_index % 2
    core_groups = [list(range(first, dp, 2)) for first in range(2)]

    def core_columns(values):
        halves = (
            values.T.reshape(dp // 2, 2, weight_rows, token_count)
            .transpose(1, 0, 2, 3)
            .reshape(2, width // 2, token_count)
        )
        return jnp.concatenate([pick(halves, core), flip(pick(halves, 1 - core), 1)], axis=1)

    def scatter(values):
        return lax.psum_scatter(
            values, "dp", scatter_dimension=0, axis_index_groups=core_groups, tiled=True
        )

    attn_full = lax.all_gather(
        jnp.concatenate(
            [
                qkv_weight.transpose(1, 0, 2).reshape(weight_rows, 3 * local_width),
                out_weight.T,
            ],
            axis=1,
        ),
        "dp",
        axis=0,
        tiled=True,
    )
    cond_float = conditioning.astype(FLOAT)
    silu_cond = jax.nn.silu(cond_float).astype(LOW)
    cond_rows = ada_weight.shape[0]
    silu_slice = lax.dynamic_slice_in_dim(silu_cond, dp_index * cond_rows, cond_rows, axis=1)
    first_rows = jnp.sum((clip_ids == 0).astype(FLOAT))
    spots = jnp.arange(ada_weight.shape[1], dtype=jnp.int32)
    early = 2 * width
    early_part = jnp.concatenate(
        [
            dot_float(silu_slice, ada_weight[:, :early]),
            jnp.where(spots[:early] == dp_index, first_rows, 0.0)[None],
        ],
        axis=0,
    )
    early_sum = sum_dp(early_part)
    bias = ada_bias.astype(FLOAT)
    early_mod = early_sum[:clip_count] + bias[:early]
    counts = early_sum[clip_count, :dp].astype(jnp.int32)

    own_ids = lax.dynamic_slice_in_dim(clip_ids, tensor_index * row_count, row_count)
    row_positions = jnp.where(
        tensor_index == 0, positions, jnp.roll(positions, row_count)
    )
    other_clip = jnp.max(clip_ids)
    first_clip = (own_ids == 0)[:, None]

    def mod_blocks(modulation):
        rows = jnp.where(
            first_clip,
            modulation[0:1],
            lax.dynamic_slice_in_dim(modulation, other_clip, 1, 0),
        )
        return jnp.split(rows, rows.shape[1] // width, axis=1)

    shift_one, scale_one = mod_blocks(early_mod)
    input_rows = inputs.astype(FLOAT)
    first_gain = first_norm_gain.astype(FLOAT)
    normed_one = modulated(input_rows, first_gain, shift_one, scale_one).astype(LOW)
    normed_all = both_rows(normed_one)
    late_sum = sum_dp(dot_float(silu_slice, ada_weight[:, early:]))

    half_size = head_size // 2
    frequency = 10000.0 ** (-(jnp.arange(half_size, dtype=FLOAT) * 2.0 / head_size))
    angles = row_positions.astype(FLOAT)[:, None] * frequency[None, :]
    cosine = jnp.cos(angles)
    sine = jnp.sin(angles)
    cosine = jnp.concatenate([cosine] * 4, axis=1)
    sine = jnp.concatenate([-sine, sine, -sine, sine], axis=1)
    gains = jnp.stack([jnp.tile(query_gain, 2), jnp.tile(key_gain, 2)]).astype(FLOAT)
    gains = jnp.concatenate([gains, jnp.zeros((6, 128), FLOAT)], axis=0)

    text_rows = text_tokens.shape[0]
    group_rows = text_rows * SPLIT
    text_tokens, late_sum = tie(text_tokens, late_sum)
    text_columns = lax.all_to_all(text_tokens, "dp", split_axis=1, concat_axis=0, tiled=True)
    text_groups = text_columns.reshape(near, group_rows, text_columns.shape[1])
    text_near = jnp.concatenate([pick(text_groups, near_index ^ mask) for mask in flips], axis=0)
    text_weight = (
        text_kv_weight.reshape(2, -1, SPLIT, each, head_size)
        .transpose(1, 2, 3, 0, 4)
        .reshape(-1, 2 * local_width)
    )
    far = far_index.astype(jnp.int32).reshape(1)
    text_sum = collect(dot_float(text_near, text_weight))
    part_shape = jax.ShapeDtypeStruct((group_rows, 2 * part_width), LOW)
    text_parts = small_call(text_split_kernel, (far, text_sum), [part_shape] * SPLIT, [])
    ky_gain = jnp.concatenate([text_key_gain.astype(FLOAT), jnp.zeros((128 - head_size,), FLOAT)])
    ky_gain = jnp.broadcast_to(ky_gain[None], (8, 128))

    lanes = jnp.arange(128, dtype=jnp.int32)[None, :]
    text_groups_at = jnp.stack([near_index ^ mask for mask in flips])
    text_clip = (
        text_groups_at[:, None] * group_rows + jnp.arange(group_rows, dtype=jnp.int32)[None, :]
    ).reshape(-1) // TXT
    text_features = (lanes == 64 + text_clip[:, None]).astype(LOW)
    block_at = jnp.stack(
        [
            ((far_index - steps) % SPLIT) * near + (near_index ^ mask)
            for mask in flips
            for steps in range(SPLIT)
        ]
    )
    block_count = jnp.sum(
        jnp.where(block_at[:, None] == jnp.arange(dp, dtype=jnp.int32)[None, :], counts[None, :], 0),
        axis=1,
    )
    row_at = (jnp.arange(token_count, dtype=jnp.int32) + tensor_index * row_count) % token_count
    key_clip = jnp.where(
        row_at[None, :] < block_count[:, None], 0, 1 + block_at[:, None] // GROUP
    ).reshape(-1)
    key_features = (lanes == 64 + key_clip[:, None]).astype(LOW)
    group_tokens = SPLIT * token_count
    query_clip = key_clip[:group_tokens, None]
    query_features = jnp.where(
        (lanes >= 64) & (lanes < 64 + clip_count) & (lanes != 64 + query_clip), MASK, 0.0
    ).astype(LOW)
    gate_heads = jnp.tanh(
        lax.dynamic_slice_in_dim(
            head_gate.astype(FLOAT), tensor_index * heads + far_index * each, each
        )
    )
    gate_lanes = jnp.broadcast_to(gate_heads[:, None, None], (each, 8, 128))

    qkv_full, normed_all, text_parts, key_features, query_features = tie(
        attn_full[:, : 3 * local_width], normed_all, text_parts, key_features, query_features
    )
    out_full = attn_full[:, 3 * local_width :]
    text_arrived = send_slots(text_parts)
    qkv_raw = dot_float(normed_all, qkv_full)
    head_slots = rope_forward(far, qkv_raw, cosine, sine, gains, heads)
    gate_one, shift_two, scale_two, gate_two = mod_blocks(late_sum + bias[early:])
    grad_two = grad_output.astype(FLOAT)
    grad_ffn = both_rows((gate_two * grad_two).astype(LOW))
    head_slots, text_arrived = tie(head_slots, text_arrived)
    text_raw, text_pairs = local_call(
        text_norm_kernel,
        (*text_arrived, ky_gain),
        [
            jax.ShapeDtypeStruct((group_rows, 2 * part_width), FLOAT),
            jax.ShapeDtypeStruct((each * group_rows, 128), LOW),
        ],
    )
    arrived = send_slots(head_slots)
    own_pairs, queries = gather_slots(arrived, text_pairs, each)
    pairs = spread_list(own_pairs)
    feed_weights, pairs, grad_ffn = tie(
        jnp.concatenate([gate_up_weight[0], gate_up_weight[1], down_weight.T], axis=1),
        pairs,
        grad_ffn,
    )
    feed_full = lax.all_gather(feed_weights, "dp", axis=0, tiled=True)
    mixed_slots, head_outs, head_stats = attention_forward(
        pairs, queries, query_features, key_features, text_features, gate_lanes
    )
    mixed = join_heads(far, return_slots(mixed_slots), heads)
    attn_rows = own_rows(dot_turned(mixed, out_full))
    after_attn = input_rows + gate_one * attn_rows
    second_gain = second_norm_gain.astype(FLOAT)
    normed_two_all = both_rows(modulated(after_attn, second_gain, shift_two, scale_two).astype(LOW))
    hidden_low, feed_grads, feed_own, feed_other, norm_own, norm_other = feed_forward(
        normed_two_all, grad_ffn, feed_full, 512
    )
    down_grads = stacked_outer(core_columns(grad_ffn), hidden_low, flip(hidden_low, 1), 512)
    down_low = scatter(down_grads)
    grad_normed_two = norm_own + swapped(norm_other).astype(FLOAT)
    grad_normed_two, feed_other = tie(grad_normed_two, feed_other)
    ffn_rows = feed_own + swapped(feed_other).astype(FLOAT)
    output = (after_attn + gate_two * ffn_rows).astype(LOW)
    grad_gate_two = grad_two * ffn_rows
    _, pull_two = jax.vjp(modulated, after_attn, second_gain, shift_two, scale_two)
    back_two, grad_second_gain, grad_shift_two, grad_scale_two = pull_two(grad_normed_two)
    grad_after = grad_two + back_two
    grad_attn = both_rows((gate_one * grad_after).astype(LOW))
    grad_gate_one = grad_after * attn_rows
    grad_slots = send_slots(split_heads(far, dot_float(grad_attn, out_full), heads))
    joint_grads = joint_outer(
        jnp.stack([core_columns(normed_two_all), core_columns(grad_attn)]),
        feed_grads,
        flip(feed_grads, 1),
        mixed,
        flip(mixed, 1),
        256,
    )
    grad_slots, joint_grads, down_low = tie(grad_slots, joint_grads, down_low)
    joint_low = scatter(joint_grads)

    def total_rows(terms, first, last):
        return sum(term[:, first:last].astype(FLOAT) for term in terms).astype(LOW)

    def start_sums(keep, send, text_keep, text_send):
        return (
            [keep, flip(send, bits[-1])],
            [text_keep, flip(text_send, bits[-1])],
        )

    def next_send(state):
        terms, text_terms = state
        size, text_size = terms[-1].shape[1], text_terms[-1].shape[1]
        return jnp.concatenate(
            [
                total_rows(terms, size // 2, size),
                total_rows(text_terms, text_size // 2, text_size),
            ],
            axis=1,
        )

    def next_state(state, sent, bit):
        terms, text_terms = state
        size = terms[-1].shape[1] // 2
        other = flip(sent, bit)
        return terms + [other[:, :size]], text_terms + [other[:, size:]]

    folded, *pieces, gate_parts = attention_backward(
        pairs,
        queries,
        query_features,
        key_features,
        text_features,
        gate_lanes,
        grad_slots,
        head_outs,
        head_stats,
    )
    state = start_sums(*pieces)
    for bit in reversed(bits[:-1]):
        state = next_state(state, next_send(state), bit)
    pair_terms, text_terms = state
    back_slots = pack_slots(pair_terms, folded)
    clip_at = jnp.arange(clip_count, dtype=jnp.int32)[:, None]

    def clip_sums(values):
        first_sum = jnp.sum(jnp.where(first_clip, values, 0.0), axis=0)[None]
        other_sum = jnp.sum(jnp.where(first_clip, 0.0, values), axis=0)[None]
        return jnp.where(clip_at == 0, first_sum, jnp.where(clip_at == other_clip, other_sum, 0.0))

    def pair_sums(blocks, gains_row):
        wide = jnp.concatenate([clip_sums(values) for values in blocks], axis=1)
        gains_row = jnp.concatenate(
            [gains_row, jnp.zeros((wide.shape[1] - gains_row.shape[0],), FLOAT)]
        )
        wide = jnp.concatenate([wide, gains_row[None]], axis=0)
        return wide + swapped(wide)

    back_parts = return_slots(back_slots)
    text_low, ky_sums = local_call(
        functools.partial(text_back_kernel, len(text_terms)),
        (*text_terms, text_raw, ky_gain),
        [part_shape, jax.ShapeDtypeStruct((8, 128), FLOAT)],
    )
    back_parts, text_low = tie(back_parts, text_low)
    qkv_grad, gain_sums = rope_backward(far, back_parts, qkv_raw, cosine, sine, gains, heads)
    grad_normed_one = own_rows(dot_turned(qkv_grad, qkv_full))
    qkv_right = qkv_grad[None]
    qkv_grads = stacked_outer(
        core_columns(normed_all), qkv_right, flip(qkv_right, 1), local_width
    )
    qkv_grads, joint_low, grad_normed_one, text_low = tie(
        qkv_grads, joint_low, grad_normed_one, text_low
    )
    qkv_low = scatter(qkv_grads)
    _, pull_one = jax.vjp(modulated, input_rows, first_gain, shift_one, scale_one)
    back_one, grad_first_gain, grad_shift_one, grad_scale_one = pull_one(grad_normed_one)
    grad_inputs = grad_after + back_one
    head_sums = (1.0 - gate_heads * gate_heads) * jnp.sum(gate_parts, axis=(1, 2))
    head_row = lax.dynamic_update_slice_in_dim(
        jnp.zeros((head_gate.shape[0],), FLOAT),
        head_sums,
        tensor_index * heads + far_index * each,
        0,
    )
    gain_halves = gain_sums[:2, :head_size] + gain_sums[:2, head_size:]
    all_pairs = pair_sums(
        (
            grad_shift_one,
            grad_scale_one,
            grad_gate_one,
            grad_shift_two,
            grad_scale_two,
            grad_gate_two,
        ),
        jnp.concatenate(
            [
                grad_first_gain,
                grad_second_gain,
                gain_halves.reshape(-1),
                ky_sums[0, :head_size],
                head_row,
            ]
        ),
    )
    text_wide = small_call(
        text_join_kernel,
        (far, *return_slots([text_low] * SPLIT)),
        [jax.ShapeDtypeStruct((group_rows, 2 * local_width), LOW)],
        [],
    )[0]
    grad_sums = sum_dp(all_pairs)
    grad_mod_low, sums = grad_sums[:clip_count].astype(LOW), grad_sums[clip_count]
    first_gain_sum = sums[:width]
    second_gain_sum = sums[width : 2 * width]
    at = 2 * width
    q_gain_sum = sums[at : at + head_size]
    k_gain_sum = sums[at + head_size : at + 2 * head_size]
    ky_gain_sum = sums[at + 2 * head_size : at + 3 * head_size]
    gate_sum = sums[at + 3 * head_size : at + 3 * head_size + head_gate.shape[0]]
    text_all = spread(text_wide)
    grad_text_kv = (
        matmul(text_near, text_all, 0, 0)
        .reshape(-1, SPLIT, each, 2, head_size)
        .transpose(3, 0, 1, 2, 4)
        .reshape(2, -1, local_width)
    )
    grad_text_part = dot_turned(text_all, text_weight).astype(LOW)
    grad_text_pair = grad_text_part.astype(FLOAT) + swapped(grad_text_part).astype(FLOAT)
    grad_text_groups = grad_text_pair.astype(LOW).reshape(near, group_rows, -1)
    orders = jnp.arange(near, dtype=jnp.int32)
    flip_at = jnp.array(flips, jnp.int32)
    grad_text_rows = jnp.concatenate(
        [
            pick(grad_text_groups, jnp.sum(jnp.where(flip_at == near_index ^ group, orders, 0)))
            for group in range(near)
        ],
        axis=0,
    )
    grad_text_all = lax.all_to_all(grad_text_rows, "dp", split_axis=0, concat_axis=1, tiled=True)
    half_text = text_tokens.shape[1] // 2
    grad_text = lax.dynamic_slice_in_dim(
        grad_text_all, tensor_index * half_text, half_text, 1
    ).astype(FLOAT)
    grad_ada_bias = jnp.sum(grad_mod_low.astype(FLOAT), axis=0)
    grad_ada = matmul(silu_slice, grad_mod_low, 0, 0)
    cond_part = lax.dynamic_update_slice_in_dim(
        jnp.zeros(cond_float.shape, FLOAT),
        dot_turned(grad_mod_low, ada_weight),
        dp_index * cond_rows,
        1,
    )
    cond_sigmoid = jax.nn.sigmoid(cond_float)
    grad_conditioning = (
        sum_dp(cond_part) * cond_sigmoid * (1.0 + cond_float * (1.0 - cond_sigmoid))
    )
    qkv_shard = qkv_low.astype(FLOAT).reshape(weight_rows, 3, local_width).transpose(1, 0, 2)
    joint_shard = joint_low.astype(FLOAT)
    gate_up_shard = jnp.stack(
        [joint_shard[:, :hidden_count], joint_shard[:, hidden_count : 2 * hidden_count]]
    )
    out_shard = joint_shard[:, 2 * hidden_count :]
    down_shard = down_low.astype(FLOAT)
    return (
        output,
        grad_inputs,
        grad_text,
        grad_conditioning,
        grad_ada,
        grad_ada_bias,
        first_gain_sum,
        q_gain_sum,
        k_gain_sum,
        ky_gain_sum,
        gate_sum,
        qkv_shard,
        out_shard.T,
        grad_text_kv,
        second_gain_sum,
        gate_up_shard,
        down_shard.T,
    )


def solution(mesh):
    placed = (
        P(("dp", "tensor"), None),
        P("dp"),
        P("dp"),
        P("dp", None),
        P(),
        P("dp", None),
        P(),
        P(),
        P(),
        P(),
        P(),
        P(),
        P(None, "dp", "tensor"),
        P("tensor", "dp"),
        P(None, "dp", "tensor"),
        P(),
        P(None, "dp", "tensor"),
        P("tensor", "dp"),
        P(("dp", "tensor"), None),
    )
    return jax.shard_map(
        shards,
        mesh=mesh,
        in_specs=placed,
        out_specs=(
            P(("dp", "tensor"), None),
            P(("dp", "tensor"), None),
            P("dp", "tensor"),
            P(),
            P("dp", None),
            P(),
            P(),
            P(),
            P(),
            P(),
            P(),
            P(None, "dp", "tensor"),
            P("tensor", "dp"),
            P(None, "dp", "tensor"),
            P(),
            P(None, "dp", "tensor"),
            P("tensor", "dp"),
        ),
        check_vma=False,
    )
```

time: 827 us -> 712 us (0.86)
  local copies, waits for them, and re-layouts: 111 us -> 59.1 us
  waiting for transfers between devices: 262 us -> 312 us
  starting transfers between devices: 143 us -> 94.1 us
  matrix products: 51.3 us -> 21.4 us
  other arithmetic: 83.2 us -> 57.8 us
  Pallas kernels: 140 us -> 131 us
    all_gather x1, waiting for transfers between devices: 0.01 us -> 33.5 us  [shards(): feed_full = lax.all_gather(feed_weights, 'dp', axis=0, tiled=True)]
    ppermute x24 -> x18, starting transfers between devices: 60.7 us -> 30 us  [shift(): return lax.ppermute(values, 'dp', pairs)]
    ppermute x24 -> x18, waiting for transfers between devices: 107 us -> 78 us  [shift(): return lax.ppermute(values, 'dp', pairs)]
    ppermute x44 -> x34, waiting for transfers between devices: 93.7 us -> 122 us  [flip(): return lax.ppermute(values, 'dp', [(j, j ^ bit) for j in range(dp)])]
    ppermute x44 -> x34, starting transfers between devices: 56.3 us -> 29.8 us  [flip(): return lax.ppermute(values, 'dp', [(j, j ^ bit) for j in range(dp)])]
    dot_general x7 -> x5, matrix products: 22.3 us -> 6.54 us  [dot_float(): return jnp.dot(left, right, preferred_element_type=FLOAT)]
    transpose x4 -> x12, local copies, waits for them, and re-layouts: 0.26 us -> 15.4 us  [the longest x4 8.05 us: core_columns(): values.T.reshape(dp // 2, 2, weight_rows, token_count).transpose(1, 0, 2, 3)]
    dot_general x8 -> x6, matrix products: 29 us -> 14.9 us  [matmul(): lax.dot_general(left, right, (((left_dim,), (right_dim,)), ((), ())), pre...]
  transfers between devices with their start and end apart: 86 -> 69, of which waited for: 43 -> 34; matrix products, arithmetic and copies ran while one was open for 26% -> 15% of each run, Pallas kernels for 17% -> 16%
where the time goes in v3:
time: 712 us; the launch traced here: 701 us
  waiting for transfers between devices  312 us (44%)
  Pallas kernels  131 us (18%)
  starting transfers between devices  94.1 us (13%)
  local copies, waits for them, and re-layouts  59.1 us (8%)
  other arithmetic  57.8 us (8%)
  between operations  25.5 us (4%)
  matrix products  21.4 us (3%)
    ppermute x34, waiting for transfers between devices, flip(): return lax.ppermute(values, 'dp', [(j, j ^ bit) for j in range(dp)])  122 us
    ppermute x18, waiting for transfers between devices, shift(): return lax.ppermute(values, 'dp', pairs)  78 us
    ppermute x10, waiting for transfers between devices, swapped(): return lax.ppermute(values, 'tensor', [(0, 1), (1, 0)])  55.1 us
    pallas_call x1, Pallas kernels, attention_backward(): pl.pallas_call(functools.partial(backward_kernel, len(pairs), pick_tile(k...  53.6 us
    all_gather x1, waiting for transfers between devices, shards(): feed_full = lax.all_gather(feed_weights, 'dp', axis=0, tiled=True)  33.5 us
    ppermute x18, starting transfers between devices, shift(): return lax.ppermute(values, 'dp', pairs)  30 us
    ppermute x34, starting transfers between devices, flip(): return lax.ppermute(values, 'dp', [(j, j ^ bit) for j in range(dp)])  29.8 us
    unnamed x245, local copies, waits for them, and re-layouts  29.3 us
  transfers between devices with their start and end apart: 69, of which 34 were waited for; matrix products, arithmetic and copies ran while one was open for 15% of the time, Pallas kernels for 16%

profile of v3, /device:TPU:0, one launch (start us, length us, event | category | flops | bytes accessed | tf_op | source)
XLA Modules:
  0.0 701.2 jit_solution(6268763250158945754)
XLA Ops:
  17.5 3.0 collective-permute-start.5
  36.9 3.2 collective-permute-start.2
  41.0 6.5 collective-permute-done.2
  47.7 6.0 collective-permute-done.3
  54.5 4.7 all-to-all-start
  62.6 15.4 %all-to-all-done = bf16[48,16,256]{2,0,1:T(8,128)(2,1)S(1)} async-done(((bf16[48,16,256]{2,0,1:T(8,128)(2,1)}), bf16[48,16,256]{2,0,1:T(8,128)(2,1)S(1)}, u32[]{:S(2)}, u32[]{:S(2)}) %all-to-all-start) | async-done | bytes 393248 | tf_op jit(solution)/shard_map/all_to_all | solution.py:960
  80.6 2.7 fusion.refs_6_
  83.7 2.3 collective-permute-start.10
  87.8 12.1 %collective-permute-done.10 = bf16[192,1536]{1,0:T(8,128)(2,1)S(1)} collective-permute-done((bf16[192,1536]{1,0:T(8,128)(2,1)S(1)}, bf16[192,1536]{1,0:T(8,128)(2,1)S(1)}, u32[]{:S(2)}, u32[]{:S(2)}) %collective-permute-start.10) | collective-permute-done | bytes 589856 | tf_op jit(solution)/shard_map/ppermute | solution.py:823
  100.1 5.1 all-gather.3.cloned.1.call-done
  105.2 3.5 slice.213
  114.7 3.3 shard_map.324
  118.1 4.8 collective-permute-done.12.refs_2_
  122.9 3.3 collective-permute-start.14
  129.6 5.4 collective-permute-done.14.refs_1_
  135.0 10.4 %collective-permute-done.15.refs_2_ = bf16[1152,128]{1,0:T(8,128)(2,1)S(1)} collective-permute-done((bf16[1152,128]{1,0:T(8,128)(2,1)S(1)}, bf16[1152,128]{1,0:T(8,128)(2,1)S(1)}, u32[]{:S(2)}, u32[]{:S(2)}) %collective-permute-start.15) | collective-permute-done | bytes 294944 | tf_op jit(solution)/shard_map/ppermute | solution.py:827
  152.2 17.1 %collective-permute-done.17.refs_1_ = bf16[3648,128]{1,0:T(8,128)(2,1)} collective-permute-done((bf16[3648,128]{1,0:T(8,128)(2,1)}, bf16[3648,128]{1,0:T(8,128)(2,1)}, u32[]{:S(2)}, u32[]{:S(2)}) %collective-permute-start.17) | collective-permute-done | bytes 933920 | tf_op jit(solution)/shard_map/ppermute | solution.py:823
  174.8 26.0 %shard_map.327 = (bf16[384,128]{1,0:T(8,128)(2,1)}, bf16[384,128]{1,0:T(8,128)(2,1)}, bf16[384,128]{1,0:T(8,128)(2,1)}, bf16[384,128]{1,0:T(8,128)(2,1)}, f32[3072,128]{1,0:T(8,128)}, /*index=5*/f32[3072,128]{1,0:T(8,128)}) custom-call(bf16[3648,128]{1,0:T(8,128)(2,1)} %get-tuple-element.129.refs_0_, bf16[3648,128]{1,0:T(8,128)(2,1)} %collective-permute-done.17.refs_1_, ...), custom_call_target="tpu_custom_call" | custom-call | flops 1024 | bytes 1024 | tf_op jit(solution)/shard_map/pallas_call | solution.py:169
  200.8 7.7 %collective-permute-start.21 = (bf16[384,128]{1,0:T(8,128)(2,1)}, bf16[384,128]{1,0:T(8,128)(2,1)S(1)}, u32[]{:S(2)}, u32[]{:S(2)}) collective-permute-start(bf16[384,128]{1,0:T(8,128)(2,1)} %get-tuple-element.137), channel_id=1, source_target_pairs={{0,24},{2,26},{4,28},{6,30},{8,0},{10,2},{12,4},{14,6},{16,8},{18,... | collective-permute-start | bytes 294920 | tf_op jit(solution)/shard_map/ppermute | solution.py:827
  209.2 4.9 collective-permute-done.21.refs_1_
  214.1 9.2 %collective-permute-done.22.refs_2_ = bf16[384,128]{1,0:T(8,128)(2,1)S(1)} collective-permute-done((bf16[384,128]{1,0:T(8,128)(2,1)}, bf16[384,128]{1,0:T(8,128)(2,1)S(1)}, u32[]{:S(2)}, u32[]{:S(2)}) %collective-permute-start.22) | collective-permute-done | bytes 98336 | tf_op jit(solution)/shard_map/ppermute | solution.py:827
  224.4 2.8 fusion.3
  228.8 8.6 %collective-permute-done.24 = bf16[128,1536]{1,0:T(8,128)(2,1)S(1)} collective-permute-done((bf16[128,1536]{1,0:T(8,128)(2,1)S(1)}, bf16[128,1536]{1,0:T(8,128)(2,1)S(1)}, u32[]{:S(2)}, u32[]{:S(2)}) %collective-permute-start.24) | collective-permute-done | bytes 393248 | tf_op jit(solution)/shard_map/ppermute | solution.py:772
  240.5 7.8 %collective-permute-done.25 = bf16[128,1536]{1,0:T(8,128)(2,1)S(1)} collective-permute-done((bf16[128,1536]{1,0:T(8,128)(2,1)S(1)}, bf16[128,1536]{1,0:T(8,128)(2,1)S(1)}, u32[]{:S(2)}, u32[]{:S(2)}) %collective-permute-start.25) | collective-permute-done | bytes 393248 | tf_op jit(solution)/shard_map/ppermute | solution.py:772
  249.5 33.5 %all-gather.5.cloned.1.call-done.gate_ref.up_ref.down_ref = bf16[1536,6144]{1,0:T(8,128)(2,1)} async-done(((bf16[96,6144]{1,0:T(8,128)(2,1)}), bf16[1536,6144]{1,0:T(8,128)(2,1)}) %all-gather.5.cloned.1.call-update) | async-done | bytes 18874384 | tf_op jit(solution)/shard_map/all_gather | solution.py:1036
  284.2 14.7 %shard_map.329 = (bf16[1,256,2048]{2,1,0:T(8,128)(2,1)}, bf16[2,256,2048]{2,1,0:T(8,128)(2,1)}, f32[128,1536]{1,0:T(8,128)S(1)}, bf16[128,1536]{1,0:T(8,128)(2,1...) custom-call(bf16[256,1536]{1,0:T(8,128)(2,1)S(1)} %copy-done.4, ...), custom_call_target="tpu_custom_call" | custom-call | flops 1024 | bytes 1024 | tf_op jit(solution)/shard_map/pallas_call | solution.py:728
  306.7 5.1 shard_map.332
  311.9 10.7 %reduce-scatter.6.cloned.1.call-start = ((), (), s32[]{:S(2)}) async-start(), calls=%async_computation.8 | async-start | bytes 8404992 | tf_op jit(solution)/shard_map/reduce_scatter | solution.py:890
  324.1 10.0 %collective-permute-done.26 = bf16[128,1536]{1,0:T(8,128)(2,1)S(1)} collective-permute-done((bf16[128,1536]{1,0:T(8,128)(2,1)}, bf16[128,1536]{1,0:T(8,128)(2,1)S(1)}, u32[]{:S(2)}, u32[]{:S(2)}) %collective-permute-start.26) | collective-permute-done | bytes 393248 | tf_op jit(solution)/shard_map/ppermute | solution.py:772
  335.8 3.0 select_reduce_fusion.3
  338.8 6.1 collective-permute-done.27
  345.0 3.0 multiply_convert_fusion
  349.3 2.3 copy.112
  354.3 3.7 collective-permute-done.29
  360.1 2.3 copy.114
  363.7 2.7 fusion.1.grad_ref
  368.4 3.5 collective-permute-start.30
  372.0 2.7 collective-permute-start.32
  376.3 13.4 %shard_map.331 = bf16[768,4864]{1,0:T(8,128)(2,1)S(1)} custom-call(bf16[2,768,512]{2,1,0:T(8,128)(2,1)S(1)} %pad_maximum_fusion.1.left_ref, bf16[2,256,2048]{2,1,0:T(8,128)(2,1)S(1)} %copy-done.9, bf16[2,256,2048]{2,1,0:T(8,128)(2,1)} %collective-permute-done.35.other_ref, bf16[256,768]{1,0:T(8,128)(2,1)S(1)} %shard_map.328.own_last_ref, ...), custom_call_target="tpu_custom_call" | custom-call | flops 1024 | bytes 1024 | tf_op jit(solution)/shard_map/pallas_call | solution.py:669
  389.7 3.1 copy-done
  392.8 2.9 reduce-scatter.4.cloned.1.call-done
  395.7 53.6 %shard_map.333 = (bf16[384,128]{1,0:T(8,128)(2,1)}, bf16[384,128]{1,0:T(8,128)(2,1)}, bf16[384,128]{1,0:T(8,128)(2,1)}, bf16[384,128]{1,0:T(8,128)(2,1)}, bf16[3...) custom-call(bf16[3648,128]{1,0:T(8,128)(2,1)} %get-tuple-element.129, ...), custom_call_target="tpu_custom_call" | custom-call | flops 1024 | bytes 1024 | tf_op jit(solution)/shard_map/pallas_call | solution.py:282
  449.9 3.5 collective-permute-done.40.refs_1_
  459.3 2.3 copy.110
  474.9 20.7 %collective-permute-done.41 = bf16[3,1216,128]{2,1,0:T(8,128)(2,1)} collective-permute-done((bf16[3,1216,128]{2,1,0:T(8,128)(2,1)}, bf16[3,1216,128]{2,1,0:T(8,128)(2,1)}, u32[]{:S(2)}, u32[]{:S(2)}) %collective-permute-start.41) | collective-permute-done | bytes 933920 | tf_op jit(solution)/shard_map/ppermute | solution.py:823
  508.8 38.8 %collective-permute-done.43.refs_2_ = bf16[1152,128]{1,0:T(8,128)(2,1)} collective-permute-done((bf16[1152,128]{1,0:T(8,128)(2,1)}, bf16[1152,128]{1,0:T(8,128)(2,1)}, u32[]{:S(2)}, u32[]{:S(2)}) %collective-permute-start.43) | collective-permute-done | bytes 294944 | tf_op jit(solution)/shard_map/ppermute | solution.py:827
  549.3 6.2 shard_map.336
  555.5 5.4 fusion.64
  562.3 10.4 %collective-permute-done.46 = bf16[128,1536]{1,0:T(8,128)(2,1)} collective-permute-done((bf16[128,1536]{1,0:T(8,128)(2,1)S(1)}, bf16[128,1536]{1,0:T(8,128)(2,1)}, u32[]{:S(2)}, u32[]{:S(2)}) %collective-permute-start.46) | collective-permute-done | bytes 393248 | tf_op jit(solution)/shard_map/ppermute | solution.py:772
  577.2 5.1 shard_map.337
  583.1 2.3 collective-permute-start.49
  585.5 3.2 select_reduce_fusion.1
  591.9 4.5 collective-permute-done.48.refs_2_
  599.6 2.6 fusion.14
  602.6 15.1 %collective-permute-done.50 = bf16[192,1536]{1,0:T(8,128)(2,1)S(1)} collective-permute-done((bf16[192,1536]{1,0:T(8,128)(2,1)S(1)}, bf16[192,1536]{1,0:T(8,128)(2,1)S(1)}, u32[]{:S(2)}, u32[]{:S(2)}) %collective-permute-start.50) | collective-permute-done | bytes 589856 | tf_op jit(solution)/shard_map/ppermute | solution.py:823
  618.5 3.4 collective-permute-done.55
  623.3 10.9 %collective-permute-done.56 = f32[4,9216]{1,0:T(4,128)S(1)} collective-permute-done((f32[4,9216]{1,0:T(4,128)S(1)}, f32[4,9216]{1,0:T(4,128)S(1)}, u32[]{:S(2)}, u32[]{:S(2)}) %collective-permute-start.56) | collective-permute-done | bytes 147488 | tf_op jit(solution)/shard_map/ppermute | solution.py:823
  635.4 7.5 %collective-permute-done.57 = f32[4,9216]{1,0:T(4,128)S(1)} collective-permute-done((f32[4,9216]{1,0:T(4,128)S(1)}, f32[4,9216]{1,0:T(4,128)S(1)}, u32[]{:S(2)}, u32[]{:S(2)}) %collective-permute-start.57) | collective-permute-done | bytes 147488 | tf_op jit(solution)/shard_map/ppermute | solution.py:823
  650.9 8.4 %collective-permute-done.52 = bf16[768,256]{1,0:T(8,128)(2,1)S(1)} collective-permute-done((bf16[768,256]{1,0:T(8,128)(2,1)S(1)}, bf16[768,256]{1,0:T(8,128)(2,1)S(1)}, u32[]{:S(2)}, u32[]{:S(2)}) %collective-permute-start.52) | collective-permute-done | bytes 393248 | tf_op jit(solution)/shard_map/ppermute | solution.py:772
  660.2 3.6 all-to-all-start.1
  666.9 11.2 %collective-permute-done.60 = f32[3,1024]{1,0:T(4,128)S(1)} collective-permute-done((f32[3,1024]{1,0:T(4,128)S(1)}, f32[3,1024]{1,0:T(4,128)S(1)}, u32[]{:S(2)}, u32[]{:S(2)}) %collective-permute-start.60) | collective-permute-done | bytes 12320 | tf_op jit(solution)/shard_map/ppermute | solution.py:823
  678.1 4.8 collective-permute-start.61
  683.6 2.4 collective-permute-done.61
  686.7 2.3 fusion.5
  (508 shorter events, 149.2 us)
Async XLA Ops:
  7.2 98.0 %all-gather.3.cloned.1.call-start = ((), (), s32[]{:S(2)}) async-start(), calls=%async_computation.5 | async-start | bytes 10027008 | tf_op jit(solution)/shard_map/all_gather | solution.py:894
  11.3 14.0 %collective-permute-start = (f32[3,6144]{1,0:T(4,128)}, f32[3,6144]{1,0:T(4,128)}, u32[]{:S(2)}, u32[]{:S(2)}) collective-permute-start(f32[3,6144]{1,0:T(4,128)} %fusion.18), channel_id=1, source_target_pairs={{0,2},{2,0},{4,6},{6,4},{8,10},{10,8},{12,14},{14,12},{16,18},{18,... | collective-permute-start | bytes 221192 | tf_op jit(solution)/shard_map/ppermute | solution.py:823
  13.2 4.2 collective-permute-start.4
  17.5 5.0 collective-permute-start.5
  22.5 7.3 %collective-permute-start.6 = (f32[4,3072]{1,0:T(4,128)S(1)}, f32[4,3072]{1,0:T(4,128)S(1)}, u32[]{:S(2)}, u32[]{:S(2)}) collective-permute-start(f32[4,3072]{1,0:T(4,128)S(1)} %add.419), channel_id=1, source_target_pairs={{0,8},{2,10},{4,12},{6,14},{8,0},{10,2},{12,4},{14,6},{16,24},{18,... | collective-permute-start | bytes 147464 | tf_op jit(solution)/shard_map/ppermute | solution.py:823
  26.2 9.7 %collective-permute-start.1 = (f32[3,6144]{1,0:T(4,128)S(1)}, f32[3,6144]{1,0:T(4,128)}, u32[]{:S(2)}, u32[]{:S(2)}) collective-permute-start(f32[3,6144]{1,0:T(4,128)S(1)} %add.410), channel_id=1, source_target_pairs={{0,4},{2,6},{4,0},{6,2},{8,12},{10,14},{12,8},{14,10},{16,20},{18,... | collective-permute-start | bytes 221192 | tf_op jit(solution)/shard_map/ppermute | solution.py:823
  30.4 9.7 %collective-permute-start.7 = (f32[4,3072]{1,0:T(4,128)}, f32[4,3072]{1,0:T(4,128)}, u32[]{:S(2)}, u32[]{:S(2)}) collective-permute-start(f32[4,3072]{1,0:T(4,128)} %add.420), channel_id=1, source_target_pairs={{0,16},{2,18},{4,20},{6,22},{8,24},{10,26},{12,28},{14,30},{16,0},... | collective-permute-start | bytes 147464 | tf_op jit(solution)/shard_map/ppermute | solution.py:823
  36.9 10.6 %collective-permute-start.2 = (f32[3,6144]{1,0:T(4,128)S(1)}, f32[3,6144]{1,0:T(4,128)S(1)}, u32[]{:S(2)}, u32[]{:S(2)}) collective-permute-start(f32[3,6144]{1,0:T(4,128)S(1)} %add.411), channel_id=1, source_target_pairs={{0,8},{2,10},{4,12},{6,14},{8,0},{10,2},{12,4},{14,6},{16,24},{18,... | collective-permute-start | bytes 221192 | tf_op jit(solution)/shard_map/ppermute | solution.py:823
  47.5 6.1 collective-permute-start.3
  54.5 23.5 %all-to-all-start = ((bf16[48,16,256]{2,0,1:T(8,128)(2,1)}), bf16[48,16,256]{2,0,1:T(8,128)(2,1)S(1)}, u32[]{:S(2)}, u32[]{:S(2)}) async-start(bf16[48,16,256]{2,0,1:T(8,128)(2,1)} %bitcast.152), calls=%async_computation | async-start | bytes 786432 | tf_op jit(solution)/shard_map/all_to_all | solution.py:960
  59.2 223.8 %all-gather.5.cloned.1.call-start = ((), (), s32[]{:S(2)}) async-start(), calls=%async_computation.6 | async-start | bytes 20054016 | tf_op jit(solution)/shard_map/all_gather | solution.py:1036
  61.0 26.0 %collective-permute-start.8 = (bf16[128,1536]{1,0:T(8,128)(2,1)S(1)}, bf16[128,1536]{1,0:T(8,128)(2,1)S(1)}, u32[]{:S(2)}, u32[]{:S(2)}) collective-permute-start(bf16[128,1536]{1,0:T(8,128)(2,1)S(1)} %fusion.11), channel_id=1, source_target_pairs={{0,1},{1,0},{2,3},{3,2},{4,5},{5,4},{6,7},{7,6},{8,9},{9,8},{10,11... | collective-permute-start | bytes 1179656 | tf_op jit(solution)/shard_map/ppermute | solution.py:772
  83.7 16.2 %collective-permute-start.10 = (bf16[192,1536]{1,0:T(8,128)(2,1)S(1)}, bf16[192,1536]{1,0:T(8,128)(2,1)S(1)}, u32[]{:S(2)}, u32[]{:S(2)}) collective-permute-start(bf16[192,1536]{1,0:T(8,128)(2,1)S(1)} %slice.297), channel_id=1, source_target_pairs={{0,4},{2,6},{4,0},{6,2},{8,12},{10,14},{12,8},{14,10},{16,20},{18,... | collective-permute-start | bytes 1769480 | tf_op jit(solution)/shard_map/ppermute | solution.py:823
  108.8 9.3 %collective-permute-start.11 = (bf16[192,384]{1,0:T(8,128)(2,1)S(1)}, bf16[192,384]{1,0:T(8,128)(2,1)S(1)}, u32[]{:S(2)}, u32[]{:S(2)}) collective-permute-start(bf16[192,384]{1,0:T(8,128)(2,1)S(1)} %get-tuple-element.116), channel_id=1, source_target_pairs={{0,8},{2,10},{4,12},{6,14},{8,16},{10,18},{12,20},{14,22},{16,24},... | collective-permute-start | bytes 442376 | tf_op jit(solution)/shard_map/ppermute | solution.py:827
  108.8 14.0 %collective-permute-start.12 = (bf16[192,384]{1,0:T(8,128)(2,1)S(1)}, bf16[192,384]{1,0:T(8,128)(2,1)S(1)}, u32[]{:S(2)}, u32[]{:S(2)}) collective-permute-start(bf16[192,384]{1,0:T(8,128)(2,1)S(1)} %get-tuple-element.117), channel_id=1, source_target_pairs={{0,16},{2,18},{4,20},{6,22},{8,24},{10,26},{12,28},{14,30},{16,0},... | collective-permute-start | bytes 442376 | tf_op jit(solution)/shard_map/ppermute | solution.py:827
  110.6 12.3 %collective-permute-start.13 = (bf16[192,384]{1,0:T(8,128)(2,1)S(1)}, bf16[192,384]{1,0:T(8,128)(2,1)S(1)}, u32[]{:S(2)}, u32[]{:S(2)}) collective-permute-start(bf16[192,384]{1,0:T(8,128)(2,1)S(1)} %get-tuple-element.118), channel_id=1, source_target_pairs={{0,24},{2,26},{4,28},{6,30},{8,0},{10,2},{12,4},{14,6},{16,8},{18,... | collective-permute-start | bytes 442376 | tf_op jit(solution)/shard_map/ppermute | solution.py:827
  122.9 12.1 %collective-permute-start.14 = (bf16[1152,128]{1,0:T(8,128)(2,1)S(1)}, bf16[1152,128]{1,0:T(8,128)(2,1)S(1)}, u32[]{:S(2)}, u32[]{:S(2)}) collective-permute-start(bf16[1152,128]{1,0:T(8,128)(2,1)S(1)} %get-tuple-element.120), channel_id=1, source_target_pairs={{0,8},{2,10},{4,12},{6,14},{8,16},{10,18},{12,20},{14,22},{16,24},... | collective-permute-start | bytes 884744 | tf_op jit(solution)/shard_map/ppermute | solution.py:827
  126.2 19.2 %collective-permute-start.15 = (bf16[1152,128]{1,0:T(8,128)(2,1)S(1)}, bf16[1152,128]{1,0:T(8,128)(2,1)S(1)}, u32[]{:S(2)}, u32[]{:S(2)}) collective-permute-start(bf16[1152,128]{1,0:T(8,128)(2,1)S(1)} %get-tuple-element.121), channel_id=1, source_target_pairs={{0,16},{2,18},{4,20},{6,22},{8,24},{10,26},{12,28},{14,30},{16,0},... | collective-permute-start | bytes 884744 | tf_op jit(solution)/shard_map/ppermute | solution.py:827
  126.5 18.9 %collective-permute-start.16 = (bf16[1152,128]{1,0:T(8,128)(2,1)S(1)}, bf16[1152,128]{1,0:T(8,128)(2,1)S(1)}, u32[]{:S(2)}, u32[]{:S(2)}) collective-permute-start(bf16[1152,128]{1,0:T(8,128)(2,1)S(1)} %get-tuple-element.122), channel_id=1, source_target_pairs={{0,24},{2,26},{4,28},{6,30},{8,0},{10,2},{12,4},{14,6},{16,8},{18,... | collective-permute-start | bytes 884744 | tf_op jit(solution)/shard_map/ppermute | solution.py:827
  146.5 22.8 %collective-permute-start.17 = (bf16[3648,128]{1,0:T(8,128)(2,1)}, bf16[3648,128]{1,0:T(8,128)(2,1)}, u32[]{:S(2)}, u32[]{:S(2)}) collective-permute-start(bf16[3648,128]{1,0:T(8,128)(2,1)} %get-tuple-element.129.refs_0_), channel_id=1, source_target_pairs={{0,4},{2,6},{4,0},{6,2},{8,12},{10,14},{12,8},{14,10},{16,20},{18,... | collective-permute-start | bytes 2801672 | tf_op jit(solution)/shard_map/ppermute | solution.py:823
  150.8 19.7 %collective-permute-start.20 = (bf16[128,1536]{1,0:T(8,128)(2,1)S(1)}, bf16[128,1536]{1,0:T(8,128)(2,1)}, u32[]{:S(2)}, u32[]{:S(2)}) collective-permute-start(bf16[128,1536]{1,0:T(8,128)(2,1)S(1)} %fusion.13), channel_id=1, source_target_pairs={{0,1},{1,0},{2,3},{3,2},{4,5},{5,4},{6,7},{7,6},{8,9},{9,8},{10,11... | collective-permute-start | bytes 1179656 | tf_op jit(solution)/shard_map/ppermute | solution.py:772
  152.2 19.3 %collective-permute-start.18 = (bf16[3648,128]{1,0:T(8,128)(2,1)}, bf16[3648,128]{1,0:T(8,128)(2,1)}, u32[]{:S(2)}, u32[]{:S(2)}) collective-permute-start(bf16[3648,128]{1,0:T(8,128)(2,1)} %get-tuple-element.129.refs_0_), channel_id=1, source_target_pairs={{0,2},{2,0},{4,6},{6,4},{8,10},{10,8},{12,14},{14,12},{16,18},{18,... | collective-permute-start | bytes 2801672 | tf_op jit(solution)/shard_map/ppermute | solution.py:823
  172.2 223.4 %reduce-scatter.4.cloned.1.call-start = ((), (), s32[]{:S(2)}) async-start(), calls=%async_computation.7 | async-start | bytes 3538944 | tf_op jit(solution)/shard_map/reduce_scatter | solution.py:890
  200.8 13.3 %collective-permute-start.21 = (bf16[384,128]{1,0:T(8,128)(2,1)}, bf16[384,128]{1,0:T(8,128)(2,1)S(1)}, u32[]{:S(2)}, u32[]{:S(2)}) collective-permute-start(bf16[384,128]{1,0:T(8,128)(2,1)} %get-tuple-element.137), channel_id=1, source_target_pairs={{0,24},{2,26},{4,28},{6,30},{8,0},{10,2},{12,4},{14,6},{16,8},{18,... | collective-permute-start | bytes 294920 | tf_op jit(solution)/shard_map/ppermute | solution.py:827
  208.5 14.8 %collective-permute-start.22 = (bf16[384,128]{1,0:T(8,128)(2,1)}, bf16[384,128]{1,0:T(8,128)(2,1)S(1)}, u32[]{:S(2)}, u32[]{:S(2)}) collective-permute-start(bf16[384,128]{1,0:T(8,128)(2,1)} %get-tuple-element.138), channel_id=1, source_target_pairs={{0,16},{2,18},{4,20},{6,22},{8,24},{10,26},{12,28},{14,30},{16,0},... | collective-permute-start | bytes 294920 | tf_op jit(solution)/shard_map/ppermute | solution.py:827
  209.2 14.1 %collective-permute-start.23 = (bf16[384,128]{1,0:T(8,128)(2,1)}, bf16[384,128]{1,0:T(8,128)(2,1)S(1)}, u32[]{:S(2)}, u32[]{:S(2)}) collective-permute-start(bf16[384,128]{1,0:T(8,128)(2,1)} %get-tuple-element.139), channel_id=1, source_target_pairs={{0,8},{2,10},{4,12},{6,14},{8,16},{10,18},{12,20},{14,22},{16,24},... | collective-permute-start | bytes 294920 | tf_op jit(solution)/shard_map/ppermute | solution.py:827
  227.3 10.1 %collective-permute-start.24 = (bf16[128,1536]{1,0:T(8,128)(2,1)S(1)}, bf16[128,1536]{1,0:T(8,128)(2,1)S(1)}, u32[]{:S(2)}, u32[]{:S(2)}) collective-permute-start(bf16[128,1536]{1,0:T(8,128)(2,1)S(1)} %slice.299), channel_id=1, source_target_pairs={{0,1},{1,0},{2,3},{3,2},{4,5},{5,4},{6,7},{7,6},{8,9},{9,8},{10,11... | collective-permute-start | bytes 1179656 | tf_op jit(solution)/shard_map/ppermute | solution.py:772
  239.0 9.3 %collective-permute-start.25 = (bf16[128,1536]{1,0:T(8,128)(2,1)S(1)}, bf16[128,1536]{1,0:T(8,128)(2,1)S(1)}, u32[]{:S(2)}, u32[]{:S(2)}) collective-permute-start(bf16[128,1536]{1,0:T(8,128)(2,1)S(1)} %fusion.17), channel_id=1, source_target_pairs={{0,1},{1,0},{2,3},{3,2},{4,5},{5,4},{6,7},{7,6},{8,9},{9,8},{10,11... | collective-permute-start | bytes 1179656 | tf_op jit(solution)/shard_map/ppermute | solution.py:772
  302.2 4.5 collective-permute-start.38
  311.9 270.4 %reduce-scatter.6.cloned.1.call-start = ((), (), s32[]{:S(2)}) async-start(), calls=%async_computation.8 | async-start | bytes 8404992 | tf_op jit(solution)/shard_map/reduce_scatter | solution.py:890
  322.6 11.6 %collective-permute-start.26 = (bf16[128,1536]{1,0:T(8,128)(2,1)}, bf16[128,1536]{1,0:T(8,128)(2,1)S(1)}, u32[]{:S(2)}, u32[]{:S(2)}) collective-permute-start(bf16[128,1536]{1,0:T(8,128)(2,1)} %copy-done.37), channel_id=1, source_target_pairs={{0,1},{1,0},{2,3},{3,2},{4,5},{5,4},{6,7},{7,6},{8,9},{9,8},{10,11... | collective-permute-start | bytes 1179656 | tf_op jit(solution)/shard_map/ppermute | solution.py:772
  324.1 50.8 %collective-permute-start.35 = (bf16[2,256,2048]{2,1,0:T(8,128)(2,1)}, bf16[2,256,2048]{2,1,0:T(8,128)(2,1)}, u32[]{:S(2)}, u32[]{:S(2)}) collective-permute-start(bf16[2,256,2048]{2,1,0:T(8,128)(2,1)} %get-tuple-element.152.own_ref), channel_id=1, source_target_pairs={{0,2},{2,0},{4,6},{6,4},{8,10},{10,8},{12,14},{14,12},{16,18},{18,... | collective-permute-start | bytes 6291464 | tf_op jit(solution)/shard_map/ppermute | solution.py:823
  334.3 10.6 %collective-permute-start.27 = (bf16[128,1536]{1,0:T(8,128)(2,1)S(1)}, bf16[128,1536]{1,0:T(8,128)(2,1)S(1)}, u32[]{:S(2)}, u32[]{:S(2)}) collective-permute-start(bf16[128,1536]{1,0:T(8,128)(2,1)S(1)} %copy-done.36), channel_id=1, source_target_pairs={{0,1},{1,0},{2,3},{3,2},{4,5},{5,4},{6,7},{7,6},{8,9},{9,8},{10,11... | collective-permute-start | bytes 1179656 | tf_op jit(solution)/shard_map/ppermute | solution.py:772
  347.9 10.1 %collective-permute-start.29 = (bf16[128,1536]{1,0:T(8,128)(2,1)}, bf16[128,1536]{1,0:T(8,128)(2,1)}, u32[]{:S(2)}, u32[]{:S(2)}) collective-permute-start(bf16[128,1536]{1,0:T(8,128)(2,1)} %get-tuple-element.308), channel_id=1, source_target_pairs={{0,1},{1,0},{2,3},{3,2},{4,5},{5,4},{6,7},{7,6},{8,9},{9,8},{10,11... | collective-permute-start | bytes 1179656 | tf_op jit(solution)/shard_map/ppermute | solution.py:772
  349.3 25.6 %collective-permute-start.36 = (bf16[256,768]{1,0:T(8,128)(2,1)S(1)}, bf16[256,768]{1,0:T(8,128)(2,1)}, u32[]{:S(2)}, u32[]{:S(2)}) collective-permute-start(bf16[256,768]{1,0:T(8,128)(2,1)S(1)} %shard_map.328.own_last_ref), channel_id=1, source_target_pairs={{0,2},{2,0},{4,6},{6,4},{8,10},{10,8},{12,14},{14,12},{16,18},{18,... | collective-permute-start | bytes 1179656 | tf_op jit(solution)/shard_map/ppermute | solution.py:823
  353.8 12.7 %collective-permute-start.33 = (bf16[768,256]{1,0:T(8,128)(2,1)}, bf16[768,256]{1,0:T(8,128)(2,1)}, u32[]{:S(2)}, u32[]{:S(2)}) collective-permute-start(bf16[768,256]{1,0:T(8,128)(2,1)} %get-tuple-element.318), channel_id=1, source_target_pairs={{0,2},{2,0},{4,6},{6,4},{8,10},{10,8},{12,14},{14,12},{16,18},{18,... | collective-permute-start | bytes 1179656 | tf_op jit(solution)/shard_map/ppermute | solution.py:823
  363.7 8.3 %collective-permute-start.34 = (bf16[768,256]{1,0:T(8,128)(2,1)S(1)}, bf16[768,256]{1,0:T(8,128)(2,1)S(1)}, u32[]{:S(2)}, u32[]{:S(2)}) collective-permute-start(bf16[768,256]{1,0:T(8,128)(2,1)S(1)} %get-tuple-element.322), channel_id=1, source_target_pairs={{0,2},{2,0},{4,6},{6,4},{8,10},{10,8},{12,14},{14,12},{16,18},{18,... | collective-permute-start | bytes 1179656 | tf_op jit(solution)/shard_map/ppermute | solution.py:823
  368.4 24.3 %collective-permute-start.30 = (bf16[384,128]{1,0:T(8,128)(2,1)}, bf16[384,128]{1,0:T(8,128)(2,1)}, u32[]{:S(2)}, u32[]{:S(2)}) collective-permute-start(bf16[384,128]{1,0:T(8,128)(2,1)} %get-tuple-element.149), channel_id=1, source_target_pairs={{0,8},{2,10},{4,12},{6,14},{8,16},{10,18},{12,20},{14,22},{16,24},... | collective-permute-start | bytes 294920 | tf_op jit(solution)/shard_map/ppermute | solution.py:827
  372.0 20.8 %collective-permute-start.31 = (bf16[384,128]{1,0:T(8,128)(2,1)}, bf16[384,128]{1,0:T(8,128)(2,1)}, u32[]{:S(2)}, u32[]{:S(2)}) collective-permute-start(bf16[384,128]{1,0:T(8,128)(2,1)} %get-tuple-element.150), channel_id=1, source_target_pairs={{0,16},{2,18},{4,20},{6,22},{8,24},{10,26},{12,28},{14,30},{16,0},... | collective-permute-start | bytes 294920 | tf_op jit(solution)/shard_map/ppermute | solution.py:827
  372.0 20.8 %collective-permute-start.32 = (bf16[384,128]{1,0:T(8,128)(2,1)}, bf16[384,128]{1,0:T(8,128)(2,1)}, u32[]{:S(2)}, u32[]{:S(2)}) collective-permute-start(bf16[384,128]{1,0:T(8,128)(2,1)} %get-tuple-element.151), channel_id=1, source_target_pairs={{0,24},{2,26},{4,28},{6,30},{8,0},{10,2},{12,4},{14,6},{16,8},{18,... | collective-permute-start | bytes 294920 | tf_op jit(solution)/shard_map/ppermute | solution.py:827
  395.7 295.9 %reduce-scatter.8.cloned.1.call-start = ((), (), s32[]{:S(2)}) async-start(), calls=%async_computation.9 | async-start | bytes 3981312 | tf_op jit(solution)/shard_map/reduce_scatter | solution.py:890
  449.4 5.2 collective-permute-start.39
  458.0 37.5 %collective-permute-start.41 = (bf16[3,1216,128]{2,1,0:T(8,128)(2,1)}, bf16[3,1216,128]{2,1,0:T(8,128)(2,1)}, u32[]{:S(2)}, u32[]{:S(2)}) collective-permute-start(bf16[3,1216,128]{2,1,0:T(8,128)(2,1)} %pad_maximum_fusion.7), channel_id=1, source_target_pairs={{0,4},{2,6},{4,0},{6,2},{8,12},{10,14},{12,8},{14,10},{16,20},{18,... | collective-permute-start | bytes 2801672 | tf_op jit(solution)/shard_map/ppermute | solution.py:823
  463.8 8.9 %collective-permute-start.28 = (bf16[768,256]{1,0:T(8,128)(2,1)}, bf16[768,256]{1,0:T(8,128)(2,1)}, u32[]{:S(2)}, u32[]{:S(2)}) collective-permute-start(bf16[768,256]{1,0:T(8,128)(2,1)} %get-tuple-element.324), channel_id=1, source_target_pairs={{0,2},{2,0},{4,6},{6,4},{8,10},{10,8},{12,14},{14,12},{16,18},{18,... | collective-permute-start | bytes 1179656 | tf_op jit(solution)/shard_map/ppermute | solution.py:823
  498.6 10.2 %collective-permute-start.42 = (bf16[1152,128]{1,0:T(8,128)(2,1)}, bf16[1152,128]{1,0:T(8,128)(2,1)}, u32[]{:S(2)}, u32[]{:S(2)}) collective-permute-start(bf16[1152,128]{1,0:T(8,128)(2,1)} %get-tuple-element.169), channel_id=1, source_target_pairs={{0,24},{2,26},{4,28},{6,30},{8,0},{10,2},{12,4},{14,6},{16,8},{18,... | collective-permute-start | bytes 884744 | tf_op jit(solution)/shard_map/ppermute | solution.py:827
  498.6 49.0 %collective-permute-start.43 = (bf16[1152,128]{1,0:T(8,128)(2,1)}, bf16[1152,128]{1,0:T(8,128)(2,1)}, u32[]{:S(2)}, u32[]{:S(2)}) collective-permute-start(bf16[1152,128]{1,0:T(8,128)(2,1)} %get-tuple-element.170), channel_id=1, source_target_pairs={{0,16},{2,18},{4,20},{6,22},{8,24},{10,26},{12,28},{14,30},{16,0},... | collective-permute-start | bytes 884744 | tf_op jit(solution)/shard_map/ppermute | solution.py:827
  500.5 47.1 %collective-permute-start.44 = (bf16[1152,128]{1,0:T(8,128)(2,1)}, bf16[1152,128]{1,0:T(8,128)(2,1)}, u32[]{:S(2)}, u32[]{:S(2)}) collective-permute-start(bf16[1152,128]{1,0:T(8,128)(2,1)} %get-tuple-element.171), channel_id=1, source_target_pairs={{0,8},{2,10},{4,12},{6,14},{8,16},{10,18},{12,20},{14,22},{16,24},... | collective-permute-start | bytes 884744 | tf_op jit(solution)/shard_map/ppermute | solution.py:827
  555.5 19.4 %collective-permute-start.45 = (bf16[1,256,2304]{2,1,0:T(8,128)(2,1)}, bf16[1,256,2304]{2,1,0:T(8,128)(2,1)S(1)}, u32[]{:S(2)}, u32[]{:S(2)}) collective-permute-start(bf16[1,256,2304]{2,1,0:T(8,128)(2,1)} %bitcast.68.own_ref), channel_id=1, source_target_pairs={{0,2},{2,0},{4,6},{6,4},{8,10},{10,8},{12,14},{14,12},{16,18},{18,... | collective-permute-start | bytes 3538952 | tf_op jit(solution)/shard_map/ppermute | solution.py:823
  561.0 11.7 %collective-permute-start.46 = (bf16[128,1536]{1,0:T(8,128)(2,1)S(1)}, bf16[128,1536]{1,0:T(8,128)(2,1)}, u32[]{:S(2)}, u32[]{:S(2)}) collective-permute-start(bf16[128,1536]{1,0:T(8,128)(2,1)S(1)} %slice.298), channel_id=1, source_target_pairs={{0,1},{1,0},{2,3},{3,2},{4,5},{5,4},{6,7},{7,6},{8,9},{9,8},{10,11... | collective-permute-start | bytes 1179656 | tf_op jit(solution)/shard_map/ppermute | solution.py:772
  582.2 9.6 %collective-permute-start.47 = (bf16[192,384]{1,0:T(8,128)(2,1)S(1)}, bf16[192,384]{1,0:T(8,128)(2,1)S(1)}, u32[]{:S(2)}, u32[]{:S(2)}) collective-permute-start(bf16[192,384]{1,0:T(8,128)(2,1)S(1)} %get-tuple-element.182.refs_0_), channel_id=1, source_target_pairs={{0,24},{2,26},{4,28},{6,30},{8,0},{10,2},{12,4},{14,6},{16,8},{18,... | collective-permute-start | bytes 442376 | tf_op jit(solution)/shard_map/ppermute | solution.py:827
  582.3 14.1 %collective-permute-start.48 = (bf16[192,384]{1,0:T(8,128)(2,1)S(1)}, bf16[192,384]{1,0:T(8,128)(2,1)S(1)}, u32[]{:S(2)}, u32[]{:S(2)}) collective-permute-start(bf16[192,384]{1,0:T(8,128)(2,1)S(1)} %get-tuple-element.182.refs_0_), channel_id=1, source_target_pairs={{0,16},{2,18},{4,20},{6,22},{8,24},{10,26},{12,28},{14,30},{16,0},... | collective-permute-start | bytes 442376 | tf_op jit(solution)/shard_map/ppermute | solution.py:827
  583.1 13.2 %collective-permute-start.49 = (bf16[192,384]{1,0:T(8,128)(2,1)S(1)}, bf16[192,384]{1,0:T(8,128)(2,1)S(1)}, u32[]{:S(2)}, u32[]{:S(2)}) collective-permute-start(bf16[192,384]{1,0:T(8,128)(2,1)S(1)} %get-tuple-element.182.refs_0_), channel_id=1, source_target_pairs={{0,8},{2,10},{4,12},{6,14},{8,16},{10,18},{12,20},{14,22},{16,24},... | collective-permute-start | bytes 442376 | tf_op jit(solution)/shard_map/ppermute | solution.py:827
  590.1 8.4 %collective-permute-start.53 = (f32[4,9216]{1,0:T(4,128)}, f32[4,9216]{1,0:T(4,128)}, u32[]{:S(2)}, u32[]{:S(2)}) collective-permute-start(f32[4,9216]{1,0:T(4,128)} %pad_maximum_fusion.18), channel_id=1, source_target_pairs={{0,1},{1,0},{2,3},{3,2},{4,5},{5,4},{6,7},{7,6},{8,9},{9,8},{10,11... | collective-permute-start | bytes 442376 | tf_op jit(solution)/shard_map/ppermute | solution.py:772
  596.4 21.2 %collective-permute-start.50 = (bf16[192,1536]{1,0:T(8,128)(2,1)S(1)}, bf16[192,1536]{1,0:T(8,128)(2,1)S(1)}, u32[]{:S(2)}, u32[]{:S(2)}) collective-permute-start(bf16[192,1536]{1,0:T(8,128)(2,1)S(1)} %shard_map.338), channel_id=1, source_target_pairs={{0,4},{2,6},{4,0},{6,2},{8,12},{10,14},{12,8},{14,10},{16,20},{18,... | collective-permute-start | bytes 1769480 | tf_op jit(solution)/shard_map/ppermute | solution.py:823
  602.4 19.5 %collective-permute-start.55 = (f32[4,9216]{1,0:T(4,128)S(1)}, f32[4,9216]{1,0:T(4,128)S(1)}, u32[]{:S(2)}, u32[]{:S(2)}) collective-permute-start(f32[4,9216]{1,0:T(4,128)S(1)} %add.495), channel_id=1, source_target_pairs={{0,4},{2,6},{4,0},{6,2},{8,12},{10,14},{12,8},{14,10},{16,20},{18,... | collective-permute-start | bytes 442376 | tf_op jit(solution)/shard_map/ppermute | solution.py:823
  617.8 27.8 %collective-permute-start.51 = (bf16[384,1536]{1,0:T(8,128)(2,1)S(1)}, bf16[384,1536]{1,0:T(8,128)(2,1)}, u32[]{:S(2)}, u32[]{:S(2)}) collective-permute-start(bf16[384,1536]{1,0:T(8,128)(2,1)S(1)} %pad_maximum_fusion.4), channel_id=1, source_target_pairs={{0,2},{2,0},{4,6},{6,4},{8,10},{10,8},{12,14},{14,12},{16,18},{18,... | collective-permute-start | bytes 3538952 | tf_op jit(solution)/shard_map/ppermute | solution.py:823
  621.9 12.2 %collective-permute-start.56 = (f32[4,9216]{1,0:T(4,128)S(1)}, f32[4,9216]{1,0:T(4,128)S(1)}, u32[]{:S(2)}, u32[]{:S(2)}) collective-permute-start(f32[4,9216]{1,0:T(4,128)S(1)} %add.496), channel_id=1, source_target_pairs={{0,8},{2,10},{4,12},{6,14},{8,0},{10,2},{12,4},{14,6},{16,24},{18,... | collective-permute-start | bytes 442376 | tf_op jit(solution)/shard_map/ppermute | solution.py:823
  634.1 8.7 %collective-permute-start.57 = (f32[4,9216]{1,0:T(4,128)S(1)}, f32[4,9216]{1,0:T(4,128)S(1)}, u32[]{:S(2)}, u32[]{:S(2)}) collective-permute-start(f32[4,9216]{1,0:T(4,128)S(1)} %add.497), channel_id=1, source_target_pairs={{0,16},{2,18},{4,20},{6,22},{8,24},{10,26},{12,28},{14,30},{16,0},... | collective-permute-start | bytes 442376 | tf_op jit(solution)/shard_map/ppermute | solution.py:823
  643.5 6.5 collective-permute-start.58
  647.6 11.6 %collective-permute-start.52 = (bf16[768,256]{1,0:T(8,128)(2,1)S(1)}, bf16[768,256]{1,0:T(8,128)(2,1)S(1)}, u32[]{:S(2)}, u32[]{:S(2)}) collective-permute-start(bf16[768,256]{1,0:T(8,128)(2,1)S(1)} %convolution_convert_fusion), channel_id=1, source_target_pairs={{0,1},{1,0},{2,3},{3,2},{4,5},{5,4},{6,7},{7,6},{8,9},{9,8},{10,11... | collective-permute-start | bytes 1179656 | tf_op jit(solution)/shard_map/ppermute | solution.py:772
  650.2 14.1 %collective-permute-start.59 = (f32[3,1024]{1,0:T(4,128)S(1)}, f32[3,1024]{1,0:T(4,128)S(1)}, u32[]{:S(2)}, u32[]{:S(2)}) collective-permute-start(f32[3,1024]{1,0:T(4,128)S(1)} %add.499), channel_id=1, source_target_pairs={{0,4},{2,6},{4,0},{6,2},{8,12},{10,14},{12,8},{14,10},{16,20},{18,... | collective-permute-start | bytes 36872 | tf_op jit(solution)/shard_map/ppermute | solution.py:823
  660.2 30.6 %all-to-all-start.1 = ((bf16[16,48,256]{2,1,0:T(8,128)(2,1)}), bf16[16,48,256]{2,1,0:T(8,128)(2,1)S(1)}, u32[]{:S(2)}, u32[]{:S(2)}) async-start(bf16[16,48,256]{2,1,0:T(8,128)(2,1)} %bitcast.74), calls=%async_computation.3 | async-start | bytes 786432 | tf_op jit(solution)/shard_map/all_to_all | solution.py:1210
  664.4 13.8 %collective-permute-start.60 = (f32[3,1024]{1,0:T(4,128)S(1)}, f32[3,1024]{1,0:T(4,128)S(1)}, u32[]{:S(2)}, u32[]{:S(2)}) collective-permute-start(f32[3,1024]{1,0:T(4,128)S(1)} %add.500), channel_id=1, source_target_pairs={{0,8},{2,10},{4,12},{6,14},{8,0},{10,2},{12,4},{14,6},{16,24},{18,... | collective-permute-start | bytes 36872 | tf_op jit(solution)/shard_map/ppermute | solution.py:823
  678.1 7.9 %collective-permute-start.61 = (f32[3,1024]{1,0:T(4,128)S(1)}, f32[3,1024]{1,0:T(4,128)S(1)}, u32[]{:S(2)}, u32[]{:S(2)}) collective-permute-start(f32[3,1024]{1,0:T(4,128)S(1)} %add.501), channel_id=1, source_target_pairs={{0,16},{2,18},{4,20},{6,22},{8,24},{10,26},{12,28},{14,30},{16,0},... | collective-permute-start | bytes 36872 | tf_op jit(solution)/shard_map/ppermute | solution.py:823
  (125 other events, 1450.9 us)
Sparse Core Ops, SparseCore 0:
  10.9 94.2 all-gather.2
  172.4 110.6 all-gather.4
  312.0 83.6 reduce-scatter.3
  399.1 156.4 reduce-scatter.5
  591.9 95.1 reduce-scatter.7

commit v4 on v3

--- a/solution.py
+++ b/solution.py
@@ -664,13 +664,16 @@
         at = jnp.minimum(i, count - 1)
         return (at // tiles, 0, at % tiles)
 
+    def left_at(i):
+        return (jnp.where(i < 2 * tiles, 0, jnp.where(i < count, 1, 2)), 0, 0)
+
     right = pl.BlockSpec((1, rows, tile), right_at)
     last = pl.BlockSpec((rows, tile), lambda i: (0, jnp.maximum(i - count, 0)))
     return pl.pallas_call(
         functools.partial(joint_kernel, count),
         grid=(count + extra,),
         in_specs=[
-            pl.BlockSpec((1, depth, tokens), lambda i: (jnp.where(i < count, 0, 1), 0, 0)),
+            pl.BlockSpec((1, depth, tokens), left_at),
             right,
             right,
             last,
@@ -685,7 +688,7 @@
 
 def feed_kernel(
     normed_ref, grad_ref, gate_ref, up_ref, down_ref,
-    hidden_ref, grads_ref, feed_own_ref, feed_other_ref, norm_own_ref, norm_other_ref,
+    grads_ref, feed_own_ref, feed_other_ref, norm_own_ref, norm_other_ref,
     feed_acc, norm_acc,
 ):
     step = pl.program_id(0)
@@ -704,7 +707,7 @@
     hidden = (silu * up).astype(LOW)
     grad_gate = (grad_hidden * up * sigmoid * (1.0 + gate * (1.0 - sigmoid))).astype(LOW)
     grad_up = (grad_hidden * silu).astype(LOW)
-    hidden_ref[0] = hidden
+    grads_ref[2] = hidden
     grads_ref[0] = grad_gate
     grads_ref[1] = grad_up
     feed_acc[...] += matmul(hidden, down_ref[...], 1, 1)
@@ -719,9 +722,8 @@
         norm_other_ref[...] = norm_acc[half:, :].astype(LOW)
 
 
-def feed_forward(normed, grads, weights, tile):
+def feed_forward(normed, grads, weights, columns, tile):
     rows, width = normed.shape
-    columns = weights.shape[1] // 3
     tiles = columns // tile
     own = jax.ShapeDtypeStruct((rows // 2, width), FLOAT)
     other = jax.ShapeDtypeStruct((rows // 2, width), LOW)
@@ -734,13 +736,11 @@
             for part in range(3)
         ],
         out_specs=[
-            pl.BlockSpec((1, rows, tile), lambda i: (0, 0, i)),
-            pl.BlockSpec((2, rows, tile), lambda i: (0, 0, i)),
+            pl.BlockSpec((3, rows, tile), lambda i: (0, 0, i)),
         ]
         + [whole(own.shape)] * 4,
         out_shape=[
-            jax.ShapeDtypeStruct((1, rows, columns), LOW),
-            jax.ShapeDtypeStruct((2, rows, columns), LOW),
+            jax.ShapeDtypeStruct((3, rows, columns), LOW),
             own,
             other,
             own,
@@ -891,14 +891,8 @@
             values, "dp", scatter_dimension=0, axis_index_groups=core_groups, tiled=True
         )
 
-    attn_full = lax.all_gather(
-        jnp.concatenate(
-            [
-                qkv_weight.transpose(1, 0, 2).reshape(weight_rows, 3 * local_width),
-                out_weight.T,
-            ],
-            axis=1,
-        ),
+    qkv_full = lax.all_gather(
+        qkv_weight.transpose(1, 0, 2).reshape(weight_rows, 3 * local_width),
         "dp",
         axis=0,
         tiled=True,
@@ -917,6 +911,8 @@
         ],
         axis=0,
     )
+    text_columns = lax.all_to_all(text_tokens, "dp", split_axis=1, concat_axis=0, tiled=True)
+    early_part, text_columns = tie(early_part, text_columns)
     early_sum = sum_dp(early_part)
     bias = ada_bias.astype(FLOAT)
     early_mod = early_sum[:clip_count] + bias[:early]
@@ -956,8 +952,6 @@
 
     text_rows = text_tokens.shape[0]
     group_rows = text_rows * SPLIT
-    text_tokens, late_sum = tie(text_tokens, late_sum)
-    text_columns = lax.all_to_all(text_tokens, "dp", split_axis=1, concat_axis=0, tiled=True)
     text_groups = text_columns.reshape(near, group_rows, text_columns.shape[1])
     text_near = jnp.concatenate([pick(text_groups, near_index ^ mask) for mask in flips], axis=0)
     text_weight = (
@@ -1006,10 +1000,19 @@
     )
     gate_lanes = jnp.broadcast_to(gate_heads[:, None, None], (each, 8, 128))
 
-    qkv_full, normed_all, text_parts, key_features, query_features = tie(
-        attn_full[:, : 3 * local_width], normed_all, text_parts, key_features, query_features
-    )
-    out_full = attn_full[:, 3 * local_width :]
+    rest_weights, qkv_full, normed_all, text_parts, late_sum, key_features, query_features = tie(
+        jnp.concatenate(
+            [gate_up_weight[0], gate_up_weight[1], down_weight.T, out_weight.T], axis=1
+        ),
+        qkv_full,
+        normed_all,
+        text_parts,
+        late_sum,
+        key_features,
+        query_features,
+    )
+    rest_full = lax.all_gather(rest_weights, "dp", axis=0, tiled=True)
+    out_full = rest_full[:, 3 * hidden_count :]
     text_arrived = send_slots(text_parts)
     qkv_raw = dot_float(normed_all, qkv_full)
     head_slots = rope_forward(far, qkv_raw, cosine, sine, gains, heads)
@@ -1028,12 +1031,7 @@
     arrived = send_slots(head_slots)
     own_pairs, queries = gather_slots(arrived, text_pairs, each)
     pairs = spread_list(own_pairs)
-    feed_weights, pairs, grad_ffn = tie(
-        jnp.concatenate([gate_up_weight[0], gate_up_weight[1], down_weight.T], axis=1),
-        pairs,
-        grad_ffn,
-    )
-    feed_full = lax.all_gather(feed_weights, "dp", axis=0, tiled=True)
+    pairs, grad_ffn = tie(pairs, grad_ffn)
     mixed_slots, head_outs, head_stats = attention_forward(
         pairs, queries, query_features, key_features, text_features, gate_lanes
     )
@@ -1042,31 +1040,31 @@
     after_attn = input_rows + gate_one * attn_rows
     second_gain = second_norm_gain.astype(FLOAT)
     normed_two_all = both_rows(modulated(after_attn, second_gain, shift_two, scale_two).astype(LOW))
-    hidden_low, feed_grads, feed_own, feed_other, norm_own, norm_other = feed_forward(
-        normed_two_all, grad_ffn, feed_full, 512
-    )
-    down_grads = stacked_outer(core_columns(grad_ffn), hidden_low, flip(hidden_low, 1), 512)
-    down_low = scatter(down_grads)
+    feed_grads, feed_own, feed_other, norm_own, norm_other = feed_forward(
+        normed_two_all, grad_ffn, rest_full, hidden_count, 512
+    )
     grad_normed_two = norm_own + swapped(norm_other).astype(FLOAT)
-    grad_normed_two, feed_other = tie(grad_normed_two, feed_other)
+    _, pull_two = jax.vjp(modulated, after_attn, second_gain, shift_two, scale_two)
+    back_two, grad_second_gain, grad_shift_two, grad_scale_two = pull_two(grad_normed_two)
+    grad_after = grad_two + back_two
+    grad_attn, feed_other = tie(both_rows((gate_one * grad_after).astype(LOW)), feed_other)
     ffn_rows = feed_own + swapped(feed_other).astype(FLOAT)
     output = (after_attn + gate_two * ffn_rows).astype(LOW)
     grad_gate_two = grad_two * ffn_rows
-    _, pull_two = jax.vjp(modulated, after_attn, second_gain, shift_two, scale_two)
-    back_two, grad_second_gain, grad_shift_two, grad_scale_two = pull_two(grad_normed_two)
-    grad_after = grad_two + back_two
-    grad_attn = both_rows((gate_one * grad_after).astype(LOW))
     grad_gate_one = grad_after * attn_rows
     grad_slots = send_slots(split_heads(far, dot_float(grad_attn, out_full), heads))
     joint_grads = joint_outer(
-        jnp.stack([core_columns(normed_two_all), core_columns(grad_attn)]),
+        jnp.stack(
+            [core_columns(normed_two_all), core_columns(grad_ffn), core_columns(grad_attn)]
+        ),
         feed_grads,
         flip(feed_grads, 1),
         mixed,
         flip(mixed, 1),
         256,
     )
-    grad_slots, joint_grads, down_low = tie(grad_slots, joint_grads, down_low)
+    normed_core = core_columns(normed_all)
+    grad_slots, joint_grads, normed_core = tie(grad_slots, joint_grads, normed_core)
     joint_low = scatter(joint_grads)
 
     def total_rows(terms, first, last):
@@ -1137,12 +1135,11 @@
     grad_normed_one = own_rows(dot_turned(qkv_grad, qkv_full))
     qkv_right = qkv_grad[None]
     qkv_grads = stacked_outer(
-        core_columns(normed_all), qkv_right, flip(qkv_right, 1), local_width
-    )
-    qkv_grads, joint_low, grad_normed_one, text_low = tie(
-        qkv_grads, joint_low, grad_normed_one, text_low
-    )
+        normed_core, qkv_right, flip(qkv_right, 1), local_width
+    )
+    qkv_grads, joint_low = tie(qkv_grads, joint_low)
     qkv_low = scatter(qkv_grads)
+    grad_normed_one, qkv_grads = tie(grad_normed_one, qkv_grads)
     _, pull_one = jax.vjp(modulated, input_rows, first_gain, shift_one, scale_one)
     back_one, grad_first_gain, grad_shift_one, grad_scale_one = pull_one(grad_normed_one)
     grad_inputs = grad_after + back_one
@@ -1179,6 +1176,8 @@
         [jax.ShapeDtypeStruct((group_rows, 2 * local_width), LOW)],
         [],
     )[0]
+    text_all = spread(text_wide)
+    all_pairs, text_all = tie(all_pairs, text_all)
     grad_sums = sum_dp(all_pairs)
     grad_mod_low, sums = grad_sums[:clip_count].astype(LOW), grad_sums[clip_count]
     first_gain_sum = sums[:width]
@@ -1188,7 +1187,6 @@
     k_gain_sum = sums[at + head_size : at + 2 * head_size]
     ky_gain_sum = sums[at + 2 * head_size : at + 3 * head_size]
     gate_sum = sums[at + 3 * head_size : at + 3 * head_size + head_gate.shape[0]]
-    text_all = spread(text_wide)
     grad_text_kv = (
         matmul(text_near, text_all, 0, 0)
         .reshape(-1, SPLIT, each, 2, head_size)
@@ -1229,8 +1227,8 @@
     gate_up_shard = jnp.stack(
         [joint_shard[:, :hidden_count], joint_shard[:, hidden_count : 2 * hidden_count]]
     )
-    out_shard = joint_shard[:, 2 * hidden_count :]
-    down_shard = down_low.astype(FLOAT)
+    out_shard = joint_shard[:, 3 * hidden_count :]
+    down_shard = joint_shard[:, 2 * hidden_count : 3 * hidden_count]
     return (
         output,
         grad_inputs,

time: 712 us -> 662 us (0.930)
  starting transfers between devices: 94.1 us -> 70.8 us
  local copies, waits for them, and re-layouts: 59.1 us -> 44.5 us
  waiting for transfers between devices: 312 us -> 303 us
    all_gather x2, waiting for transfers between devices: 38.6 us -> 0.34 us  [the longest x1 0.32 us: shards(): lax.all_gather(qkv_weight.transpose(1, 0, 2).reshape(weight_rows, 3 * loc...]
    reduce_scatter x3 -> x2, waiting for transfers between devices: 2.87 us -> 28.1 us  [scatter(): lax.psum_scatter(values, 'dp', scatter_dimension=0, axis_index_groups=cor...]
    ppermute x34 -> x33, waiting for transfers between devices: 122 us -> 141 us  [flip(): return lax.ppermute(values, 'dp', [(j, j ^ bit) for j in range(dp)])]
    all_to_all x1, waiting for transfers between devices: 15.4 us -> 0.01 us  [shards(): lax.all_to_all(text_tokens, 'dp', split_axis=1, concat_axis=0, tiled=True)]
    unnamed x245 -> x217, local copies, waits for them, and re-layouts: 29.3 us -> 17.1 us
    ppermute x34 -> x33, starting transfers between devices: 29.8 us -> 18.1 us  [flip(): return lax.ppermute(values, 'dp', [(j, j ^ bit) for j in range(dp)])]
    reduce_scatter x3 -> x2, starting transfers between devices: 10.8 us -> 0.21 us  [scatter(): lax.psum_scatter(values, 'dp', scatter_dimension=0, axis_index_groups=cor...]
    ppermute x18, waiting for transfers between devices: 78 us -> 87.7 us  [shift(): return lax.ppermute(values, 'dp', pairs)]
  transfers between devices with their start and end apart: 69 -> 67, of which waited for: 34 -> 37; matrix products, arithmetic and copies ran while one was open for 15% -> 15% of each run, Pallas kernels for 16% -> 18%
where the time goes in v4:
time: 662 us; the launch traced here: 652 us
  waiting for transfers between devices  303 us (46%)
  Pallas kernels  131 us (20%)
  starting transfers between devices  70.8 us (11%)
  other arithmetic  54 us (8%)
  local copies, waits for them, and re-layouts  44.5 us (7%)
  between operations  26.1 us (4%)
  matrix products  22 us (3%)
    ppermute x33, waiting for transfers between devices, flip(): return lax.ppermute(values, 'dp', [(j, j ^ bit) for j in range(dp)])  141 us
    ppermute x18, waiting for transfers between devices, shift(): return lax.ppermute(values, 'dp', pairs)  87.7 us
    pallas_call x1, Pallas kernels, attention_backward(): pl.pallas_call(functools.partial(backward_kernel, len(pairs), pick_tile(k...  53.6 us
    ppermute x10, waiting for transfers between devices, swapped(): return lax.ppermute(values, 'tensor', [(0, 1), (1, 0)])  46.3 us
    ppermute x18, starting transfers between devices, shift(): return lax.ppermute(values, 'dp', pairs)  28.8 us
    reduce_scatter x2, waiting for transfers between devices, scatter(): lax.psum_scatter(values, 'dp', scatter_dimension=0, axis_index_groups=cor...  28.1 us
    pallas_call x1, Pallas kernels, attention_forward(): pl.pallas_call(functools.partial(forward_kernel, len(pairs), pick_tile(kf...  26.1 us
    pallas_call x1, Pallas kernels, joint_outer(): pl.pallas_call(functools.partial(joint_kernel, count), grid=(count + extr...  20.4 us
  transfers between devices with their start and end apart: 67, of which 37 were waited for; matrix products, arithmetic and copies ran while one was open for 15% of the time, Pallas kernels for 18%

profile of v4, /device:TPU:0, one launch (start us, length us, event | category | flops | bytes accessed | tf_op | source)
XLA Modules:
  0.0 652.1 jit_solution(2391977896804869384)
XLA Ops:
  10.0 7.4 %all-to-all-start = ((bf16[48,16,256]{2,0,1:T(8,128)(2,1)}), bf16[48,16,256]{2,0,1:T(8,128)(2,1)S(1)}, u32[]{:S(2)}, u32[]{:S(2)}) async-start(bf16[48,16,256]{2,0,1:T(8,128)(2,1)} %bitcast.157), calls=%async_computation | async-start | bytes 786432 | tf_op jit(solution)/shard_map/all_to_all | solution.py:914
  21.1 2.2 pad_maximum_fusion.3
  25.4 6.7 %collective-permute-done.8 = f32[3,6144]{1,0:T(4,128)S(1)} collective-permute-done((f32[3,6144]{1,0:T(4,128)S(1)}, f32[3,6144]{1,0:T(4,128)S(1)}, u32[]{:S(2)}, u32[]{:S(2)}) %collective-permute-start.8) | collective-permute-done | bytes 73760 | tf_op jit(solution)/shard_map/ppermute | solution.py:823
  33.8 10.3 %collective-permute-done.9 = f32[3,6144]{1,0:T(4,128)S(1)} collective-permute-done((f32[3,6144]{1,0:T(4,128)S(1)}, f32[3,6144]{1,0:T(4,128)S(1)}, u32[]{:S(2)}, u32[]{:S(2)}) %collective-permute-start.9) | collective-permute-done | bytes 73760 | tf_op jit(solution)/shard_map/ppermute | solution.py:823
  51.6 6.3 collective-permute-done.2
  59.9 7.1 %collective-permute-done.3 = f32[4,3072]{1,0:T(4,128)S(1)} collective-permute-done((f32[4,3072]{1,0:T(4,128)S(1)}, f32[4,3072]{1,0:T(4,128)S(1)}, u32[]{:S(2)}, u32[]{:S(2)}) %collective-permute-start.3) | collective-permute-done | bytes 49184 | tf_op jit(solution)/shard_map/ppermute | solution.py:823
  67.5 2.0 collective-permute-start.4
  69.8 2.7 fusion.refs_6_
  77.3 8.7 %collective-permute-done.6 = bf16[192,1536]{1,0:T(8,128)(2,1)S(1)} collective-permute-done((bf16[192,1536]{1,0:T(8,128)(2,1)S(1)}, bf16[192,1536]{1,0:T(8,128)(2,1)S(1)}, u32[]{:S(2)}, u32[]{:S(2)}) %collective-permute-start.6) | collective-permute-done | bytes 589856 | tf_op jit(solution)/shard_map/ppermute | solution.py:823
  89.4 2.9 collective-permute-start.12
  92.8 6.1 fusion.61.qkv_ref.refs_4_
  99.0 3.3 shard_map.324
  102.4 3.8 collective-permute-done.12.refs_2_
  106.2 7.9 %collective-permute-start.14 = (bf16[1152,128]{1,0:T(8,128)(2,1)S(1)}, bf16[1152,128]{1,0:T(8,128)(2,1)S(1)}, u32[]{:S(2)}, u32[]{:S(2)}) collective-permute-start(bf16[1152,128]{1,0:T(8,128)(2,1)S(1)} %get-tuple-element.122), channel_id=1, source_target_pairs={{0,8},{2,10},{4,12},{6,14},{8,16},{10,18},{12,20},{14,22},{16,24},... | collective-permute-start | bytes 884744 | tf_op jit(solution)/shard_map/ppermute | solution.py:827
  114.1 2.7 collective-permute-start.16
  117.8 10.0 %collective-permute-done.14.refs_1_ = bf16[1152,128]{1,0:T(8,128)(2,1)S(1)} collective-permute-done((bf16[1152,128]{1,0:T(8,128)(2,1)S(1)}, bf16[1152,128]{1,0:T(8,128)(2,1)S(1)}, u32[]{:S(2)}, u32[]{:S(2)}) %collective-permute-start.14) | collective-permute-done | bytes 294944 | tf_op jit(solution)/shard_map/ppermute | solution.py:827
  127.8 12.6 %collective-permute-done.15.refs_2_ = bf16[1152,128]{1,0:T(8,128)(2,1)S(1)} collective-permute-done((bf16[1152,128]{1,0:T(8,128)(2,1)S(1)}, bf16[1152,128]{1,0:T(8,128)(2,1)S(1)}, u32[]{:S(2)}, u32[]{:S(2)}) %collective-permute-start.15) | collective-permute-done | bytes 294944 | tf_op jit(solution)/shard_map/ppermute | solution.py:827
  140.5 11.2 %collective-permute-done.16.refs_3_ = bf16[1152,128]{1,0:T(8,128)(2,1)S(1)} collective-permute-done((bf16[1152,128]{1,0:T(8,128)(2,1)S(1)}, bf16[1152,128]{1,0:T(8,128)(2,1)S(1)}, u32[]{:S(2)}, u32[]{:S(2)}) %collective-permute-start.16) | collective-permute-done | bytes 294944 | tf_op jit(solution)/shard_map/ppermute | solution.py:827
  154.4 40.6 %collective-permute-done.17.refs_1_ = bf16[3648,128]{1,0:T(8,128)(2,1)} collective-permute-done((bf16[3648,128]{1,0:T(8,128)(2,1)}, bf16[3648,128]{1,0:T(8,128)(2,1)}, u32[]{:S(2)}, u32[]{:S(2)}) %collective-permute-start.17) | collective-permute-done | bytes 933920 | tf_op jit(solution)/shard_map/ppermute | solution.py:823
  197.3 9.5 %collective-permute-done.20 = bf16[128,1536]{1,0:T(8,128)(2,1)} collective-permute-done((bf16[128,1536]{1,0:T(8,128)(2,1)S(1)}, bf16[128,1536]{1,0:T(8,128)(2,1)}, u32[]{:S(2)}, u32[]{:S(2)}) %collective-permute-start.20) | collective-permute-done | bytes 393248 | tf_op jit(solution)/shard_map/ppermute | solution.py:772
  208.5 26.1 %shard_map.327 = (bf16[384,128]{1,0:T(8,128)(2,1)}, bf16[384,128]{1,0:T(8,128)(2,1)}, bf16[384,128]{1,0:T(8,128)(2,1)}, bf16[384,128]{1,0:T(8,128)(2,1)}, f32[3072,128]{1,0:T(8,128)}, /*index=5*/f32[3072,128]{1,0:T(8,128)}) custom-call(bf16[3648,128]{1,0:T(8,128)(2,1)} %get-tuple-element.131.refs_0_, bf16[3648,128]{1,0:T(8,128)(2,1)} %collective-permute-done.17.refs_1_, ...), custom_call_target="tpu_custom_call" | custom-call | flops 1024 | bytes 1024 | tf_op jit(solution)/shard_map/pallas_call | solution.py:169
  234.6 3.4 collective-permute-start.21
  238.6 2.9 collective-permute-done.21.refs_1_
  241.5 5.3 collective-permute-done.22.refs_2_
  248.0 2.6 fusion.3
  251.7 9.7 %collective-permute-done.24 = bf16[128,1536]{1,0:T(8,128)(2,1)S(1)} collective-permute-done((bf16[128,1536]{1,0:T(8,128)(2,1)S(1)}, bf16[128,1536]{1,0:T(8,128)(2,1)S(1)}, u32[]{:S(2)}, u32[]{:S(2)}) %collective-permute-start.24) | collective-permute-done | bytes 393248 | tf_op jit(solution)/shard_map/ppermute | solution.py:772
  263.4 8.8 %collective-permute-done.25 = bf16[128,1536]{1,0:T(8,128)(2,1)S(1)} collective-permute-done((bf16[128,1536]{1,0:T(8,128)(2,1)S(1)}, bf16[128,1536]{1,0:T(8,128)(2,1)S(1)}, u32[]{:S(2)}, u32[]{:S(2)}) %collective-permute-start.25) | collective-permute-done | bytes 393248 | tf_op jit(solution)/shard_map/ppermute | solution.py:772
  273.2 14.9 %shard_map.329 = (bf16[3,256,2048]{2,1,0:T(8,128)(2,1)}, f32[128,1536]{1,0:T(8,128)S(1)}, bf16[128,1536]{1,0:T(8,128)(2,1)S(1)}, f32[128,1536]{1,0:T(8,128)S(1)}, bf16[128,1536]{1,0:T(8,128)(2,1)}) custom-call(bf16[256,1536]{1,0:T(8,128)(2,1)S(1)} %get-tuple-element.324.normed_ref, bf16[256,1536]{1,0:T(8,128)(2,1)S(1)} %pad_maximum_fusion.7.grad_ref, ...), custom_call_target="tpu_custom_call" | custom-call | flops 1024 | bytes 1024 | tf_op jit(solution)/shard_map/pallas_call | solution.py:730
  291.6 2.3 copy.116
  299.1 3.4 collective-permute-done.26
  302.5 3.0 select_reduce_fusion.3
  305.5 2.4 multiply_convert_fusion
  308.9 2.0 pad_maximum_fusion.10.left_ref
  311.8 2.3 copy.110
  316.7 2.1 collective-permute-done.27
  320.7 2.3 copy.114
  324.5 2.5 fusion.1.grad_ref
  329.6 2.8 collective-permute-start.31
  334.5 20.4 %shard_map.331 = bf16[768,6912]{1,0:T(8,128)(2,1)} custom-call(bf16[3,768,512]{2,1,0:T(8,128)(2,1)S(1)} %pad_maximum_fusion.left_ref, bf16[3,256,2048]{2,1,0:T(8,128)(2,1)S(1)} %copy-done.1, bf16[3,256,2048]{2,1,0:T(8,128)(2,1)} %collective-permute-done.35.other_ref, bf16[256,768]{1,0:T(8,128)(2,1)S(1)} %shard_map.328.own_last_ref, ...), custom_call_target="tpu_custom_call" | custom-call | flops 1024 | bytes 1024 | tf_op jit(solution)/shard_map/pallas_call | solution.py:672
  355.6 53.6 %shard_map.332 = (bf16[384,128]{1,0:T(8,128)(2,1)}, bf16[384,128]{1,0:T(8,128)(2,1)}, bf16[384,128]{1,0:T(8,128)(2,1)}, bf16[384,128]{1,0:T(8,128)(2,1)}, bf16[3...) custom-call(bf16[3648,128]{1,0:T(8,128)(2,1)} %get-tuple-element.131, ...), custom_call_target="tpu_custom_call" | custom-call | flops 1024 | bytes 1024 | tf_op jit(solution)/shard_map/pallas_call | solution.py:282
  409.9 3.5 collective-permute-done.39.refs_1_
  416.6 22.1 %collective-permute-done.40 = bf16[3,1216,128]{2,1,0:T(8,128)(2,1)S(1)} collective-permute-done((bf16[3,1216,128]{2,1,0:T(8,128)(2,1)S(1)}, bf16[3,1216,128]{2,1,0:T(8,128)(2,1)S(1)}, u32[]{:S(2)}, u32[]{:S(2)}) %collective-permute-start.40) | collective-permute-done | bytes 933920 | tf_op jit(solution)/shard_map/ppermute | solution.py:823
  440.9 1.9 collective-permute-start.43
  443.2 10.5 %collective-permute-done.41.refs_1_ = bf16[1152,128]{1,0:T(8,128)(2,1)S(1)} collective-permute-done((bf16[1152,128]{1,0:T(8,128)(2,1)S(1)}, bf16[1152,128]{1,0:T(8,128)(2,1)S(1)}, u32[]{:S(2)}, u32[]{:S(2)}) %collective-permute-start.41) | collective-permute-done | bytes 294944 | tf_op jit(solution)/shard_map/ppermute | solution.py:827
  454.4 20.1 %collective-permute-done.42.refs_2_ = bf16[1152,128]{1,0:T(8,128)(2,1)S(1)} collective-permute-done((bf16[1152,128]{1,0:T(8,128)(2,1)S(1)}, bf16[1152,128]{1,0:T(8,128)(2,1)S(1)}, u32[]{:S(2)}, u32[]{:S(2)}) %collective-permute-start.42) | collective-permute-done | bytes 294944 | tf_op jit(solution)/shard_map/ppermute | solution.py:827
  475.9 2.2 collective-permute-start.49
  478.2 4.6 collective-permute-done.47.refs_1_
  482.8 6.4 collective-permute-done.48.refs_2_
  507.0 5.2 shard_map.335
  512.2 2.2 pad_maximum_fusion.4
  514.9 5.5 fusion.62
  522.3 9.2 %collective-permute-done.44 = bf16[128,1536]{1,0:T(8,128)(2,1)S(1)} collective-permute-done((bf16[128,1536]{1,0:T(8,128)(2,1)S(1)}, bf16[128,1536]{1,0:T(8,128)(2,1)S(1)}, u32[]{:S(2)}, u32[]{:S(2)}) %collective-permute-start.44) | collective-permute-done | bytes 393248 | tf_op jit(solution)/shard_map/ppermute | solution.py:772
  531.5 2.1 slice_add_fusion.2
  533.6 5.2 shard_map.336
  538.8 3.0 pad_maximum_fusion.1
  541.8 6.9 %reduce-scatter.3.cloned.1.call-done = bf16[96,6912]{1,0:T(8,128)(2,1)} async-done(((bf16[768,6912]{1,0:T(8,128)(2,1)}), bf16[96,6912]{1,0:T(8,128)(2,1)}) %reduce-scatter.3.cloned.1.call-update) | async-done | bytes 1327120 | tf_op jit(solution)/shard_map/reduce_scatter | solution.py:890
  548.9 4.6 select_reduce_fusion.1
  572.4 2.6 collective-permute-done.52
  575.0 9.8 %collective-permute-done.55 = f32[4,9216]{1,0:T(4,128)S(1)} collective-permute-done((f32[4,9216]{1,0:T(4,128)S(1)}, f32[4,9216]{1,0:T(4,128)S(1)}, u32[]{:S(2)}, u32[]{:S(2)}) %collective-permute-start.55) | collective-permute-done | bytes 147488 | tf_op jit(solution)/shard_map/ppermute | solution.py:823
  585.8 5.1 all-to-all-start.1
  591.0 13.3 %collective-permute-done.56 = f32[4,9216]{1,0:T(4,128)S(1)} collective-permute-done((f32[4,9216]{1,0:T(4,128)S(1)}, f32[4,9216]{1,0:T(4,128)S(1)}, u32[]{:S(2)}, u32[]{:S(2)}) %collective-permute-start.56) | collective-permute-done | bytes 147488 | tf_op jit(solution)/shard_map/ppermute | solution.py:823
  612.2 3.0 collective-permute-done.59
  615.9 4.0 collective-permute-done.60
  621.3 21.1 %reduce-scatter.5.cloned.1.call-done = bf16[96,2304]{1,0:T(8,128)(2,1)} async-done(((bf16[768,2304]{1,0:T(8,128)(2,1)}), bf16[96,2304]{1,0:T(8,128)(2,1)}) %reduce-scatter.5.cloned.1.call-update) | async-done | bytes 442384 | tf_op jit(solution)/shard_map/reduce_scatter | solution.py:890
  (471 shorter events, 114.7 us)
Async XLA Ops:
  7.2 79.4 %all-gather.3.cloned.1.call-start = ((), (), s32[]{:S(2)}) async-start(), calls=%async_computation.4 | async-start | bytes 7520256 | tf_op jit(solution)/shard_map/all_gather | solution.py:894
  10.0 23.8 %all-to-all-start = ((bf16[48,16,256]{2,0,1:T(8,128)(2,1)}), bf16[48,16,256]{2,0,1:T(8,128)(2,1)S(1)}, u32[]{:S(2)}, u32[]{:S(2)}) async-start(bf16[48,16,256]{2,0,1:T(8,128)(2,1)} %bitcast.157), calls=%async_computation | async-start | bytes 786432 | tf_op jit(solution)/shard_map/all_to_all | solution.py:914
  17.4 230.6 %all-gather.5.cloned.1.call-start = ((), (), s32[]{:S(2)}) async-start(), calls=%async_computation.5 | async-start | bytes 22560768 | tf_op jit(solution)/shard_map/all_gather | solution.py:1014
  17.8 5.8 collective-permute-start.7
  23.7 8.5 %collective-permute-start.8 = (f32[3,6144]{1,0:T(4,128)S(1)}, f32[3,6144]{1,0:T(4,128)S(1)}, u32[]{:S(2)}, u32[]{:S(2)}) collective-permute-start(f32[3,6144]{1,0:T(4,128)S(1)} %add.425), channel_id=1, source_target_pairs={{0,4},{2,6},{4,0},{6,2},{8,12},{10,14},{12,8},{14,10},{16,20},{18,... | collective-permute-start | bytes 221192 | tf_op jit(solution)/shard_map/ppermute | solution.py:823
  32.2 11.9 %collective-permute-start.9 = (f32[3,6144]{1,0:T(4,128)S(1)}, f32[3,6144]{1,0:T(4,128)S(1)}, u32[]{:S(2)}, u32[]{:S(2)}) collective-permute-start(f32[3,6144]{1,0:T(4,128)S(1)} %add.426), channel_id=1, source_target_pairs={{0,8},{2,10},{4,12},{6,14},{8,0},{10,2},{12,4},{14,6},{16,24},{18,... | collective-permute-start | bytes 221192 | tf_op jit(solution)/shard_map/ppermute | solution.py:823
  33.8 11.0 %collective-permute-start = (f32[4,3072]{1,0:T(4,128)S(1)}, f32[4,3072]{1,0:T(4,128)S(1)}, u32[]{:S(2)}, u32[]{:S(2)}) collective-permute-start(f32[4,3072]{1,0:T(4,128)S(1)} %pad_maximum_fusion.18), channel_id=1, source_target_pairs={{0,2},{2,0},{4,6},{6,4},{8,10},{10,8},{12,14},{14,12},{16,18},{18,... | collective-permute-start | bytes 147464 | tf_op jit(solution)/shard_map/ppermute | solution.py:823
  44.1 6.6 %collective-permute-start.10 = (f32[3,6144]{1,0:T(4,128)S(1)}, f32[3,6144]{1,0:T(4,128)S(1)}, u32[]{:S(2)}, u32[]{:S(2)}) collective-permute-start(f32[3,6144]{1,0:T(4,128)S(1)} %add.427), channel_id=1, source_target_pairs={{0,16},{2,18},{4,20},{6,22},{8,24},{10,26},{12,28},{14,30},{16,0},... | collective-permute-start | bytes 221192 | tf_op jit(solution)/shard_map/ppermute | solution.py:823
  44.8 6.0 collective-permute-start.1
  50.8 7.1 %collective-permute-start.2 = (f32[4,3072]{1,0:T(4,128)S(1)}, f32[4,3072]{1,0:T(4,128)S(1)}, u32[]{:S(2)}, u32[]{:S(2)}) collective-permute-start(f32[4,3072]{1,0:T(4,128)S(1)} %add.410), channel_id=1, source_target_pairs={{0,8},{2,10},{4,12},{6,14},{8,0},{10,2},{12,4},{14,6},{16,24},{18,... | collective-permute-start | bytes 147464 | tf_op jit(solution)/shard_map/ppermute | solution.py:823
  57.9 9.0 %collective-permute-start.3 = (f32[4,3072]{1,0:T(4,128)S(1)}, f32[4,3072]{1,0:T(4,128)S(1)}, u32[]{:S(2)}, u32[]{:S(2)}) collective-permute-start(f32[4,3072]{1,0:T(4,128)S(1)} %add.411), channel_id=1, source_target_pairs={{0,16},{2,18},{4,20},{6,22},{8,24},{10,26},{12,28},{14,30},{16,0},... | collective-permute-start | bytes 147464 | tf_op jit(solution)/shard_map/ppermute | solution.py:823
  59.8 12.8 %collective-permute-start.5 = (bf16[384,1536]{1,0:T(8,128)(2,1)S(1)}, bf16[384,1536]{1,0:T(8,128)(2,1)S(1)}, u32[]{:S(2)}, u32[]{:S(2)}) collective-permute-start(bf16[384,1536]{1,0:T(8,128)(2,1)S(1)} %slice.297), channel_id=1, source_target_pairs={{0,2},{2,0},{4,6},{6,4},{8,10},{10,8},{12,14},{14,12},{16,18},{18,... | collective-permute-start | bytes 3538952 | tf_op jit(solution)/shard_map/ppermute | solution.py:823
  67.5 8.9 %collective-permute-start.4 = (bf16[128,1536]{1,0:T(8,128)(2,1)S(1)}, bf16[128,1536]{1,0:T(8,128)(2,1)S(1)}, u32[]{:S(2)}, u32[]{:S(2)}) collective-permute-start(bf16[128,1536]{1,0:T(8,128)(2,1)S(1)} %fusion.10), channel_id=1, source_target_pairs={{0,1},{1,0},{2,3},{3,2},{4,5},{5,4},{6,7},{7,6},{8,9},{9,8},{10,11... | collective-permute-start | bytes 1179656 | tf_op jit(solution)/shard_map/ppermute | solution.py:772
  73.0 13.1 %collective-permute-start.6 = (bf16[192,1536]{1,0:T(8,128)(2,1)S(1)}, bf16[192,1536]{1,0:T(8,128)(2,1)S(1)}, u32[]{:S(2)}, u32[]{:S(2)}) collective-permute-start(bf16[192,1536]{1,0:T(8,128)(2,1)S(1)} %slice.298), channel_id=1, source_target_pairs={{0,4},{2,6},{4,0},{6,2},{8,12},{10,14},{12,8},{14,10},{16,20},{18,... | collective-permute-start | bytes 1769480 | tf_op jit(solution)/shard_map/ppermute | solution.py:823
  86.6 462.2 %reduce-scatter.3.cloned.1.call-start = ((), (), s32[]{:S(2)}) async-start(), calls=%async_computation.6 | async-start | bytes 11943936 | tf_op jit(solution)/shard_map/reduce_scatter | solution.py:890
  88.9 13.5 %collective-permute-start.11 = (bf16[192,384]{1,0:T(8,128)(2,1)S(1)}, bf16[192,384]{1,0:T(8,128)(2,1)S(1)}, u32[]{:S(2)}, u32[]{:S(2)}) collective-permute-start(bf16[192,384]{1,0:T(8,128)(2,1)S(1)} %get-tuple-element.118), channel_id=1, source_target_pairs={{0,8},{2,10},{4,12},{6,14},{8,16},{10,18},{12,20},{14,22},{16,24},... | collective-permute-start | bytes 442376 | tf_op jit(solution)/shard_map/ppermute | solution.py:827
  89.4 16.8 %collective-permute-start.12 = (bf16[192,384]{1,0:T(8,128)(2,1)S(1)}, bf16[192,384]{1,0:T(8,128)(2,1)S(1)}, u32[]{:S(2)}, u32[]{:S(2)}) collective-permute-start(bf16[192,384]{1,0:T(8,128)(2,1)S(1)} %get-tuple-element.119), channel_id=1, source_target_pairs={{0,16},{2,18},{4,20},{6,22},{8,24},{10,26},{12,28},{14,30},{16,0},... | collective-permute-start | bytes 442376 | tf_op jit(solution)/shard_map/ppermute | solution.py:827
  92.3 13.9 %collective-permute-start.13 = (bf16[192,384]{1,0:T(8,128)(2,1)S(1)}, bf16[192,384]{1,0:T(8,128)(2,1)S(1)}, u32[]{:S(2)}, u32[]{:S(2)}) collective-permute-start(bf16[192,384]{1,0:T(8,128)(2,1)S(1)} %get-tuple-element.120), channel_id=1, source_target_pairs={{0,24},{2,26},{4,28},{6,30},{8,0},{10,2},{12,4},{14,6},{16,8},{18,... | collective-permute-start | bytes 442376 | tf_op jit(solution)/shard_map/ppermute | solution.py:827
  106.2 21.6 %collective-permute-start.14 = (bf16[1152,128]{1,0:T(8,128)(2,1)S(1)}, bf16[1152,128]{1,0:T(8,128)(2,1)S(1)}, u32[]{:S(2)}, u32[]{:S(2)}) collective-permute-start(bf16[1152,128]{1,0:T(8,128)(2,1)S(1)} %get-tuple-element.122), channel_id=1, source_target_pairs={{0,8},{2,10},{4,12},{6,14},{8,16},{10,18},{12,20},{14,22},{16,24},... | collective-permute-start | bytes 884744 | tf_op jit(solution)/shard_map/ppermute | solution.py:827
  114.1 26.3 %collective-permute-start.15 = (bf16[1152,128]{1,0:T(8,128)(2,1)S(1)}, bf16[1152,128]{1,0:T(8,128)(2,1)S(1)}, u32[]{:S(2)}, u32[]{:S(2)}) collective-permute-start(bf16[1152,128]{1,0:T(8,128)(2,1)S(1)} %get-tuple-element.123), channel_id=1, source_target_pairs={{0,16},{2,18},{4,20},{6,22},{8,24},{10,26},{12,28},{14,30},{16,0},... | collective-permute-start | bytes 884744 | tf_op jit(solution)/shard_map/ppermute | solution.py:827
  114.1 37.5 %collective-permute-start.16 = (bf16[1152,128]{1,0:T(8,128)(2,1)S(1)}, bf16[1152,128]{1,0:T(8,128)(2,1)S(1)}, u32[]{:S(2)}, u32[]{:S(2)}) collective-permute-start(bf16[1152,128]{1,0:T(8,128)(2,1)S(1)} %get-tuple-element.124), channel_id=1, source_target_pairs={{0,24},{2,26},{4,28},{6,30},{8,0},{10,2},{12,4},{14,6},{16,8},{18,... | collective-permute-start | bytes 884744 | tf_op jit(solution)/shard_map/ppermute | solution.py:827
  152.8 42.2 %collective-permute-start.17 = (bf16[3648,128]{1,0:T(8,128)(2,1)}, bf16[3648,128]{1,0:T(8,128)(2,1)}, u32[]{:S(2)}, u32[]{:S(2)}) collective-permute-start(bf16[3648,128]{1,0:T(8,128)(2,1)} %get-tuple-element.131.refs_0_), channel_id=1, source_target_pairs={{0,4},{2,6},{4,0},{6,2},{8,12},{10,14},{12,8},{14,10},{16,20},{18,... | collective-permute-start | bytes 2801672 | tf_op jit(solution)/shard_map/ppermute | solution.py:823
  154.3 53.5 %collective-permute-start.18 = (bf16[3648,128]{1,0:T(8,128)(2,1)}, bf16[3648,128]{1,0:T(8,128)(2,1)}, u32[]{:S(2)}, u32[]{:S(2)}) collective-permute-start(bf16[3648,128]{1,0:T(8,128)(2,1)} %get-tuple-element.131.refs_0_), channel_id=1, source_target_pairs={{0,2},{2,0},{4,6},{6,4},{8,10},{10,8},{12,14},{14,12},{16,18},{18,... | collective-permute-start | bytes 2801672 | tf_op jit(solution)/shard_map/ppermute | solution.py:823
  195.0 12.8 %collective-permute-start.19 = (bf16[3648,128]{1,0:T(8,128)(2,1)}, bf16[3648,128]{1,0:T(8,128)(2,1)}, u32[]{:S(2)}, u32[]{:S(2)}) collective-permute-start(bf16[3648,128]{1,0:T(8,128)(2,1)} %collective-permute-done.17.refs_1_), channel_id=1, source_target_pairs={{0,2},{2,0},{4,6},{6,4},{8,10},{10,8},{12,14},{14,12},{16,18},{18,... | collective-permute-start | bytes 2801672 | tf_op jit(solution)/shard_map/ppermute | solution.py:823
  195.1 11.7 %collective-permute-start.20 = (bf16[128,1536]{1,0:T(8,128)(2,1)S(1)}, bf16[128,1536]{1,0:T(8,128)(2,1)}, u32[]{:S(2)}, u32[]{:S(2)}) collective-permute-start(bf16[128,1536]{1,0:T(8,128)(2,1)S(1)} %fusion.12), channel_id=1, source_target_pairs={{0,1},{1,0},{2,3},{3,2},{4,5},{5,4},{6,7},{7,6},{8,9},{9,8},{10,11... | collective-permute-start | bytes 1179656 | tf_op jit(solution)/shard_map/ppermute | solution.py:772
  234.6 6.9 %collective-permute-start.21 = (bf16[384,128]{1,0:T(8,128)(2,1)}, bf16[384,128]{1,0:T(8,128)(2,1)S(1)}, u32[]{:S(2)}, u32[]{:S(2)}) collective-permute-start(bf16[384,128]{1,0:T(8,128)(2,1)} %get-tuple-element.139), channel_id=1, source_target_pairs={{0,24},{2,26},{4,28},{6,30},{8,0},{10,2},{12,4},{14,6},{16,8},{18,... | collective-permute-start | bytes 294920 | tf_op jit(solution)/shard_map/ppermute | solution.py:827
  238.0 8.9 %collective-permute-start.22 = (bf16[384,128]{1,0:T(8,128)(2,1)}, bf16[384,128]{1,0:T(8,128)(2,1)S(1)}, u32[]{:S(2)}, u32[]{:S(2)}) collective-permute-start(bf16[384,128]{1,0:T(8,128)(2,1)} %get-tuple-element.140), channel_id=1, source_target_pairs={{0,16},{2,18},{4,20},{6,22},{8,24},{10,26},{12,28},{14,30},{16,0},... | collective-permute-start | bytes 294920 | tf_op jit(solution)/shard_map/ppermute | solution.py:827
  238.0 8.9 %collective-permute-start.23 = (bf16[384,128]{1,0:T(8,128)(2,1)}, bf16[384,128]{1,0:T(8,128)(2,1)S(1)}, u32[]{:S(2)}, u32[]{:S(2)}) collective-permute-start(bf16[384,128]{1,0:T(8,128)(2,1)} %get-tuple-element.141), channel_id=1, source_target_pairs={{0,8},{2,10},{4,12},{6,14},{8,16},{10,18},{12,20},{14,22},{16,24},... | collective-permute-start | bytes 294920 | tf_op jit(solution)/shard_map/ppermute | solution.py:827
  250.7 10.7 %collective-permute-start.24 = (bf16[128,1536]{1,0:T(8,128)(2,1)S(1)}, bf16[128,1536]{1,0:T(8,128)(2,1)S(1)}, u32[]{:S(2)}, u32[]{:S(2)}) collective-permute-start(bf16[128,1536]{1,0:T(8,128)(2,1)S(1)} %slice.300), channel_id=1, source_target_pairs={{0,1},{1,0},{2,3},{3,2},{4,5},{5,4},{6,7},{7,6},{8,9},{9,8},{10,11... | collective-permute-start | bytes 1179656 | tf_op jit(solution)/shard_map/ppermute | solution.py:772
  262.5 9.8 %collective-permute-start.25 = (bf16[128,1536]{1,0:T(8,128)(2,1)S(1)}, bf16[128,1536]{1,0:T(8,128)(2,1)S(1)}, u32[]{:S(2)}, u32[]{:S(2)}) collective-permute-start(bf16[128,1536]{1,0:T(8,128)(2,1)S(1)} %fusion.16), channel_id=1, source_target_pairs={{0,1},{1,0},{2,3},{3,2},{4,5},{5,4},{6,7},{7,6},{8,9},{9,8},{10,11... | collective-permute-start | bytes 1179656 | tf_op jit(solution)/shard_map/ppermute | solution.py:772
  290.6 42.2 %collective-permute-start.35 = (bf16[3,256,2048]{2,1,0:T(8,128)(2,1)}, bf16[3,256,2048]{2,1,0:T(8,128)(2,1)}, u32[]{:S(2)}, u32[]{:S(2)}) collective-permute-start(bf16[3,256,2048]{2,1,0:T(8,128)(2,1)} %get-tuple-element.154.own_ref), channel_id=1, source_target_pairs={{0,2},{2,0},{4,6},{6,4},{8,10},{10,8},{12,14},{14,12},{16,18},{18,... | collective-permute-start | bytes 9437192 | tf_op jit(solution)/shard_map/ppermute | solution.py:823
  290.7 11.8 %collective-permute-start.26 = (bf16[128,1536]{1,0:T(8,128)(2,1)}, bf16[128,1536]{1,0:T(8,128)(2,1)}, u32[]{:S(2)}, u32[]{:S(2)}) collective-permute-start(bf16[128,1536]{1,0:T(8,128)(2,1)} %get-tuple-element.146), channel_id=1, source_target_pairs={{0,1},{1,0},{2,3},{3,2},{4,5},{5,4},{6,7},{7,6},{8,9},{9,8},{10,11... | collective-permute-start | bytes 1179656 | tf_op jit(solution)/shard_map/ppermute | solution.py:772
  296.0 12.9 %collective-permute-start.37 = (bf16[768,256]{1,0:T(8,128)(2,1)}, bf16[768,256]{1,0:T(8,128)(2,1)}, u32[]{:S(2)}, u32[]{:S(2)}) collective-permute-start(bf16[768,256]{1,0:T(8,128)(2,1)} %get-tuple-element.320), channel_id=1, source_target_pairs={{0,2},{2,0},{4,6},{6,4},{8,10},{10,8},{12,14},{14,12},{16,18},{18,... | collective-permute-start | bytes 1179656 | tf_op jit(solution)/shard_map/ppermute | solution.py:823
  298.8 12.1 %collective-permute-start.33 = (bf16[768,256]{1,0:T(8,128)(2,1)S(1)}, bf16[768,256]{1,0:T(8,128)(2,1)S(1)}, u32[]{:S(2)}, u32[]{:S(2)}) collective-permute-start(bf16[768,256]{1,0:T(8,128)(2,1)S(1)} %get-tuple-element.326), channel_id=1, source_target_pairs={{0,2},{2,0},{4,6},{6,4},{8,10},{10,8},{12,14},{14,12},{16,18},{18,... | collective-permute-start | bytes 1179656 | tf_op jit(solution)/shard_map/ppermute | solution.py:823
  308.0 10.9 %collective-permute-start.27 = (bf16[128,1536]{1,0:T(8,128)(2,1)S(1)}, bf16[128,1536]{1,0:T(8,128)(2,1)}, u32[]{:S(2)}, u32[]{:S(2)}) collective-permute-start(bf16[128,1536]{1,0:T(8,128)(2,1)S(1)} %get-tuple-element.310), channel_id=1, source_target_pairs={{0,1},{1,0},{2,3},{3,2},{4,5},{5,4},{6,7},{7,6},{8,9},{9,8},{10,11... | collective-permute-start | bytes 1179656 | tf_op jit(solution)/shard_map/ppermute | solution.py:772
  310.8 22.0 %collective-permute-start.36 = (bf16[256,768]{1,0:T(8,128)(2,1)S(1)}, bf16[256,768]{1,0:T(8,128)(2,1)S(1)}, u32[]{:S(2)}, u32[]{:S(2)}) collective-permute-start(bf16[256,768]{1,0:T(8,128)(2,1)S(1)} %shard_map.328.own_last_ref), channel_id=1, source_target_pairs={{0,2},{2,0},{4,6},{6,4},{8,10},{10,8},{12,14},{14,12},{16,18},{18,... | collective-permute-start | bytes 1179656 | tf_op jit(solution)/shard_map/ppermute | solution.py:823
  316.2 10.8 %collective-permute-start.32 = (bf16[768,256]{1,0:T(8,128)(2,1)}, bf16[768,256]{1,0:T(8,128)(2,1)}, u32[]{:S(2)}, u32[]{:S(2)}) collective-permute-start(bf16[768,256]{1,0:T(8,128)(2,1)} %get-tuple-element.322), channel_id=1, source_target_pairs={{0,2},{2,0},{4,6},{6,4},{8,10},{10,8},{12,14},{14,12},{16,18},{18,... | collective-permute-start | bytes 1179656 | tf_op jit(solution)/shard_map/ppermute | solution.py:823
  324.4 5.3 collective-permute-start.34
  328.3 26.6 %collective-permute-start.29 = (bf16[384,128]{1,0:T(8,128)(2,1)S(1)}, bf16[384,128]{1,0:T(8,128)(2,1)S(1)}, u32[]{:S(2)}, u32[]{:S(2)}) collective-permute-start(bf16[384,128]{1,0:T(8,128)(2,1)S(1)} %get-tuple-element.151), channel_id=1, source_target_pairs={{0,8},{2,10},{4,12},{6,14},{8,16},{10,18},{12,20},{14,22},{16,24},... | collective-permute-start | bytes 294920 | tf_op jit(solution)/shard_map/ppermute | solution.py:827
  328.3 26.5 %collective-permute-start.30 = (bf16[384,128]{1,0:T(8,128)(2,1)S(1)}, bf16[384,128]{1,0:T(8,128)(2,1)}, u32[]{:S(2)}, u32[]{:S(2)}) collective-permute-start(bf16[384,128]{1,0:T(8,128)(2,1)S(1)} %get-tuple-element.152), channel_id=1, source_target_pairs={{0,16},{2,18},{4,20},{6,22},{8,24},{10,26},{12,28},{14,30},{16,0},... | collective-permute-start | bytes 294920 | tf_op jit(solution)/shard_map/ppermute | solution.py:827
  329.6 25.2 %collective-permute-start.31 = (bf16[384,128]{1,0:T(8,128)(2,1)S(1)}, bf16[384,128]{1,0:T(8,128)(2,1)}, u32[]{:S(2)}, u32[]{:S(2)}) collective-permute-start(bf16[384,128]{1,0:T(8,128)(2,1)S(1)} %get-tuple-element.153), channel_id=1, source_target_pairs={{0,24},{2,26},{4,28},{6,30},{8,0},{10,2},{12,4},{14,6},{16,8},{18,... | collective-permute-start | bytes 294920 | tf_op jit(solution)/shard_map/ppermute | solution.py:827
  355.5 287.0 %reduce-scatter.5.cloned.1.call-start = ((), (), s32[]{:S(2)}) async-start(), calls=%async_computation.7 | async-start | bytes 3981312 | tf_op jit(solution)/shard_map/reduce_scatter | solution.py:890
  409.3 5.1 collective-permute-start.38
  409.4 4.0 collective-permute-start.39
  415.8 22.8 %collective-permute-start.40 = (bf16[3,1216,128]{2,1,0:T(8,128)(2,1)S(1)}, bf16[3,1216,128]{2,1,0:T(8,128)(2,1)S(1)}, u32[]{:S(2)}, u32[]{:S(2)}) collective-permute-start(bf16[3,1216,128]{2,1,0:T(8,128)(2,1)S(1)} %pad_maximum_fusion.5), channel_id=1, source_target_pairs={{0,4},{2,6},{4,0},{6,2},{8,12},{10,14},{12,8},{14,10},{16,20},{18,... | collective-permute-start | bytes 2801672 | tf_op jit(solution)/shard_map/ppermute | solution.py:823
  439.1 14.6 %collective-permute-start.41 = (bf16[1152,128]{1,0:T(8,128)(2,1)S(1)}, bf16[1152,128]{1,0:T(8,128)(2,1)S(1)}, u32[]{:S(2)}, u32[]{:S(2)}) collective-permute-start(bf16[1152,128]{1,0:T(8,128)(2,1)S(1)} %get-tuple-element.170), channel_id=1, source_target_pairs={{0,24},{2,26},{4,28},{6,30},{8,0},{10,2},{12,4},{14,6},{16,8},{18,... | collective-permute-start | bytes 884744 | tf_op jit(solution)/shard_map/ppermute | solution.py:827
  439.5 35.1 %collective-permute-start.42 = (bf16[1152,128]{1,0:T(8,128)(2,1)S(1)}, bf16[1152,128]{1,0:T(8,128)(2,1)S(1)}, u32[]{:S(2)}, u32[]{:S(2)}) collective-permute-start(bf16[1152,128]{1,0:T(8,128)(2,1)S(1)} %get-tuple-element.171), channel_id=1, source_target_pairs={{0,16},{2,18},{4,20},{6,22},{8,24},{10,26},{12,28},{14,30},{16,0},... | collective-permute-start | bytes 884744 | tf_op jit(solution)/shard_map/ppermute | solution.py:827
  440.9 34.3 %collective-permute-start.43 = (bf16[1152,128]{1,0:T(8,128)(2,1)S(1)}, bf16[1152,128]{1,0:T(8,128)(2,1)S(1)}, u32[]{:S(2)}, u32[]{:S(2)}) collective-permute-start(bf16[1152,128]{1,0:T(8,128)(2,1)S(1)} %get-tuple-element.172), channel_id=1, source_target_pairs={{0,8},{2,10},{4,12},{6,14},{8,16},{10,18},{12,20},{14,22},{16,24},... | collective-permute-start | bytes 884744 | tf_op jit(solution)/shard_map/ppermute | solution.py:827
  475.9 6.9 %collective-permute-start.47 = (bf16[192,384]{1,0:T(8,128)(2,1)S(1)}, bf16[192,384]{1,0:T(8,128)(2,1)S(1)}, u32[]{:S(2)}, u32[]{:S(2)}) collective-permute-start(bf16[192,384]{1,0:T(8,128)(2,1)S(1)} %get-tuple-element.187.refs_0_), channel_id=1, source_target_pairs={{0,24},{2,26},{4,28},{6,30},{8,0},{10,2},{12,4},{14,6},{16,8},{18,... | collective-permute-start | bytes 442376 | tf_op jit(solution)/shard_map/ppermute | solution.py:827
  475.9 13.3 %collective-permute-start.48 = (bf16[192,384]{1,0:T(8,128)(2,1)S(1)}, bf16[192,384]{1,0:T(8,128)(2,1)S(1)}, u32[]{:S(2)}, u32[]{:S(2)}) collective-permute-start(bf16[192,384]{1,0:T(8,128)(2,1)S(1)} %get-tuple-element.187.refs_0_), channel_id=1, source_target_pairs={{0,16},{2,18},{4,20},{6,22},{8,24},{10,26},{12,28},{14,30},{16,0},... | collective-permute-start | bytes 442376 | tf_op jit(solution)/shard_map/ppermute | solution.py:827
  475.9 13.3 %collective-permute-start.49 = (bf16[192,384]{1,0:T(8,128)(2,1)S(1)}, bf16[192,384]{1,0:T(8,128)(2,1)S(1)}, u32[]{:S(2)}, u32[]{:S(2)}) collective-permute-start(bf16[192,384]{1,0:T(8,128)(2,1)S(1)} %get-tuple-element.187.refs_0_), channel_id=1, source_target_pairs={{0,8},{2,10},{4,12},{6,14},{8,16},{10,18},{12,20},{14,22},{16,24},... | collective-permute-start | bytes 442376 | tf_op jit(solution)/shard_map/ppermute | solution.py:827
  489.3 22.9 %collective-permute-start.50 = (bf16[192,1536]{1,0:T(8,128)(2,1)S(1)}, bf16[192,1536]{1,0:T(8,128)(2,1)}, u32[]{:S(2)}, u32[]{:S(2)}) collective-permute-start(bf16[192,1536]{1,0:T(8,128)(2,1)S(1)} %shard_map.337), channel_id=1, source_target_pairs={{0,4},{2,6},{4,0},{6,2},{8,12},{10,14},{12,8},{14,10},{16,20},{18,... | collective-permute-start | bytes 1769480 | tf_op jit(solution)/shard_map/ppermute | solution.py:823
  500.8 48.0 %collective-permute-start.28 = (bf16[128,1536]{1,0:T(8,128)(2,1)}, bf16[128,1536]{1,0:T(8,128)(2,1)}, u32[]{:S(2)}, u32[]{:S(2)}) collective-permute-start(bf16[128,1536]{1,0:T(8,128)(2,1)} %copy-done.27), channel_id=1, source_target_pairs={{0,1},{1,0},{2,3},{3,2},{4,5},{5,4},{6,7},{7,6},{8,9},{9,8},{10,11... | collective-permute-start | bytes 1179656 | tf_op jit(solution)/shard_map/ppermute | solution.py:772
  512.2 21.4 %collective-permute-start.45 = (bf16[1,256,2304]{2,1,0:T(8,128)(2,1)}, bf16[1,256,2304]{2,1,0:T(8,128)(2,1)S(1)}, u32[]{:S(2)}, u32[]{:S(2)}) collective-permute-start(bf16[1,256,2304]{2,1,0:T(8,128)(2,1)} %bitcast.69.own_ref), channel_id=1, source_target_pairs={{0,2},{2,0},{4,6},{6,4},{8,10},{10,8},{12,14},{14,12},{16,18},{18,... | collective-permute-start | bytes 3538952 | tf_op jit(solution)/shard_map/ppermute | solution.py:823
  514.3 24.5 %collective-permute-start.51 = (bf16[384,1536]{1,0:T(8,128)(2,1)}, bf16[384,1536]{1,0:T(8,128)(2,1)}, u32[]{:S(2)}, u32[]{:S(2)}) collective-permute-start(bf16[384,1536]{1,0:T(8,128)(2,1)} %pad_maximum_fusion.4), channel_id=1, source_target_pairs={{0,2},{2,0},{4,6},{6,4},{8,10},{10,8},{12,14},{14,12},{16,18},{18,... | collective-permute-start | bytes 3538952 | tf_op jit(solution)/shard_map/ppermute | solution.py:823
  520.4 11.1 %collective-permute-start.44 = (bf16[128,1536]{1,0:T(8,128)(2,1)S(1)}, bf16[128,1536]{1,0:T(8,128)(2,1)S(1)}, u32[]{:S(2)}, u32[]{:S(2)}) collective-permute-start(bf16[128,1536]{1,0:T(8,128)(2,1)S(1)} %slice.299), channel_id=1, source_target_pairs={{0,1},{1,0},{2,3},{3,2},{4,5},{5,4},{6,7},{7,6},{8,9},{9,8},{10,11... | collective-permute-start | bytes 1179656 | tf_op jit(solution)/shard_map/ppermute | solution.py:772
  555.0 7.3 %collective-permute-start.46 = (f32[4,9216]{1,0:T(4,128)S(1)}, f32[4,9216]{1,0:T(4,128)S(1)}, u32[]{:S(2)}, u32[]{:S(2)}) collective-permute-start(f32[4,9216]{1,0:T(4,128)S(1)} %pad_maximum_fusion.13), channel_id=1, source_target_pairs={{0,1},{1,0},{2,3},{3,2},{4,5},{5,4},{6,7},{7,6},{8,9},{9,8},{10,11... | collective-permute-start | bytes 442376 | tf_op jit(solution)/shard_map/ppermute | solution.py:772
  564.4 10.6 %collective-permute-start.52 = (bf16[768,256]{1,0:T(8,128)(2,1)S(1)}, bf16[768,256]{1,0:T(8,128)(2,1)S(1)}, u32[]{:S(2)}, u32[]{:S(2)}) collective-permute-start(bf16[768,256]{1,0:T(8,128)(2,1)S(1)} %convolution_convert_fusion), channel_id=1, source_target_pairs={{0,1},{1,0},{2,3},{3,2},{4,5},{5,4},{6,7},{7,6},{8,9},{9,8},{10,11... | collective-permute-start | bytes 1179656 | tf_op jit(solution)/shard_map/ppermute | solution.py:772
  566.2 6.0 collective-permute-start.54
  572.2 12.6 %collective-permute-start.55 = (f32[4,9216]{1,0:T(4,128)S(1)}, f32[4,9216]{1,0:T(4,128)S(1)}, u32[]{:S(2)}, u32[]{:S(2)}) collective-permute-start(f32[4,9216]{1,0:T(4,128)S(1)} %add.494), channel_id=1, source_target_pairs={{0,8},{2,10},{4,12},{6,14},{8,0},{10,2},{12,4},{14,6},{16,24},{18,... | collective-permute-start | bytes 442376 | tf_op jit(solution)/shard_map/ppermute | solution.py:823
  584.9 19.3 %collective-permute-start.56 = (f32[4,9216]{1,0:T(4,128)S(1)}, f32[4,9216]{1,0:T(4,128)S(1)}, u32[]{:S(2)}, u32[]{:S(2)}) collective-permute-start(f32[4,9216]{1,0:T(4,128)S(1)} %add.495), channel_id=1, source_target_pairs={{0,16},{2,18},{4,20},{6,22},{8,24},{10,26},{12,28},{14,30},{16,0},... | collective-permute-start | bytes 442376 | tf_op jit(solution)/shard_map/ppermute | solution.py:823
  585.8 34.7 %all-to-all-start.1 = ((bf16[16,48,256]{2,1,0:T(8,128)(2,1)}), bf16[16,48,256]{2,1,0:T(8,128)(2,1)S(1)}, u32[]{:S(2)}, u32[]{:S(2)}) async-start(bf16[16,48,256]{2,1,0:T(8,128)(2,1)} %bitcast.77), calls=%async_computation.2 | async-start | bytes 786432 | tf_op jit(solution)/shard_map/all_to_all | solution.py:1208
  607.6 3.8 collective-permute-start.58
  615.2 4.6 collective-permute-start.60
  (109 other events, 1253.5 us)
Sparse Core Ops, SparseCore 0:
  10.9 75.6 all-gather.2
  88.8 145.1 all-gather.4
  355.0 193.7 reduce-scatter.2
  552.7 89.6 reduce-scatter.4

commit v5 on v4

--- a/solution.py
+++ b/solution.py
@@ -13,7 +13,6 @@
 EPS = 1e-06
 MASK = -1e4
 FORWARD_SLOTS = 4
-BACKWARD_SLOTS = 4
 LOW = jnp.bfloat16
 FLOAT = jnp.float32
 MIB = 1024 * 1024
@@ -167,7 +166,7 @@
     folded = jax.ShapeDtypeStruct((heads * half, 128), LOW)
     wide = jax.ShapeDtypeStruct((heads * rows, 128), FLOAT)
     out = pl.pallas_call(
-        functools.partial(forward_kernel, len(pairs), pick_tile(kf.shape[0], 1024)),
+        functools.partial(forward_kernel, len(pairs), pick_tile(kf.shape[0], 2048)),
         grid=(heads,),
         in_specs=attention_specs(pairs, queries, qf, kf, tf),
         out_specs=[pl.BlockSpec((half, 128), lambda i: (i, 0))] * SPLIT
@@ -195,10 +194,8 @@
     )
     for index, ref in enumerate(grad_refs):
         grad_hold[index] = ref[...]
-    acc[...] = jnp.zeros_like(acc)
-    text_acc[...] = jnp.zeros_like(text_acc)
     dg_ref[...] = jnp.zeros_like(dg_ref)
-    rows = queries.shape[0] // SPLIT * BACKWARD_SLOTS
+    rows = queries.shape[0]
     text_chunk = pick_tile(text_keys.shape[0], 256)
     gate = gate_ref[0, 0:1, :]
 
@@ -207,10 +204,7 @@
         query = queries[spot, :]
         lanes = lane_ids(query.shape)
         query_low = jnp.where(lanes < 64, query, jnp.zeros_like(query))
-        grads = jnp.concatenate(
-            [unfold_high(grad_hold[tile * BACKWARD_SLOTS + slot]) for slot in range(BACKWARD_SLOTS)],
-            axis=0,
-        )
+        grads = jnp.concatenate([unfold_high(grad_hold[slot]) for slot in range(SPLIT)], axis=0)
         grads = jnp.where(lanes < 64, 0.0, grads)
         outs = outs_ref[spot, :]
         cross_out = jnp.where(lanes < 64, 0.0, turn(outs))
@@ -242,7 +236,7 @@
         def step(index, total):
             part = pl.ds(pl.multiple_of(index * chunk, chunk), chunk)
             grad_pair, grad_query = attend(keys[part, :], values[part, :], own_wide, own_pair)
-            acc[part, :] += grad_pair
+            acc[part, :] = grad_pair
             return total + grad_query
 
         def text_step(index, total):
@@ -250,19 +244,19 @@
             grad_pair, grad_query = attend(
                 text_keys[part, :], text_values[part, :], cross_wide, cross_pair
             )
-            text_acc[part, :] += grad_pair
+            text_acc[part, :] = grad_pair
             return total + grad_query
 
         blank = jnp.zeros((rows, 128), FLOAT)
-        total = lax.fori_loop(0, keys.shape[0] // chunk, step, blank, unroll=2)
+        total = lax.fori_loop(0, keys.shape[0] // chunk, step, blank, unroll=4)
         total = lax.fori_loop(0, text_keys.shape[0] // text_chunk, text_step, total, unroll=True)
         total = total * 0.125
-        each = rows // BACKWARD_SLOTS
-        for slot in range(BACKWARD_SLOTS):
-            hold[tile * BACKWARD_SLOTS + slot] = fold_low(total[each * slot : each * slot + each])
+        each = rows // SPLIT
+        for slot in range(SPLIT):
+            hold[slot] = fold_low(total[each * slot : each * slot + each])
         return carry
 
-    lax.fori_loop(0, SPLIT // BACKWARD_SLOTS, tile_step, 0)
+    lax.fori_loop(0, 1, tile_step, 0)
     for index, ref in enumerate(dq_refs):
         ref[...] = hold[index]
     for values, refs in ((acc, dkv_refs), (text_acc, dt_refs)):
@@ -280,7 +274,7 @@
     text = jax.ShapeDtypeStruct((heads, tf.shape[0] // 2, 128), LOW)
     sums = jax.ShapeDtypeStruct((heads, 8, 128), FLOAT)
     out = pl.pallas_call(
-        functools.partial(backward_kernel, len(pairs), pick_tile(kf.shape[0], 512)),
+        functools.partial(backward_kernel, len(pairs), pick_tile(kf.shape[0], 1024)),
         grid=(heads,),
         in_specs=attention_specs(pairs, queries, qf, kf, tf)
         + [pl.BlockSpec((half, 128), lambda i: (i, 0))] * SPLIT
@@ -610,85 +604,82 @@
     return lax.optimization_barrier(values)
 
 
-def stacked_kernel(left_ref, own_ref, other_ref, out_ref):
-    rows = own_ref.shape[1]
-    out_ref[...] = (
-        matmul(left_ref[:, :rows], own_ref[0], 1, 0)
-        + matmul(left_ref[:, rows:], other_ref[0], 1, 0)
+def outer_kernel(bound, *refs):
+    first, second, out_ref = refs[:4], refs[4:8], refs[8]
+    step = pl.program_id(0)
+
+    def run(group):
+        own_left, other_left, own_right, other_right = group
+        out_ref[...] = (
+            matmul(own_left[...], own_right[0], 1, 0)
+            + matmul(other_left[...], other_right[0], 1, 0)
+        ).astype(LOW)
+
+    @pl.when(step < bound)
+    def _():
+        run(first)
+
+    @pl.when(step >= bound)
+    def _():
+        run(second)
+
+
+def outer_products(first, second, tile):
+    depth = first[0].shape[0]
+    steps = [group[2].shape[0] * group[2].shape[2] // tile for group in (first, second)]
+    specs, operands = [], []
+    for index, group in enumerate((first, second)):
+        rows, columns = group[2].shape[1:]
+        tiles = columns // tile
+
+        def right_at(i, index=index, tiles=tiles):
+            if index == 0:
+                at = jnp.minimum(i, steps[0] - 1)
+            else:
+                at = jnp.maximum(i - steps[0], 0)
+            return (at // tiles, 0, at % tiles)
+
+        specs += [whole(group[0].shape)] * 2
+        specs += [pl.BlockSpec((1, rows, tile), right_at)] * 2
+        operands += group
+    return pl.pallas_call(
+        functools.partial(outer_kernel, steps[0]),
+        grid=(sum(steps),),
+        in_specs=specs,
+        out_specs=pl.BlockSpec((depth, tile), lambda i: (0, i)),
+        out_shape=jax.ShapeDtypeStruct((depth, sum(steps) * tile), LOW),
+        compiler_params=pltpu.CompilerParams(vmem_limit_bytes=48 * MIB),
+        cost_estimate=SMALL,
+    )(*operands)
+
+
+def columns_kernel(core_ref, values_ref, own_ref, other_ref, hold):
+    turned = jnp.transpose(values_ref[...].astype(FLOAT))
+    hold[...] = turned.reshape(hold.shape)
+    pairs = hold.shape[0] // 2
+    core = core_ref[0]
+    own_ref[...] = jnp.concatenate(
+        [hold[2 * pair + core] for pair in range(pairs)], axis=0
     ).astype(LOW)
-
-
-def stacked_outer(left, own, other, tile):
-    depth = left.shape[0]
-    count, rows, columns = own.shape
-    tiles = columns // tile
-    part = pl.BlockSpec((1, rows, tile), lambda i: (i // tiles, 0, i % tiles))
-    return pl.pallas_call(
-        stacked_kernel,
-        grid=(count * tiles,),
-        in_specs=[pl.BlockSpec(left.shape, lambda i: (0, 0)), part, part],
-        out_specs=pl.BlockSpec((depth, tile), lambda i: (0, i)),
-        out_shape=jax.ShapeDtypeStruct((depth, count * columns), LOW),
-        compiler_params=pltpu.CompilerParams(vmem_limit_bytes=40 * MIB),
-        cost_estimate=SMALL,
-    )(left, own, other)
-
-
-def joint_kernel(count, left_ref, own_ref, other_ref, own_last_ref, other_last_ref, out_ref):
-    step = pl.program_id(0)
-    rows = own_ref.shape[1]
-
-    @pl.when(step < count)
-    def _():
-        out_ref[...] = (
-            matmul(left_ref[0, :, :rows], own_ref[0], 1, 0)
-            + matmul(left_ref[0, :, rows:], other_ref[0], 1, 0)
-        ).astype(LOW)
-
-    @pl.when(step >= count)
-    def _():
-        out_ref[...] = (
-            matmul(left_ref[0, :, :rows], own_last_ref[...], 1, 0)
-            + matmul(left_ref[0, :, rows:], other_last_ref[...], 1, 0)
-        ).astype(LOW)
-
-
-def joint_outer(left, own, other, own_last, other_last, tile):
-    depth, tokens = left.shape[1:]
-    rows, columns = own.shape[1:]
-    tiles = columns // tile
-    count = own.shape[0] * tiles
-    extra = own_last.shape[1] // tile
-
-    def right_at(i):
-        at = jnp.minimum(i, count - 1)
-        return (at // tiles, 0, at % tiles)
-
-    def left_at(i):
-        return (jnp.where(i < 2 * tiles, 0, jnp.where(i < count, 1, 2)), 0, 0)
-
-    right = pl.BlockSpec((1, rows, tile), right_at)
-    last = pl.BlockSpec((rows, tile), lambda i: (0, jnp.maximum(i - count, 0)))
-    return pl.pallas_call(
-        functools.partial(joint_kernel, count),
-        grid=(count + extra,),
-        in_specs=[
-            pl.BlockSpec((1, depth, tokens), left_at),
-            right,
-            right,
-            last,
-            last,
-        ],
-        out_specs=pl.BlockSpec((depth, tile), lambda i: (0, i)),
-        out_shape=jax.ShapeDtypeStruct((depth, (count + extra) * tile), LOW),
-        compiler_params=pltpu.CompilerParams(vmem_limit_bytes=40 * MIB),
-        cost_estimate=SMALL,
-    )(left, own, other, own_last, other_last)
+    other_ref[...] = jnp.concatenate(
+        [hold[2 * pair + 1 - core] for pair in range(pairs)], axis=0
+    ).astype(LOW)
+
+
+def split_columns(core, values, block):
+    rows, width = values.shape
+    half = jax.ShapeDtypeStruct((width // 2, rows), LOW)
+    return small_call(
+        columns_kernel,
+        (core, values),
+        [half, half],
+        [pltpu.VMEM((width // block, block, rows), FLOAT)],
+    )
 
 
 def feed_kernel(
     normed_ref, grad_ref, gate_ref, up_ref, down_ref,
-    grads_ref, feed_own_ref, feed_other_ref, norm_own_ref, norm_other_ref,
+    hidden_ref, grads_ref, feed_own_ref, feed_other_ref, norm_own_ref, norm_other_ref,
     feed_acc, norm_acc,
 ):
     step = pl.program_id(0)
@@ -707,7 +698,7 @@
     hidden = (silu * up).astype(LOW)
     grad_gate = (grad_hidden * up * sigmoid * (1.0 + gate * (1.0 - sigmoid))).astype(LOW)
     grad_up = (grad_hidden * silu).astype(LOW)
-    grads_ref[2] = hidden
+    hidden_ref[0] = hidden
     grads_ref[0] = grad_gate
     grads_ref[1] = grad_up
     feed_acc[...] += matmul(hidden, down_ref[...], 1, 1)
@@ -736,11 +727,13 @@
             for part in range(3)
         ],
         out_specs=[
-            pl.BlockSpec((3, rows, tile), lambda i: (0, 0, i)),
+            pl.BlockSpec((1, rows, tile), lambda i: (0, 0, i)),
+            pl.BlockSpec((2, rows, tile), lambda i: (0, 0, i)),
         ]
         + [whole(own.shape)] * 4,
         out_shape=[
-            jax.ShapeDtypeStruct((3, rows, columns), LOW),
+            jax.ShapeDtypeStruct((1, rows, columns), LOW),
+            jax.ShapeDtypeStruct((2, rows, columns), LOW),
             own,
             other,
             own,
@@ -878,13 +871,11 @@
     core = dp_index % 2
     core_groups = [list(range(first, dp, 2)) for first in range(2)]
 
+    core_at = core.astype(jnp.int32).reshape(1)
+
     def core_columns(values):
-        halves = (
-            values.T.reshape(dp // 2, 2, weight_rows, token_count)
-            .transpose(1, 0, 2, 3)
-            .reshape(2, width // 2, token_count)
-        )
-        return jnp.concatenate([pick(halves, core), flip(pick(halves, 1 - core), 1)], axis=1)
+        own, other = split_columns(core_at, values, weight_rows)
+        return own, flip(other, 1)
 
     def scatter(values):
         return lax.psum_scatter(
@@ -1029,9 +1020,9 @@
         ],
     )
     arrived = send_slots(head_slots)
+    arrived, grad_ffn = tie(arrived, grad_ffn)
     own_pairs, queries = gather_slots(arrived, text_pairs, each)
     pairs = spread_list(own_pairs)
-    pairs, grad_ffn = tie(pairs, grad_ffn)
     mixed_slots, head_outs, head_stats = attention_forward(
         pairs, queries, query_features, key_features, text_features, gate_lanes
     )
@@ -1040,10 +1031,16 @@
     after_attn = input_rows + gate_one * attn_rows
     second_gain = second_norm_gain.astype(FLOAT)
     normed_two_all = both_rows(modulated(after_attn, second_gain, shift_two, scale_two).astype(LOW))
-    feed_grads, feed_own, feed_other, norm_own, norm_other = feed_forward(
+    hidden_low, feed_grads, feed_own, feed_other, norm_own, norm_other = feed_forward(
         normed_two_all, grad_ffn, rest_full, hidden_count, 512
     )
-    grad_normed_two = norm_own + swapped(norm_other).astype(FLOAT)
+    feed_weights_grad = outer_products(
+        [*core_columns(normed_two_all), feed_grads, flip(feed_grads, 1)],
+        [*core_columns(grad_ffn), hidden_low, flip(hidden_low, 1)],
+        512,
+    )
+    norm_other = swapped(norm_other)
+    grad_normed_two = norm_own + norm_other.astype(FLOAT)
     _, pull_two = jax.vjp(modulated, after_attn, second_gain, shift_two, scale_two)
     back_two, grad_second_gain, grad_shift_two, grad_scale_two = pull_two(grad_normed_two)
     grad_after = grad_two + back_two
@@ -1053,19 +1050,14 @@
     grad_gate_two = grad_two * ffn_rows
     grad_gate_one = grad_after * attn_rows
     grad_slots = send_slots(split_heads(far, dot_float(grad_attn, out_full), heads))
-    joint_grads = joint_outer(
-        jnp.stack(
-            [core_columns(normed_two_all), core_columns(grad_ffn), core_columns(grad_attn)]
-        ),
-        feed_grads,
-        flip(feed_grads, 1),
-        mixed,
-        flip(mixed, 1),
-        256,
-    )
     normed_core = core_columns(normed_all)
-    grad_slots, joint_grads, normed_core = tie(grad_slots, joint_grads, normed_core)
-    joint_low = scatter(joint_grads)
+    last_left = [normed_core, core_columns(grad_attn)]
+    mixed_right = mixed[None]
+    mixed_other = flip(mixed_right, 1)
+    grad_slots, feed_weights_grad, last_left, mixed_other = tie(
+        grad_slots, feed_weights_grad, last_left, mixed_other
+    )
+    feed_low = scatter(feed_weights_grad)
 
     def total_rows(terms, first, last):
         return sum(term[:, first:last].astype(FLOAT) for term in terms).astype(LOW)
@@ -1130,16 +1122,18 @@
         (*text_terms, text_raw, ky_gain),
         [part_shape, jax.ShapeDtypeStruct((8, 128), FLOAT)],
     )
-    back_parts, text_low = tie(back_parts, text_low)
     qkv_grad, gain_sums = rope_backward(far, back_parts, qkv_raw, cosine, sine, gains, heads)
-    grad_normed_one = own_rows(dot_turned(qkv_grad, qkv_full))
+    normed_part = dot_turned(qkv_grad, qkv_full)
     qkv_right = qkv_grad[None]
-    qkv_grads = stacked_outer(
-        normed_core, qkv_right, flip(qkv_right, 1), local_width
-    )
-    qkv_grads, joint_low = tie(qkv_grads, joint_low)
-    qkv_low = scatter(qkv_grads)
-    grad_normed_one, qkv_grads = tie(grad_normed_one, qkv_grads)
+    last_grads = outer_products(
+        [*last_left[0], qkv_right, flip(qkv_right, 1)],
+        [*last_left[1], mixed_right, mixed_other],
+        local_width,
+    )
+    last_grads, feed_low = tie(last_grads, feed_low)
+    last_low = scatter(last_grads)
+    normed_part, last_grads, text_low = tie(normed_part, last_grads, text_low)
+    grad_normed_one = own_rows(normed_part)
     _, pull_one = jax.vjp(modulated, input_rows, first_gain, shift_one, scale_one)
     back_one, grad_first_gain, grad_shift_one, grad_scale_one = pull_one(grad_normed_one)
     grad_inputs = grad_after + back_one
@@ -1222,13 +1216,14 @@
     grad_conditioning = (
         sum_dp(cond_part) * cond_sigmoid * (1.0 + cond_float * (1.0 - cond_sigmoid))
     )
-    qkv_shard = qkv_low.astype(FLOAT).reshape(weight_rows, 3, local_width).transpose(1, 0, 2)
-    joint_shard = joint_low.astype(FLOAT)
+    last_shard = last_low.astype(FLOAT)
+    qkv_shard = last_shard[:, : 3 * local_width].reshape(weight_rows, 3, local_width).transpose(1, 0, 2)
+    feed_shard = feed_low.astype(FLOAT)
     gate_up_shard = jnp.stack(
-        [joint_shard[:, :hidden_count], joint_shard[:, hidden_count : 2 * hidden_count]]
-    )
-    out_shard = joint_shard[:, 3 * hidden_count :]
-    down_shard = joint_shard[:, 2 * hidden_count : 3 * hidden_count]
+        [feed_shard[:, :hidden_count], feed_shard[:, hidden_count : 2 * hidden_count]]
+    )
+    out_shard = last_shard[:, 3 * local_width :]
+    down_shard = feed_shard[:, 2 * hidden_count : 3 * hidden_count]
     return (
         output,
         grad_inputs,

time: 662 us -> 621 us (0.938)
  waiting for transfers between devices: 303 us -> 276 us
  starting transfers between devices: 70.8 us -> 91.7 us
  local copies, waits for them, and re-layouts: 44.5 us -> 27.9 us
  other arithmetic: 54 us -> 38.9 us
    ppermute x33 -> x34, starting transfers between devices: 18.1 us -> 35.3 us  [flip(): return lax.ppermute(values, 'dp', [(j, j ^ bit) for j in range(dp)])]
    ppermute x18, waiting for transfers between devices: 87.7 us -> 71 us  [shift(): return lax.ppermute(values, 'dp', pairs)]
    transpose x9 -> x0, local copies, waits for them, and re-layouts: 14.5 us -> none  [the longest x4 8.05 us: core_columns(): values.T.reshape(dp // 2, 2, weight_rows, token_count).transpose(1, 0, 2, 3)]
    ppermute x10, waiting for transfers between devices: 46.3 us -> 31.9 us  [swapped(): return lax.ppermute(values, 'tensor', [(0, 1), (1, 0)])]
    reduce_scatter x2, waiting for transfers between devices: 28.1 us -> 37.3 us  [scatter(): lax.psum_scatter(values, 'dp', scatter_dimension=0, axis_index_groups=cor...]
    pallas_call x2, Pallas kernels: 25.6 us -> 18.9 us  [outer_products(): pl.pallas_call(functools.partial(outer_kernel, steps[0]), grid=(sum(steps...]
    ppermute x33 -> x34, waiting for transfers between devices: 141 us -> 136 us  [flip(): return lax.ppermute(values, 'dp', [(j, j ^ bit) for j in range(dp)])]
    unnamed x217 -> x207, local copies, waits for them, and re-layouts: 17.1 us -> 13.3 us
  transfers between devices with their start and end apart: 67 -> 68, of which waited for: 37 -> 34; matrix products, arithmetic and copies ran while one was open for 15% -> 11% of each run, Pallas kernels for 18% -> 19%
where the time goes in v5:
time: 621 us; the launch traced here: 611 us
  waiting for transfers between devices  276 us (44%)
  Pallas kernels  128 us (21%)
  starting transfers between devices  91.7 us (15%)
  other arithmetic  38.9 us (6%)
  local copies, waits for them, and re-layouts  27.9 us (4%)
  between operations  25.7 us (4%)
  matrix products  22.2 us (4%)
    ppermute x34, waiting for transfers between devices, flip(): return lax.ppermute(values, 'dp', [(j, j ^ bit) for j in range(dp)])  136 us
    ppermute x18, waiting for transfers between devices, shift(): return lax.ppermute(values, 'dp', pairs)  71 us
    pallas_call x1, Pallas kernels, attention_backward(): pl.pallas_call(functools.partial(backward_kernel, len(pairs), pick_tile(k...  54.4 us
    reduce_scatter x2, waiting for transfers between devices, scatter(): lax.psum_scatter(values, 'dp', scatter_dimension=0, axis_index_groups=cor...  37.3 us
    ppermute x34, starting transfers between devices, flip(): return lax.ppermute(values, 'dp', [(j, j ^ bit) for j in range(dp)])  35.3 us
    ppermute x10, waiting for transfers between devices, swapped(): return lax.ppermute(values, 'tensor', [(0, 1), (1, 0)])  31.9 us
    ppermute x18, starting transfers between devices, shift(): return lax.ppermute(values, 'dp', pairs)  30.9 us
    pallas_call x1, Pallas kernels, attention_forward(): pl.pallas_call(functools.partial(forward_kernel, len(pairs), pick_tile(kf...  24.9 us
  transfers between devices with their start and end apart: 68, of which 34 were waited for; matrix products, arithmetic and copies ran while one was open for 11% of the time, Pallas kernels for 19%

profile of v5, /device:TPU:0, one launch (start us, length us, event | category | flops | bytes accessed | tf_op | source)
XLA Modules:
  0.0 611.1 jit_solution(16177498288920315396)
XLA Ops:
  7.3 1.9 copy.85
  10.0 7.4 %all-to-all-start = ((bf16[48,16,256]{2,0,1:T(8,128)(2,1)}), bf16[48,16,256]{2,0,1:T(8,128)(2,1)S(1)}, u32[]{:S(2)}, u32[]{:S(2)}) async-start(bf16[48,16,256]{2,0,1:T(8,128)(2,1)} %bitcast.116), calls=%async_computation | async-start | bytes 786432 | tf_op jit(solution)/shard_map/all_to_all | solution.py:905
  21.1 2.2 pad_maximum_fusion.2
  23.7 1.8 collective-permute-start.8
  25.4 6.7 %collective-permute-done.8 = f32[3,6144]{1,0:T(4,128)S(1)} collective-permute-done((f32[3,6144]{1,0:T(4,128)S(1)}, f32[3,6144]{1,0:T(4,128)S(1)}, u32[]{:S(2)}, u32[]{:S(2)}) %collective-permute-start.8) | collective-permute-done | bytes 73760 | tf_op jit(solution)/shard_map/ppermute | solution.py:816
  33.8 10.3 %collective-permute-done.9 = f32[3,6144]{1,0:T(4,128)S(1)} collective-permute-done((f32[3,6144]{1,0:T(4,128)S(1)}, f32[3,6144]{1,0:T(4,128)S(1)}, u32[]{:S(2)}, u32[]{:S(2)}) %collective-permute-start.9) | collective-permute-done | bytes 73760 | tf_op jit(solution)/shard_map/ppermute | solution.py:816
  49.0 1.8 collective-permute-done.10
  51.6 6.3 %collective-permute-done.2 = f32[4,3072]{1,0:T(4,128)S(1)} collective-permute-done((f32[4,3072]{1,0:T(4,128)S(1)}, f32[4,3072]{1,0:T(4,128)S(1)}, u32[]{:S(2)}, u32[]{:S(2)}) %collective-permute-start.2) | collective-permute-done | bytes 49184 | tf_op jit(solution)/shard_map/ppermute | solution.py:816
  59.9 7.1 %collective-permute-done.3 = f32[4,3072]{1,0:T(4,128)S(1)} collective-permute-done((f32[4,3072]{1,0:T(4,128)S(1)}, f32[4,3072]{1,0:T(4,128)S(1)}, u32[]{:S(2)}, u32[]{:S(2)}) %collective-permute-start.3) | collective-permute-done | bytes 49184 | tf_op jit(solution)/shard_map/ppermute | solution.py:816
  67.5 2.1 collective-permute-start.4
  70.0 2.7 fusion.refs_6_
  76.6 9.4 %collective-permute-done.6 = bf16[192,1536]{1,0:T(8,128)(2,1)S(1)} collective-permute-done((bf16[192,1536]{1,0:T(8,128)(2,1)S(1)}, bf16[192,1536]{1,0:T(8,128)(2,1)S(1)}, u32[]{:S(2)}, u32[]{:S(2)}) %collective-permute-start.6) | collective-permute-done | bytes 589856 | tf_op jit(solution)/shard_map/ppermute | solution.py:816
  88.5 3.2 collective-permute-start.12
  93.3 1.7 collective-permute-start.17
  95.0 5.0 fusion.60.qkv_ref.refs_4_
  100.0 3.3 shard_map.324
  103.4 2.2 collective-permute-done.12.refs_2_
  105.5 8.4 %collective-permute-start.14 = (bf16[1152,128]{1,0:T(8,128)(2,1)S(1)}, bf16[1152,128]{1,0:T(8,128)(2,1)S(1)}, u32[]{:S(2)}, u32[]{:S(2)}) collective-permute-start(bf16[1152,128]{1,0:T(8,128)(2,1)S(1)} %get-tuple-element.131), channel_id=1, source_target_pairs={{0,8},{2,10},{4,12},{6,14},{8,16},{10,18},{12,20},{14,22},{16,24},... | collective-permute-start | bytes 884744 | tf_op jit(solution)/shard_map/ppermute | solution.py:820
  113.9 2.4 collective-permute-start.16
  116.7 10.9 %collective-permute-done.14.refs_1_ = bf16[1152,128]{1,0:T(8,128)(2,1)S(1)} collective-permute-done((bf16[1152,128]{1,0:T(8,128)(2,1)S(1)}, bf16[1152,128]{1,0:T(8,128)(2,1)S(1)}, u32[]{:S(2)}, u32[]{:S(2)}) %collective-permute-start.14) | collective-permute-done | bytes 294944 | tf_op jit(solution)/shard_map/ppermute | solution.py:820
  127.6 12.6 %collective-permute-done.15.refs_2_ = bf16[1152,128]{1,0:T(8,128)(2,1)S(1)} collective-permute-done((bf16[1152,128]{1,0:T(8,128)(2,1)S(1)}, bf16[1152,128]{1,0:T(8,128)(2,1)S(1)}, u32[]{:S(2)}, u32[]{:S(2)}) %collective-permute-start.15) | collective-permute-done | bytes 294944 | tf_op jit(solution)/shard_map/ppermute | solution.py:820
  140.2 11.2 %collective-permute-done.16.refs_3_ = bf16[1152,128]{1,0:T(8,128)(2,1)S(1)} collective-permute-done((bf16[1152,128]{1,0:T(8,128)(2,1)S(1)}, bf16[1152,128]{1,0:T(8,128)(2,1)S(1)}, u32[]{:S(2)}, u32[]{:S(2)}) %collective-permute-start.16) | collective-permute-done | bytes 294944 | tf_op jit(solution)/shard_map/ppermute | solution.py:820
  153.9 41.5 %collective-permute-done.18.refs_1_ = bf16[3648,128]{1,0:T(8,128)(2,1)} collective-permute-done((bf16[3648,128]{1,0:T(8,128)(2,1)}, bf16[3648,128]{1,0:T(8,128)(2,1)}, u32[]{:S(2)}, u32[]{:S(2)}) %collective-permute-start.18) | collective-permute-done | bytes 933920 | tf_op jit(solution)/shard_map/ppermute | solution.py:816
  199.4 24.9 %shard_map.327 = (bf16[384,128]{1,0:T(8,128)(2,1)}, bf16[384,128]{1,0:T(8,128)(2,1)}, bf16[384,128]{1,0:T(8,128)(2,1)}, bf16[384,128]{1,0:T(8,128)(2,1)}, f32[3072,128]{1,0:T(8,128)}, /*index=5*/f32[3072,128]{1,0:T(8,128)}) custom-call(bf16[3648,128]{1,0:T(8,128)(2,1)} %get-tuple-element.143.refs_0_, bf16[3648,128]{1,0:T(8,128)(2,1)} %collective-permute-done.18.refs_1_, ...), custom_call_target="tpu_custom_call" | custom-call | flops 1024 | bytes 1024 | tf_op jit(solution)/shard_map/pallas_call | solution.py:168
  224.3 3.2 collective-permute-start.21
  228.2 2.9 collective-permute-done.21.refs_1_
  231.1 7.0 %collective-permute-done.22.refs_2_ = bf16[384,128]{1,0:T(8,128)(2,1)S(1)} collective-permute-done((bf16[384,128]{1,0:T(8,128)(2,1)}, bf16[384,128]{1,0:T(8,128)(2,1)S(1)}, u32[]{:S(2)}, u32[]{:S(2)}) %collective-permute-start.22) | collective-permute-done | bytes 98336 | tf_op jit(solution)/shard_map/ppermute | solution.py:820
  239.3 2.6 fusion.3
  242.0 1.8 collective-permute-start.24
  243.8 9.3 %collective-permute-done.24 = bf16[128,1536]{1,0:T(8,128)(2,1)S(1)} collective-permute-done((bf16[128,1536]{1,0:T(8,128)(2,1)S(1)}, bf16[128,1536]{1,0:T(8,128)(2,1)S(1)}, u32[]{:S(2)}, u32[]{:S(2)}) %collective-permute-start.24) | collective-permute-done | bytes 393248 | tf_op jit(solution)/shard_map/ppermute | solution.py:765
  254.1 1.7 collective-permute-start.25
  255.8 8.6 %collective-permute-done.25 = bf16[128,1536]{1,0:T(8,128)(2,1)S(1)} collective-permute-done((bf16[128,1536]{1,0:T(8,128)(2,1)S(1)}, bf16[128,1536]{1,0:T(8,128)(2,1)S(1)}, u32[]{:S(2)}, u32[]{:S(2)}) %collective-permute-start.25) | collective-permute-done | bytes 393248 | tf_op jit(solution)/shard_map/ppermute | solution.py:765
  264.5 15.0 %shard_map.329 = (bf16[1,256,2048]{2,1,0:T(8,128)(2,1)}, bf16[2,256,2048]{2,1,0:T(8,128)(2,1)}, f32[128,1536]{1,0:T(8,128)S(1)}, bf16[128,1536]{1,0:T(8,128)(2,1...) custom-call(bf16[256,1536]{1,0:T(8,128)(2,1)S(1)} %pad_maximum_fusion.7.normed_ref.values_ref, ...), custom_call_target="tpu_custom_call" | custom-call | flops 1024 | bytes 1024 | tf_op jit(solution)/shard_map/pallas_call | solution.py:721
  281.6 7.3 %collective-permute-done.26 = bf16[128,1536]{1,0:T(8,128)(2,1)S(1)} collective-permute-done((bf16[128,1536]{1,0:T(8,128)(2,1)S(1)}, bf16[128,1536]{1,0:T(8,128)(2,1)S(1)}, u32[]{:S(2)}, u32[]{:S(2)}) %collective-permute-start.26) | collective-permute-done | bytes 393248 | tf_op jit(solution)/shard_map/ppermute | solution.py:765
  296.7 3.8 collective-permute-done.27
  303.4 2.6 fusion.1.grad_ref
  306.8 3.4 collective-permute-start.29
  310.2 2.4 collective-permute-start.31
  312.6 12.7 %shard_map.333 = bf16[768,6144]{1,0:T(8,128)(2,1)} custom-call(bf16[768,256]{1,0:T(8,128)(2,1)S(1)} %get-tuple-element.163.refs_0_, bf16[768,256]{1,0:T(8,128)(2,1)S(1)} %collective-permute-done.32.refs_1_, bf16[2,256,2048]{2,1,0:T(8,128)(2,1)S(1)} %copy-done.6, bf16[2,256,2048]{2,1,0:T(8,128)(2,1)} %collective-permute-done.33.refs_3_, ...), custom_call_target="tpu_custom_call" | custom-call | flops 1024 | bytes 1024 | tf_op jit(solution)/shard_map/pallas_call | solution.py:645
  326.0 54.4 %shard_map.336 = (bf16[384,128]{1,0:T(8,128)(2,1)}, bf16[384,128]{1,0:T(8,128)(2,1)}, bf16[384,128]{1,0:T(8,128)(2,1)}, bf16[384,128]{1,0:T(8,128)(2,1)}, bf16[3...) custom-call(bf16[3648,128]{1,0:T(8,128)(2,1)} %get-tuple-element.143, ...), custom_call_target="tpu_custom_call" | custom-call | flops 1024 | bytes 1024 | tf_op jit(solution)/shard_map/pallas_call | solution.py:276
  380.9 3.5 collective-permute-done.40.refs_1_
  387.0 29.2 %collective-permute-done.41 = bf16[3,1216,128]{2,1,0:T(8,128)(2,1)S(1)} collective-permute-done((bf16[3,1216,128]{2,1,0:T(8,128)(2,1)S(1)}, bf16[3,1216,128]{2,1,0:T(8,128)(2,1)S(1)}, u32[]{:S(2)}, u32[]{:S(2)}) %collective-permute-start.41) | collective-permute-done | bytes 933920 | tf_op jit(solution)/shard_map/ppermute | solution.py:816
  418.9 2.2 collective-permute-start.42
  430.2 13.5 %collective-permute-done.43.refs_2_ = bf16[1152,128]{1,0:T(8,128)(2,1)} collective-permute-done((bf16[1152,128]{1,0:T(8,128)(2,1)}, bf16[1152,128]{1,0:T(8,128)(2,1)}, u32[]{:S(2)}, u32[]{:S(2)}) %collective-permute-start.43) | collective-permute-done | bytes 294944 | tf_op jit(solution)/shard_map/ppermute | solution.py:820
  444.7 6.3 %shard_map.338 = (bf16[256,2304]{1,0:T(8,128)(2,1)}, f32[8,128]{1,0:T(8,128)S(1)}) custom-call(s32[1]{0:T(128)} %bitcast.10.far_ref, bf16[1152,128]{1,0:T(8,128)(2,1)S(1)} %copy-done.21, bf16[1152,128]{1,0:T(8,128)(2,1)} %collective-permute-done.42.refs_1_, bf16[1152,128]{1,0:T(8,128)(2,1)} %collective-permute-done.43.refs_2_, ...), custom_call_target="tpu_custom_call" | custom-call | flops 1024 | bytes 1024 | tf_op jit(solution)/shard_map/pallas_call | solution.py:355
  453.7 6.6 %fusion.61 = f32[256,1536]{1,0:T(8,128)} fusion(bf16[256,2304]{1,0:T(8,128)(2,1)} %get-tuple-element.191, bf16[1536,2304]{1,0:T(8,128)(2,1)} %all-gather.3.cloned.1.call-done), kind=kOutput, calls=%fused_computation.209 | convolution fusion | flops 1811939328 | bytes 9830400 | tf_op jit(solution)/shard_map/dot_general | solution.py:30
  460.3 6.2 %shard_map.339 = bf16[768,3072]{1,0:T(8,128)(2,1)} custom-call(bf16[768,256]{1,0:T(8,128)(2,1)S(1)} %copy-done.15, bf16[768,256]{1,0:T(8,128)(2,1)S(1)} %copy-done.17, bf16[1,256,2304]{2,1,0:T(8,128)(2,1)} %bitcast.44.refs_2_, bf16[1,256,2304]{2,1,0:T(8,128)(2,1)S(1)} %collective-permute-done.45.refs_3_, bf16[768,256]{1,0:T(8,128)(2,1)S(1)} %copy-done.19, ...), custom_call_target="tpu_custom_call" | custom-call | flops 1024 | bytes 1024 | tf_op jit(solution)/shard_map/pallas_call | solution.py:645
  466.5 25.6 %reduce-scatter.3.cloned.1.call-done = bf16[96,6144]{1,0:T(8,128)(2,1)} async-done(((bf16[768,6144]{1,0:T(8,128)(2,1)}), bf16[96,6144]{1,0:T(8,128)(2,1)}) %reduce-scatter.3.cloned.1.call-update) | async-done | bytes 1179664 | tf_op jit(solution)/shard_map/reduce_scatter | solution.py:881
  493.8 2.1 collective-permute-start.50
  501.3 10.7 %collective-permute-done.49.refs_2_ = bf16[192,384]{1,0:T(8,128)(2,1)S(1)} collective-permute-done((bf16[192,384]{1,0:T(8,128)(2,1)S(1)}, bf16[192,384]{1,0:T(8,128)(2,1)S(1)}, u32[]{:S(2)}, u32[]{:S(2)}) %collective-permute-start.49) | collective-permute-done | bytes 147488 | tf_op jit(solution)/shard_map/ppermute | solution.py:820
  513.2 3.8 select_reduce_fusion.1
  525.3 1.8 collective-permute-done.47
  535.4 1.6 copy.82
  537.0 2.0 collective-permute-done.55
  539.0 16.5 %collective-permute-start.56 = (f32[4,9216]{1,0:T(4,128)S(1)}, f32[4,9216]{1,0:T(4,128)S(1)}, u32[]{:S(2)}, u32[]{:S(2)}) collective-permute-start(f32[4,9216]{1,0:T(4,128)S(1)} %add.478), channel_id=1, source_target_pairs={{0,8},{2,10},{4,12},{6,14},{8,0},{10,2},{12,4},{14,6},{16,24},{18,... | collective-permute-start | bytes 442376 | tf_op jit(solution)/shard_map/ppermute | solution.py:816
  556.6 2.8 collective-permute-done.56
  559.4 3.7 collective-permute-start.57
  564.0 3.6 all-to-all-start.1
  567.5 1.8 collective-permute-done.57
  570.1 1.9 fusion.54
  573.6 3.5 collective-permute-done.59
  577.8 3.5 collective-permute-done.60
  582.7 4.8 collective-permute-done.61
  589.0 11.7 %reduce-scatter.5.cloned.1.call-done = bf16[96,3072]{1,0:T(8,128)(2,1)} async-done(((bf16[768,3072]{1,0:T(8,128)(2,1)}), bf16[96,3072]{1,0:T(8,128)(2,1)}) %reduce-scatter.5.cloned.1.call-update) | async-done | bytes 589840 | tf_op jit(solution)/shard_map/reduce_scatter | solution.py:881
  (451 shorter events, 91.0 us)
Async XLA Ops:
  7.2 79.8 %all-gather.3.cloned.1.call-start = ((), (), s32[]{:S(2)}) async-start(), calls=%async_computation.4 | async-start | bytes 7520256 | tf_op jit(solution)/shard_map/all_gather | solution.py:885
  10.0 23.8 %all-to-all-start = ((bf16[48,16,256]{2,0,1:T(8,128)(2,1)}), bf16[48,16,256]{2,0,1:T(8,128)(2,1)S(1)}, u32[]{:S(2)}, u32[]{:S(2)}) async-start(bf16[48,16,256]{2,0,1:T(8,128)(2,1)} %bitcast.116), calls=%async_computation | async-start | bytes 786432 | tf_op jit(solution)/shard_map/all_to_all | solution.py:905
  17.4 221.8 %all-gather.5.cloned.1.call-start = ((), (), s32[]{:S(2)}) async-start(), calls=%async_computation.5 | async-start | bytes 22560768 | tf_op jit(solution)/shard_map/all_gather | solution.py:1005
  17.8 5.8 collective-permute-start.7
  23.7 8.5 %collective-permute-start.8 = (f32[3,6144]{1,0:T(4,128)S(1)}, f32[3,6144]{1,0:T(4,128)S(1)}, u32[]{:S(2)}, u32[]{:S(2)}) collective-permute-start(f32[3,6144]{1,0:T(4,128)S(1)} %add.411), channel_id=1, source_target_pairs={{0,4},{2,6},{4,0},{6,2},{8,12},{10,14},{12,8},{14,10},{16,20},{18,... | collective-permute-start | bytes 221192 | tf_op jit(solution)/shard_map/ppermute | solution.py:816
  32.2 11.9 %collective-permute-start.9 = (f32[3,6144]{1,0:T(4,128)S(1)}, f32[3,6144]{1,0:T(4,128)S(1)}, u32[]{:S(2)}, u32[]{:S(2)}) collective-permute-start(f32[3,6144]{1,0:T(4,128)S(1)} %add.412), channel_id=1, source_target_pairs={{0,8},{2,10},{4,12},{6,14},{8,0},{10,2},{12,4},{14,6},{16,24},{18,... | collective-permute-start | bytes 221192 | tf_op jit(solution)/shard_map/ppermute | solution.py:816
  33.8 11.0 %collective-permute-start = (f32[4,3072]{1,0:T(4,128)S(1)}, f32[4,3072]{1,0:T(4,128)S(1)}, u32[]{:S(2)}, u32[]{:S(2)}) collective-permute-start(f32[4,3072]{1,0:T(4,128)S(1)} %pad_maximum_fusion.16), channel_id=1, source_target_pairs={{0,2},{2,0},{4,6},{6,4},{8,10},{10,8},{12,14},{14,12},{16,18},{18,... | collective-permute-start | bytes 147464 | tf_op jit(solution)/shard_map/ppermute | solution.py:816
  44.1 6.6 %collective-permute-start.10 = (f32[3,6144]{1,0:T(4,128)S(1)}, f32[3,6144]{1,0:T(4,128)S(1)}, u32[]{:S(2)}, u32[]{:S(2)}) collective-permute-start(f32[3,6144]{1,0:T(4,128)S(1)} %add.413), channel_id=1, source_target_pairs={{0,16},{2,18},{4,20},{6,22},{8,24},{10,26},{12,28},{14,30},{16,0},... | collective-permute-start | bytes 221192 | tf_op jit(solution)/shard_map/ppermute | solution.py:816
  44.8 6.0 collective-permute-start.1
  50.8 7.1 %collective-permute-start.2 = (f32[4,3072]{1,0:T(4,128)S(1)}, f32[4,3072]{1,0:T(4,128)S(1)}, u32[]{:S(2)}, u32[]{:S(2)}) collective-permute-start(f32[4,3072]{1,0:T(4,128)S(1)} %add.396), channel_id=1, source_target_pairs={{0,8},{2,10},{4,12},{6,14},{8,0},{10,2},{12,4},{14,6},{16,24},{18,... | collective-permute-start | bytes 147464 | tf_op jit(solution)/shard_map/ppermute | solution.py:816
  57.9 9.0 %collective-permute-start.3 = (f32[4,3072]{1,0:T(4,128)S(1)}, f32[4,3072]{1,0:T(4,128)S(1)}, u32[]{:S(2)}, u32[]{:S(2)}) collective-permute-start(f32[4,3072]{1,0:T(4,128)S(1)} %add.397), channel_id=1, source_target_pairs={{0,16},{2,18},{4,20},{6,22},{8,24},{10,26},{12,28},{14,30},{16,0},... | collective-permute-start | bytes 147464 | tf_op jit(solution)/shard_map/ppermute | solution.py:816
  59.8 12.9 %collective-permute-start.5 = (bf16[384,1536]{1,0:T(8,128)(2,1)S(1)}, bf16[384,1536]{1,0:T(8,128)(2,1)S(1)}, u32[]{:S(2)}, u32[]{:S(2)}) collective-permute-start(bf16[384,1536]{1,0:T(8,128)(2,1)S(1)} %slice.301), channel_id=1, source_target_pairs={{0,2},{2,0},{4,6},{6,4},{8,10},{10,8},{12,14},{14,12},{16,18},{18,... | collective-permute-start | bytes 3538952 | tf_op jit(solution)/shard_map/ppermute | solution.py:816
  67.5 9.0 %collective-permute-start.4 = (bf16[128,1536]{1,0:T(8,128)(2,1)S(1)}, bf16[128,1536]{1,0:T(8,128)(2,1)S(1)}, u32[]{:S(2)}, u32[]{:S(2)}) collective-permute-start(bf16[128,1536]{1,0:T(8,128)(2,1)S(1)} %fusion.10), channel_id=1, source_target_pairs={{0,1},{1,0},{2,3},{3,2},{4,5},{5,4},{6,7},{7,6},{8,9},{9,8},{10,11... | collective-permute-start | bytes 1179656 | tf_op jit(solution)/shard_map/ppermute | solution.py:765
  73.1 12.9 %collective-permute-start.6 = (bf16[192,1536]{1,0:T(8,128)(2,1)S(1)}, bf16[192,1536]{1,0:T(8,128)(2,1)S(1)}, u32[]{:S(2)}, u32[]{:S(2)}) collective-permute-start(bf16[192,1536]{1,0:T(8,128)(2,1)S(1)} %slice.302), channel_id=1, source_target_pairs={{0,4},{2,6},{4,0},{6,2},{8,12},{10,14},{12,8},{14,10},{16,20},{18,... | collective-permute-start | bytes 1769480 | tf_op jit(solution)/shard_map/ppermute | solution.py:816
  87.0 405.1 %reduce-scatter.3.cloned.1.call-start = ((), (), s32[]{:S(2)}) async-start(), calls=%async_computation.6 | async-start | bytes 10616832 | tf_op jit(solution)/shard_map/reduce_scatter | solution.py:881
  88.2 15.1 %collective-permute-start.11 = (bf16[192,384]{1,0:T(8,128)(2,1)}, bf16[192,384]{1,0:T(8,128)(2,1)S(1)}, u32[]{:S(2)}, u32[]{:S(2)}) collective-permute-start(bf16[192,384]{1,0:T(8,128)(2,1)} %get-tuple-element.127), channel_id=1, source_target_pairs={{0,8},{2,10},{4,12},{6,14},{8,16},{10,18},{12,20},{14,22},{16,24},... | collective-permute-start | bytes 442376 | tf_op jit(solution)/shard_map/ppermute | solution.py:820
  88.5 17.1 %collective-permute-start.12 = (bf16[192,384]{1,0:T(8,128)(2,1)}, bf16[192,384]{1,0:T(8,128)(2,1)S(1)}, u32[]{:S(2)}, u32[]{:S(2)}) collective-permute-start(bf16[192,384]{1,0:T(8,128)(2,1)} %get-tuple-element.128), channel_id=1, source_target_pairs={{0,16},{2,18},{4,20},{6,22},{8,24},{10,26},{12,28},{14,30},{16,0},... | collective-permute-start | bytes 442376 | tf_op jit(solution)/shard_map/ppermute | solution.py:820
  91.7 13.9 %collective-permute-start.13 = (bf16[192,384]{1,0:T(8,128)(2,1)S(1)}, bf16[192,384]{1,0:T(8,128)(2,1)S(1)}, u32[]{:S(2)}, u32[]{:S(2)}) collective-permute-start(bf16[192,384]{1,0:T(8,128)(2,1)S(1)} %get-tuple-element.129), channel_id=1, source_target_pairs={{0,24},{2,26},{4,28},{6,30},{8,0},{10,2},{12,4},{14,6},{16,8},{18,... | collective-permute-start | bytes 442376 | tf_op jit(solution)/shard_map/ppermute | solution.py:820
  93.3 23.3 %collective-permute-start.17 = (bf16[128,1536]{1,0:T(8,128)(2,1)S(1)}, bf16[128,1536]{1,0:T(8,128)(2,1)S(1)}, u32[]{:S(2)}, u32[]{:S(2)}) collective-permute-start(bf16[128,1536]{1,0:T(8,128)(2,1)S(1)} %fusion.12), channel_id=1, source_target_pairs={{0,1},{1,0},{2,3},{3,2},{4,5},{5,4},{6,7},{7,6},{8,9},{9,8},{10,11... | collective-permute-start | bytes 1179656 | tf_op jit(solution)/shard_map/ppermute | solution.py:765
  105.5 22.0 %collective-permute-start.14 = (bf16[1152,128]{1,0:T(8,128)(2,1)S(1)}, bf16[1152,128]{1,0:T(8,128)(2,1)S(1)}, u32[]{:S(2)}, u32[]{:S(2)}) collective-permute-start(bf16[1152,128]{1,0:T(8,128)(2,1)S(1)} %get-tuple-element.131), channel_id=1, source_target_pairs={{0,8},{2,10},{4,12},{6,14},{8,16},{10,18},{12,20},{14,22},{16,24},... | collective-permute-start | bytes 884744 | tf_op jit(solution)/shard_map/ppermute | solution.py:820
  113.9 26.3 %collective-permute-start.15 = (bf16[1152,128]{1,0:T(8,128)(2,1)S(1)}, bf16[1152,128]{1,0:T(8,128)(2,1)S(1)}, u32[]{:S(2)}, u32[]{:S(2)}) collective-permute-start(bf16[1152,128]{1,0:T(8,128)(2,1)S(1)} %get-tuple-element.132), channel_id=1, source_target_pairs={{0,16},{2,18},{4,20},{6,22},{8,24},{10,26},{12,28},{14,30},{16,0},... | collective-permute-start | bytes 884744 | tf_op jit(solution)/shard_map/ppermute | solution.py:820
  113.9 37.5 %collective-permute-start.16 = (bf16[1152,128]{1,0:T(8,128)(2,1)S(1)}, bf16[1152,128]{1,0:T(8,128)(2,1)S(1)}, u32[]{:S(2)}, u32[]{:S(2)}) collective-permute-start(bf16[1152,128]{1,0:T(8,128)(2,1)S(1)} %get-tuple-element.133), channel_id=1, source_target_pairs={{0,24},{2,26},{4,28},{6,30},{8,0},{10,2},{12,4},{14,6},{16,8},{18,... | collective-permute-start | bytes 884744 | tf_op jit(solution)/shard_map/ppermute | solution.py:820
  153.5 42.0 %collective-permute-start.18 = (bf16[3648,128]{1,0:T(8,128)(2,1)}, bf16[3648,128]{1,0:T(8,128)(2,1)}, u32[]{:S(2)}, u32[]{:S(2)}) collective-permute-start(bf16[3648,128]{1,0:T(8,128)(2,1)} %get-tuple-element.143.refs_0_), channel_id=1, source_target_pairs={{0,4},{2,6},{4,0},{6,2},{8,12},{10,14},{12,8},{14,10},{16,20},{18,... | collective-permute-start | bytes 2801672 | tf_op jit(solution)/shard_map/ppermute | solution.py:816
  153.9 44.0 %collective-permute-start.19 = (bf16[3648,128]{1,0:T(8,128)(2,1)}, bf16[3648,128]{1,0:T(8,128)(2,1)}, u32[]{:S(2)}, u32[]{:S(2)}) collective-permute-start(bf16[3648,128]{1,0:T(8,128)(2,1)} %get-tuple-element.143.refs_0_), channel_id=1, source_target_pairs={{0,2},{2,0},{4,6},{6,4},{8,10},{10,8},{12,14},{14,12},{16,18},{18,... | collective-permute-start | bytes 2801672 | tf_op jit(solution)/shard_map/ppermute | solution.py:816
  224.3 6.7 %collective-permute-start.21 = (bf16[384,128]{1,0:T(8,128)(2,1)}, bf16[384,128]{1,0:T(8,128)(2,1)S(1)}, u32[]{:S(2)}, u32[]{:S(2)}) collective-permute-start(bf16[384,128]{1,0:T(8,128)(2,1)} %get-tuple-element.148), channel_id=1, source_target_pairs={{0,24},{2,26},{4,28},{6,30},{8,0},{10,2},{12,4},{14,6},{16,8},{18,... | collective-permute-start | bytes 294920 | tf_op jit(solution)/shard_map/ppermute | solution.py:820
  227.5 10.6 %collective-permute-start.22 = (bf16[384,128]{1,0:T(8,128)(2,1)}, bf16[384,128]{1,0:T(8,128)(2,1)S(1)}, u32[]{:S(2)}, u32[]{:S(2)}) collective-permute-start(bf16[384,128]{1,0:T(8,128)(2,1)} %get-tuple-element.149), channel_id=1, source_target_pairs={{0,16},{2,18},{4,20},{6,22},{8,24},{10,26},{12,28},{14,30},{16,0},... | collective-permute-start | bytes 294920 | tf_op jit(solution)/shard_map/ppermute | solution.py:820
  227.5 10.6 %collective-permute-start.23 = (bf16[384,128]{1,0:T(8,128)(2,1)}, bf16[384,128]{1,0:T(8,128)(2,1)S(1)}, u32[]{:S(2)}, u32[]{:S(2)}) collective-permute-start(bf16[384,128]{1,0:T(8,128)(2,1)} %get-tuple-element.150), channel_id=1, source_target_pairs={{0,8},{2,10},{4,12},{6,14},{8,16},{10,18},{12,20},{14,22},{16,24},... | collective-permute-start | bytes 294920 | tf_op jit(solution)/shard_map/ppermute | solution.py:820
  242.0 11.1 %collective-permute-start.24 = (bf16[128,1536]{1,0:T(8,128)(2,1)S(1)}, bf16[128,1536]{1,0:T(8,128)(2,1)S(1)}, u32[]{:S(2)}, u32[]{:S(2)}) collective-permute-start(bf16[128,1536]{1,0:T(8,128)(2,1)S(1)} %slice.304), channel_id=1, source_target_pairs={{0,1},{1,0},{2,3},{3,2},{4,5},{5,4},{6,7},{7,6},{8,9},{9,8},{10,11... | collective-permute-start | bytes 1179656 | tf_op jit(solution)/shard_map/ppermute | solution.py:765
  254.1 10.3 %collective-permute-start.25 = (bf16[128,1536]{1,0:T(8,128)(2,1)S(1)}, bf16[128,1536]{1,0:T(8,128)(2,1)S(1)}, u32[]{:S(2)}, u32[]{:S(2)}) collective-permute-start(bf16[128,1536]{1,0:T(8,128)(2,1)S(1)} %fusion.16), channel_id=1, source_target_pairs={{0,1},{1,0},{2,3},{3,2},{4,5},{5,4},{6,7},{7,6},{8,9},{9,8},{10,11... | collective-permute-start | bytes 1179656 | tf_op jit(solution)/shard_map/ppermute | solution.py:765
  279.5 9.4 %collective-permute-start.26 = (bf16[128,1536]{1,0:T(8,128)(2,1)S(1)}, bf16[128,1536]{1,0:T(8,128)(2,1)S(1)}, u32[]{:S(2)}, u32[]{:S(2)}) collective-permute-start(bf16[128,1536]{1,0:T(8,128)(2,1)S(1)} %get-tuple-element.155), channel_id=1, source_target_pairs={{0,1},{1,0},{2,3},{3,2},{4,5},{5,4},{6,7},{7,6},{8,9},{9,8},{10,11... | collective-permute-start | bytes 1179656 | tf_op jit(solution)/shard_map/ppermute | solution.py:765
  281.0 29.2 %collective-permute-start.33 = (bf16[2,256,2048]{2,1,0:T(8,128)(2,1)}, bf16[2,256,2048]{2,1,0:T(8,128)(2,1)}, u32[]{:S(2)}, u32[]{:S(2)}) collective-permute-start(bf16[2,256,2048]{2,1,0:T(8,128)(2,1)} %get-tuple-element.165.refs_2_), channel_id=1, source_target_pairs={{0,2},{2,0},{4,6},{6,4},{8,10},{10,8},{12,14},{14,12},{16,18},{18,... | collective-permute-start | bytes 6291464 | tf_op jit(solution)/shard_map/ppermute | solution.py:816
  281.1 29.1 %collective-permute-start.35 = (bf16[1,256,2048]{2,1,0:T(8,128)(2,1)}, bf16[1,256,2048]{2,1,0:T(8,128)(2,1)}, u32[]{:S(2)}, u32[]{:S(2)}) collective-permute-start(bf16[1,256,2048]{2,1,0:T(8,128)(2,1)} %get-tuple-element.168.refs_6_), channel_id=1, source_target_pairs={{0,2},{2,0},{4,6},{6,4},{8,10},{10,8},{12,14},{14,12},{16,18},{18,... | collective-permute-start | bytes 3145736 | tf_op jit(solution)/shard_map/ppermute | solution.py:816
  291.8 8.7 %collective-permute-start.27 = (bf16[128,1536]{1,0:T(8,128)(2,1)}, bf16[128,1536]{1,0:T(8,128)(2,1)}, u32[]{:S(2)}, u32[]{:S(2)}) collective-permute-start(bf16[128,1536]{1,0:T(8,128)(2,1)} %get-tuple-element.329), channel_id=1, source_target_pairs={{0,1},{1,0},{2,3},{3,2},{4,5},{5,4},{6,7},{7,6},{8,9},{9,8},{10,11... | collective-permute-start | bytes 1179656 | tf_op jit(solution)/shard_map/ppermute | solution.py:765
  295.4 7.4 %collective-permute-start.36 = (bf16[768,256]{1,0:T(8,128)(2,1)S(1)}, bf16[768,256]{1,0:T(8,128)(2,1)S(1)}, u32[]{:S(2)}, u32[]{:S(2)}) collective-permute-start(bf16[768,256]{1,0:T(8,128)(2,1)S(1)} %get-tuple-element.170), channel_id=1, source_target_pairs={{0,2},{2,0},{4,6},{6,4},{8,10},{10,8},{12,14},{14,12},{16,18},{18,... | collective-permute-start | bytes 1179656 | tf_op jit(solution)/shard_map/ppermute | solution.py:816
  295.8 7.5 %collective-permute-start.34 = (bf16[768,256]{1,0:T(8,128)(2,1)S(1)}, bf16[768,256]{1,0:T(8,128)(2,1)S(1)}, u32[]{:S(2)}, u32[]{:S(2)}) collective-permute-start(bf16[768,256]{1,0:T(8,128)(2,1)S(1)} %get-tuple-element.167), channel_id=1, source_target_pairs={{0,2},{2,0},{4,6},{6,4},{8,10},{10,8},{12,14},{14,12},{16,18},{18,... | collective-permute-start | bytes 1179656 | tf_op jit(solution)/shard_map/ppermute | solution.py:816
  300.5 6.4 %collective-permute-start.32 = (bf16[768,256]{1,0:T(8,128)(2,1)S(1)}, bf16[768,256]{1,0:T(8,128)(2,1)S(1)}, u32[]{:S(2)}, u32[]{:S(2)}) collective-permute-start(bf16[768,256]{1,0:T(8,128)(2,1)S(1)} %get-tuple-element.164), channel_id=1, source_target_pairs={{0,2},{2,0},{4,6},{6,4},{8,10},{10,8},{12,14},{14,12},{16,18},{18,... | collective-permute-start | bytes 1179656 | tf_op jit(solution)/shard_map/ppermute | solution.py:816
  302.8 22.6 %collective-permute-start.38 = (bf16[1,256,768]{2,1,0:T(8,128)(2,1)S(1)}, bf16[1,256,768]{2,1,0:T(8,128)(2,1)}, u32[]{:S(2)}, u32[]{:S(2)}) collective-permute-start(bf16[1,256,768]{2,1,0:T(8,128)(2,1)S(1)} %bitcast.117), channel_id=1, source_target_pairs={{0,2},{2,0},{4,6},{6,4},{8,10},{10,8},{12,14},{14,12},{16,18},{18,... | collective-permute-start | bytes 1179656 | tf_op jit(solution)/shard_map/ppermute | solution.py:816
  303.3 22.1 %collective-permute-start.37 = (bf16[768,256]{1,0:T(8,128)(2,1)S(1)}, bf16[768,256]{1,0:T(8,128)(2,1)}, u32[]{:S(2)}, u32[]{:S(2)}) collective-permute-start(bf16[768,256]{1,0:T(8,128)(2,1)S(1)} %get-tuple-element.172), channel_id=1, source_target_pairs={{0,2},{2,0},{4,6},{6,4},{8,10},{10,8},{12,14},{14,12},{16,18},{18,... | collective-permute-start | bytes 1179656 | tf_op jit(solution)/shard_map/ppermute | solution.py:816
  306.8 18.5 %collective-permute-start.29 = (bf16[384,128]{1,0:T(8,128)(2,1)S(1)}, bf16[384,128]{1,0:T(8,128)(2,1)S(1)}, u32[]{:S(2)}, u32[]{:S(2)}) collective-permute-start(bf16[384,128]{1,0:T(8,128)(2,1)S(1)} %get-tuple-element.160), channel_id=1, source_target_pairs={{0,8},{2,10},{4,12},{6,14},{8,16},{10,18},{12,20},{14,22},{16,24},... | collective-permute-start | bytes 294920 | tf_op jit(solution)/shard_map/ppermute | solution.py:820
  310.2 15.1 %collective-permute-start.30 = (bf16[384,128]{1,0:T(8,128)(2,1)S(1)}, bf16[384,128]{1,0:T(8,128)(2,1)}, u32[]{:S(2)}, u32[]{:S(2)}) collective-permute-start(bf16[384,128]{1,0:T(8,128)(2,1)S(1)} %get-tuple-element.161), channel_id=1, source_target_pairs={{0,16},{2,18},{4,20},{6,22},{8,24},{10,26},{12,28},{14,30},{16,0},... | collective-permute-start | bytes 294920 | tf_op jit(solution)/shard_map/ppermute | solution.py:820
  310.2 15.2 %collective-permute-start.31 = (bf16[384,128]{1,0:T(8,128)(2,1)S(1)}, bf16[384,128]{1,0:T(8,128)(2,1)}, u32[]{:S(2)}, u32[]{:S(2)}) collective-permute-start(bf16[384,128]{1,0:T(8,128)(2,1)S(1)} %get-tuple-element.162), channel_id=1, source_target_pairs={{0,24},{2,26},{4,28},{6,30},{8,0},{10,2},{12,4},{14,6},{16,8},{18,... | collective-permute-start | bytes 294920 | tf_op jit(solution)/shard_map/ppermute | solution.py:820
  326.0 274.7 %reduce-scatter.5.cloned.1.call-start = ((), (), s32[]{:S(2)}) async-start(), calls=%async_computation.7 | async-start | bytes 5308416 | tf_op jit(solution)/shard_map/reduce_scatter | solution.py:881
  380.4 5.1 collective-permute-start.39
  380.4 4.0 collective-permute-start.40
  386.9 29.2 %collective-permute-start.41 = (bf16[3,1216,128]{2,1,0:T(8,128)(2,1)S(1)}, bf16[3,1216,128]{2,1,0:T(8,128)(2,1)S(1)}, u32[]{:S(2)}, u32[]{:S(2)}) collective-permute-start(bf16[3,1216,128]{2,1,0:T(8,128)(2,1)S(1)} %pad_maximum_fusion.4), channel_id=1, source_target_pairs={{0,4},{2,6},{4,0},{6,2},{8,12},{10,14},{12,8},{14,10},{16,20},{18,... | collective-permute-start | bytes 2801672 | tf_op jit(solution)/shard_map/ppermute | solution.py:816
  418.9 11.3 %collective-permute-start.42 = (bf16[1152,128]{1,0:T(8,128)(2,1)}, bf16[1152,128]{1,0:T(8,128)(2,1)}, u32[]{:S(2)}, u32[]{:S(2)}) collective-permute-start(bf16[1152,128]{1,0:T(8,128)(2,1)} %get-tuple-element.188), channel_id=1, source_target_pairs={{0,24},{2,26},{4,28},{6,30},{8,0},{10,2},{12,4},{14,6},{16,8},{18,... | collective-permute-start | bytes 884744 | tf_op jit(solution)/shard_map/ppermute | solution.py:820
  421.1 22.6 %collective-permute-start.43 = (bf16[1152,128]{1,0:T(8,128)(2,1)}, bf16[1152,128]{1,0:T(8,128)(2,1)}, u32[]{:S(2)}, u32[]{:S(2)}) collective-permute-start(bf16[1152,128]{1,0:T(8,128)(2,1)} %get-tuple-element.189), channel_id=1, source_target_pairs={{0,16},{2,18},{4,20},{6,22},{8,24},{10,26},{12,28},{14,30},{16,0},... | collective-permute-start | bytes 884744 | tf_op jit(solution)/shard_map/ppermute | solution.py:820
  421.1 22.6 %collective-permute-start.44 = (bf16[1152,128]{1,0:T(8,128)(2,1)}, bf16[1152,128]{1,0:T(8,128)(2,1)}, u32[]{:S(2)}, u32[]{:S(2)}) collective-permute-start(bf16[1152,128]{1,0:T(8,128)(2,1)} %get-tuple-element.190), channel_id=1, source_target_pairs={{0,8},{2,10},{4,12},{6,14},{8,16},{10,18},{12,20},{14,22},{16,24},... | collective-permute-start | bytes 884744 | tf_op jit(solution)/shard_map/ppermute | solution.py:820
  430.0 83.0 %collective-permute-start.28 = (bf16[128,1536]{1,0:T(8,128)(2,1)}, bf16[128,1536]{1,0:T(8,128)(2,1)}, u32[]{:S(2)}, u32[]{:S(2)}) collective-permute-start(bf16[128,1536]{1,0:T(8,128)(2,1)} %copy-done.30), channel_id=1, source_target_pairs={{0,1},{1,0},{2,3},{3,2},{4,5},{5,4},{6,7},{7,6},{8,9},{9,8},{10,11... | collective-permute-start | bytes 1179656 | tf_op jit(solution)/shard_map/ppermute | solution.py:765
  451.0 9.3 %collective-permute-start.45 = (bf16[1,256,2304]{2,1,0:T(8,128)(2,1)}, bf16[1,256,2304]{2,1,0:T(8,128)(2,1)S(1)}, u32[]{:S(2)}, u32[]{:S(2)}) collective-permute-start(bf16[1,256,2304]{2,1,0:T(8,128)(2,1)} %bitcast.44.refs_2_), channel_id=1, source_target_pairs={{0,2},{2,0},{4,6},{6,4},{8,10},{10,8},{12,14},{14,12},{16,18},{18,... | collective-permute-start | bytes 3538952 | tf_op jit(solution)/shard_map/ppermute | solution.py:816
  492.1 9.2 %collective-permute-start.48 = (bf16[192,384]{1,0:T(8,128)(2,1)S(1)}, bf16[192,384]{1,0:T(8,128)(2,1)S(1)}, u32[]{:S(2)}, u32[]{:S(2)}) collective-permute-start(bf16[192,384]{1,0:T(8,128)(2,1)S(1)} %get-tuple-element.205.refs_0_), channel_id=1, source_target_pairs={{0,24},{2,26},{4,28},{6,30},{8,0},{10,2},{12,4},{14,6},{16,8},{18,... | collective-permute-start | bytes 442376 | tf_op jit(solution)/shard_map/ppermute | solution.py:820
  493.3 18.7 %collective-permute-start.49 = (bf16[192,384]{1,0:T(8,128)(2,1)S(1)}, bf16[192,384]{1,0:T(8,128)(2,1)S(1)}, u32[]{:S(2)}, u32[]{:S(2)}) collective-permute-start(bf16[192,384]{1,0:T(8,128)(2,1)S(1)} %get-tuple-element.205.refs_0_), channel_id=1, source_target_pairs={{0,16},{2,18},{4,20},{6,22},{8,24},{10,26},{12,28},{14,30},{16,0},... | collective-permute-start | bytes 442376 | tf_op jit(solution)/shard_map/ppermute | solution.py:820
  493.8 18.1 %collective-permute-start.50 = (bf16[192,384]{1,0:T(8,128)(2,1)S(1)}, bf16[192,384]{1,0:T(8,128)(2,1)S(1)}, u32[]{:S(2)}, u32[]{:S(2)}) collective-permute-start(bf16[192,384]{1,0:T(8,128)(2,1)S(1)} %get-tuple-element.205.refs_0_), channel_id=1, source_target_pairs={{0,8},{2,10},{4,12},{6,14},{8,16},{10,18},{12,20},{14,22},{16,24},... | collective-permute-start | bytes 442376 | tf_op jit(solution)/shard_map/ppermute | solution.py:820
  497.1 16.0 %collective-permute-start.46 = (bf16[128,1536]{1,0:T(8,128)(2,1)S(1)}, bf16[128,1536]{1,0:T(8,128)(2,1)S(1)}, u32[]{:S(2)}, u32[]{:S(2)}) collective-permute-start(bf16[128,1536]{1,0:T(8,128)(2,1)S(1)} %slice.303), channel_id=1, source_target_pairs={{0,1},{1,0},{2,3},{3,2},{4,5},{5,4},{6,7},{7,6},{8,9},{9,8},{10,11... | collective-permute-start | bytes 1179656 | tf_op jit(solution)/shard_map/ppermute | solution.py:765
  512.0 12.1 %collective-permute-start.51 = (bf16[192,1536]{1,0:T(8,128)(2,1)S(1)}, bf16[192,1536]{1,0:T(8,128)(2,1)}, u32[]{:S(2)}, u32[]{:S(2)}) collective-permute-start(bf16[192,1536]{1,0:T(8,128)(2,1)S(1)} %shard_map.341), channel_id=1, source_target_pairs={{0,4},{2,6},{4,0},{6,2},{8,12},{10,14},{12,8},{14,10},{16,20},{18,... | collective-permute-start | bytes 1769480 | tf_op jit(solution)/shard_map/ppermute | solution.py:816
  521.8 5.2 collective-permute-start.47
  530.2 25.4 %collective-permute-start.53 = (bf16[768,256]{1,0:T(8,128)(2,1)S(1)}, bf16[768,256]{1,0:T(8,128)(2,1)}, u32[]{:S(2)}, u32[]{:S(2)}) collective-permute-start(bf16[768,256]{1,0:T(8,128)(2,1)S(1)} %convolution_convert_fusion), channel_id=1, source_target_pairs={{0,1},{1,0},{2,3},{3,2},{4,5},{5,4},{6,7},{7,6},{8,9},{9,8},{10,11... | collective-permute-start | bytes 1179656 | tf_op jit(solution)/shard_map/ppermute | solution.py:765
  532.8 6.1 %collective-permute-start.55 = (f32[4,9216]{1,0:T(4,128)S(1)}, f32[4,9216]{1,0:T(4,128)S(1)}, u32[]{:S(2)}, u32[]{:S(2)}) collective-permute-start(f32[4,9216]{1,0:T(4,128)S(1)} %add.477), channel_id=1, source_target_pairs={{0,4},{2,6},{4,0},{6,2},{8,12},{10,14},{12,8},{14,10},{16,20},{18,... | collective-permute-start | bytes 442376 | tf_op jit(solution)/shard_map/ppermute | solution.py:816
  539.0 20.4 %collective-permute-start.56 = (f32[4,9216]{1,0:T(4,128)S(1)}, f32[4,9216]{1,0:T(4,128)S(1)}, u32[]{:S(2)}, u32[]{:S(2)}) collective-permute-start(f32[4,9216]{1,0:T(4,128)S(1)} %add.478), channel_id=1, source_target_pairs={{0,8},{2,10},{4,12},{6,14},{8,0},{10,2},{12,4},{14,6},{16,24},{18,... | collective-permute-start | bytes 442376 | tf_op jit(solution)/shard_map/ppermute | solution.py:816
  559.4 9.9 %collective-permute-start.57 = (f32[4,9216]{1,0:T(4,128)S(1)}, f32[4,9216]{1,0:T(4,128)S(1)}, u32[]{:S(2)}, u32[]{:S(2)}) collective-permute-start(f32[4,9216]{1,0:T(4,128)S(1)} %add.479), channel_id=1, source_target_pairs={{0,16},{2,18},{4,20},{6,22},{8,24},{10,26},{12,28},{14,30},{16,0},... | collective-permute-start | bytes 442376 | tf_op jit(solution)/shard_map/ppermute | solution.py:816
  564.0 24.2 %all-to-all-start.1 = ((bf16[16,48,256]{2,1,0:T(8,128)(2,1)}), bf16[16,48,256]{2,1,0:T(8,128)(2,1)S(1)}, u32[]{:S(2)}, u32[]{:S(2)}) async-start(bf16[16,48,256]{2,1,0:T(8,128)(2,1)} %bitcast.52), calls=%async_computation.2 | async-start | bytes 786432 | tf_op jit(solution)/shard_map/all_to_all | solution.py:1202
  572.8 4.3 collective-permute-start.59
  577.1 4.2 collective-permute-start.60
  581.3 6.2 %collective-permute-start.61 = (f32[3,1024]{1,0:T(4,128)S(1)}, f32[3,1024]{1,0:T(4,128)S(1)}, u32[]{:S(2)}, u32[]{:S(2)}) collective-permute-start(f32[3,1024]{1,0:T(4,128)S(1)} %add.483), channel_id=1, source_target_pairs={{0,16},{2,18},{4,20},{6,22},{8,24},{10,26},{12,28},{14,30},{16,0},... | collective-permute-start | bytes 36872 | tf_op jit(solution)/shard_map/ppermute | solution.py:816
  (105 other events, 1282.3 us)
Sparse Core Ops, SparseCore 0:
  10.9 75.6 all-gather.2
  88.8 144.4 all-gather.4
  325.5 166.5 reduce-scatter.2
  496.0 104.6 reduce-scatter.4

commit v6 on v5

--- a/solution.py
+++ b/solution.py
@@ -16,6 +16,7 @@
 LOW = jnp.bfloat16
 FLOAT = jnp.float32
 MIB = 1024 * 1024
+LARGE = pl.CostEstimate(flops=25 * 10**9, bytes_accessed=1024, transcendentals=0)
 SMALL = pl.CostEstimate(flops=1024, bytes_accessed=1024, transcendentals=0)
 
 
@@ -86,17 +87,19 @@
         )
 
 
-def forward_kernel(near, chunk, *refs):
+def forward_kernel(near, chunk, last, *refs):
     near_refs, refs = refs[:near], refs[near:]
     query_ref, qf_ref, kf_ref, tf_ref, gate_ref = refs[:5]
-    mixed_refs, refs = refs[5 : 5 + SPLIT], refs[5 + SPLIT :]
+    refs = refs[5:]
+    if last:
+        before_refs, mixed_refs, refs = refs[:2], refs[2 : 2 + SPLIT], refs[2 + SPLIT :]
     outs_ref, stats_ref, queries, keys, values, text_keys, text_values, hold = refs
     build_inputs(
         pl.program_id(0), near_refs, query_ref, qf_ref, kf_ref, tf_ref,
         queries, keys, values, text_keys, text_values,
     )
     rows = queries.shape[0] // SPLIT * FORWARD_SLOTS
-    text_chunk = pick_tile(text_keys.shape[0], 256)
+    text_chunk = pick_tile(text_keys.shape[0], 384)
 
     def tile_step(tile, carry):
         spot = pl.ds(pl.multiple_of(tile * rows, rows), rows)
@@ -117,6 +120,12 @@
         blank = jnp.zeros((rows, 128), FLOAT)
         own = lax.fori_loop(0, keys.shape[0] // chunk, step, blank)
         cross = lax.fori_loop(0, text_keys.shape[0] // text_chunk, text_step, blank, unroll=True)
+        if not last:
+            outs_ref[spot, :] = own
+            stats_ref[spot, :] = cross
+            return carry
+        own = own + before_refs[0][spot, :]
+        cross = cross + before_refs[1][spot, :]
         own_inverse = 1.0 / own[:, 0:1]
         cross_inverse = 1.0 / cross[:, 0:1]
         own = own * own_inverse
@@ -131,72 +140,80 @@
         return carry
 
     lax.fori_loop(0, SPLIT // FORWARD_SLOTS, tile_step, 0)
-    for index, ref in enumerate(mixed_refs):
-        ref[...] = hold[index]
+    if last:
+        for index, ref in enumerate(mixed_refs):
+            ref[...] = hold[index]
 
 
 def whole(shape):
     return pl.BlockSpec(shape, lambda i: (0,) * len(shape))
 
 
-def attention_specs(pairs, queries, qf, kf, tf):
+def attention_specs(part, pairs, queries, qf, kf, tf):
     return [whole(value.shape) for value in pairs] + [
         pl.BlockSpec(qf.shape, lambda i: (i, 0)),
         whole(qf.shape),
-        whole(kf.shape),
-        whole(tf.shape),
+        pl.BlockSpec((kf.shape[0] // 2, 128), lambda i: (part, 0)),
+        pl.BlockSpec((tf.shape[0] // 2, 128), lambda i: (part, 0)),
         pl.BlockSpec((1, 8, 128), lambda i: (i, 0, 0)),
     ]
 
 
 def attention_scratch(qf, kf, tf):
+    keys, text_keys = (kf.shape[0] // 2, 128), (tf.shape[0] // 2, 128)
     return [
         pltpu.VMEM(qf.shape, LOW),
-        pltpu.VMEM(kf.shape, LOW),
-        pltpu.VMEM(kf.shape, LOW),
-        pltpu.VMEM(tf.shape, LOW),
-        pltpu.VMEM(tf.shape, LOW),
+        pltpu.VMEM(keys, LOW),
+        pltpu.VMEM(keys, LOW),
+        pltpu.VMEM(text_keys, LOW),
+        pltpu.VMEM(text_keys, LOW),
     ]
 
 
-def attention_forward(pairs, queries, qf, kf, tf, gates):
+def attention_forward(pairs, queries, qf, kf, tf, gates, before):
     rows = qf.shape[0]
     heads = gates.shape[0]
     half = rows // SPLIT // 2
     folded = jax.ShapeDtypeStruct((heads * half, 128), LOW)
     wide = jax.ShapeDtypeStruct((heads * rows, 128), FLOAT)
+    wide_spec = pl.BlockSpec((rows, 128), lambda i: (i, 0))
+    last = len(before) > 0
+    slots = SPLIT if last else 0
     out = pl.pallas_call(
-        functools.partial(forward_kernel, len(pairs), pick_tile(kf.shape[0], 2048)),
+        functools.partial(forward_kernel, len(pairs), pick_tile(kf.shape[0] // 2, 2048), last),
         grid=(heads,),
-        in_specs=attention_specs(pairs, queries, qf, kf, tf),
-        out_specs=[pl.BlockSpec((half, 128), lambda i: (i, 0))] * SPLIT
-        + [pl.BlockSpec((rows, 128), lambda i: (i, 0))] * 2,
-        out_shape=[folded] * SPLIT + [wide] * 2,
+        in_specs=attention_specs(int(last), pairs, queries, qf, kf, tf) + [wide_spec] * len(before),
+        out_specs=[pl.BlockSpec((half, 128), lambda i: (i, 0))] * slots + [wide_spec] * 2,
+        out_shape=[folded] * slots + [wide] * 2,
         scratch_shapes=attention_scratch(qf, kf, tf) + [pltpu.VMEM((SPLIT, half, 128), LOW)],
         compiler_params=pltpu.CompilerParams(vmem_limit_bytes=60 * MIB),
-        cost_estimate=SMALL,
-    )(*pairs, queries, qf, kf, tf, gates)
-    return out[:SPLIT], out[SPLIT], out[SPLIT + 1]
-
-
-def backward_kernel(near, chunk, *refs):
+        cost_estimate=LARGE,
+    )(*pairs, queries, qf, kf, tf, gates, *before)
+    return (out[:slots], out[slots], out[slots + 1]) if last else tuple(out)
+
+
+def backward_kernel(near, chunk, last, *refs):
     near_refs, refs = refs[:near], refs[near:]
     query_ref, qf_ref, kf_ref, tf_ref, gate_ref = refs[:5]
     refs = refs[5:]
     grad_refs, refs = refs[:SPLIT], refs[SPLIT:]
     outs_ref, stats_ref, refs = refs[0], refs[1], refs[2:]
-    dq_refs, refs = refs[:SPLIT], refs[SPLIT:]
-    dkv_refs, dt_refs, dg_ref = refs[:2], refs[2:4], refs[4]
-    queries, keys, values, text_keys, text_values, hold, grad_hold, acc, text_acc = refs[5:]
+    if last:
+        before_ref, dq_refs, dg_ref, refs = refs[0], refs[1 : 1 + SPLIT], refs[1 + SPLIT], refs[2 + SPLIT :]
+    else:
+        dq_ref, refs = refs[0], refs[1:]
+    dkv_refs, dt_refs = refs[:2], refs[2:4]
+    queries, keys, values, text_keys, text_values, hold, grad_hold, acc, text_acc = refs[4:]
     build_inputs(
         pl.program_id(0), near_refs, query_ref, qf_ref, kf_ref, tf_ref,
         queries, keys, values, text_keys, text_values,
     )
     for index, ref in enumerate(grad_refs):
         grad_hold[index] = ref[...]
-    dg_ref[...] = jnp.zeros_like(dg_ref)
+    if last:
+        dg_ref[...] = jnp.zeros_like(dg_ref)
     rows = queries.shape[0]
-    text_chunk = pick_tile(text_keys.shape[0], 256)
+    text_chunk = pick_tile(text_keys.shape[0], 384)
     gate = gate_ref[0, 0:1, :]
 
     def tile_step(tile, carry):
@@ -208,7 +225,8 @@
         grads = jnp.where(lanes < 64, 0.0, grads)
         outs = outs_ref[spot, :]
         cross_out = jnp.where(lanes < 64, 0.0, turn(outs))
-        dg_ref[0] += jnp.sum((grads * cross_out).reshape(rows // 8, 8, 128), axis=0)
+        if last:
+            dg_ref[0] += jnp.sum((grads * cross_out).reshape(rows // 8, 8, 128), axis=0)
         cross_grads = (gate * grads).astype(LOW).astype(FLOAT)
 
         def widen(grad, out, inverse):
@@ -250,52 +268,63 @@
         blank = jnp.zeros((rows, 128), FLOAT)
         total = lax.fori_loop(0, keys.shape[0] // chunk, step, blank, unroll=4)
         total = lax.fori_loop(0, text_keys.shape[0] // text_chunk, text_step, total, unroll=True)
-        total = total * 0.125
+        if not last:
+            dq_ref[spot, :] = total
+            return carry
+        total = (total + before_ref[spot, :]) * 0.125
         each = rows // SPLIT
         for slot in range(SPLIT):
             hold[slot] = fold_low(total[each * slot : each * slot + each])
         return carry
 
     lax.fori_loop(0, 1, tile_step, 0)
-    for index, ref in enumerate(dq_refs):
-        ref[...] = hold[index]
+    if last:
+        for index, ref in enumerate(dq_refs):
+            ref[...] = hold[index]
     for values, refs in ((acc, dkv_refs), (text_acc, dt_refs)):
         size = refs[0].shape[1]
         refs[0][0] = values[:size, :].astype(LOW)
         refs[1][0] = values[size:, :].astype(LOW)
 
 
-def attention_backward(pairs, queries, qf, kf, tf, gates, grads, outs, stats):
+def attention_backward(pairs, queries, qf, kf, tf, gates, grads, outs, stats, before):
     rows = qf.shape[0]
     heads = gates.shape[0]
     half = rows // SPLIT // 2
+    last = len(before) > 0
     folded = jax.ShapeDtypeStruct((heads * half, 128), LOW)
-    piece = jax.ShapeDtypeStruct((heads, kf.shape[0] // 2, 128), LOW)
-    text = jax.ShapeDtypeStruct((heads, tf.shape[0] // 2, 128), LOW)
+    piece = jax.ShapeDtypeStruct((heads, kf.shape[0] // 4, 128), LOW)
+    text = jax.ShapeDtypeStruct((heads, tf.shape[0] // 4, 128), LOW)
     sums = jax.ShapeDtypeStruct((heads, 8, 128), FLOAT)
+    wide = jax.ShapeDtypeStruct((heads * rows, 128), FLOAT)
+    wide_spec = pl.BlockSpec((rows, 128), lambda i: (i, 0))
+    folded_spec = pl.BlockSpec((half, 128), lambda i: (i, 0))
+    split = [piece, piece, text, text]
+
+    def split_spec(value):
+        return pl.BlockSpec((1,) + value.shape[1:], lambda i: (i, 0, 0))
+
+    first_shapes = [folded] * SPLIT + [sums] if last else [wide]
+    first_specs = [folded_spec] * SPLIT + [split_spec(sums)] if last else [wide_spec]
     out = pl.pallas_call(
-        functools.partial(backward_kernel, len(pairs), pick_tile(kf.shape[0], 1024)),
+        functools.partial(backward_kernel, len(pairs), pick_tile(kf.shape[0] // 2, 2048), last),
         grid=(heads,),
-        in_specs=attention_specs(pairs, queries, qf, kf, tf)
-        + [pl.BlockSpec((half, 128), lambda i: (i, 0))] * SPLIT
-        + [pl.BlockSpec((rows, 128), lambda i: (i, 0))] * 2,
-        out_specs=[pl.BlockSpec((half, 128), lambda i: (i, 0))] * SPLIT
-        + [
-            pl.BlockSpec((1,) + value.shape[1:], lambda i: (i, 0, 0))
-            for value in (piece, piece, text, text, sums)
-        ],
-        out_shape=[folded] * SPLIT + [piece, piece, text, text, sums],
+        in_specs=attention_specs(int(not last), pairs, queries, qf, kf, tf)
+        + [folded_spec] * SPLIT
+        + [wide_spec] * (2 + len(before)),
+        out_specs=first_specs + [split_spec(value) for value in split],
+        out_shape=first_shapes + split,
         scratch_shapes=attention_scratch(qf, kf, tf)
         + [
             pltpu.VMEM((SPLIT, half, 128), LOW),
             pltpu.VMEM((SPLIT, half, 128), LOW),
-            pltpu.VMEM(kf.shape, FLOAT),
-            pltpu.VMEM(tf.shape, FLOAT),
+            pltpu.VMEM((kf.shape[0] // 2, 128), FLOAT),
+            pltpu.VMEM((tf.shape[0] // 2, 128), FLOAT),
         ],
         compiler_params=pltpu.CompilerParams(vmem_limit_bytes=60 * MIB),
-        cost_estimate=SMALL,
-    )(*pairs, queries, qf, kf, tf, gates, *grads, outs, stats)
-    return (out[:SPLIT],) + tuple(out[SPLIT:])
+        cost_estimate=LARGE,
+    )(*pairs, queries, qf, kf, tf, gates, *grads, outs, stats, *before)
+    return out[: len(first_shapes)], out[len(first_shapes) :]
 
 
 def half_means(values, lanes):
@@ -653,24 +682,23 @@
     )(*operands)
 
 
-def columns_kernel(core_ref, values_ref, own_ref, other_ref, hold):
+def columns_kernel(order, core_ref, values_ref, own_ref, other_ref, hold):
     turned = jnp.transpose(values_ref[...].astype(FLOAT))
     hold[...] = turned.reshape(hold.shape)
-    pairs = hold.shape[0] // 2
     core = core_ref[0]
     own_ref[...] = jnp.concatenate(
-        [hold[2 * pair + core] for pair in range(pairs)], axis=0
+        [hold[2 * pair + core] for pair in order], axis=0
     ).astype(LOW)
     other_ref[...] = jnp.concatenate(
-        [hold[2 * pair + 1 - core] for pair in range(pairs)], axis=0
+        [hold[2 * pair + 1 - core] for pair in order], axis=0
     ).astype(LOW)
 
 
-def split_columns(core, values, block):
+def split_columns(core, values, block, order):
     rows, width = values.shape
     half = jax.ShapeDtypeStruct((width // 2, rows), LOW)
     return small_call(
-        columns_kernel,
+        functools.partial(columns_kernel, order),
         (core, values),
         [half, half],
         [pltpu.VMEM((width // block, block, rows), FLOAT)],
@@ -833,7 +861,7 @@
 
     def spread_list(values):
         values = [values]
-        for bit in bits:
+        for bit in bits[1:]:
             values = values + [flip(value, bit) for value in values]
         return values
 
@@ -869,12 +897,16 @@
         flips.append(mask)
 
     core = dp_index % 2
-    core_groups = [list(range(first, dp, 2)) for first in range(2)]
+    pair_order = []
+    for column in range(near // 2):
+        line = [group * (near // 2) + column for group in range(SPLIT)]
+        pair_order += line if column % 2 == 0 else line[::-1]
+    core_groups = [[2 * pair + first for pair in pair_order] for first in range(2)]
 
     core_at = core.astype(jnp.int32).reshape(1)
 
     def core_columns(values):
-        own, other = split_columns(core_at, values, weight_rows)
+        own, other = split_columns(core_at, values, weight_rows, pair_order)
         return own, flip(other, 1)
 
     def scatter(values):
@@ -958,7 +990,8 @@
     ky_gain = jnp.broadcast_to(ky_gain[None], (8, 128))
 
     lanes = jnp.arange(128, dtype=jnp.int32)[None, :]
-    text_groups_at = jnp.stack([near_index ^ mask for mask in flips])
+    ordered = flips[0::2] + flips[1::2]
+    text_groups_at = jnp.stack([near_index ^ mask for mask in ordered])
     text_clip = (
         text_groups_at[:, None] * group_rows + jnp.arange(group_rows, dtype=jnp.int32)[None, :]
     ).reshape(-1) // TXT
@@ -966,7 +999,7 @@
     block_at = jnp.stack(
         [
             ((far_index - steps) % SPLIT) * near + (near_index ^ mask)
-            for mask in flips
+            for mask in ordered
             for steps in range(SPLIT)
         ]
     )
@@ -1022,10 +1055,13 @@
     arrived = send_slots(head_slots)
     arrived, grad_ffn = tie(arrived, grad_ffn)
     own_pairs, queries = gather_slots(arrived, text_pairs, each)
-    pairs = spread_list(own_pairs)
-    mixed_slots, head_outs, head_stats = attention_forward(
-        pairs, queries, query_features, key_features, text_features, gate_lanes
-    )
+    far_pairs = flip(own_pairs, bits[0])
+    near_keys = spread_list(own_pairs)
+    shared = (queries, query_features, key_features, text_features, gate_lanes)
+    partial_sums = attention_forward(near_keys, *shared, ())
+    far_pairs, partial_sums = tie(far_pairs, partial_sums)
+    far_keys = spread_list(far_pairs)
+    mixed_slots, head_outs, head_stats = attention_forward(far_keys, *shared, partial_sums)
     mixed = join_heads(far, return_slots(mixed_slots), heads)
     attn_rows = own_rows(dot_turned(mixed, out_full))
     after_attn = input_rows + gate_one * attn_rows
@@ -1085,21 +1121,30 @@
         other = flip(sent, bit)
         return terms + [other[:, :size]], text_terms + [other[:, size:]]
 
-    folded, *pieces, gate_parts = attention_backward(
-        pairs,
-        queries,
-        query_features,
-        key_features,
-        text_features,
-        gate_lanes,
-        grad_slots,
-        head_outs,
-        head_stats,
-    )
-    state = start_sums(*pieces)
-    for bit in reversed(bits[:-1]):
-        state = next_state(state, next_send(state), bit)
-    pair_terms, text_terms = state
+    def reduce_near(pieces):
+        state = start_sums(*pieces)
+        for bit in reversed(bits[1:-1]):
+            state = next_state(state, next_send(state), bit)
+        return state
+
+    saved = (head_outs, head_stats)
+    query_part, far_pieces = attention_backward(far_keys, *shared, grad_slots, *saved, ())
+    far_terms, far_text = reduce_near(far_pieces)
+    sent = jnp.concatenate(
+        [
+            total_rows(far_terms, 0, group_tokens),
+            total_rows(far_text, 0, group_rows),
+        ],
+        axis=1,
+    )
+    grad_slots, sent = tie(grad_slots, sent)
+    came = flip(sent, bits[0])
+    (*folded, gate_parts), own_pieces = attention_backward(
+        near_keys, *shared, grad_slots, *saved, query_part
+    )
+    pair_terms, text_terms = reduce_near(own_pieces)
+    pair_terms = pair_terms + [came[:, :group_tokens]]
+    text_terms = text_terms + [came[:, group_tokens:]]
     back_slots = pack_slots(pair_terms, folded)
     clip_at = jnp.arange(clip_count, dtype=jnp.int32)[:, None]
 
@@ -1130,9 +1175,9 @@
         [*last_left[1], mixed_right, mixed_other],
         local_width,
     )
+    normed_part, last_grads, text_low = tie(normed_part, last_grads, text_low)
     last_grads, feed_low = tie(last_grads, feed_low)
     last_low = scatter(last_grads)
-    normed_part, last_grads, text_low = tie(normed_part, last_grads, text_low)
     grad_normed_one = own_rows(normed_part)
     _, pull_one = jax.vjp(modulated, input_rows, first_gain, shift_one, scale_one)
     back_one, grad_first_gain, grad_shift_one, grad_scale_one = pull_one(grad_normed_one)

time: 621 us -> 593 us (0.955)
  starting transfers between devices: 91.7 us -> 74.8 us
  waiting for transfers between devices: 276 us -> 266 us
    reduce_scatter x2, waiting for transfers between devices: 37.3 us -> 0.02 us  [scatter(): lax.psum_scatter(values, 'dp', scatter_dimension=0, axis_index_groups=cor...]
    ppermute x34 -> x36, starting transfers between devices: 35.3 us -> 13.1 us  [flip(): return lax.ppermute(values, 'dp', [(j, j ^ bit) for j in range(dp)])]
    ppermute x18, waiting for transfers between devices: 71 us -> 92.8 us  [shift(): return lax.ppermute(values, 'dp', pairs)]
    ppermute x34 -> x36, waiting for transfers between devices: 136 us -> 144 us  [flip(): return lax.ppermute(values, 'dp', [(j, j ^ bit) for j in range(dp)])]
    unnamed x207 -> x213, local copies, waits for them, and re-layouts: 13.3 us -> 18.2 us
    pallas_call x1 -> x2, Pallas kernels: 54.4 us -> 50.1 us  [attention_backward(): pl.pallas_call(functools.partial(backward_kernel, len(pairs), pick_tile(k...]
    pallas_call x1 -> x2, Pallas kernels: 24.9 us -> 25.1 us  [attention_forward(): pl.pallas_call(functools.partial(forward_kernel, len(pairs), pick_tile(kf...]
  transfers between devices with their start and end apart: 68 -> 70, of which waited for: 34 -> 35; matrix products, arithmetic and copies ran while one was open for 11% -> 12% of each run, Pallas kernels for 19% -> 19%
where the time goes in v6:
time: 593 us; the launch traced here: 583 us
  waiting for transfers between devices  266 us (45%)
  Pallas kernels  124 us (21%)
  starting transfers between devices  74.8 us (13%)
  other arithmetic  38.9 us (7%)
  local copies, waits for them, and re-layouts  32.5 us (5%)
  between operations  25.4 us (4%)
  matrix products  22.2 us (4%)
    ppermute x36, waiting for transfers between devices, flip(): return lax.ppermute(values, 'dp', [(j, j ^ bit) for j in range(dp)])  144 us
    ppermute x18, waiting for transfers between devices, shift(): return lax.ppermute(values, 'dp', pairs)  92.8 us
    pallas_call x2, Pallas kernels, attention_backward(): pl.pallas_call(functools.partial(backward_kernel, len(pairs), pick_tile(k...  50.1 us
    ppermute x18, starting transfers between devices, shift(): return lax.ppermute(values, 'dp', pairs)  35.3 us
    ppermute x10, waiting for transfers between devices, swapped(): return lax.ppermute(values, 'tensor', [(0, 1), (1, 0)])  28.7 us
    pallas_call x2, Pallas kernels, attention_forward(): pl.pallas_call(functools.partial(forward_kernel, len(pairs), pick_tile(kf...  25.1 us
    pallas_call x2, Pallas kernels, outer_products(): pl.pallas_call(functools.partial(outer_kernel, steps[0]), grid=(sum(steps...  18.9 us
    unnamed x213, local copies, waits for them, and re-layouts  18.2 us
  transfers between devices with their start and end apart: 70, of which 35 were waited for; matrix products, arithmetic and copies ran while one was open for 12% of the time, Pallas kernels for 19%

profile of v6, /device:TPU:0, one launch (start us, length us, event | category | flops | bytes accessed | tf_op | source)
XLA Modules:
  0.0 583.4 jit_solution(5853818075464314849)
XLA Ops:
  7.3 1.9 copy.85
  10.0 7.4 %all-to-all-start = ((bf16[48,16,256]{2,0,1:T(8,128)(2,1)}), bf16[48,16,256]{2,0,1:T(8,128)(2,1)S(1)}, u32[]{:S(2)}, u32[]{:S(2)}) async-start(bf16[48,16,256]{2,0,1:T(8,128)(2,1)} %bitcast.116), calls=%async_computation | async-start | bytes 786432 | tf_op jit(solution)/shard_map/all_to_all | solution.py:937
  21.1 2.2 pad_maximum_fusion.2
  25.4 6.7 %collective-permute-done.8 = f32[3,6144]{1,0:T(4,128)S(1)} collective-permute-done((f32[3,6144]{1,0:T(4,128)S(1)}, f32[3,6144]{1,0:T(4,128)S(1)}, u32[]{:S(2)}, u32[]{:S(2)}) %collective-permute-start.8) | collective-permute-done | bytes 73760 | tf_op jit(solution)/shard_map/ppermute | solution.py:844
  33.8 10.3 %collective-permute-done.9 = f32[3,6144]{1,0:T(4,128)S(1)} collective-permute-done((f32[3,6144]{1,0:T(4,128)S(1)}, f32[3,6144]{1,0:T(4,128)S(1)}, u32[]{:S(2)}, u32[]{:S(2)}) %collective-permute-start.9) | collective-permute-done | bytes 73760 | tf_op jit(solution)/shard_map/ppermute | solution.py:844
  49.0 1.8 collective-permute-done.10
  51.6 6.3 %collective-permute-done.2 = f32[4,3072]{1,0:T(4,128)S(1)} collective-permute-done((f32[4,3072]{1,0:T(4,128)S(1)}, f32[4,3072]{1,0:T(4,128)S(1)}, u32[]{:S(2)}, u32[]{:S(2)}) %collective-permute-start.2) | collective-permute-done | bytes 49184 | tf_op jit(solution)/shard_map/ppermute | solution.py:844
  59.9 7.1 %collective-permute-done.3 = f32[4,3072]{1,0:T(4,128)S(1)} collective-permute-done((f32[4,3072]{1,0:T(4,128)S(1)}, f32[4,3072]{1,0:T(4,128)S(1)}, u32[]{:S(2)}, u32[]{:S(2)}) %collective-permute-start.3) | collective-permute-done | bytes 49184 | tf_op jit(solution)/shard_map/ppermute | solution.py:844
  67.5 2.0 collective-permute-start.4
  69.8 2.7 fusion.refs_4_
  76.5 9.6 %collective-permute-done.6 = bf16[192,1536]{1,0:T(8,128)(2,1)S(1)} collective-permute-done((bf16[192,1536]{1,0:T(8,128)(2,1)S(1)}, bf16[192,1536]{1,0:T(8,128)(2,1)S(1)}, u32[]{:S(2)}, u32[]{:S(2)}) %collective-permute-start.6) | collective-permute-done | bytes 589856 | tf_op jit(solution)/shard_map/ppermute | solution.py:844
  88.9 3.3 collective-permute-start.12
  96.9 5.0 fusion.60.qkv_ref.refs_4_
  101.9 4.2 shard_map.324
  108.1 4.2 collective-permute-start.14
  112.3 2.4 collective-permute-start.16
  119.6 7.0 %collective-permute-done.14.refs_1_ = bf16[1152,128]{1,0:T(8,128)(2,1)} collective-permute-done((bf16[1152,128]{1,0:T(8,128)(2,1)}, bf16[1152,128]{1,0:T(8,128)(2,1)}, u32[]{:S(2)}, u32[]{:S(2)}) %collective-permute-start.14) | collective-permute-done | bytes 294944 | tf_op jit(solution)/shard_map/ppermute | solution.py:848
  126.6 13.6 %collective-permute-done.15.refs_2_ = bf16[1152,128]{1,0:T(8,128)(2,1)} collective-permute-done((bf16[1152,128]{1,0:T(8,128)(2,1)}, bf16[1152,128]{1,0:T(8,128)(2,1)}, u32[]{:S(2)}, u32[]{:S(2)}) %collective-permute-start.15) | collective-permute-done | bytes 294944 | tf_op jit(solution)/shard_map/ppermute | solution.py:848
  140.2 10.2 %collective-permute-done.16.refs_3_ = bf16[1152,128]{1,0:T(8,128)(2,1)} collective-permute-done((bf16[1152,128]{1,0:T(8,128)(2,1)}, bf16[1152,128]{1,0:T(8,128)(2,1)}, u32[]{:S(2)}, u32[]{:S(2)}) %collective-permute-start.16) | collective-permute-done | bytes 294944 | tf_op jit(solution)/shard_map/ppermute | solution.py:848
  150.4 2.3 shard_map.326
  157.1 11.9 %shard_map.327 = (f32[3072,128]{1,0:T(8,128)}, f32[3072,128]{1,0:T(8,128)}) custom-call(bf16[3648,128]{1,0:T(8,128)(2,1)} %get-tuple-element.159.refs_0_, bf16[3648,128]{1,0:T(8,128)(2,1)} %collective-permute-done.19.refs_1_, bf16[3072,128]{1,0:T(8,128)(2,1)} %copy-done.34, bf16[1024,128]{1,0:T(8,128)(2,1)} %select_convert_fusion.refs_3_, ...), custom_call_target="tpu_custom_call" | custom-call | flops 24999999488 | bytes 1024 | tf_op jit(solution)/shard_map/pallas_call | solution.py:182
  169.0 30.2 %collective-permute-done.18.refs_0_ = bf16[3648,128]{1,0:T(8,128)(2,1)} collective-permute-done((bf16[3648,128]{1,0:T(8,128)(2,1)}, bf16[3648,128]{1,0:T(8,128)(2,1)}, u32[]{:S(2)}, u32[]{:S(2)}) %collective-permute-start.18) | collective-permute-done | bytes 933920 | tf_op jit(solution)/shard_map/ppermute | solution.py:844
  199.2 2.8 collective-permute-done.20.refs_1_
  202.1 13.2 %shard_map.328 = (bf16[384,128]{1,0:T(8,128)(2,1)}, bf16[384,128]{1,0:T(8,128)(2,1)}, bf16[384,128]{1,0:T(8,128)(2,1)}, bf16[384,128]{1,0:T(8,128)(2,1)}, f32[3072,128]{1,0:T(8,128)}, /*index=5*/f32[3072,128]{1,0:T(8,128)}) custom-call(bf16[3648,128]{1,0:T(8,128)(2,1)} %collective-permute-done.18.refs_0_, bf16[3648,128]{1,0:T(8,128)(2,1)} %collective-permute-done.20.refs_1_, ...), custom_call_target="tpu_custom_call" | custom-call | flops 24999999488 | bytes 1024 | tf_op jit(solution)/shard_map/pallas_call | solution.py:182
  215.3 4.7 collective-permute-start.21
  221.0 2.8 collective-permute-done.21.refs_1_
  223.9 8.8 %collective-permute-done.22.refs_2_ = bf16[384,128]{1,0:T(8,128)(2,1)S(1)} collective-permute-done((bf16[384,128]{1,0:T(8,128)(2,1)}, bf16[384,128]{1,0:T(8,128)(2,1)S(1)}, u32[]{:S(2)}, u32[]{:S(2)}) %collective-permute-start.22) | collective-permute-done | bytes 98336 | tf_op jit(solution)/shard_map/ppermute | solution.py:848
  233.8 2.6 fusion.3
  238.2 9.0 %collective-permute-done.24 = bf16[128,1536]{1,0:T(8,128)(2,1)S(1)} collective-permute-done((bf16[128,1536]{1,0:T(8,128)(2,1)S(1)}, bf16[128,1536]{1,0:T(8,128)(2,1)S(1)}, u32[]{:S(2)}, u32[]{:S(2)}) %collective-permute-start.24) | collective-permute-done | bytes 393248 | tf_op jit(solution)/shard_map/ppermute | solution.py:793
  249.7 8.2 %collective-permute-done.25 = bf16[128,1536]{1,0:T(8,128)(2,1)S(1)} collective-permute-done((bf16[128,1536]{1,0:T(8,128)(2,1)S(1)}, bf16[128,1536]{1,0:T(8,128)(2,1)S(1)}, u32[]{:S(2)}, u32[]{:S(2)}) %collective-permute-start.25) | collective-permute-done | bytes 393248 | tf_op jit(solution)/shard_map/ppermute | solution.py:793
  258.0 15.0 %shard_map.330 = (bf16[1,256,2048]{2,1,0:T(8,128)(2,1)}, bf16[2,256,2048]{2,1,0:T(8,128)(2,1)}, f32[128,1536]{1,0:T(8,128)S(1)}, bf16[128,1536]{1,0:T(8,128)(2,1...) custom-call(bf16[256,1536]{1,0:T(8,128)(2,1)S(1)} %pad_maximum_fusion.7.normed_ref.values_ref, ...), custom_call_target="tpu_custom_call" | custom-call | flops 1024 | bytes 1024 | tf_op jit(solution)/shard_map/pallas_call | solution.py:749
  274.9 7.0 %collective-permute-done.26 = bf16[128,1536]{1,0:T(8,128)(2,1)S(1)} collective-permute-done((bf16[128,1536]{1,0:T(8,128)(2,1)S(1)}, bf16[128,1536]{1,0:T(8,128)(2,1)S(1)}, u32[]{:S(2)}, u32[]{:S(2)}) %collective-permute-start.26) | collective-permute-done | bytes 393248 | tf_op jit(solution)/shard_map/ppermute | solution.py:793
  289.5 3.5 collective-permute-done.27
  295.9 2.6 fusion.1.grad_ref
  299.3 9.8 %collective-permute-start.29 = (bf16[384,128]{1,0:T(8,128)(2,1)S(1)}, bf16[384,128]{1,0:T(8,128)(2,1)S(1)}, u32[]{:S(2)}, u32[]{:S(2)}) collective-permute-start(bf16[384,128]{1,0:T(8,128)(2,1)S(1)} %get-tuple-element.181), channel_id=1, source_target_pairs={{0,8},{2,10},{4,12},{6,14},{8,16},{10,18},{12,20},{14,22},{16,24},... | collective-permute-start | bytes 294920 | tf_op jit(solution)/shard_map/ppermute | solution.py:848
  309.1 2.4 collective-permute-start.31
  311.6 12.8 %shard_map.334 = bf16[768,6144]{1,0:T(8,128)(2,1)} custom-call(bf16[768,256]{1,0:T(8,128)(2,1)S(1)} %get-tuple-element.184.refs_0_, bf16[768,256]{1,0:T(8,128)(2,1)S(1)} %collective-permute-done.32.refs_1_, bf16[2,256,2048]{2,1,0:T(8,128)(2,1)S(1)} %copy-done.4, bf16[2,256,2048]{2,1,0:T(8,128)(2,1)} %collective-permute-done.33.refs_3_, ...), custom_call_target="tpu_custom_call" | custom-call | flops 1024 | bytes 1024 | tf_op jit(solution)/shard_map/pallas_call | solution.py:674
  325.2 24.6 %shard_map.337 = (f32[3072,128]{1,0:T(8,128)}, bf16[3,1024,128]{2,1,0:T(8,128)(2,1)}, bf16[3,1024,128]{2,1,0:T(8,128)(2,1)}, bf16[3,192,128]{2,1,0:T(8,128)(2,1)}, bf16[3,192,128]{2,1,0:T(8,128)(2,1)}) custom-call(bf16[3648,128]{1,0:T(8,128)(2,1)} %collective-permute-done.18.refs_0_, bf16[3648,128]{1,0:T(8,128)(2,1)} %collective-permute-done.20.refs_1_, ...), custom_call_target="tpu_custom_call" | custom-call | flops 24999999488 | bytes 1024 | tf_op jit(solution)/shard_map/pallas_call | solution.py:309
  350.4 2.2 collective-permute-done.40
  356.6 25.5 %shard_map.338 = (bf16[384,128]{1,0:T(8,128)(2,1)}, bf16[384,128]{1,0:T(8,128)(2,1)}, bf16[384,128]{1,0:T(8,128)(2,1)}, bf16[384,128]{1,0:T(8,128)(2,1)}, f32[3,...) custom-call(bf16[3648,128]{1,0:T(8,128)(2,1)} %get-tuple-element.159, ...), custom_call_target="tpu_custom_call" | custom-call | flops 24999999488 | bytes 1024 | tf_op jit(solution)/shard_map/pallas_call | solution.py:309
  382.2 17.4 %collective-permute-done.42 = bf16[3,1216,128]{2,1,0:T(8,128)(2,1)} collective-permute-done((bf16[3,1216,128]{2,1,0:T(8,128)(2,1)}, bf16[3,1216,128]{2,1,0:T(8,128)(2,1)}, u32[]{:S(2)}, u32[]{:S(2)}) %collective-permute-start.42) | collective-permute-done | bytes 933920 | tf_op jit(solution)/shard_map/ppermute | solution.py:844
  401.1 2.0 collective-permute-start.43
  404.0 17.9 %collective-permute-done.43.refs_1_ = bf16[1152,128]{1,0:T(8,128)(2,1)S(1)} collective-permute-done((bf16[1152,128]{1,0:T(8,128)(2,1)S(1)}, bf16[1152,128]{1,0:T(8,128)(2,1)S(1)}, u32[]{:S(2)}, u32[]{:S(2)}) %collective-permute-start.43) | collective-permute-done | bytes 294944 | tf_op jit(solution)/shard_map/ppermute | solution.py:848
  421.9 7.4 %collective-permute-done.44.refs_2_ = bf16[1152,128]{1,0:T(8,128)(2,1)S(1)} collective-permute-done((bf16[1152,128]{1,0:T(8,128)(2,1)S(1)}, bf16[1152,128]{1,0:T(8,128)(2,1)S(1)}, u32[]{:S(2)}, u32[]{:S(2)}) %collective-permute-start.44) | collective-permute-done | bytes 294944 | tf_op jit(solution)/shard_map/ppermute | solution.py:848
  429.4 12.5 %collective-permute-done.45.refs_3_ = bf16[1152,128]{1,0:T(8,128)(2,1)S(1)} collective-permute-done((bf16[1152,128]{1,0:T(8,128)(2,1)S(1)}, bf16[1152,128]{1,0:T(8,128)(2,1)S(1)}, u32[]{:S(2)}, u32[]{:S(2)}) %collective-permute-start.45) | collective-permute-done | bytes 294944 | tf_op jit(solution)/shard_map/ppermute | solution.py:848
  441.9 5.1 shard_map.340
  458.4 6.6 %fusion.61 = f32[256,1536]{1,0:T(8,128)} fusion(bf16[256,2304]{1,0:T(8,128)(2,1)} %get-tuple-element.220, bf16[1536,2304]{1,0:T(8,128)(2,1)} %all-gather.3.cloned.1.call-done), kind=kOutput, calls=%fused_computation.209 | convolution fusion | flops 1811939328 | bytes 9830400 | tf_op jit(solution)/shard_map/dot_general | solution.py:31
  465.1 6.2 %shard_map.341 = bf16[768,3072]{1,0:T(8,128)(2,1)} custom-call(bf16[768,256]{1,0:T(8,128)(2,1)S(1)} %copy-done.13, bf16[768,256]{1,0:T(8,128)(2,1)S(1)} %copy-done.15, bf16[1,256,2304]{2,1,0:T(8,128)(2,1)} %bitcast.44.refs_2_, bf16[1,256,2304]{2,1,0:T(8,128)(2,1)S(1)} %collective-permute-done.46.refs_3_, bf16[768,256]{1,0:T(8,128)(2,1)S(1)} %copy-done.17, ...), custom_call_target="tpu_custom_call" | custom-call | flops 1024 | bytes 1024 | tf_op jit(solution)/shard_map/pallas_call | solution.py:674
  471.3 2.1 slice.281
  473.7 3.4 collective-permute-start.51
  477.7 1.9 collective-permute-done.50.refs_1_
  479.6 10.7 %collective-permute-done.51.refs_2_ = bf16[192,384]{1,0:T(8,128)(2,1)S(1)} collective-permute-done((bf16[192,384]{1,0:T(8,128)(2,1)S(1)}, bf16[192,384]{1,0:T(8,128)(2,1)S(1)}, u32[]{:S(2)}, u32[]{:S(2)}) %collective-permute-start.51) | collective-permute-done | bytes 147488 | tf_op jit(solution)/shard_map/ppermute | solution.py:848
  490.8 4.4 select_reduce_fusion.1
  498.2 10.9 %collective-permute-done.53 = bf16[192,1536]{1,0:T(8,128)(2,1)} collective-permute-done((bf16[192,1536]{1,0:T(8,128)(2,1)S(1)}, bf16[192,1536]{1,0:T(8,128)(2,1)}, u32[]{:S(2)}, u32[]{:S(2)}) %collective-permute-start.53) | collective-permute-done | bytes 589856 | tf_op jit(solution)/shard_map/ppermute | solution.py:844
  510.4 2.7 collective-permute-done.54
  515.1 2.0 collective-permute-start.55
  521.5 6.8 %collective-permute-done.57 = f32[4,9216]{1,0:T(4,128)S(1)} collective-permute-done((f32[4,9216]{1,0:T(4,128)S(1)}, f32[4,9216]{1,0:T(4,128)S(1)}, u32[]{:S(2)}, u32[]{:S(2)}) %collective-permute-start.57) | collective-permute-done | bytes 147488 | tf_op jit(solution)/shard_map/ppermute | solution.py:844
  529.6 8.4 %collective-permute-done.58 = f32[4,9216]{1,0:T(4,128)S(1)} collective-permute-done((f32[4,9216]{1,0:T(4,128)S(1)}, f32[4,9216]{1,0:T(4,128)S(1)}, u32[]{:S(2)}, u32[]{:S(2)}) %collective-permute-start.58) | collective-permute-done | bytes 147488 | tf_op jit(solution)/shard_map/ppermute | solution.py:844
  538.9 4.3 all-to-all-start.1
  543.2 10.0 %collective-permute-done.59 = f32[4,9216]{1,0:T(4,128)S(1)} collective-permute-done((f32[4,9216]{1,0:T(4,128)S(1)}, f32[4,9216]{1,0:T(4,128)S(1)}, u32[]{:S(2)}, u32[]{:S(2)}) %collective-permute-start.59) | collective-permute-done | bytes 147488 | tf_op jit(solution)/shard_map/ppermute | solution.py:844
  554.0 1.9 fusion.54
  557.3 3.1 collective-permute-done.61
  561.2 3.0 collective-permute-done.62
  564.9 4.0 collective-permute-done.63
  (463 shorter events, 93.3 us)
Async XLA Ops:
  7.2 80.4 %all-gather.3.cloned.1.call-start = ((), (), s32[]{:S(2)}) async-start(), calls=%async_computation.4 | async-start | bytes 7520256 | tf_op jit(solution)/shard_map/all_gather | solution.py:917
  10.0 23.8 %all-to-all-start = ((bf16[48,16,256]{2,0,1:T(8,128)(2,1)}), bf16[48,16,256]{2,0,1:T(8,128)(2,1)S(1)}, u32[]{:S(2)}, u32[]{:S(2)}) async-start(bf16[48,16,256]{2,0,1:T(8,128)(2,1)} %bitcast.116), calls=%async_computation | async-start | bytes 786432 | tf_op jit(solution)/shard_map/all_to_all | solution.py:937
  17.4 216.4 %all-gather.5.cloned.1.call-start = ((), (), s32[]{:S(2)}) async-start(), calls=%async_computation.5 | async-start | bytes 22560768 | tf_op jit(solution)/shard_map/all_gather | solution.py:1038
  17.8 5.8 collective-permute-start.7
  23.7 8.5 %collective-permute-start.8 = (f32[3,6144]{1,0:T(4,128)S(1)}, f32[3,6144]{1,0:T(4,128)S(1)}, u32[]{:S(2)}, u32[]{:S(2)}) collective-permute-start(f32[3,6144]{1,0:T(4,128)S(1)} %add.411), channel_id=1, source_target_pairs={{0,4},{2,6},{4,0},{6,2},{8,12},{10,14},{12,8},{14,10},{16,20},{18,... | collective-permute-start | bytes 221192 | tf_op jit(solution)/shard_map/ppermute | solution.py:844
  32.2 11.9 %collective-permute-start.9 = (f32[3,6144]{1,0:T(4,128)S(1)}, f32[3,6144]{1,0:T(4,128)S(1)}, u32[]{:S(2)}, u32[]{:S(2)}) collective-permute-start(f32[3,6144]{1,0:T(4,128)S(1)} %add.412), channel_id=1, source_target_pairs={{0,8},{2,10},{4,12},{6,14},{8,0},{10,2},{12,4},{14,6},{16,24},{18,... | collective-permute-start | bytes 221192 | tf_op jit(solution)/shard_map/ppermute | solution.py:844
  33.8 11.0 %collective-permute-start = (f32[4,3072]{1,0:T(4,128)S(1)}, f32[4,3072]{1,0:T(4,128)S(1)}, u32[]{:S(2)}, u32[]{:S(2)}) collective-permute-start(f32[4,3072]{1,0:T(4,128)S(1)} %pad_maximum_fusion.16), channel_id=1, source_target_pairs={{0,2},{2,0},{4,6},{6,4},{8,10},{10,8},{12,14},{14,12},{16,18},{18,... | collective-permute-start | bytes 147464 | tf_op jit(solution)/shard_map/ppermute | solution.py:844
  44.1 6.6 %collective-permute-start.10 = (f32[3,6144]{1,0:T(4,128)S(1)}, f32[3,6144]{1,0:T(4,128)S(1)}, u32[]{:S(2)}, u32[]{:S(2)}) collective-permute-start(f32[3,6144]{1,0:T(4,128)S(1)} %add.413), channel_id=1, source_target_pairs={{0,16},{2,18},{4,20},{6,22},{8,24},{10,26},{12,28},{14,30},{16,0},... | collective-permute-start | bytes 221192 | tf_op jit(solution)/shard_map/ppermute | solution.py:844
  44.8 6.0 %collective-permute-start.1 = (f32[4,3072]{1,0:T(4,128)S(1)}, f32[4,3072]{1,0:T(4,128)S(1)}, u32[]{:S(2)}, u32[]{:S(2)}) collective-permute-start(f32[4,3072]{1,0:T(4,128)S(1)} %add.395), channel_id=1, source_target_pairs={{0,4},{2,6},{4,0},{6,2},{8,12},{10,14},{12,8},{14,10},{16,20},{18,... | collective-permute-start | bytes 147464 | tf_op jit(solution)/shard_map/ppermute | solution.py:844
  50.8 7.1 %collective-permute-start.2 = (f32[4,3072]{1,0:T(4,128)S(1)}, f32[4,3072]{1,0:T(4,128)S(1)}, u32[]{:S(2)}, u32[]{:S(2)}) collective-permute-start(f32[4,3072]{1,0:T(4,128)S(1)} %add.396), channel_id=1, source_target_pairs={{0,8},{2,10},{4,12},{6,14},{8,0},{10,2},{12,4},{14,6},{16,24},{18,... | collective-permute-start | bytes 147464 | tf_op jit(solution)/shard_map/ppermute | solution.py:844
  57.9 9.0 %collective-permute-start.3 = (f32[4,3072]{1,0:T(4,128)S(1)}, f32[4,3072]{1,0:T(4,128)S(1)}, u32[]{:S(2)}, u32[]{:S(2)}) collective-permute-start(f32[4,3072]{1,0:T(4,128)S(1)} %add.397), channel_id=1, source_target_pairs={{0,16},{2,18},{4,20},{6,22},{8,24},{10,26},{12,28},{14,30},{16,0},... | collective-permute-start | bytes 147464 | tf_op jit(solution)/shard_map/ppermute | solution.py:844
  59.8 12.7 %collective-permute-start.5 = (bf16[384,1536]{1,0:T(8,128)(2,1)S(1)}, bf16[384,1536]{1,0:T(8,128)(2,1)S(1)}, u32[]{:S(2)}, u32[]{:S(2)}) collective-permute-start(bf16[384,1536]{1,0:T(8,128)(2,1)S(1)} %slice.279), channel_id=1, source_target_pairs={{0,2},{2,0},{4,6},{6,4},{8,10},{10,8},{12,14},{14,12},{16,18},{18,... | collective-permute-start | bytes 3538952 | tf_op jit(solution)/shard_map/ppermute | solution.py:844
  67.5 8.9 %collective-permute-start.4 = (bf16[128,1536]{1,0:T(8,128)(2,1)S(1)}, bf16[128,1536]{1,0:T(8,128)(2,1)S(1)}, u32[]{:S(2)}, u32[]{:S(2)}) collective-permute-start(bf16[128,1536]{1,0:T(8,128)(2,1)S(1)} %fusion.10), channel_id=1, source_target_pairs={{0,1},{1,0},{2,3},{3,2},{4,5},{5,4},{6,7},{7,6},{8,9},{9,8},{10,11... | collective-permute-start | bytes 1179656 | tf_op jit(solution)/shard_map/ppermute | solution.py:793
  72.9 13.1 %collective-permute-start.6 = (bf16[192,1536]{1,0:T(8,128)(2,1)S(1)}, bf16[192,1536]{1,0:T(8,128)(2,1)S(1)}, u32[]{:S(2)}, u32[]{:S(2)}) collective-permute-start(bf16[192,1536]{1,0:T(8,128)(2,1)S(1)} %slice.280), channel_id=1, source_target_pairs={{0,4},{2,6},{4,0},{6,2},{8,12},{10,14},{12,8},{14,10},{16,20},{18,... | collective-permute-start | bytes 1769480 | tf_op jit(solution)/shard_map/ppermute | solution.py:844
  87.6 408.0 %reduce-scatter.3.cloned.1.call-start = ((), (), s32[]{:S(2)}) async-start(), calls=%async_computation.6 | async-start | bytes 10616832 | tf_op jit(solution)/shard_map/reduce_scatter | solution.py:913
  88.8 17.3 %collective-permute-start.11 = (bf16[192,384]{1,0:T(8,128)(2,1)}, bf16[192,384]{1,0:T(8,128)(2,1)S(1)}, u32[]{:S(2)}, u32[]{:S(2)}) collective-permute-start(bf16[192,384]{1,0:T(8,128)(2,1)} %get-tuple-element.143), channel_id=1, source_target_pairs={{0,8},{2,10},{4,12},{6,14},{8,16},{10,18},{12,20},{14,22},{16,24},... | collective-permute-start | bytes 442376 | tf_op jit(solution)/shard_map/ppermute | solution.py:848
  88.9 17.9 %collective-permute-start.12 = (bf16[192,384]{1,0:T(8,128)(2,1)S(1)}, bf16[192,384]{1,0:T(8,128)(2,1)S(1)}, u32[]{:S(2)}, u32[]{:S(2)}) collective-permute-start(bf16[192,384]{1,0:T(8,128)(2,1)S(1)} %get-tuple-element.144), channel_id=1, source_target_pairs={{0,16},{2,18},{4,20},{6,22},{8,24},{10,26},{12,28},{14,30},{16,0},... | collective-permute-start | bytes 442376 | tf_op jit(solution)/shard_map/ppermute | solution.py:848
  92.3 15.2 %collective-permute-start.13 = (bf16[192,384]{1,0:T(8,128)(2,1)S(1)}, bf16[192,384]{1,0:T(8,128)(2,1)S(1)}, u32[]{:S(2)}, u32[]{:S(2)}) collective-permute-start(bf16[192,384]{1,0:T(8,128)(2,1)S(1)} %get-tuple-element.145), channel_id=1, source_target_pairs={{0,24},{2,26},{4,28},{6,30},{8,0},{10,2},{12,4},{14,6},{16,8},{18,... | collective-permute-start | bytes 442376 | tf_op jit(solution)/shard_map/ppermute | solution.py:848
  95.6 22.8 %collective-permute-start.17 = (bf16[128,1536]{1,0:T(8,128)(2,1)}, bf16[128,1536]{1,0:T(8,128)(2,1)}, u32[]{:S(2)}, u32[]{:S(2)}) collective-permute-start(bf16[128,1536]{1,0:T(8,128)(2,1)} %fusion.12), channel_id=1, source_target_pairs={{0,1},{1,0},{2,3},{3,2},{4,5},{5,4},{6,7},{7,6},{8,9},{9,8},{10,11... | collective-permute-start | bytes 1179656 | tf_op jit(solution)/shard_map/ppermute | solution.py:793
  108.1 18.5 %collective-permute-start.14 = (bf16[1152,128]{1,0:T(8,128)(2,1)}, bf16[1152,128]{1,0:T(8,128)(2,1)}, u32[]{:S(2)}, u32[]{:S(2)}) collective-permute-start(bf16[1152,128]{1,0:T(8,128)(2,1)} %get-tuple-element.147), channel_id=1, source_target_pairs={{0,8},{2,10},{4,12},{6,14},{8,16},{10,18},{12,20},{14,22},{16,24},... | collective-permute-start | bytes 884744 | tf_op jit(solution)/shard_map/ppermute | solution.py:848
  112.3 27.8 %collective-permute-start.15 = (bf16[1152,128]{1,0:T(8,128)(2,1)}, bf16[1152,128]{1,0:T(8,128)(2,1)}, u32[]{:S(2)}, u32[]{:S(2)}) collective-permute-start(bf16[1152,128]{1,0:T(8,128)(2,1)} %get-tuple-element.148), channel_id=1, source_target_pairs={{0,16},{2,18},{4,20},{6,22},{8,24},{10,26},{12,28},{14,30},{16,0},... | collective-permute-start | bytes 884744 | tf_op jit(solution)/shard_map/ppermute | solution.py:848
  112.3 38.1 %collective-permute-start.16 = (bf16[1152,128]{1,0:T(8,128)(2,1)}, bf16[1152,128]{1,0:T(8,128)(2,1)}, u32[]{:S(2)}, u32[]{:S(2)}) collective-permute-start(bf16[1152,128]{1,0:T(8,128)(2,1)} %get-tuple-element.149), channel_id=1, source_target_pairs={{0,24},{2,26},{4,28},{6,30},{8,0},{10,2},{12,4},{14,6},{16,8},{18,... | collective-permute-start | bytes 884744 | tf_op jit(solution)/shard_map/ppermute | solution.py:848
  155.9 43.3 %collective-permute-start.18 = (bf16[3648,128]{1,0:T(8,128)(2,1)}, bf16[3648,128]{1,0:T(8,128)(2,1)}, u32[]{:S(2)}, u32[]{:S(2)}) collective-permute-start(bf16[3648,128]{1,0:T(8,128)(2,1)} %get-tuple-element.159.refs_0_), channel_id=1, source_target_pairs={{0,4},{2,6},{4,0},{6,2},{8,12},{10,14},{12,8},{14,10},{16,20},{18,... | collective-permute-start | bytes 2801672 | tf_op jit(solution)/shard_map/ppermute | solution.py:844
  215.3 8.6 %collective-permute-start.21 = (bf16[384,128]{1,0:T(8,128)(2,1)}, bf16[384,128]{1,0:T(8,128)(2,1)S(1)}, u32[]{:S(2)}, u32[]{:S(2)}) collective-permute-start(bf16[384,128]{1,0:T(8,128)(2,1)} %get-tuple-element.169), channel_id=1, source_target_pairs={{0,24},{2,26},{4,28},{6,30},{8,0},{10,2},{12,4},{14,6},{16,8},{18,... | collective-permute-start | bytes 294920 | tf_op jit(solution)/shard_map/ppermute | solution.py:848
  220.0 12.6 %collective-permute-start.22 = (bf16[384,128]{1,0:T(8,128)(2,1)}, bf16[384,128]{1,0:T(8,128)(2,1)S(1)}, u32[]{:S(2)}, u32[]{:S(2)}) collective-permute-start(bf16[384,128]{1,0:T(8,128)(2,1)} %get-tuple-element.170), channel_id=1, source_target_pairs={{0,16},{2,18},{4,20},{6,22},{8,24},{10,26},{12,28},{14,30},{16,0},... | collective-permute-start | bytes 294920 | tf_op jit(solution)/shard_map/ppermute | solution.py:848
  220.0 12.6 %collective-permute-start.23 = (bf16[384,128]{1,0:T(8,128)(2,1)}, bf16[384,128]{1,0:T(8,128)(2,1)S(1)}, u32[]{:S(2)}, u32[]{:S(2)}) collective-permute-start(bf16[384,128]{1,0:T(8,128)(2,1)} %get-tuple-element.171), channel_id=1, source_target_pairs={{0,8},{2,10},{4,12},{6,14},{8,16},{10,18},{12,20},{14,22},{16,24},... | collective-permute-start | bytes 294920 | tf_op jit(solution)/shard_map/ppermute | solution.py:848
  236.5 10.7 %collective-permute-start.24 = (bf16[128,1536]{1,0:T(8,128)(2,1)S(1)}, bf16[128,1536]{1,0:T(8,128)(2,1)S(1)}, u32[]{:S(2)}, u32[]{:S(2)}) collective-permute-start(bf16[128,1536]{1,0:T(8,128)(2,1)S(1)} %slice.282), channel_id=1, source_target_pairs={{0,1},{1,0},{2,3},{3,2},{4,5},{5,4},{6,7},{7,6},{8,9},{9,8},{10,11... | collective-permute-start | bytes 1179656 | tf_op jit(solution)/shard_map/ppermute | solution.py:793
  248.2 9.8 %collective-permute-start.25 = (bf16[128,1536]{1,0:T(8,128)(2,1)S(1)}, bf16[128,1536]{1,0:T(8,128)(2,1)S(1)}, u32[]{:S(2)}, u32[]{:S(2)}) collective-permute-start(bf16[128,1536]{1,0:T(8,128)(2,1)S(1)} %fusion.16), channel_id=1, source_target_pairs={{0,1},{1,0},{2,3},{3,2},{4,5},{5,4},{6,7},{7,6},{8,9},{9,8},{10,11... | collective-permute-start | bytes 1179656 | tf_op jit(solution)/shard_map/ppermute | solution.py:793
  273.1 8.8 %collective-permute-start.26 = (bf16[128,1536]{1,0:T(8,128)(2,1)S(1)}, bf16[128,1536]{1,0:T(8,128)(2,1)S(1)}, u32[]{:S(2)}, u32[]{:S(2)}) collective-permute-start(bf16[128,1536]{1,0:T(8,128)(2,1)S(1)} %get-tuple-element.176), channel_id=1, source_target_pairs={{0,1},{1,0},{2,3},{3,2},{4,5},{5,4},{6,7},{7,6},{8,9},{9,8},{10,11... | collective-permute-start | bytes 1179656 | tf_op jit(solution)/shard_map/ppermute | solution.py:793
  274.4 34.7 %collective-permute-start.33 = (bf16[2,256,2048]{2,1,0:T(8,128)(2,1)}, bf16[2,256,2048]{2,1,0:T(8,128)(2,1)}, u32[]{:S(2)}, u32[]{:S(2)}) collective-permute-start(bf16[2,256,2048]{2,1,0:T(8,128)(2,1)} %get-tuple-element.186.refs_2_), channel_id=1, source_target_pairs={{0,2},{2,0},{4,6},{6,4},{8,10},{10,8},{12,14},{14,12},{16,18},{18,... | collective-permute-start | bytes 6291464 | tf_op jit(solution)/shard_map/ppermute | solution.py:844
  274.4 34.7 %collective-permute-start.35 = (bf16[1,256,2048]{2,1,0:T(8,128)(2,1)}, bf16[1,256,2048]{2,1,0:T(8,128)(2,1)}, u32[]{:S(2)}, u32[]{:S(2)}) collective-permute-start(bf16[1,256,2048]{2,1,0:T(8,128)(2,1)} %get-tuple-element.189.refs_6_), channel_id=1, source_target_pairs={{0,2},{2,0},{4,6},{6,4},{8,10},{10,8},{12,14},{14,12},{16,18},{18,... | collective-permute-start | bytes 3145736 | tf_op jit(solution)/shard_map/ppermute | solution.py:844
  284.8 8.2 %collective-permute-start.27 = (bf16[128,1536]{1,0:T(8,128)(2,1)}, bf16[128,1536]{1,0:T(8,128)(2,1)}, u32[]{:S(2)}, u32[]{:S(2)}) collective-permute-start(bf16[128,1536]{1,0:T(8,128)(2,1)} %get-tuple-element.361), channel_id=1, source_target_pairs={{0,1},{1,0},{2,3},{3,2},{4,5},{5,4},{6,7},{7,6},{8,9},{9,8},{10,11... | collective-permute-start | bytes 1179656 | tf_op jit(solution)/shard_map/ppermute | solution.py:793
  288.2 7.1 %collective-permute-start.36 = (bf16[768,256]{1,0:T(8,128)(2,1)S(1)}, bf16[768,256]{1,0:T(8,128)(2,1)S(1)}, u32[]{:S(2)}, u32[]{:S(2)}) collective-permute-start(bf16[768,256]{1,0:T(8,128)(2,1)S(1)} %get-tuple-element.191), channel_id=1, source_target_pairs={{0,2},{2,0},{4,6},{6,4},{8,10},{10,8},{12,14},{14,12},{16,18},{18,... | collective-permute-start | bytes 1179656 | tf_op jit(solution)/shard_map/ppermute | solution.py:844
  288.6 7.2 %collective-permute-start.34 = (bf16[768,256]{1,0:T(8,128)(2,1)S(1)}, bf16[768,256]{1,0:T(8,128)(2,1)S(1)}, u32[]{:S(2)}, u32[]{:S(2)}) collective-permute-start(bf16[768,256]{1,0:T(8,128)(2,1)S(1)} %get-tuple-element.188), channel_id=1, source_target_pairs={{0,2},{2,0},{4,6},{6,4},{8,10},{10,8},{12,14},{14,12},{16,18},{18,... | collective-permute-start | bytes 1179656 | tf_op jit(solution)/shard_map/ppermute | solution.py:844
  293.0 6.4 %collective-permute-start.32 = (bf16[768,256]{1,0:T(8,128)(2,1)S(1)}, bf16[768,256]{1,0:T(8,128)(2,1)S(1)}, u32[]{:S(2)}, u32[]{:S(2)}) collective-permute-start(bf16[768,256]{1,0:T(8,128)(2,1)S(1)} %get-tuple-element.185), channel_id=1, source_target_pairs={{0,2},{2,0},{4,6},{6,4},{8,10},{10,8},{12,14},{14,12},{16,18},{18,... | collective-permute-start | bytes 1179656 | tf_op jit(solution)/shard_map/ppermute | solution.py:844
  295.3 29.1 %collective-permute-start.38 = (bf16[1,256,768]{2,1,0:T(8,128)(2,1)S(1)}, bf16[1,256,768]{2,1,0:T(8,128)(2,1)}, u32[]{:S(2)}, u32[]{:S(2)}) collective-permute-start(bf16[1,256,768]{2,1,0:T(8,128)(2,1)S(1)} %bitcast.117), channel_id=1, source_target_pairs={{0,2},{2,0},{4,6},{6,4},{8,10},{10,8},{12,14},{14,12},{16,18},{18,... | collective-permute-start | bytes 1179656 | tf_op jit(solution)/shard_map/ppermute | solution.py:844
  295.8 28.6 %collective-permute-start.37 = (bf16[768,256]{1,0:T(8,128)(2,1)S(1)}, bf16[768,256]{1,0:T(8,128)(2,1)}, u32[]{:S(2)}, u32[]{:S(2)}) collective-permute-start(bf16[768,256]{1,0:T(8,128)(2,1)S(1)} %get-tuple-element.193), channel_id=1, source_target_pairs={{0,2},{2,0},{4,6},{6,4},{8,10},{10,8},{12,14},{14,12},{16,18},{18,... | collective-permute-start | bytes 1179656 | tf_op jit(solution)/shard_map/ppermute | solution.py:844
  299.3 25.0 %collective-permute-start.29 = (bf16[384,128]{1,0:T(8,128)(2,1)S(1)}, bf16[384,128]{1,0:T(8,128)(2,1)S(1)}, u32[]{:S(2)}, u32[]{:S(2)}) collective-permute-start(bf16[384,128]{1,0:T(8,128)(2,1)S(1)} %get-tuple-element.181), channel_id=1, source_target_pairs={{0,8},{2,10},{4,12},{6,14},{8,16},{10,18},{12,20},{14,22},{16,24},... | collective-permute-start | bytes 294920 | tf_op jit(solution)/shard_map/ppermute | solution.py:848
  309.1 15.2 %collective-permute-start.30 = (bf16[384,128]{1,0:T(8,128)(2,1)S(1)}, bf16[384,128]{1,0:T(8,128)(2,1)}, u32[]{:S(2)}, u32[]{:S(2)}) collective-permute-start(bf16[384,128]{1,0:T(8,128)(2,1)S(1)} %get-tuple-element.182), channel_id=1, source_target_pairs={{0,16},{2,18},{4,20},{6,22},{8,24},{10,26},{12,28},{14,30},{16,0},... | collective-permute-start | bytes 294920 | tf_op jit(solution)/shard_map/ppermute | solution.py:848
  309.1 15.2 %collective-permute-start.31 = (bf16[384,128]{1,0:T(8,128)(2,1)S(1)}, bf16[384,128]{1,0:T(8,128)(2,1)}, u32[]{:S(2)}, u32[]{:S(2)}) collective-permute-start(bf16[384,128]{1,0:T(8,128)(2,1)S(1)} %get-tuple-element.183), channel_id=1, source_target_pairs={{0,24},{2,26},{4,28},{6,30},{8,0},{10,2},{12,4},{14,6},{16,8},{18,... | collective-permute-start | bytes 294920 | tf_op jit(solution)/shard_map/ppermute | solution.py:848
  325.0 247.9 %reduce-scatter.5.cloned.1.call-start = ((), (), s32[]{:S(2)}) async-start(), calls=%async_computation.7 | async-start | bytes 5308416 | tf_op jit(solution)/shard_map/reduce_scatter | solution.py:913
  349.8 3.7 collective-permute-start.39
  355.9 43.7 %collective-permute-start.42 = (bf16[3,1216,128]{2,1,0:T(8,128)(2,1)}, bf16[3,1216,128]{2,1,0:T(8,128)(2,1)}, u32[]{:S(2)}, u32[]{:S(2)}) collective-permute-start(bf16[3,1216,128]{2,1,0:T(8,128)(2,1)} %pad_maximum_fusion.4), channel_id=1, source_target_pairs={{0,4},{2,6},{4,0},{6,2},{8,12},{10,14},{12,8},{14,10},{16,20},{18,... | collective-permute-start | bytes 2801672 | tf_op jit(solution)/shard_map/ppermute | solution.py:844
  382.1 18.7 %collective-permute-start.41 = (bf16[3,1024,128]{2,1,0:T(8,128)(2,1)}, bf16[3,1024,128]{2,1,0:T(8,128)(2,1)S(1)}, u32[]{:S(2)}, u32[]{:S(2)}) collective-permute-start(bf16[3,1024,128]{2,1,0:T(8,128)(2,1)} %get-tuple-element.210), channel_id=1, source_target_pairs={{0,2},{2,0},{4,6},{6,4},{8,10},{10,8},{12,14},{14,12},{16,18},{18,... | collective-permute-start | bytes 2359304 | tf_op jit(solution)/shard_map/ppermute | solution.py:844
  401.1 20.8 %collective-permute-start.43 = (bf16[1152,128]{1,0:T(8,128)(2,1)S(1)}, bf16[1152,128]{1,0:T(8,128)(2,1)S(1)}, u32[]{:S(2)}, u32[]{:S(2)}) collective-permute-start(bf16[1152,128]{1,0:T(8,128)(2,1)S(1)} %get-tuple-element.217), channel_id=1, source_target_pairs={{0,24},{2,26},{4,28},{6,30},{8,0},{10,2},{12,4},{14,6},{16,8},{18,... | collective-permute-start | bytes 884744 | tf_op jit(solution)/shard_map/ppermute | solution.py:848
  403.2 26.2 %collective-permute-start.44 = (bf16[1152,128]{1,0:T(8,128)(2,1)S(1)}, bf16[1152,128]{1,0:T(8,128)(2,1)S(1)}, u32[]{:S(2)}, u32[]{:S(2)}) collective-permute-start(bf16[1152,128]{1,0:T(8,128)(2,1)S(1)} %get-tuple-element.218), channel_id=1, source_target_pairs={{0,16},{2,18},{4,20},{6,22},{8,24},{10,26},{12,28},{14,30},{16,0},... | collective-permute-start | bytes 884744 | tf_op jit(solution)/shard_map/ppermute | solution.py:848
  403.2 38.7 %collective-permute-start.45 = (bf16[1152,128]{1,0:T(8,128)(2,1)S(1)}, bf16[1152,128]{1,0:T(8,128)(2,1)S(1)}, u32[]{:S(2)}, u32[]{:S(2)}) collective-permute-start(bf16[1152,128]{1,0:T(8,128)(2,1)S(1)} %get-tuple-element.219), channel_id=1, source_target_pairs={{0,8},{2,10},{4,12},{6,14},{8,16},{10,18},{12,20},{14,22},{16,24},... | collective-permute-start | bytes 884744 | tf_op jit(solution)/shard_map/ppermute | solution.py:848
  447.1 18.0 %collective-permute-start.46 = (bf16[1,256,2304]{2,1,0:T(8,128)(2,1)}, bf16[1,256,2304]{2,1,0:T(8,128)(2,1)S(1)}, u32[]{:S(2)}, u32[]{:S(2)}) collective-permute-start(bf16[1,256,2304]{2,1,0:T(8,128)(2,1)} %bitcast.44.refs_2_), channel_id=1, source_target_pairs={{0,2},{2,0},{4,6},{6,4},{8,10},{10,8},{12,14},{14,12},{16,18},{18,... | collective-permute-start | bytes 3538952 | tf_op jit(solution)/shard_map/ppermute | solution.py:844
  454.9 35.9 %collective-permute-start.28 = (bf16[128,1536]{1,0:T(8,128)(2,1)}, bf16[128,1536]{1,0:T(8,128)(2,1)}, u32[]{:S(2)}, u32[]{:S(2)}) collective-permute-start(bf16[128,1536]{1,0:T(8,128)(2,1)} %copy-done.35), channel_id=1, source_target_pairs={{0,1},{1,0},{2,3},{3,2},{4,5},{5,4},{6,7},{7,6},{8,9},{9,8},{10,11... | collective-permute-start | bytes 1179656 | tf_op jit(solution)/shard_map/ppermute | solution.py:793
  473.3 17.4 %collective-permute-start.48 = (bf16[128,1536]{1,0:T(8,128)(2,1)}, bf16[128,1536]{1,0:T(8,128)(2,1)}, u32[]{:S(2)}, u32[]{:S(2)}) collective-permute-start(bf16[128,1536]{1,0:T(8,128)(2,1)} %slice.281), channel_id=1, source_target_pairs={{0,1},{1,0},{2,3},{3,2},{4,5},{5,4},{6,7},{7,6},{8,9},{9,8},{10,11... | collective-permute-start | bytes 1179656 | tf_op jit(solution)/shard_map/ppermute | solution.py:793
  473.7 5.9 %collective-permute-start.50 = (bf16[192,384]{1,0:T(8,128)(2,1)S(1)}, bf16[192,384]{1,0:T(8,128)(2,1)S(1)}, u32[]{:S(2)}, u32[]{:S(2)}) collective-permute-start(bf16[192,384]{1,0:T(8,128)(2,1)S(1)} %get-tuple-element.234.refs_0_), channel_id=1, source_target_pairs={{0,24},{2,26},{4,28},{6,30},{8,0},{10,2},{12,4},{14,6},{16,8},{18,... | collective-permute-start | bytes 442376 | tf_op jit(solution)/shard_map/ppermute | solution.py:848
  473.7 16.6 %collective-permute-start.51 = (bf16[192,384]{1,0:T(8,128)(2,1)S(1)}, bf16[192,384]{1,0:T(8,128)(2,1)S(1)}, u32[]{:S(2)}, u32[]{:S(2)}) collective-permute-start(bf16[192,384]{1,0:T(8,128)(2,1)S(1)} %get-tuple-element.234.refs_0_), channel_id=1, source_target_pairs={{0,16},{2,18},{4,20},{6,22},{8,24},{10,26},{12,28},{14,30},{16,0},... | collective-permute-start | bytes 442376 | tf_op jit(solution)/shard_map/ppermute | solution.py:848
  477.1 13.2 %collective-permute-start.52 = (bf16[192,384]{1,0:T(8,128)(2,1)S(1)}, bf16[192,384]{1,0:T(8,128)(2,1)S(1)}, u32[]{:S(2)}, u32[]{:S(2)}) collective-permute-start(bf16[192,384]{1,0:T(8,128)(2,1)S(1)} %get-tuple-element.234.refs_0_), channel_id=1, source_target_pairs={{0,8},{2,10},{4,12},{6,14},{8,16},{10,18},{12,20},{14,22},{16,24},... | collective-permute-start | bytes 442376 | tf_op jit(solution)/shard_map/ppermute | solution.py:848
  490.4 18.7 %collective-permute-start.53 = (bf16[192,1536]{1,0:T(8,128)(2,1)S(1)}, bf16[192,1536]{1,0:T(8,128)(2,1)}, u32[]{:S(2)}, u32[]{:S(2)}) collective-permute-start(bf16[192,1536]{1,0:T(8,128)(2,1)S(1)} %shard_map.343), channel_id=1, source_target_pairs={{0,4},{2,6},{4,0},{6,2},{8,12},{10,14},{12,8},{14,10},{16,20},{18,... | collective-permute-start | bytes 1769480 | tf_op jit(solution)/shard_map/ppermute | solution.py:844
  496.6 13.6 %collective-permute-start.49 = (f32[4,9216]{1,0:T(4,128)S(1)}, f32[4,9216]{1,0:T(4,128)S(1)}, u32[]{:S(2)}, u32[]{:S(2)}) collective-permute-start(f32[4,9216]{1,0:T(4,128)S(1)} %pad_maximum_fusion.11), channel_id=1, source_target_pairs={{0,1},{1,0},{2,3},{3,2},{4,5},{5,4},{6,7},{7,6},{8,9},{9,8},{10,11... | collective-permute-start | bytes 442376 | tf_op jit(solution)/shard_map/ppermute | solution.py:793
  510.2 2.9 collective-permute-start.54
  515.1 13.3 %collective-permute-start.55 = (bf16[768,256]{1,0:T(8,128)(2,1)S(1)}, bf16[768,256]{1,0:T(8,128)(2,1)}, u32[]{:S(2)}, u32[]{:S(2)}) collective-permute-start(bf16[768,256]{1,0:T(8,128)(2,1)S(1)} %convolution_convert_fusion), channel_id=1, source_target_pairs={{0,1},{1,0},{2,3},{3,2},{4,5},{5,4},{6,7},{7,6},{8,9},{9,8},{10,11... | collective-permute-start | bytes 1179656 | tf_op jit(solution)/shard_map/ppermute | solution.py:793
  518.5 9.8 %collective-permute-start.57 = (f32[4,9216]{1,0:T(4,128)S(1)}, f32[4,9216]{1,0:T(4,128)S(1)}, u32[]{:S(2)}, u32[]{:S(2)}) collective-permute-start(f32[4,9216]{1,0:T(4,128)S(1)} %add.477), channel_id=1, source_target_pairs={{0,4},{2,6},{4,0},{6,2},{8,12},{10,14},{12,8},{14,10},{16,20},{18,... | collective-permute-start | bytes 442376 | tf_op jit(solution)/shard_map/ppermute | solution.py:844
  528.4 9.6 %collective-permute-start.58 = (f32[4,9216]{1,0:T(4,128)S(1)}, f32[4,9216]{1,0:T(4,128)S(1)}, u32[]{:S(2)}, u32[]{:S(2)}) collective-permute-start(f32[4,9216]{1,0:T(4,128)S(1)} %add.478), channel_id=1, source_target_pairs={{0,8},{2,10},{4,12},{6,14},{8,0},{10,2},{12,4},{14,6},{16,24},{18,... | collective-permute-start | bytes 442376 | tf_op jit(solution)/shard_map/ppermute | solution.py:844
  538.0 15.2 %collective-permute-start.59 = (f32[4,9216]{1,0:T(4,128)S(1)}, f32[4,9216]{1,0:T(4,128)S(1)}, u32[]{:S(2)}, u32[]{:S(2)}) collective-permute-start(f32[4,9216]{1,0:T(4,128)S(1)} %add.479), channel_id=1, source_target_pairs={{0,16},{2,18},{4,20},{6,22},{8,24},{10,26},{12,28},{14,30},{16,0},... | collective-permute-start | bytes 442376 | tf_op jit(solution)/shard_map/ppermute | solution.py:844
  538.9 30.6 %all-to-all-start.1 = ((bf16[16,48,256]{2,1,0:T(8,128)(2,1)}), bf16[16,48,256]{2,1,0:T(8,128)(2,1)S(1)}, u32[]{:S(2)}, u32[]{:S(2)}) async-start(bf16[16,48,256]{2,1,0:T(8,128)(2,1)} %bitcast.52), calls=%async_computation.1 | async-start | bytes 786432 | tf_op jit(solution)/shard_map/all_to_all | solution.py:1247
  556.7 3.8 collective-permute-start.61
  560.5 3.7 collective-permute-start.62
  564.2 4.6 collective-permute-start.63
  (110 other events, 1163.8 us)
Sparse Core Ops, SparseCore 0:
  10.9 75.6 all-gather.2
  88.8 144.3 all-gather.4
  324.5 126.8 reduce-scatter.2
  495.8 65.5 reduce-scatter.4

commit v7 on v6

--- a/solution.py
+++ b/solution.py
@@ -1168,6 +1168,7 @@
         [part_shape, jax.ShapeDtypeStruct((8, 128), FLOAT)],
     )
     qkv_grad, gain_sums = rope_backward(far, back_parts, qkv_raw, cosine, sine, gains, heads)
+    qkv_grad, text_low = tie(qkv_grad, text_low)
     normed_part = dot_turned(qkv_grad, qkv_full)
     qkv_right = qkv_grad[None]
     last_grads = outer_products(
@@ -1175,7 +1176,8 @@
         [*last_left[1], mixed_right, mixed_other],
         local_width,
     )
-    normed_part, last_grads, text_low = tie(normed_part, last_grads, text_low)
+    text_arrived = return_slots([text_low] * SPLIT)
+    normed_part, last_grads, text_arrived = tie(normed_part, last_grads, text_arrived)
     last_grads, feed_low = tie(last_grads, feed_low)
     last_low = scatter(last_grads)
     grad_normed_one = own_rows(normed_part)
@@ -1211,7 +1213,7 @@
     )
     text_wide = small_call(
         text_join_kernel,
-        (far, *return_slots([text_low] * SPLIT)),
+        (far, *text_arrived),
         [jax.ShapeDtypeStruct((group_rows, 2 * local_width), LOW)],
         [],
     )[0]

time: 593 us -> 580 us (0.978)
  waiting for transfers between devices: 266 us -> 252 us
    ppermute x36, waiting for transfers between devices: 144 us -> 129 us  [flip(): return lax.ppermute(values, 'dp', [(j, j ^ bit) for j in range(dp)])]
    ppermute x18, waiting for transfers between devices: 92.8 us -> 79.1 us  [shift(): return lax.ppermute(values, 'dp', pairs)]
    ppermute x10, waiting for transfers between devices: 28.7 us -> 41.8 us  [swapped(): return lax.ppermute(values, 'tensor', [(0, 1), (1, 0)])]
    unnamed x213 -> x217, local copies, waits for them, and re-layouts: 18.2 us -> 18.3 us
  transfers between devices with their start and end apart: 70 -> 70, of which waited for: 35 -> 36; matrix products, arithmetic and copies ran while one was open for 12% -> 12% of each run, Pallas kernels for 19% -> 19%
where the time goes in v7:
time: 580 us; the launch traced here: 570 us
  waiting for transfers between devices  252 us (43%)
  Pallas kernels  124 us (21%)
  starting transfers between devices  74.9 us (13%)
  other arithmetic  39.1 us (7%)
  local copies, waits for them, and re-layouts  32.6 us (6%)
  between operations  25.4 us (4%)
  matrix products  22.1 us (4%)
    ppermute x36, waiting for transfers between devices, flip(): return lax.ppermute(values, 'dp', [(j, j ^ bit) for j in range(dp)])  129 us
    ppermute x18, waiting for transfers between devices, shift(): return lax.ppermute(values, 'dp', pairs)  79.1 us
    pallas_call x2, Pallas kernels, attention_backward(): pl.pallas_call(functools.partial(backward_kernel, len(pairs), pick_tile(k...  50.1 us
    ppermute x10, waiting for transfers between devices, swapped(): return lax.ppermute(values, 'tensor', [(0, 1), (1, 0)])  41.8 us
    ppermute x18, starting transfers between devices, shift(): return lax.ppermute(values, 'dp', pairs)  35 us
    pallas_call x2, Pallas kernels, attention_forward(): pl.pallas_call(functools.partial(forward_kernel, len(pairs), pick_tile(kf...  25.1 us
    pallas_call x2, Pallas kernels, outer_products(): pl.pallas_call(functools.partial(outer_kernel, steps[0]), grid=(sum(steps...  18.8 us
    unnamed x217, local copies, waits for them, and re-layouts  18.3 us
  transfers between devices with their start and end apart: 70, of which 36 were waited for; matrix products, arithmetic and copies ran while one was open for 12% of the time, Pallas kernels for 19%

profile of v7, /device:TPU:0, one launch (start us, length us, event | category | flops | bytes accessed | tf_op | source)
XLA Modules:
  0.0 570.2 jit_solution(13063102709045830580)
XLA Ops:
  7.3 1.9 copy.85
  10.0 7.4 %all-to-all-start = ((bf16[48,16,256]{2,0,1:T(8,128)(2,1)}), bf16[48,16,256]{2,0,1:T(8,128)(2,1)S(1)}, u32[]{:S(2)}, u32[]{:S(2)}) async-start(bf16[48,16,256]{2,0,1:T(8,128)(2,1)} %bitcast.116), calls=%async_computation | async-start | bytes 786432 | tf_op jit(solution)/shard_map/all_to_all | solution.py:937
  21.1 2.2 pad_maximum_fusion.2
  23.7 1.8 collective-permute-start.8
  25.4 6.7 %collective-permute-done.8 = f32[3,6144]{1,0:T(4,128)S(1)} collective-permute-done((f32[3,6144]{1,0:T(4,128)S(1)}, f32[3,6144]{1,0:T(4,128)S(1)}, u32[]{:S(2)}, u32[]{:S(2)}) %collective-permute-start.8) | collective-permute-done | bytes 73760 | tf_op jit(solution)/shard_map/ppermute | solution.py:844
  33.8 10.3 %collective-permute-done.9 = f32[3,6144]{1,0:T(4,128)S(1)} collective-permute-done((f32[3,6144]{1,0:T(4,128)S(1)}, f32[3,6144]{1,0:T(4,128)S(1)}, u32[]{:S(2)}, u32[]{:S(2)}) %collective-permute-start.9) | collective-permute-done | bytes 73760 | tf_op jit(solution)/shard_map/ppermute | solution.py:844
  49.0 1.8 collective-permute-done.10
  51.6 6.3 %collective-permute-done.2 = f32[4,3072]{1,0:T(4,128)S(1)} collective-permute-done((f32[4,3072]{1,0:T(4,128)S(1)}, f32[4,3072]{1,0:T(4,128)S(1)}, u32[]{:S(2)}, u32[]{:S(2)}) %collective-permute-start.2) | collective-permute-done | bytes 49184 | tf_op jit(solution)/shard_map/ppermute | solution.py:844
  59.9 7.1 %collective-permute-done.3 = f32[4,3072]{1,0:T(4,128)S(1)} collective-permute-done((f32[4,3072]{1,0:T(4,128)S(1)}, f32[4,3072]{1,0:T(4,128)S(1)}, u32[]{:S(2)}, u32[]{:S(2)}) %collective-permute-start.3) | collective-permute-done | bytes 49184 | tf_op jit(solution)/shard_map/ppermute | solution.py:844
  67.5 2.0 collective-permute-start.4
  69.8 2.7 fusion.refs_4_
  76.5 9.6 %collective-permute-done.6 = bf16[192,1536]{1,0:T(8,128)(2,1)S(1)} collective-permute-done((bf16[192,1536]{1,0:T(8,128)(2,1)S(1)}, bf16[192,1536]{1,0:T(8,128)(2,1)S(1)}, u32[]{:S(2)}, u32[]{:S(2)}) %collective-permute-start.6) | collective-permute-done | bytes 589856 | tf_op jit(solution)/shard_map/ppermute | solution.py:844
  88.9 3.3 collective-permute-start.12
  96.9 5.0 fusion.60.qkv_ref.refs_4_
  101.9 4.2 shard_map.324
  108.1 4.2 collective-permute-start.14
  112.3 2.4 collective-permute-start.16
  119.6 7.0 %collective-permute-done.14.refs_1_ = bf16[1152,128]{1,0:T(8,128)(2,1)} collective-permute-done((bf16[1152,128]{1,0:T(8,128)(2,1)}, bf16[1152,128]{1,0:T(8,128)(2,1)}, u32[]{:S(2)}, u32[]{:S(2)}) %collective-permute-start.14) | collective-permute-done | bytes 294944 | tf_op jit(solution)/shard_map/ppermute | solution.py:848
  126.6 13.6 %collective-permute-done.15.refs_2_ = bf16[1152,128]{1,0:T(8,128)(2,1)} collective-permute-done((bf16[1152,128]{1,0:T(8,128)(2,1)}, bf16[1152,128]{1,0:T(8,128)(2,1)}, u32[]{:S(2)}, u32[]{:S(2)}) %collective-permute-start.15) | collective-permute-done | bytes 294944 | tf_op jit(solution)/shard_map/ppermute | solution.py:848
  140.2 10.2 %collective-permute-done.16.refs_3_ = bf16[1152,128]{1,0:T(8,128)(2,1)} collective-permute-done((bf16[1152,128]{1,0:T(8,128)(2,1)}, bf16[1152,128]{1,0:T(8,128)(2,1)}, u32[]{:S(2)}, u32[]{:S(2)}) %collective-permute-start.16) | collective-permute-done | bytes 294944 | tf_op jit(solution)/shard_map/ppermute | solution.py:848
  150.4 2.3 shard_map.326
  157.1 11.9 %shard_map.327 = (f32[3072,128]{1,0:T(8,128)}, f32[3072,128]{1,0:T(8,128)}) custom-call(bf16[3648,128]{1,0:T(8,128)(2,1)} %get-tuple-element.164.refs_0_, bf16[3648,128]{1,0:T(8,128)(2,1)} %collective-permute-done.19.refs_1_, bf16[3072,128]{1,0:T(8,128)(2,1)} %copy-done.34, bf16[1024,128]{1,0:T(8,128)(2,1)} %select_convert_fusion.refs_3_, ...), custom_call_target="tpu_custom_call" | custom-call | flops 24999999488 | bytes 1024 | tf_op jit(solution)/shard_map/pallas_call | solution.py:182
  169.0 30.3 %collective-permute-done.18.refs_0_ = bf16[3648,128]{1,0:T(8,128)(2,1)} collective-permute-done((bf16[3648,128]{1,0:T(8,128)(2,1)}, bf16[3648,128]{1,0:T(8,128)(2,1)}, u32[]{:S(2)}, u32[]{:S(2)}) %collective-permute-start.18) | collective-permute-done | bytes 933920 | tf_op jit(solution)/shard_map/ppermute | solution.py:844
  199.3 2.8 collective-permute-done.20.refs_1_
  202.2 13.2 %shard_map.328 = (bf16[384,128]{1,0:T(8,128)(2,1)}, bf16[384,128]{1,0:T(8,128)(2,1)}, bf16[384,128]{1,0:T(8,128)(2,1)}, bf16[384,128]{1,0:T(8,128)(2,1)}, f32[3072,128]{1,0:T(8,128)}, /*index=5*/f32[3072,128]{1,0:T(8,128)}) custom-call(bf16[3648,128]{1,0:T(8,128)(2,1)} %collective-permute-done.18.refs_0_, bf16[3648,128]{1,0:T(8,128)(2,1)} %collective-permute-done.20.refs_1_, ...), custom_call_target="tpu_custom_call" | custom-call | flops 24999999488 | bytes 1024 | tf_op jit(solution)/shard_map/pallas_call | solution.py:182
  215.4 4.7 collective-permute-start.21
  221.1 2.8 collective-permute-done.21.refs_1_
  223.9 8.9 %collective-permute-done.22.refs_2_ = bf16[384,128]{1,0:T(8,128)(2,1)S(1)} collective-permute-done((bf16[384,128]{1,0:T(8,128)(2,1)}, bf16[384,128]{1,0:T(8,128)(2,1)S(1)}, u32[]{:S(2)}, u32[]{:S(2)}) %collective-permute-start.22) | collective-permute-done | bytes 98336 | tf_op jit(solution)/shard_map/ppermute | solution.py:848
  233.9 2.6 fusion.3
  236.6 1.7 collective-permute-start.24
  238.3 8.9 %collective-permute-done.24 = bf16[128,1536]{1,0:T(8,128)(2,1)S(1)} collective-permute-done((bf16[128,1536]{1,0:T(8,128)(2,1)S(1)}, bf16[128,1536]{1,0:T(8,128)(2,1)S(1)}, u32[]{:S(2)}, u32[]{:S(2)}) %collective-permute-start.24) | collective-permute-done | bytes 393248 | tf_op jit(solution)/shard_map/ppermute | solution.py:793
  249.7 8.2 %collective-permute-done.25 = bf16[128,1536]{1,0:T(8,128)(2,1)S(1)} collective-permute-done((bf16[128,1536]{1,0:T(8,128)(2,1)S(1)}, bf16[128,1536]{1,0:T(8,128)(2,1)S(1)}, u32[]{:S(2)}, u32[]{:S(2)}) %collective-permute-start.25) | collective-permute-done | bytes 393248 | tf_op jit(solution)/shard_map/ppermute | solution.py:793
  257.9 15.0 %shard_map.330 = (bf16[1,256,2048]{2,1,0:T(8,128)(2,1)}, bf16[2,256,2048]{2,1,0:T(8,128)(2,1)}, f32[128,1536]{1,0:T(8,128)S(1)}, bf16[128,1536]{1,0:T(8,128)(2,1...) custom-call(bf16[256,1536]{1,0:T(8,128)(2,1)S(1)} %pad_maximum_fusion.7.normed_ref.values_ref, ...), custom_call_target="tpu_custom_call" | custom-call | flops 1024 | bytes 1024 | tf_op jit(solution)/shard_map/pallas_call | solution.py:749
  274.9 6.9 %collective-permute-done.26 = bf16[128,1536]{1,0:T(8,128)(2,1)S(1)} collective-permute-done((bf16[128,1536]{1,0:T(8,128)(2,1)S(1)}, bf16[128,1536]{1,0:T(8,128)(2,1)S(1)}, u32[]{:S(2)}, u32[]{:S(2)}) %collective-permute-start.26) | collective-permute-done | bytes 393248 | tf_op jit(solution)/shard_map/ppermute | solution.py:793
  289.4 3.4 collective-permute-done.27
  295.7 2.6 fusion.1.grad_ref
  299.2 9.9 %collective-permute-start.29 = (bf16[384,128]{1,0:T(8,128)(2,1)S(1)}, bf16[384,128]{1,0:T(8,128)(2,1)S(1)}, u32[]{:S(2)}, u32[]{:S(2)}) collective-permute-start(bf16[384,128]{1,0:T(8,128)(2,1)S(1)} %get-tuple-element.186), channel_id=1, source_target_pairs={{0,8},{2,10},{4,12},{6,14},{8,16},{10,18},{12,20},{14,22},{16,24},... | collective-permute-start | bytes 294920 | tf_op jit(solution)/shard_map/ppermute | solution.py:848
  309.1 2.4 collective-permute-start.31
  311.5 12.7 %shard_map.334 = bf16[768,6144]{1,0:T(8,128)(2,1)} custom-call(bf16[768,256]{1,0:T(8,128)(2,1)S(1)} %get-tuple-element.189.refs_0_, bf16[768,256]{1,0:T(8,128)(2,1)S(1)} %collective-permute-done.32.refs_1_, bf16[2,256,2048]{2,1,0:T(8,128)(2,1)S(1)} %copy-done.4, bf16[2,256,2048]{2,1,0:T(8,128)(2,1)} %collective-permute-done.33.refs_3_, ...), custom_call_target="tpu_custom_call" | custom-call | flops 1024 | bytes 1024 | tf_op jit(solution)/shard_map/pallas_call | solution.py:674
  325.0 24.7 %shard_map.337 = (f32[3072,128]{1,0:T(8,128)}, bf16[3,1024,128]{2,1,0:T(8,128)(2,1)}, bf16[3,1024,128]{2,1,0:T(8,128)(2,1)}, bf16[3,192,128]{2,1,0:T(8,128)(2,1)}, bf16[3,192,128]{2,1,0:T(8,128)(2,1)}) custom-call(bf16[3648,128]{1,0:T(8,128)(2,1)} %collective-permute-done.18.refs_0_, bf16[3648,128]{1,0:T(8,128)(2,1)} %collective-permute-done.20.refs_1_, ...), custom_call_target="tpu_custom_call" | custom-call | flops 24999999488 | bytes 1024 | tf_op jit(solution)/shard_map/pallas_call | solution.py:309
  350.3 2.2 collective-permute-done.40
  356.5 25.5 %shard_map.338 = (bf16[384,128]{1,0:T(8,128)(2,1)}, bf16[384,128]{1,0:T(8,128)(2,1)}, bf16[384,128]{1,0:T(8,128)(2,1)}, bf16[384,128]{1,0:T(8,128)(2,1)}, f32[3,...) custom-call(bf16[3648,128]{1,0:T(8,128)(2,1)} %get-tuple-element.164, ...), custom_call_target="tpu_custom_call" | custom-call | flops 24999999488 | bytes 1024 | tf_op jit(solution)/shard_map/pallas_call | solution.py:309
  382.1 17.3 %collective-permute-done.42 = bf16[3,1216,128]{2,1,0:T(8,128)(2,1)} collective-permute-done((bf16[3,1216,128]{2,1,0:T(8,128)(2,1)}, bf16[3,1216,128]{2,1,0:T(8,128)(2,1)}, u32[]{:S(2)}, u32[]{:S(2)}) %collective-permute-start.42) | collective-permute-done | bytes 933920 | tf_op jit(solution)/shard_map/ppermute | solution.py:844
  401.0 2.0 collective-permute-start.43
  405.4 16.4 %collective-permute-done.43.refs_1_ = bf16[1152,128]{1,0:T(8,128)(2,1)S(1)} collective-permute-done((bf16[1152,128]{1,0:T(8,128)(2,1)S(1)}, bf16[1152,128]{1,0:T(8,128)(2,1)S(1)}, u32[]{:S(2)}, u32[]{:S(2)}) %collective-permute-start.43) | collective-permute-done | bytes 294944 | tf_op jit(solution)/shard_map/ppermute | solution.py:848
  421.8 7.5 %collective-permute-done.44.refs_2_ = bf16[1152,128]{1,0:T(8,128)(2,1)S(1)} collective-permute-done((bf16[1152,128]{1,0:T(8,128)(2,1)S(1)}, bf16[1152,128]{1,0:T(8,128)(2,1)S(1)}, u32[]{:S(2)}, u32[]{:S(2)}) %collective-permute-start.44) | collective-permute-done | bytes 294944 | tf_op jit(solution)/shard_map/ppermute | solution.py:848
  429.2 12.5 %collective-permute-done.45.refs_3_ = bf16[1152,128]{1,0:T(8,128)(2,1)S(1)} collective-permute-done((bf16[1152,128]{1,0:T(8,128)(2,1)S(1)}, bf16[1152,128]{1,0:T(8,128)(2,1)S(1)}, u32[]{:S(2)}, u32[]{:S(2)}) %collective-permute-start.45) | collective-permute-done | bytes 294944 | tf_op jit(solution)/shard_map/ppermute | solution.py:848
  441.8 5.1 shard_map.340
  454.9 1.8 collective-permute-start.28
  457.0 3.4 collective-permute-start.49
  460.8 6.5 %fusion.61 = f32[256,1536]{1,0:T(8,128)} fusion(bf16[256,2304]{1,0:T(8,128)(2,1)} %get-tuple-element.230, bf16[1536,2304]{1,0:T(8,128)(2,1)} %all-gather.3.cloned.1.call-done), kind=kOutput, calls=%fused_computation.209 | convolution fusion | flops 1811939328 | bytes 9830400 | tf_op jit(solution)/shard_map/dot_general | solution.py:31
  467.3 6.2 %shard_map.342 = bf16[768,3072]{1,0:T(8,128)(2,1)} custom-call(bf16[768,256]{1,0:T(8,128)(2,1)S(1)} %copy-done.13, bf16[768,256]{1,0:T(8,128)(2,1)S(1)} %copy-done.15, bf16[1,256,2304]{2,1,0:T(8,128)(2,1)} %bitcast.44.refs_2_, bf16[1,256,2304]{2,1,0:T(8,128)(2,1)S(1)} %collective-permute-done.47.refs_3_, bf16[768,256]{1,0:T(8,128)(2,1)S(1)} %copy-done.17, ...), custom_call_target="tpu_custom_call" | custom-call | flops 1024 | bytes 1024 | tf_op jit(solution)/shard_map/pallas_call | solution.py:674
  473.9 2.1 slice.281
  476.8 9.8 %collective-permute-done.51 = bf16[128,1536]{1,0:T(8,128)(2,1)} collective-permute-done((bf16[128,1536]{1,0:T(8,128)(2,1)}, bf16[128,1536]{1,0:T(8,128)(2,1)}, u32[]{:S(2)}, u32[]{:S(2)}) %collective-permute-start.51) | collective-permute-done | bytes 393248 | tf_op jit(solution)/shard_map/ppermute | solution.py:793
  486.6 4.6 select_reduce_fusion.1
  494.3 3.6 collective-permute-done.52
  505.4 6.7 %collective-permute-done.57 = f32[4,9216]{1,0:T(4,128)S(1)} collective-permute-done((f32[4,9216]{1,0:T(4,128)S(1)}, f32[4,9216]{1,0:T(4,128)S(1)}, u32[]{:S(2)}, u32[]{:S(2)}) %collective-permute-start.57) | collective-permute-done | bytes 147488 | tf_op jit(solution)/shard_map/ppermute | solution.py:844
  513.4 8.4 %collective-permute-done.58 = f32[4,9216]{1,0:T(4,128)S(1)} collective-permute-done((f32[4,9216]{1,0:T(4,128)S(1)}, f32[4,9216]{1,0:T(4,128)S(1)}, u32[]{:S(2)}, u32[]{:S(2)}) %collective-permute-start.58) | collective-permute-done | bytes 147488 | tf_op jit(solution)/shard_map/ppermute | solution.py:844
  524.2 3.9 all-to-all-start.1
  528.1 9.5 %collective-permute-done.59 = f32[4,9216]{1,0:T(4,128)S(1)} collective-permute-done((f32[4,9216]{1,0:T(4,128)S(1)}, f32[4,9216]{1,0:T(4,128)S(1)}, u32[]{:S(2)}, u32[]{:S(2)}) %collective-permute-start.59) | collective-permute-done | bytes 147488 | tf_op jit(solution)/shard_map/ppermute | solution.py:844
  538.3 1.9 fusion.54
  541.6 3.2 collective-permute-done.61
  545.6 3.2 collective-permute-done.62
  551.0 3.1 collective-permute-done.63
  (467 shorter events, 92.9 us)
Async XLA Ops:
  7.2 80.4 %all-gather.3.cloned.1.call-start = ((), (), s32[]{:S(2)}) async-start(), calls=%async_computation.4 | async-start | bytes 7520256 | tf_op jit(solution)/shard_map/all_gather | solution.py:917
  10.0 23.8 %all-to-all-start = ((bf16[48,16,256]{2,0,1:T(8,128)(2,1)}), bf16[48,16,256]{2,0,1:T(8,128)(2,1)S(1)}, u32[]{:S(2)}, u32[]{:S(2)}) async-start(bf16[48,16,256]{2,0,1:T(8,128)(2,1)} %bitcast.116), calls=%async_computation | async-start | bytes 786432 | tf_op jit(solution)/shard_map/all_to_all | solution.py:937
  17.4 216.5 %all-gather.5.cloned.1.call-start = ((), (), s32[]{:S(2)}) async-start(), calls=%async_computation.5 | async-start | bytes 22560768 | tf_op jit(solution)/shard_map/all_gather | solution.py:1038
  17.8 5.8 %collective-permute-start.7 = (f32[3,6144]{1,0:T(4,128)S(1)}, f32[3,6144]{1,0:T(4,128)S(1)}, u32[]{:S(2)}, u32[]{:S(2)}) collective-permute-start(f32[3,6144]{1,0:T(4,128)S(1)} %fusion.17), channel_id=1, source_target_pairs={{0,2},{2,0},{4,6},{6,4},{8,10},{10,8},{12,14},{14,12},{16,18},{18,... | collective-permute-start | bytes 221192 | tf_op jit(solution)/shard_map/ppermute | solution.py:844
  23.7 8.5 %collective-permute-start.8 = (f32[3,6144]{1,0:T(4,128)S(1)}, f32[3,6144]{1,0:T(4,128)S(1)}, u32[]{:S(2)}, u32[]{:S(2)}) collective-permute-start(f32[3,6144]{1,0:T(4,128)S(1)} %add.411), channel_id=1, source_target_pairs={{0,4},{2,6},{4,0},{6,2},{8,12},{10,14},{12,8},{14,10},{16,20},{18,... | collective-permute-start | bytes 221192 | tf_op jit(solution)/shard_map/ppermute | solution.py:844
  32.2 11.9 %collective-permute-start.9 = (f32[3,6144]{1,0:T(4,128)S(1)}, f32[3,6144]{1,0:T(4,128)S(1)}, u32[]{:S(2)}, u32[]{:S(2)}) collective-permute-start(f32[3,6144]{1,0:T(4,128)S(1)} %add.412), channel_id=1, source_target_pairs={{0,8},{2,10},{4,12},{6,14},{8,0},{10,2},{12,4},{14,6},{16,24},{18,... | collective-permute-start | bytes 221192 | tf_op jit(solution)/shard_map/ppermute | solution.py:844
  33.8 11.0 %collective-permute-start = (f32[4,3072]{1,0:T(4,128)S(1)}, f32[4,3072]{1,0:T(4,128)S(1)}, u32[]{:S(2)}, u32[]{:S(2)}) collective-permute-start(f32[4,3072]{1,0:T(4,128)S(1)} %pad_maximum_fusion.16), channel_id=1, source_target_pairs={{0,2},{2,0},{4,6},{6,4},{8,10},{10,8},{12,14},{14,12},{16,18},{18,... | collective-permute-start | bytes 147464 | tf_op jit(solution)/shard_map/ppermute | solution.py:844
  44.1 6.6 %collective-permute-start.10 = (f32[3,6144]{1,0:T(4,128)S(1)}, f32[3,6144]{1,0:T(4,128)S(1)}, u32[]{:S(2)}, u32[]{:S(2)}) collective-permute-start(f32[3,6144]{1,0:T(4,128)S(1)} %add.413), channel_id=1, source_target_pairs={{0,16},{2,18},{4,20},{6,22},{8,24},{10,26},{12,28},{14,30},{16,0},... | collective-permute-start | bytes 221192 | tf_op jit(solution)/shard_map/ppermute | solution.py:844
  44.8 6.0 %collective-permute-start.1 = (f32[4,3072]{1,0:T(4,128)S(1)}, f32[4,3072]{1,0:T(4,128)S(1)}, u32[]{:S(2)}, u32[]{:S(2)}) collective-permute-start(f32[4,3072]{1,0:T(4,128)S(1)} %add.395), channel_id=1, source_target_pairs={{0,4},{2,6},{4,0},{6,2},{8,12},{10,14},{12,8},{14,10},{16,20},{18,... | collective-permute-start | bytes 147464 | tf_op jit(solution)/shard_map/ppermute | solution.py:844
  50.8 7.1 %collective-permute-start.2 = (f32[4,3072]{1,0:T(4,128)S(1)}, f32[4,3072]{1,0:T(4,128)S(1)}, u32[]{:S(2)}, u32[]{:S(2)}) collective-permute-start(f32[4,3072]{1,0:T(4,128)S(1)} %add.396), channel_id=1, source_target_pairs={{0,8},{2,10},{4,12},{6,14},{8,0},{10,2},{12,4},{14,6},{16,24},{18,... | collective-permute-start | bytes 147464 | tf_op jit(solution)/shard_map/ppermute | solution.py:844
  57.9 9.0 %collective-permute-start.3 = (f32[4,3072]{1,0:T(4,128)S(1)}, f32[4,3072]{1,0:T(4,128)S(1)}, u32[]{:S(2)}, u32[]{:S(2)}) collective-permute-start(f32[4,3072]{1,0:T(4,128)S(1)} %add.397), channel_id=1, source_target_pairs={{0,16},{2,18},{4,20},{6,22},{8,24},{10,26},{12,28},{14,30},{16,0},... | collective-permute-start | bytes 147464 | tf_op jit(solution)/shard_map/ppermute | solution.py:844
  59.8 12.7 %collective-permute-start.5 = (bf16[384,1536]{1,0:T(8,128)(2,1)S(1)}, bf16[384,1536]{1,0:T(8,128)(2,1)S(1)}, u32[]{:S(2)}, u32[]{:S(2)}) collective-permute-start(bf16[384,1536]{1,0:T(8,128)(2,1)S(1)} %slice.279), channel_id=1, source_target_pairs={{0,2},{2,0},{4,6},{6,4},{8,10},{10,8},{12,14},{14,12},{16,18},{18,... | collective-permute-start | bytes 3538952 | tf_op jit(solution)/shard_map/ppermute | solution.py:844
  67.5 8.9 %collective-permute-start.4 = (bf16[128,1536]{1,0:T(8,128)(2,1)S(1)}, bf16[128,1536]{1,0:T(8,128)(2,1)S(1)}, u32[]{:S(2)}, u32[]{:S(2)}) collective-permute-start(bf16[128,1536]{1,0:T(8,128)(2,1)S(1)} %fusion.10), channel_id=1, source_target_pairs={{0,1},{1,0},{2,3},{3,2},{4,5},{5,4},{6,7},{7,6},{8,9},{9,8},{10,11... | collective-permute-start | bytes 1179656 | tf_op jit(solution)/shard_map/ppermute | solution.py:793
  72.9 13.1 %collective-permute-start.6 = (bf16[192,1536]{1,0:T(8,128)(2,1)S(1)}, bf16[192,1536]{1,0:T(8,128)(2,1)S(1)}, u32[]{:S(2)}, u32[]{:S(2)}) collective-permute-start(bf16[192,1536]{1,0:T(8,128)(2,1)S(1)} %slice.280), channel_id=1, source_target_pairs={{0,4},{2,6},{4,0},{6,2},{8,12},{10,14},{12,8},{14,10},{16,20},{18,... | collective-permute-start | bytes 1769480 | tf_op jit(solution)/shard_map/ppermute | solution.py:844
  87.6 404.0 %reduce-scatter.3.cloned.1.call-start = ((), (), s32[]{:S(2)}) async-start(), calls=%async_computation.6 | async-start | bytes 10616832 | tf_op jit(solution)/shard_map/reduce_scatter | solution.py:913
  88.8 17.3 %collective-permute-start.11 = (bf16[192,384]{1,0:T(8,128)(2,1)}, bf16[192,384]{1,0:T(8,128)(2,1)S(1)}, u32[]{:S(2)}, u32[]{:S(2)}) collective-permute-start(bf16[192,384]{1,0:T(8,128)(2,1)} %get-tuple-element.148), channel_id=1, source_target_pairs={{0,8},{2,10},{4,12},{6,14},{8,16},{10,18},{12,20},{14,22},{16,24},... | collective-permute-start | bytes 442376 | tf_op jit(solution)/shard_map/ppermute | solution.py:848
  88.9 17.9 %collective-permute-start.12 = (bf16[192,384]{1,0:T(8,128)(2,1)S(1)}, bf16[192,384]{1,0:T(8,128)(2,1)S(1)}, u32[]{:S(2)}, u32[]{:S(2)}) collective-permute-start(bf16[192,384]{1,0:T(8,128)(2,1)S(1)} %get-tuple-element.149), channel_id=1, source_target_pairs={{0,16},{2,18},{4,20},{6,22},{8,24},{10,26},{12,28},{14,30},{16,0},... | collective-permute-start | bytes 442376 | tf_op jit(solution)/shard_map/ppermute | solution.py:848
  92.3 15.2 %collective-permute-start.13 = (bf16[192,384]{1,0:T(8,128)(2,1)S(1)}, bf16[192,384]{1,0:T(8,128)(2,1)S(1)}, u32[]{:S(2)}, u32[]{:S(2)}) collective-permute-start(bf16[192,384]{1,0:T(8,128)(2,1)S(1)} %get-tuple-element.150), channel_id=1, source_target_pairs={{0,24},{2,26},{4,28},{6,30},{8,0},{10,2},{12,4},{14,6},{16,8},{18,... | collective-permute-start | bytes 442376 | tf_op jit(solution)/shard_map/ppermute | solution.py:848
  95.6 22.8 %collective-permute-start.17 = (bf16[128,1536]{1,0:T(8,128)(2,1)}, bf16[128,1536]{1,0:T(8,128)(2,1)}, u32[]{:S(2)}, u32[]{:S(2)}) collective-permute-start(bf16[128,1536]{1,0:T(8,128)(2,1)} %fusion.12), channel_id=1, source_target_pairs={{0,1},{1,0},{2,3},{3,2},{4,5},{5,4},{6,7},{7,6},{8,9},{9,8},{10,11... | collective-permute-start | bytes 1179656 | tf_op jit(solution)/shard_map/ppermute | solution.py:793
  108.1 18.5 %collective-permute-start.14 = (bf16[1152,128]{1,0:T(8,128)(2,1)}, bf16[1152,128]{1,0:T(8,128)(2,1)}, u32[]{:S(2)}, u32[]{:S(2)}) collective-permute-start(bf16[1152,128]{1,0:T(8,128)(2,1)} %get-tuple-element.152), channel_id=1, source_target_pairs={{0,8},{2,10},{4,12},{6,14},{8,16},{10,18},{12,20},{14,22},{16,24},... | collective-permute-start | bytes 884744 | tf_op jit(solution)/shard_map/ppermute | solution.py:848
  112.3 27.8 %collective-permute-start.15 = (bf16[1152,128]{1,0:T(8,128)(2,1)}, bf16[1152,128]{1,0:T(8,128)(2,1)}, u32[]{:S(2)}, u32[]{:S(2)}) collective-permute-start(bf16[1152,128]{1,0:T(8,128)(2,1)} %get-tuple-element.153), channel_id=1, source_target_pairs={{0,16},{2,18},{4,20},{6,22},{8,24},{10,26},{12,28},{14,30},{16,0},... | collective-permute-start | bytes 884744 | tf_op jit(solution)/shard_map/ppermute | solution.py:848
  112.3 38.1 %collective-permute-start.16 = (bf16[1152,128]{1,0:T(8,128)(2,1)}, bf16[1152,128]{1,0:T(8,128)(2,1)}, u32[]{:S(2)}, u32[]{:S(2)}) collective-permute-start(bf16[1152,128]{1,0:T(8,128)(2,1)} %get-tuple-element.154), channel_id=1, source_target_pairs={{0,24},{2,26},{4,28},{6,30},{8,0},{10,2},{12,4},{14,6},{16,8},{18,... | collective-permute-start | bytes 884744 | tf_op jit(solution)/shard_map/ppermute | solution.py:848
  156.0 43.3 %collective-permute-start.18 = (bf16[3648,128]{1,0:T(8,128)(2,1)}, bf16[3648,128]{1,0:T(8,128)(2,1)}, u32[]{:S(2)}, u32[]{:S(2)}) collective-permute-start(bf16[3648,128]{1,0:T(8,128)(2,1)} %get-tuple-element.164.refs_0_), channel_id=1, source_target_pairs={{0,4},{2,6},{4,0},{6,2},{8,12},{10,14},{12,8},{14,10},{16,20},{18,... | collective-permute-start | bytes 2801672 | tf_op jit(solution)/shard_map/ppermute | solution.py:844
  215.4 8.5 %collective-permute-start.21 = (bf16[384,128]{1,0:T(8,128)(2,1)}, bf16[384,128]{1,0:T(8,128)(2,1)S(1)}, u32[]{:S(2)}, u32[]{:S(2)}) collective-permute-start(bf16[384,128]{1,0:T(8,128)(2,1)} %get-tuple-element.174), channel_id=1, source_target_pairs={{0,24},{2,26},{4,28},{6,30},{8,0},{10,2},{12,4},{14,6},{16,8},{18,... | collective-permute-start | bytes 294920 | tf_op jit(solution)/shard_map/ppermute | solution.py:848
  220.1 12.6 %collective-permute-start.22 = (bf16[384,128]{1,0:T(8,128)(2,1)}, bf16[384,128]{1,0:T(8,128)(2,1)S(1)}, u32[]{:S(2)}, u32[]{:S(2)}) collective-permute-start(bf16[384,128]{1,0:T(8,128)(2,1)} %get-tuple-element.175), channel_id=1, source_target_pairs={{0,16},{2,18},{4,20},{6,22},{8,24},{10,26},{12,28},{14,30},{16,0},... | collective-permute-start | bytes 294920 | tf_op jit(solution)/shard_map/ppermute | solution.py:848
  220.1 12.6 %collective-permute-start.23 = (bf16[384,128]{1,0:T(8,128)(2,1)}, bf16[384,128]{1,0:T(8,128)(2,1)S(1)}, u32[]{:S(2)}, u32[]{:S(2)}) collective-permute-start(bf16[384,128]{1,0:T(8,128)(2,1)} %get-tuple-element.176), channel_id=1, source_target_pairs={{0,8},{2,10},{4,12},{6,14},{8,16},{10,18},{12,20},{14,22},{16,24},... | collective-permute-start | bytes 294920 | tf_op jit(solution)/shard_map/ppermute | solution.py:848
  236.6 10.6 %collective-permute-start.24 = (bf16[128,1536]{1,0:T(8,128)(2,1)S(1)}, bf16[128,1536]{1,0:T(8,128)(2,1)S(1)}, u32[]{:S(2)}, u32[]{:S(2)}) collective-permute-start(bf16[128,1536]{1,0:T(8,128)(2,1)S(1)} %slice.282), channel_id=1, source_target_pairs={{0,1},{1,0},{2,3},{3,2},{4,5},{5,4},{6,7},{7,6},{8,9},{9,8},{10,11... | collective-permute-start | bytes 1179656 | tf_op jit(solution)/shard_map/ppermute | solution.py:793
  248.2 9.7 %collective-permute-start.25 = (bf16[128,1536]{1,0:T(8,128)(2,1)S(1)}, bf16[128,1536]{1,0:T(8,128)(2,1)S(1)}, u32[]{:S(2)}, u32[]{:S(2)}) collective-permute-start(bf16[128,1536]{1,0:T(8,128)(2,1)S(1)} %fusion.16), channel_id=1, source_target_pairs={{0,1},{1,0},{2,3},{3,2},{4,5},{5,4},{6,7},{7,6},{8,9},{9,8},{10,11... | collective-permute-start | bytes 1179656 | tf_op jit(solution)/shard_map/ppermute | solution.py:793
  273.0 8.8 %collective-permute-start.26 = (bf16[128,1536]{1,0:T(8,128)(2,1)S(1)}, bf16[128,1536]{1,0:T(8,128)(2,1)S(1)}, u32[]{:S(2)}, u32[]{:S(2)}) collective-permute-start(bf16[128,1536]{1,0:T(8,128)(2,1)S(1)} %get-tuple-element.181), channel_id=1, source_target_pairs={{0,1},{1,0},{2,3},{3,2},{4,5},{5,4},{6,7},{7,6},{8,9},{9,8},{10,11... | collective-permute-start | bytes 1179656 | tf_op jit(solution)/shard_map/ppermute | solution.py:793
  274.3 34.8 %collective-permute-start.33 = (bf16[2,256,2048]{2,1,0:T(8,128)(2,1)}, bf16[2,256,2048]{2,1,0:T(8,128)(2,1)}, u32[]{:S(2)}, u32[]{:S(2)}) collective-permute-start(bf16[2,256,2048]{2,1,0:T(8,128)(2,1)} %get-tuple-element.191.refs_2_), channel_id=1, source_target_pairs={{0,2},{2,0},{4,6},{6,4},{8,10},{10,8},{12,14},{14,12},{16,18},{18,... | collective-permute-start | bytes 6291464 | tf_op jit(solution)/shard_map/ppermute | solution.py:844
  274.4 34.7 %collective-permute-start.35 = (bf16[1,256,2048]{2,1,0:T(8,128)(2,1)}, bf16[1,256,2048]{2,1,0:T(8,128)(2,1)}, u32[]{:S(2)}, u32[]{:S(2)}) collective-permute-start(bf16[1,256,2048]{2,1,0:T(8,128)(2,1)} %get-tuple-element.194.refs_6_), channel_id=1, source_target_pairs={{0,2},{2,0},{4,6},{6,4},{8,10},{10,8},{12,14},{14,12},{16,18},{18,... | collective-permute-start | bytes 3145736 | tf_op jit(solution)/shard_map/ppermute | solution.py:844
  284.7 8.1 %collective-permute-start.27 = (bf16[128,1536]{1,0:T(8,128)(2,1)}, bf16[128,1536]{1,0:T(8,128)(2,1)}, u32[]{:S(2)}, u32[]{:S(2)}) collective-permute-start(bf16[128,1536]{1,0:T(8,128)(2,1)} %get-tuple-element.371), channel_id=1, source_target_pairs={{0,1},{1,0},{2,3},{3,2},{4,5},{5,4},{6,7},{7,6},{8,9},{9,8},{10,11... | collective-permute-start | bytes 1179656 | tf_op jit(solution)/shard_map/ppermute | solution.py:793
  288.1 7.0 %collective-permute-start.36 = (bf16[768,256]{1,0:T(8,128)(2,1)S(1)}, bf16[768,256]{1,0:T(8,128)(2,1)S(1)}, u32[]{:S(2)}, u32[]{:S(2)}) collective-permute-start(bf16[768,256]{1,0:T(8,128)(2,1)S(1)} %get-tuple-element.196), channel_id=1, source_target_pairs={{0,2},{2,0},{4,6},{6,4},{8,10},{10,8},{12,14},{14,12},{16,18},{18,... | collective-permute-start | bytes 1179656 | tf_op jit(solution)/shard_map/ppermute | solution.py:844
  288.5 7.1 %collective-permute-start.34 = (bf16[768,256]{1,0:T(8,128)(2,1)S(1)}, bf16[768,256]{1,0:T(8,128)(2,1)S(1)}, u32[]{:S(2)}, u32[]{:S(2)}) collective-permute-start(bf16[768,256]{1,0:T(8,128)(2,1)S(1)} %get-tuple-element.193), channel_id=1, source_target_pairs={{0,2},{2,0},{4,6},{6,4},{8,10},{10,8},{12,14},{14,12},{16,18},{18,... | collective-permute-start | bytes 1179656 | tf_op jit(solution)/shard_map/ppermute | solution.py:844
  292.8 6.4 %collective-permute-start.32 = (bf16[768,256]{1,0:T(8,128)(2,1)S(1)}, bf16[768,256]{1,0:T(8,128)(2,1)S(1)}, u32[]{:S(2)}, u32[]{:S(2)}) collective-permute-start(bf16[768,256]{1,0:T(8,128)(2,1)S(1)} %get-tuple-element.190), channel_id=1, source_target_pairs={{0,2},{2,0},{4,6},{6,4},{8,10},{10,8},{12,14},{14,12},{16,18},{18,... | collective-permute-start | bytes 1179656 | tf_op jit(solution)/shard_map/ppermute | solution.py:844
  295.1 29.1 %collective-permute-start.38 = (bf16[1,256,768]{2,1,0:T(8,128)(2,1)S(1)}, bf16[1,256,768]{2,1,0:T(8,128)(2,1)}, u32[]{:S(2)}, u32[]{:S(2)}) collective-permute-start(bf16[1,256,768]{2,1,0:T(8,128)(2,1)S(1)} %bitcast.117), channel_id=1, source_target_pairs={{0,2},{2,0},{4,6},{6,4},{8,10},{10,8},{12,14},{14,12},{16,18},{18,... | collective-permute-start | bytes 1179656 | tf_op jit(solution)/shard_map/ppermute | solution.py:844
  295.6 28.6 %collective-permute-start.37 = (bf16[768,256]{1,0:T(8,128)(2,1)S(1)}, bf16[768,256]{1,0:T(8,128)(2,1)}, u32[]{:S(2)}, u32[]{:S(2)}) collective-permute-start(bf16[768,256]{1,0:T(8,128)(2,1)S(1)} %get-tuple-element.198), channel_id=1, source_target_pairs={{0,2},{2,0},{4,6},{6,4},{8,10},{10,8},{12,14},{14,12},{16,18},{18,... | collective-permute-start | bytes 1179656 | tf_op jit(solution)/shard_map/ppermute | solution.py:844
  299.2 25.1 %collective-permute-start.29 = (bf16[384,128]{1,0:T(8,128)(2,1)S(1)}, bf16[384,128]{1,0:T(8,128)(2,1)S(1)}, u32[]{:S(2)}, u32[]{:S(2)}) collective-permute-start(bf16[384,128]{1,0:T(8,128)(2,1)S(1)} %get-tuple-element.186), channel_id=1, source_target_pairs={{0,8},{2,10},{4,12},{6,14},{8,16},{10,18},{12,20},{14,22},{16,24},... | collective-permute-start | bytes 294920 | tf_op jit(solution)/shard_map/ppermute | solution.py:848
  309.1 15.1 %collective-permute-start.30 = (bf16[384,128]{1,0:T(8,128)(2,1)S(1)}, bf16[384,128]{1,0:T(8,128)(2,1)}, u32[]{:S(2)}, u32[]{:S(2)}) collective-permute-start(bf16[384,128]{1,0:T(8,128)(2,1)S(1)} %get-tuple-element.187), channel_id=1, source_target_pairs={{0,16},{2,18},{4,20},{6,22},{8,24},{10,26},{12,28},{14,30},{16,0},... | collective-permute-start | bytes 294920 | tf_op jit(solution)/shard_map/ppermute | solution.py:848
  309.1 15.1 %collective-permute-start.31 = (bf16[384,128]{1,0:T(8,128)(2,1)S(1)}, bf16[384,128]{1,0:T(8,128)(2,1)}, u32[]{:S(2)}, u32[]{:S(2)}) collective-permute-start(bf16[384,128]{1,0:T(8,128)(2,1)S(1)} %get-tuple-element.188), channel_id=1, source_target_pairs={{0,24},{2,26},{4,28},{6,30},{8,0},{10,2},{12,4},{14,6},{16,8},{18,... | collective-permute-start | bytes 294920 | tf_op jit(solution)/shard_map/ppermute | solution.py:848
  324.8 234.9 %reduce-scatter.5.cloned.1.call-start = ((), (), s32[]{:S(2)}) async-start(), calls=%async_computation.7 | async-start | bytes 5308416 | tf_op jit(solution)/shard_map/reduce_scatter | solution.py:913
  349.7 3.7 collective-permute-start.39
  355.8 43.7 %collective-permute-start.42 = (bf16[3,1216,128]{2,1,0:T(8,128)(2,1)}, bf16[3,1216,128]{2,1,0:T(8,128)(2,1)}, u32[]{:S(2)}, u32[]{:S(2)}) collective-permute-start(bf16[3,1216,128]{2,1,0:T(8,128)(2,1)} %pad_maximum_fusion.4), channel_id=1, source_target_pairs={{0,4},{2,6},{4,0},{6,2},{8,12},{10,14},{12,8},{14,10},{16,20},{18,... | collective-permute-start | bytes 2801672 | tf_op jit(solution)/shard_map/ppermute | solution.py:844
  382.0 18.7 %collective-permute-start.41 = (bf16[3,1024,128]{2,1,0:T(8,128)(2,1)}, bf16[3,1024,128]{2,1,0:T(8,128)(2,1)S(1)}, u32[]{:S(2)}, u32[]{:S(2)}) collective-permute-start(bf16[3,1024,128]{2,1,0:T(8,128)(2,1)} %get-tuple-element.215), channel_id=1, source_target_pairs={{0,2},{2,0},{4,6},{6,4},{8,10},{10,8},{12,14},{14,12},{16,18},{18,... | collective-permute-start | bytes 2359304 | tf_op jit(solution)/shard_map/ppermute | solution.py:844
  401.0 20.8 %collective-permute-start.43 = (bf16[1152,128]{1,0:T(8,128)(2,1)S(1)}, bf16[1152,128]{1,0:T(8,128)(2,1)S(1)}, u32[]{:S(2)}, u32[]{:S(2)}) collective-permute-start(bf16[1152,128]{1,0:T(8,128)(2,1)S(1)} %get-tuple-element.222), channel_id=1, source_target_pairs={{0,24},{2,26},{4,28},{6,30},{8,0},{10,2},{12,4},{14,6},{16,8},{18,... | collective-permute-start | bytes 884744 | tf_op jit(solution)/shard_map/ppermute | solution.py:848
  403.0 26.2 %collective-permute-start.44 = (bf16[1152,128]{1,0:T(8,128)(2,1)S(1)}, bf16[1152,128]{1,0:T(8,128)(2,1)S(1)}, u32[]{:S(2)}, u32[]{:S(2)}) collective-permute-start(bf16[1152,128]{1,0:T(8,128)(2,1)S(1)} %get-tuple-element.223), channel_id=1, source_target_pairs={{0,16},{2,18},{4,20},{6,22},{8,24},{10,26},{12,28},{14,30},{16,0},... | collective-permute-start | bytes 884744 | tf_op jit(solution)/shard_map/ppermute | solution.py:848
  403.0 38.7 %collective-permute-start.45 = (bf16[1152,128]{1,0:T(8,128)(2,1)S(1)}, bf16[1152,128]{1,0:T(8,128)(2,1)S(1)}, u32[]{:S(2)}, u32[]{:S(2)}) collective-permute-start(bf16[1152,128]{1,0:T(8,128)(2,1)S(1)} %get-tuple-element.224), channel_id=1, source_target_pairs={{0,8},{2,10},{4,12},{6,14},{8,16},{10,18},{12,20},{14,22},{16,24},... | collective-permute-start | bytes 884744 | tf_op jit(solution)/shard_map/ppermute | solution.py:848
  446.9 20.4 %collective-permute-start.47 = (bf16[1,256,2304]{2,1,0:T(8,128)(2,1)}, bf16[1,256,2304]{2,1,0:T(8,128)(2,1)S(1)}, u32[]{:S(2)}, u32[]{:S(2)}) collective-permute-start(bf16[1,256,2304]{2,1,0:T(8,128)(2,1)} %bitcast.44.refs_2_), channel_id=1, source_target_pairs={{0,2},{2,0},{4,6},{6,4},{8,10},{10,8},{12,14},{14,12},{16,18},{18,... | collective-permute-start | bytes 3538952 | tf_op jit(solution)/shard_map/ppermute | solution.py:844
  454.9 21.9 %collective-permute-start.28 = (bf16[128,1536]{1,0:T(8,128)(2,1)S(1)}, bf16[128,1536]{1,0:T(8,128)(2,1)}, u32[]{:S(2)}, u32[]{:S(2)}) collective-permute-start(bf16[128,1536]{1,0:T(8,128)(2,1)S(1)} %copy-done.36), channel_id=1, source_target_pairs={{0,1},{1,0},{2,3},{3,2},{4,5},{5,4},{6,7},{7,6},{8,9},{9,8},{10,11... | collective-permute-start | bytes 1179656 | tf_op jit(solution)/shard_map/ppermute | solution.py:793
  457.0 16.6 %collective-permute-start.48 = (bf16[192,384]{1,0:T(8,128)(2,1)S(1)}, bf16[192,384]{1,0:T(8,128)(2,1)S(1)}, u32[]{:S(2)}, u32[]{:S(2)}) collective-permute-start(bf16[192,384]{1,0:T(8,128)(2,1)S(1)} %get-tuple-element.241.refs_0_), channel_id=1, source_target_pairs={{0,24},{2,26},{4,28},{6,30},{8,0},{10,2},{12,4},{14,6},{16,8},{18,... | collective-permute-start | bytes 442376 | tf_op jit(solution)/shard_map/ppermute | solution.py:848
  457.0 16.8 %collective-permute-start.49 = (bf16[192,384]{1,0:T(8,128)(2,1)S(1)}, bf16[192,384]{1,0:T(8,128)(2,1)S(1)}, u32[]{:S(2)}, u32[]{:S(2)}) collective-permute-start(bf16[192,384]{1,0:T(8,128)(2,1)S(1)} %get-tuple-element.241.refs_0_), channel_id=1, source_target_pairs={{0,16},{2,18},{4,20},{6,22},{8,24},{10,26},{12,28},{14,30},{16,0},... | collective-permute-start | bytes 442376 | tf_op jit(solution)/shard_map/ppermute | solution.py:848
  460.4 13.4 %collective-permute-start.50 = (bf16[192,384]{1,0:T(8,128)(2,1)S(1)}, bf16[192,384]{1,0:T(8,128)(2,1)S(1)}, u32[]{:S(2)}, u32[]{:S(2)}) collective-permute-start(bf16[192,384]{1,0:T(8,128)(2,1)S(1)} %get-tuple-element.241.refs_0_), channel_id=1, source_target_pairs={{0,8},{2,10},{4,12},{6,14},{8,16},{10,18},{12,20},{14,22},{16,24},... | collective-permute-start | bytes 442376 | tf_op jit(solution)/shard_map/ppermute | solution.py:848
  475.9 10.7 %collective-permute-start.51 = (bf16[128,1536]{1,0:T(8,128)(2,1)}, bf16[128,1536]{1,0:T(8,128)(2,1)}, u32[]{:S(2)}, u32[]{:S(2)}) collective-permute-start(bf16[128,1536]{1,0:T(8,128)(2,1)} %slice.281), channel_id=1, source_target_pairs={{0,1},{1,0},{2,3},{3,2},{4,5},{5,4},{6,7},{7,6},{8,9},{9,8},{10,11... | collective-permute-start | bytes 1179656 | tf_op jit(solution)/shard_map/ppermute | solution.py:793
  476.4 16.6 %collective-permute-start.53 = (bf16[192,1536]{1,0:T(8,128)(2,1)S(1)}, bf16[192,1536]{1,0:T(8,128)(2,1)}, u32[]{:S(2)}, u32[]{:S(2)}) collective-permute-start(bf16[192,1536]{1,0:T(8,128)(2,1)S(1)} %shard_map.343), channel_id=1, source_target_pairs={{0,4},{2,6},{4,0},{6,2},{8,12},{10,14},{12,8},{14,10},{16,20},{18,... | collective-permute-start | bytes 1769480 | tf_op jit(solution)/shard_map/ppermute | solution.py:844
  492.7 5.2 collective-permute-start.52
  494.2 3.8 collective-permute-start.54
  500.1 12.1 %collective-permute-start.55 = (bf16[768,256]{1,0:T(8,128)(2,1)S(1)}, bf16[768,256]{1,0:T(8,128)(2,1)}, u32[]{:S(2)}, u32[]{:S(2)}) collective-permute-start(bf16[768,256]{1,0:T(8,128)(2,1)S(1)} %convolution_convert_fusion), channel_id=1, source_target_pairs={{0,1},{1,0},{2,3},{3,2},{4,5},{5,4},{6,7},{7,6},{8,9},{9,8},{10,11... | collective-permute-start | bytes 1179656 | tf_op jit(solution)/shard_map/ppermute | solution.py:793
  502.4 9.7 %collective-permute-start.57 = (f32[4,9216]{1,0:T(4,128)S(1)}, f32[4,9216]{1,0:T(4,128)S(1)}, u32[]{:S(2)}, u32[]{:S(2)}) collective-permute-start(f32[4,9216]{1,0:T(4,128)S(1)} %add.477), channel_id=1, source_target_pairs={{0,4},{2,6},{4,0},{6,2},{8,12},{10,14},{12,8},{14,10},{16,20},{18,... | collective-permute-start | bytes 442376 | tf_op jit(solution)/shard_map/ppermute | solution.py:844
  512.2 9.6 %collective-permute-start.58 = (f32[4,9216]{1,0:T(4,128)S(1)}, f32[4,9216]{1,0:T(4,128)S(1)}, u32[]{:S(2)}, u32[]{:S(2)}) collective-permute-start(f32[4,9216]{1,0:T(4,128)S(1)} %add.478), channel_id=1, source_target_pairs={{0,8},{2,10},{4,12},{6,14},{8,0},{10,2},{12,4},{14,6},{16,24},{18,... | collective-permute-start | bytes 442376 | tf_op jit(solution)/shard_map/ppermute | solution.py:844
  521.8 15.7 %collective-permute-start.59 = (f32[4,9216]{1,0:T(4,128)S(1)}, f32[4,9216]{1,0:T(4,128)S(1)}, u32[]{:S(2)}, u32[]{:S(2)}) collective-permute-start(f32[4,9216]{1,0:T(4,128)S(1)} %add.479), channel_id=1, source_target_pairs={{0,16},{2,18},{4,20},{6,22},{8,24},{10,26},{12,28},{14,30},{16,0},... | collective-permute-start | bytes 442376 | tf_op jit(solution)/shard_map/ppermute | solution.py:844
  524.2 30.5 %all-to-all-start.1 = ((bf16[16,48,256]{2,1,0:T(8,128)(2,1)}), bf16[16,48,256]{2,1,0:T(8,128)(2,1)S(1)}, u32[]{:S(2)}, u32[]{:S(2)}) async-start(bf16[16,48,256]{2,1,0:T(8,128)(2,1)} %bitcast.52), calls=%async_computation.1 | async-start | bytes 786432 | tf_op jit(solution)/shard_map/all_to_all | solution.py:1249
  541.0 3.9 collective-permute-start.61
  544.9 3.9 collective-permute-start.62
  548.8 5.3 collective-permute-start.63
  (112 other events, 1111.0 us)
Sparse Core Ops, SparseCore 0:
  10.9 75.6 all-gather.2
  88.8 144.3 all-gather.4
  324.4 126.8 reduce-scatter.2
  491.8 67.9 reduce-scatter.4
